TPU v7x, 32 devices: a whole 2x2x4 slice. The times are simulated.
32 devices in a mesh: pipe: 4 (over z), expert: 4 (over y, x), dp: 2 (over core).
Axes of the slice: x: 2, y: 2, z: 4, core: 2. Of those that a mesh axis runs over, the one named last changes fastest.
Arguments:
- section_inputs: bfloat16 [4, 256, 2048], P('pipe', ('expert', 'dp')), may hold values from -6 to 6
- saved_inputs: bfloat16 [4, 256, 2048], P('pipe', ('expert', 'dp')), may hold values from -6 to 6
- output_grads: bfloat16 [4, 256, 2048], P('pipe', ('expert', 'dp')), may hold values from -6 to 6
- forward_routes: int32 [4, 256, 8], P('pipe', ('expert', 'dp')), may hold values from 0 to 63, as said below
- backward_routes: int32 [4, 256, 8], P('pipe', ('expert', 'dp')), may hold values from 0 to 63, as said below
- forward_gates: float32 [4, 256, 8], P('pipe', ('expert', 'dp')), may hold values from 0.1 to 0.9
- backward_gates: float32 [4, 256, 8], P('pipe', ('expert', 'dp')), may hold values from 0.1 to 0.9
- expert_weights: bfloat16 [4, 64, 2048, 768], P('pipe', 'expert'), may hold values from -0.125 to 0.125
Outputs:
- next_inputs: bfloat16 [4, 256, 2048], P('pipe', ('expert', 'dp'))
- prior_grads: bfloat16 [4, 256, 2048], P('pipe', ('expert', 'dp'))
- weight_grads: bfloat16 [4, 64, 2048, 768], P('pipe', 'expert', 'dp')
Inputs may be any that keep to these rules, and one draw needn't show every extreme that they name: `forward_routes`: each token names 8 different experts. Among the tokens of one aligned block of 32 (the tokens of one device) no expert is named more than 5 times, and in each section one expert is named exactly 5 times in every block. `backward_routes`: as for forward_routes.
All inputs are finite; a program needn't handle non-finite values.
Results may differ from a plain program's by a relative error of at most 0.012.
Values may be sent and summed in bfloat16 or wider, within the bound.
No kernel may reach another device: no remote copies, remote signals or barrier semaphores. Data moves between devices by JAX's collectives and lax.ppermute only.
A program may use at most 320 MiB of HBM per device.

v0:
```python
import jax
import jax.numpy as jnp
from jax import lax
from jax.sharding import PartitionSpec as P

CAP = 5


def shifted(value, axis, steps):
    count = lax.axis_size(axis)
    pairs = [(source, (source + steps) % count) for source in range(count)]
    return lax.ppermute(value, axis, pairs)


def slot_index(routing, experts, capacity):
    one_hot = (routing[..., None] == jnp.arange(experts, dtype=jnp.int32)).astype(jnp.int32)
    before = jnp.cumsum(one_hot, axis=-2) - one_hot
    return routing * capacity + jnp.sum(before * one_hot, axis=-1)


def pack_rows(source, slot_ids, slot_total, spread):
    row_count = slot_ids.shape[0]
    owner_row = (
        jnp.zeros((slot_total,), jnp.int32)
        .at[slot_ids]
        .set(jnp.arange(row_count, dtype=jnp.int32) + 1)
    )
    filled = owner_row > 0
    picked = jnp.take(source, jnp.maximum(owner_row - 1, 0) // spread, axis=0)
    return jnp.where(filled[:, None], picked, jnp.zeros_like(picked))


def expert_forward(slot_rows, weights):
    hidden = jnp.einsum("nlcd,ldh->nlch", slot_rows, weights, preferred_element_type=jnp.float32)
    active = jax.nn.silu(hidden).astype(jnp.bfloat16)
    return jnp.einsum("nlch,ldh->nlcd", active, weights, preferred_element_type=jnp.float32).astype(
        jnp.bfloat16
    )


def expert_backward(saved_rows, slot_grads, weights):
    hidden = jnp.einsum("nlcd,ldh->nlch", saved_rows, weights, preferred_element_type=jnp.float32)
    active = jax.nn.silu(hidden).astype(jnp.bfloat16)
    active_grads = jnp.einsum(
        "nlcd,ldh->nlch", slot_grads, weights, preferred_element_type=jnp.float32
    )
    sigma = jax.nn.sigmoid(hidden)
    hidden_grads = (active_grads * sigma * (1.0 + hidden * (1.0 - sigma))).astype(jnp.bfloat16)
    row_grads = jnp.einsum(
        "nlch,ldh->nlcd", hidden_grads, weights, preferred_element_type=jnp.float32
    ).astype(jnp.bfloat16)
    weight_part = jnp.einsum(
        "nlcd,nlch->ldh", saved_rows, hidden_grads, preferred_element_type=jnp.float32
    )
    weight_part = weight_part + jnp.einsum(
        "nlcd,nlch->ldh", slot_grads, active, preferred_element_type=jnp.float32
    )
    return (row_grads, weight_part)


def on_device(
    section_inputs,
    saved_inputs,
    output_grads,
    forward_routes,
    backward_routes,
    forward_gates,
    backward_gates,
    expert_weights,
):
    token_count = section_inputs.shape[1]
    route_count = forward_routes.shape[2]
    local_count = expert_weights.shape[1]
    model_width = expert_weights.shape[2]
    groups = lax.axis_size("expert")
    experts = groups * local_count
    slot_total = experts * CAP
    block_shape = (groups, local_count, CAP, model_width)
    weights = expert_weights[0]
    forward_slot = slot_index(forward_routes[0].reshape(-1), experts, CAP)
    backward_slot = slot_index(backward_routes[0].reshape(-1), experts, CAP)
    forward_rows = pack_rows(section_inputs[0], forward_slot, slot_total, route_count).reshape(
        block_shape
    )
    saved_rows = pack_rows(saved_inputs[0], backward_slot, slot_total, route_count).reshape(
        block_shape
    )
    grad_block = output_grads[0]
    scaled = backward_gates[0][:, :, None] * grad_block.astype(jnp.float32)[:, None, :]
    scaled = scaled.astype(jnp.bfloat16).reshape(token_count * route_count, model_width)
    slot_grads = pack_rows(scaled, backward_slot, slot_total, 1).reshape(block_shape)
    forward_back = lax.all_to_all(
        expert_forward(
            lax.all_to_all(forward_rows, "expert", split_axis=0, concat_axis=0, tiled=True), weights
        ),
        "expert",
        split_axis=0,
        concat_axis=0,
        tiled=True,
    )
    saved_recv, grads_recv = (
        lax.all_to_all(saved_rows, "expert", split_axis=0, concat_axis=0, tiled=True),
        lax.all_to_all(slot_grads, "expert", split_axis=0, concat_axis=0, tiled=True),
    )
    row_grads, weight_part = expert_backward(saved_recv, grads_recv, weights)
    grads_back = lax.all_to_all(row_grads, "expert", split_axis=0, concat_axis=0, tiled=True)
    forward_pick = jnp.take(forward_back.reshape(slot_total, model_width), forward_slot, axis=0)
    forward_pick = forward_pick.reshape(token_count, route_count, model_width).astype(jnp.float32)
    layer_out = section_inputs[0].astype(jnp.float32) + jnp.sum(
        forward_gates[0][:, :, None] * forward_pick, axis=1
    )
    layer_out = layer_out.astype(jnp.bfloat16)
    grads_pick = jnp.take(grads_back.reshape(slot_total, model_width), backward_slot, axis=0)
    grads_pick = grads_pick.reshape(token_count, route_count, model_width).astype(jnp.float32)
    input_grads = (grad_block.astype(jnp.float32) + jnp.sum(grads_pick, axis=1)).astype(
        jnp.bfloat16
    )
    next_inputs = shifted(layer_out, "pipe", 1)[None]
    prior_grads = shifted(input_grads, "pipe", -1)[None]
    weight_grads = lax.psum_scatter(
        weight_part.astype(jnp.bfloat16), "dp", scatter_dimension=1, tiled=True
    )[None]
    return (next_inputs, prior_grads, weight_grads)


def solution(mesh):
    placed = (
        P("pipe", ("expert", "dp"), None),
        P("pipe", ("expert", "dp"), None),
        P("pipe", ("expert", "dp"), None),
        P("pipe", ("expert", "dp"), None),
        P("pipe", ("expert", "dp"), None),
        P("pipe", ("expert", "dp"), None),
        P("pipe", ("expert", "dp"), None),
        P("pipe", "expert", None, None),
    )
    return jax.shard_map(
        on_device,
        mesh=mesh,
        in_specs=placed,
        out_specs=(
            P("pipe", ("expert", "dp"), None),
            P("pipe", ("expert", "dp"), None),
            P("pipe", "expert", "dp", None),
        ),
        check_vma=False,
    )
```

profile of v0, /device:TPU:0, one launch (start us, length us, event | category | flops | bytes accessed | tf_op | source)
XLA Modules:
  0.0 321.0 jit_solution(8674415091116090945)
XLA Ops:
  7.2 0.7 broadcast_multiply_fusion
  7.9 0.8 copy.38
  9.0 0.1 mul.89
  9.1 0.6 reduce-window.16
  9.7 0.2 slice_reduce_fusion
  9.9 0.1 fusion.67
  10.0 1.4 scatter_custom_fusion.1
  11.4 0.5 compare_and_fusion.1
  12.0 2.4 gather_fusion.3
  14.5 0.2 select_select_fusion.1
  14.7 0.6 reshape.160
  15.3 1.9 copy.45
  17.2 5.3 %all-to-all-start.3 = ((bf16[4,16,5,2048]{3,1,2,0:T(8,128)(2,1)}), bf16[4,16,5,2048]{3,1,2,0:T(8,128)(2,1)S(1)}, u32[]{:S(2)}, u32[]{:S(2)}) async-start(bf16[4,16,5,2048]{3,1,2,0:T(8,128)(2,1)} %copy.45), calls=%async_computation.3 | async-start | bytes 2621440 | tf_op jit(solution)/shard_map/all_to_all | solution.py:102
  22.5 0.1 broadcast_in_dim.72
  22.7 0.1 mul.91
  22.9 0.1 broadcast_in_dim.74
  23.0 0.2 fusion.29
  23.2 3.0 gather_fusion
  26.2 2.4 gather.13
  28.6 0.5 select_select_fusion
  29.1 1.9 copy.43
  31.0 7.9 %all-to-all-done.3 = bf16[4,16,5,2048]{3,1,2,0:T(8,128)(2,1)S(1)} async-done(((bf16[4,16,5,2048]{3,1,2,0:T(8,128)(2,1)}), bf16[4,16,5,2048]{3,1,2,0:T(8,128)(2,1)S(1)}, u32[]{:S(2)}, u32[]{:S(2)}) %all-to-all-start.3) | async-done | bytes 1310752 | tf_op jit(solution)/shard_map/all_to_all | solution.py:102
  38.9 4.3 %all-to-all-start.2 = ((bf16[4,16,5,2048]{3,1,2,0:T(8,128)(2,1)}), bf16[4,16,5,2048]{3,1,2,0:T(8,128)(2,1)}, u32[]{:S(2)}, u32[]{:S(2)}) async-start(bf16[4,16,5,2048]{3,1,2,0:T(8,128)(2,1)} %copy.43), calls=%async_computation.2 | async-start | bytes 2621440 | tf_op jit(solution)/shard_map/all_to_all | solution.py:103
  43.2 0.2 reduce-scatter.2.cloned.1.call-start
  43.5 20.3 %fusion.3 = f32[16,4,5,768]{3,2,1,0:T(8,128)S(1)} fusion(bf16[1,16,2048,768]{3,2,1,0:T(8,128)(2,1)} %param.19, bf16[4,16,5,2048]{3,1,2,0:T(8,128)(2,1)S(1)} %all-to-all-done.3), kind=kOutput, calls=%fused_computation.11 | convolution fusion | flops 1006632960 | bytes 52625408 | tf_op jit(solution)/shard_map/nlcd,ldh->nlch/dot_general | solution.py:42
  63.8 22.1 %fusion.5 = f32[16,4,5,768]{3,2,1,0:T(8,128)} fusion(bf16[1,16,2048,768]{3,2,1,0:T(8,128)(2,1)} %param.19, bf16[4,16,5,2048]{3,1,2,0:T(8,128)(2,1)} %all-to-all-done.2), kind=kOutput, calls=%fused_computation.13 | convolution fusion | flops 1006632960 | bytes 52625408 | tf_op jit(solution)/shard_map/nlcd,ldh->nlch/dot_general | solution.py:44
  85.9 36.4 %fusion.23 = f32[16,2048,768,1]{2,1,3,0:T(8,128)} fusion(bf16[4,16,5,2048]{3,1,2,0:T(8,128)(2,1)S(1)} %all-to-all-done.3, f32[16,4,5,768]{3,2,1,0:T(8,128)S(1)} %fusion.3, f32[16,4,5,768]{3,2,1,0:T(8,128)} %fusion.5), kind=kOutput, calls=%fused_computation.23 | convolution fusion | flops 1008844800 | bytes 103940096 | tf_op jit(solution)/shard_map/nlcd,nlch->ldh/dot_general | solution.py:52
  122.2 49.1 %fusion = bf16[16,2048,768]{2,1,0:T(8,128)(2,1)} fusion(f32[16,2048,768,1]{2,1,3,0:T(8,128)} %fusion.23, bf16[4,16,5,2048]{3,1,2,0:T(8,128)(2,1)} %all-to-all-done.2, f32[16,4,5,768]{3,2,1,0:T(8,128)S(1)} %fusion.3), kind=kOutput, calls=%fused_computation.8 | convolution fusion | flops 1058193408 | bytes 153288704 | tf_op jit(solution)/shard_map/nlcd,nlch->ldh/dot_general | solution.py:55
  171.4 0.7 copy-done.6
  172.5 0.6 reduce-window.14
  173.1 0.2 slice_reduce_fusion.1
  173.3 0.1 fusion.70
  173.4 1.6 scatter_custom_fusion
  175.1 2.4 gather_fusion.1
  177.5 0.2 select_select_fusion.2
  177.8 0.6 reshape.157
  178.3 1.9 copy.34
  180.2 4.5 %all-to-all-start = ((bf16[4,16,5,2048]{3,1,2,0:T(8,128)(2,1)}), bf16[4,16,5,2048]{3,1,2,0:T(8,128)(2,1)S(1)}, u32[]{:S(2)}, u32[]{:S(2)}) async-start(bf16[4,16,5,2048]{3,1,2,0:T(8,128)(2,1)} %copy.34), calls=%async_computation | async-start | bytes 2621440 | tf_op jit(solution)/shard_map/all_to_all | solution.py:94
  184.8 0.6 compare_and_fusion
  185.4 0.6 pad_clamp_fusion
  186.0 14.1 %all-to-all-done = bf16[4,16,5,2048]{3,1,2,0:T(8,128)(2,1)S(1)} async-done(((bf16[4,16,5,2048]{3,1,2,0:T(8,128)(2,1)}), bf16[4,16,5,2048]{3,1,2,0:T(8,128)(2,1)S(1)}, u32[]{:S(2)}, u32[]{:S(2)}) %all-to-all-start) | async-done | bytes 1310752 | tf_op jit(solution)/shard_map/all_to_all | solution.py:94
  200.1 50.6 %fusion.20 = bf16[4,16,5,2048]{3,2,0,1:T(8,128)(2,1)S(1)} fusion(bf16[1,16,2048,768]{3,2,1,0:T(8,128)(2,1)} %param.19, bf16[4,16,5,2048]{3,1,2,0:T(8,128)(2,1)S(1)} %all-to-all-done), kind=kOutput, calls=%fused_computation.22 | convolution fusion | flops 2015150080 | bytes 52953088 | tf_op jit(solution)/shard_map/nlch,ldh->nlcd/dot_general | solution.py:36
  250.7 1.9 copy.36
  252.6 3.5 %all-to-all-start.1 = ((bf16[4,16,5,2048]{3,1,2,0:T(8,128)(2,1)}), bf16[4,16,5,2048]{3,1,2,0:T(8,128)(2,1)S(1)}, u32[]{:S(2)}, u32[]{:S(2)}) async-start(bf16[4,16,5,2048]{3,1,2,0:T(8,128)(2,1)} %copy.36), calls=%async_computation.1 | async-start | bytes 2621440 | tf_op jit(solution)/shard_map/all_to_all | solution.py:92
  256.2 21.1 %fusion.17 = bf16[4,16,5,2048]{3,2,0,1:T(8,128)(2,1)S(1)} fusion(bf16[1,16,2048,768]{3,2,1,0:T(8,128)(2,1)} %param.19, f32[16,4,5,768]{3,2,1,0:T(8,128)} %copy-done.3, f32[16,4,5,768]{3,2,1,0:T(8,128)} %fusion.5), kind=kOutput, calls=%fused_computation.21 | convolution fusion | flops 1009500160 | bytes 53608448 | tf_op jit(solution)/shard_map/nlch,ldh->nlcd/dot_general | solution.py:49
  277.3 1.9 copy.47
  279.2 4.3 %all-to-all-start.4 = ((bf16[4,16,5,2048]{3,1,2,0:T(8,128)(2,1)}), bf16[4,16,5,2048]{3,1,2,0:T(8,128)(2,1)}, u32[]{:S(2)}, u32[]{:S(2)}) async-start(bf16[4,16,5,2048]{3,1,2,0:T(8,128)(2,1)} %copy.47), calls=%async_computation.4 | async-start | bytes 2621440 | tf_op jit(solution)/shard_map/all_to_all | solution.py:106
  283.5 0.6 compare_and_fusion.2
  284.1 0.6 pad_clamp_fusion.3
  284.7 0.8 copy.37
  285.6 0.6 reshape.158
  286.2 1.5 gather_fusion.2
  287.7 1.6 fusion.28
  289.2 0.7 add_convert_fusion.1
  289.9 1.9 collective-permute-start
  291.9 8.0 %all-to-all-done.4 = bf16[4,16,5,2048]{3,1,2,0:T(8,128)(2,1)} async-done(((bf16[4,16,5,2048]{3,1,2,0:T(8,128)(2,1)}), bf16[4,16,5,2048]{3,1,2,0:T(8,128)(2,1)}, u32[]{:S(2)}, u32[]{:S(2)}) %all-to-all-start.4) | async-done | bytes 1310752 | tf_op jit(solution)/shard_map/all_to_all | solution.py:106
  299.8 2.1 copy.48
  301.9 0.6 reshape.161
  302.5 1.6 gather_fusion.4
  304.2 0.9 convert_reduce_fusion
  305.2 3.8 %collective-permute-start.1 = (bf16[32,2048]{1,0:T(8,128)(2,1)S(1)}, bf16[32,2048]{1,0:T(8,128)(2,1)S(1)}, u32[]{:S(2)}, u32[]{:S(2)}) collective-permute-start(bf16[32,2048]{1,0:T(8,128)(2,1)S(1)} %add_convert_fusion), channel_id=1, source_target_pairs={{0,24},{8,0},{16,8},{24,16},{1,25},{9,1},{17,9},{25,17},{2,26},{10... | collective-permute-start | bytes 393224 | tf_op jit(solution)/shard_map/ppermute | solution.py:12
  308.9 2.5 collective-permute-done.1
  311.4 1.6 copy.77
  313.0 0.7 copy.78
  (73 shorter events, 1.1 us)
Async XLA Ops:
  7.2 4.9 %copy-start = (bf16[1,32,2048]{2,1,0:T(8,128)(2,1)S(1)}, bf16[1,32,2048]{2,1,0:T(8,128)(2,1)}, u32[]{:S(2)}) copy-start(bf16[1,32,2048]{2,1,0:T(8,128)(2,1)} %param.13) | copy-start | bytes 393220
  7.2 4.8 %copy-start.20 = (s32[256]{0:T(256)}, s32[256]{0:T(256)S(1)}, u32[]{:S(2)}) copy-start(s32[256]{0:T(256)S(1)} %iota_add_fusion) | copy-start | bytes 3076
  8.8 3.2 %copy-start.7 = (s32[256]{0:T(256)}, s32[256]{0:T(256)S(1)}, u32[]{:S(2)}) copy-start(s32[256]{0:T(256)S(1)} %eq.58) | copy-start | bytes 3076
  10.0 2.0 copy-start.9
  17.2 5.5 %copy-start.15 = (f32[1,32,8]{1,2,0:T(8,128)S(1)}, f32[1,32,8]{1,2,0:T(8,128)}, u32[]{:S(2)}) copy-start(f32[1,32,8]{1,2,0:T(8,128)} %param.18) | copy-start | bytes 3076
  17.2 5.6 %copy-start.19 = (pred[320]{0:T(512)(128)(4,1)S(1)}, pred[320]{0:T(512)(128)(4,1)}, u32[]{:S(2)}) copy-start(pred[320]{0:T(512)(128)(4,1)} %get-tuple-element.13) | copy-start | bytes 964
  17.2 5.8 %copy-start.4 = (bf16[1,32,2048]{2,1,0:T(8,128)(2,1)S(1)}, bf16[1,32,2048]{2,1,0:T(8,128)(2,1)}, u32[]{:S(2)}) copy-start(bf16[1,32,2048]{2,1,0:T(8,128)(2,1)} %param.14) | copy-start | bytes 393220
  17.2 21.7 %all-to-all-start.3 = ((bf16[4,16,5,2048]{3,1,2,0:T(8,128)(2,1)}), bf16[4,16,5,2048]{3,1,2,0:T(8,128)(2,1)S(1)}, u32[]{:S(2)}, u32[]{:S(2)}) async-start(bf16[4,16,5,2048]{3,1,2,0:T(8,128)(2,1)} %copy.45), calls=%async_computation.3 | async-start | bytes 2621440 | tf_op jit(solution)/shard_map/all_to_all | solution.py:102
  38.9 24.8 %all-to-all-start.2 = ((bf16[4,16,5,2048]{3,1,2,0:T(8,128)(2,1)}), bf16[4,16,5,2048]{3,1,2,0:T(8,128)(2,1)}, u32[]{:S(2)}, u32[]{:S(2)}) async-start(bf16[4,16,5,2048]{3,1,2,0:T(8,128)(2,1)} %copy.43), calls=%async_computation.2 | async-start | bytes 2621440 | tf_op jit(solution)/shard_map/all_to_all | solution.py:103
  43.2 268.2 %reduce-scatter.2.cloned.1.call-start = ((), (), s32[]{:S(2)}) async-start(), calls=%async_computation.6 | async-start | bytes 75497472 | tf_op jit(solution)/shard_map/reduce_scatter | solution.py:120
  63.8 58.5 %copy-start.3 = (f32[16,4,5,768]{3,2,1,0:T(8,128)}, f32[16,4,5,768]{3,2,1,0:T(8,128)S(1)}, u32[]{:S(2)}) copy-start(f32[16,4,5,768]{3,2,1,0:T(8,128)S(1)} %fusion.3) | copy-start | bytes 2949124
  171.3 0.7 copy-start.6
  172.0 3.0 copy-start.2
  172.2 2.9 copy-start.11
  173.4 1.6 copy-start.13
  180.2 4.5 %copy-start.16 = (f32[1,32,8]{1,2,0:T(8,128)S(1)}, f32[1,32,8]{1,2,0:T(8,128)}, u32[]{:S(2)}) copy-start(f32[1,32,8]{1,2,0:T(8,128)} %param.17) | copy-start | bytes 3076
  180.2 4.6 %copy-start.8 = (s32[256]{0:T(256)S(1)}, s32[256]{0:T(256)}, u32[]{:S(2)}) copy-start(s32[256]{0:T(256)} %copy-done.7) | copy-start | bytes 3076
  180.2 4.6 %copy-start.10 = (s32[256]{0:T(256)S(1)}, s32[256]{0:T(256)}, u32[]{:S(2)}) copy-start(s32[256]{0:T(256)} %copy-done.9) | copy-start | bytes 3076
  180.2 19.8 %all-to-all-start = ((bf16[4,16,5,2048]{3,1,2,0:T(8,128)(2,1)}), bf16[4,16,5,2048]{3,1,2,0:T(8,128)(2,1)S(1)}, u32[]{:S(2)}, u32[]{:S(2)}) async-start(bf16[4,16,5,2048]{3,1,2,0:T(8,128)(2,1)} %copy.34), calls=%async_computation | async-start | bytes 2621440 | tf_op jit(solution)/shard_map/all_to_all | solution.py:94
  252.6 26.6 %all-to-all-start.1 = ((bf16[4,16,5,2048]{3,1,2,0:T(8,128)(2,1)}), bf16[4,16,5,2048]{3,1,2,0:T(8,128)(2,1)S(1)}, u32[]{:S(2)}, u32[]{:S(2)}) async-start(bf16[4,16,5,2048]{3,1,2,0:T(8,128)(2,1)} %copy.36), calls=%async_computation.1 | async-start | bytes 2621440 | tf_op jit(solution)/shard_map/all_to_all | solution.py:92
  279.2 4.3 %copy-start.12 = (s32[256]{0:T(256)S(1)}, s32[256]{0:T(256)}, u32[]{:S(2)}) copy-start(s32[256]{0:T(256)} %copy-done.11) | copy-start | bytes 3076
  279.2 4.3 %copy-start.14 = (s32[256]{0:T(256)S(1)}, s32[256]{0:T(256)}, u32[]{:S(2)}) copy-start(s32[256]{0:T(256)} %copy-done.13) | copy-start | bytes 3076
  279.2 20.6 %all-to-all-start.4 = ((bf16[4,16,5,2048]{3,1,2,0:T(8,128)(2,1)}), bf16[4,16,5,2048]{3,1,2,0:T(8,128)(2,1)}, u32[]{:S(2)}, u32[]{:S(2)}) async-start(bf16[4,16,5,2048]{3,1,2,0:T(8,128)(2,1)} %copy.47), calls=%async_computation.4 | async-start | bytes 2621440 | tf_op jit(solution)/shard_map/all_to_all | solution.py:106
  286.1 1.5 copy-start.17
  289.9 19.0 %collective-permute-start = (bf16[32,2048]{1,0:T(8,128)(2,1)}, bf16[32,2048]{1,0:T(8,128)(2,1)}, u32[]{:S(2)}, u32[]{:S(2)}) collective-permute-start(bf16[32,2048]{1,0:T(8,128)(2,1)} %add_convert_fusion.1), channel_id=1, source_target_pairs={{0,8},{8,16},{16,24},{24,0},{1,9},{9,17},{17,25},{25,1},{2,10},{10... | collective-permute-start | bytes 393224 | tf_op jit(solution)/shard_map/ppermute | solution.py:12
  302.5 1.7 copy-start.18
  302.5 2.6 copy-start.5
  302.5 11.1 %copy-start.1 = (bf16[1,32,2048]{2,1,0:T(8,128)(2,1)S(1)}, bf16[1,32,2048]{2,1,0:T(8,128)(2,1)}, u32[]{:S(2)}) copy-start(bf16[1,32,2048]{2,1,0:T(8,128)(2,1)} %param.13) | copy-start | bytes 393220
  305.2 6.3 %collective-permute-start.1 = (bf16[32,2048]{1,0:T(8,128)(2,1)S(1)}, bf16[32,2048]{1,0:T(8,128)(2,1)S(1)}, u32[]{:S(2)}, u32[]{:S(2)}) collective-permute-start(bf16[32,2048]{1,0:T(8,128)(2,1)S(1)} %add_convert_fusion), channel_id=1, source_target_pairs={{0,24},{8,0},{16,8},{24,16},{1,25},{9,1},{17,9},{25,17},{2,26},{10... | collective-permute-start | bytes 393224 | tf_op jit(solution)/shard_map/ppermute | solution.py:12
Sparse Core Ops, SparseCore 0:
  171.5 65.0 reduce-scatter.1
where the time goes:
time: 327 us; the launch traced here: 321 us
  matrix products  200 us (61%)
  local copies, waits for them, and re-layouts  36.5 us (11%)
  waiting for transfers between devices  32.5 us (10%)
  starting transfers between devices  27.8 us (9%)
  between operations  15.1 us (5%)
  other arithmetic  9.55 us (3%)
    dot_general x1, matrix products, expert_forward(): jnp.einsum('nlch,ldh->nlcd', active, weights, preferred_element_type=jnp....  50.6 us
    dot_general x1, matrix products, expert_backward(): jnp.einsum('nlcd,nlch->ldh', slot_grads, active, preferred_element_type=j...  49.1 us
    dot_general x1, matrix products, expert_backward(): jnp.einsum('nlcd,nlch->ldh', saved_rows, hidden_grads, preferred_element_...  36.4 us
    dot_general x1, matrix products, expert_backward(): jnp.einsum('nlcd,ldh->nlch', slot_grads, weights, preferred_element_type=...  22.1 us
    dot_general x1, matrix products, expert_backward(): jnp.einsum('nlch,ldh->nlcd', hidden_grads, weights, preferred_element_typ...  21.1 us
    dot_general x1, matrix products, expert_backward(): jnp.einsum('nlcd,ldh->nlch', saved_rows, weights, preferred_element_type=...  20.3 us
    all_to_all x1, waiting for transfers between devices, on_device(): lax.all_to_all(forward_rows, 'expert', split_axis=0, concat_axis=0, tiled...  14.1 us
    gather x4, local copies, waits for them, and re-layouts, pack_rows(): picked = jnp.take(source, jnp.maximum(owner_row - 1, 0) // spread, axis=0)  10.2 us
  transfers between devices with their start and end apart: 8, of which 4 were waited for; matrix products, arithmetic and copies ran while one was open for 39% of the time, Pallas kernels for 0%

commit v1 on v0

--- a/solution.py
+++ b/solution.py
@@ -1,9 +1,16 @@
+import functools
+
 import jax
 import jax.numpy as jnp
 from jax import lax
+from jax.experimental import pallas as pl
+from jax.experimental.pallas import tpu as pltpu
 from jax.sharding import PartitionSpec as P
 
 CAP = 5
+LANES = 128
+CHUNK = 256
+VMEM_LIMIT = 48 * 1024 * 1024
 
 
 def shifted(value, axis, steps):
@@ -58,7 +65,7 @@
     return (row_grads, weight_part)
 
 
-def on_device(
+def packed_plan(
     section_inputs,
     saved_inputs,
     output_grads,
@@ -123,6 +130,346 @@
     return (next_inputs, prior_grads, weight_grads)
 
 
+def fill_picks(notes_ref, first, count, start, top, slots, picks, gates):
+    tokens = notes_ref.shape[0]
+    turned = notes_ref[...].T
+    ids = (first + lax.broadcasted_iota(jnp.int32, (count, tokens), 0)).astype(jnp.float32)
+    named = jnp.zeros((count, tokens), jnp.float32)
+    gated = jnp.zeros((count, tokens), jnp.float32)
+    for column in range(top):
+        same = turned[start + column : start + column + 1, :] == ids
+        named = named + jnp.where(same, 1.0, 0.0)
+        gated = gated + jnp.where(same, turned[start + top + column : start + top + column + 1, :], 0.0)
+    row = lax.broadcasted_iota(jnp.int32, (tokens, tokens), 0)
+    column = lax.broadcasted_iota(jnp.int32, (tokens, tokens), 1)
+    earlier = jnp.where(row < column, 1.0, 0.0).astype(jnp.bfloat16)
+    place = jnp.dot(named.astype(jnp.bfloat16), earlier, preferred_element_type=jnp.float32)
+    place = jnp.where(named > 0.0, place, -1.0)
+    slot = lax.broadcasted_iota(jnp.int32, (slots, tokens), 0).astype(jnp.float32)
+    for expert in range(count):
+        rows = pl.ds(expert * slots, slots)
+        hit = place[expert : expert + 1, :] == slot
+        picks[rows, :] = jnp.where(hit, 1.0, 0.0).astype(jnp.bfloat16)
+        own = jnp.sum(jnp.where(hit, gated[expert : expert + 1, :], 0.0), axis=1, keepdims=True)
+        gates[rows, :] = jnp.broadcast_to(own, (slots, LANES))
+
+
+def spread_gate(gates, rows, width):
+    return jnp.broadcast_to(gates[rows, 0:1], (gates[rows, 0:1].shape[0], width))
+
+
+def combine(picks, results, out_ref):
+    width = out_ref.shape[1]
+    for start in range(0, width, CHUNK):
+        columns = pl.ds(start, CHUNK)
+        out_ref[:, columns] = lax.dot_general(
+            picks[...],
+            results[:, columns],
+            (((0,), (0,)), ((), ())),
+            preferred_element_type=jnp.float32,
+        ).astype(out_ref.dtype)
+
+
+def forward_kernel(
+    count, top, slots, place_ref, notes_ref, tokens_ref, weights_ref, out_ref, picks, gates, rows, results
+):
+    step = pl.program_id(0)
+    width = tokens_ref.shape[1]
+
+    @pl.when(step == 0)
+    def _():
+        fill_picks(notes_ref, place_ref[1], count, 2 * top, top, slots, picks, gates)
+        for start in range(0, width, CHUNK):
+            columns = pl.ds(start, CHUNK)
+            rows[:, columns] = jnp.dot(
+                picks[...], tokens_ref[:, columns], preferred_element_type=jnp.float32
+            ).astype(rows.dtype)
+
+    mine = pl.ds(pl.multiple_of(step * slots, slots), slots)
+    hidden = jnp.dot(rows[mine, :], weights_ref[0], preferred_element_type=jnp.float32)
+    active = (hidden * jax.nn.sigmoid(hidden)).astype(jnp.bfloat16)
+    result = lax.dot_general(
+        active, weights_ref[0], (((1,), (1,)), ((), ())), preferred_element_type=jnp.float32
+    )
+    results[mine, :] = (result * spread_gate(gates, mine, width)).astype(results.dtype)
+
+    @pl.when(step == count - 1)
+    def _():
+        combine(picks, results, out_ref)
+
+
+def backward_kernel(
+    count,
+    top,
+    slots,
+    place_ref,
+    notes_ref,
+    saved_ref,
+    grads_ref,
+    weights_ref,
+    out_ref,
+    inner_ref,
+    picks,
+    gates,
+    rows,
+    results,
+):
+    step = pl.program_id(0)
+    width = saved_ref.shape[1]
+
+    @pl.when(step == 0)
+    def _():
+        fill_picks(notes_ref, place_ref[1], count, 0, top, slots, picks, gates)
+        gate = spread_gate(gates, pl.ds(0, count * slots), CHUNK)
+        for start in range(0, width, CHUNK):
+            columns = pl.ds(start, CHUNK)
+            saved = jnp.dot(
+                picks[...], saved_ref[:, columns], preferred_element_type=jnp.float32
+            ).astype(rows.dtype)
+            grads = jnp.dot(picks[...], grads_ref[:, columns], preferred_element_type=jnp.float32)
+            grads = (grads * gate).astype(rows.dtype)
+            for expert in range(count):
+                part = slice(expert * slots, (expert + 1) * slots)
+                rows[pl.ds(expert * 2 * slots, slots), columns] = saved[part]
+                rows[pl.ds(expert * 2 * slots + slots, slots), columns] = grads[part]
+
+    mine = pl.ds(pl.multiple_of(step * slots, slots), slots)
+    both = pl.ds(pl.multiple_of(step * 2 * slots, 2 * slots), 2 * slots)
+    product = jnp.dot(rows[both, :], weights_ref[0], preferred_element_type=jnp.float32)
+    hidden, active_grads = product[:slots], product[slots:]
+    sigma = jax.nn.sigmoid(hidden)
+    hidden_grads = (active_grads * sigma * (1.0 + hidden * (1.0 - sigma))).astype(jnp.bfloat16)
+    inner_ref[0, :slots, :] = hidden_grads
+    inner_ref[0, slots:, :] = (hidden * sigma).astype(jnp.bfloat16)
+    results[mine, :] = lax.dot_general(
+        hidden_grads, weights_ref[0], (((1,), (1,)), ((), ())), preferred_element_type=jnp.float32
+    ).astype(results.dtype)
+
+    @pl.when(step == count - 1)
+    def _():
+        combine(picks, results, out_ref)
+
+
+def weight_kernel(
+    count,
+    top,
+    slots,
+    place_ref,
+    notes_ref,
+    saved_ref,
+    grads_ref,
+    own_ref,
+    other_ref,
+    out_ref,
+    picks,
+    gates,
+    rows,
+):
+    step = pl.program_id(0)
+    width = saved_ref.shape[1]
+
+    def gather(first):
+        fill_picks(notes_ref, first, count, 0, top, slots, picks, gates)
+        gate = spread_gate(gates, pl.ds(0, count * slots), CHUNK)
+        for start in range(0, width, CHUNK):
+            columns = pl.ds(start, CHUNK)
+            saved = jnp.dot(
+                picks[...], saved_ref[:, columns], preferred_element_type=jnp.float32
+            ).astype(rows.dtype)
+            grads = jnp.dot(picks[...], grads_ref[:, columns], preferred_element_type=jnp.float32)
+            grads = (grads * gate).astype(rows.dtype)
+            for expert in range(count):
+                part = slice(expert * slots, (expert + 1) * slots)
+                rows[pl.ds(expert * 2 * slots, slots), columns] = saved[part]
+                rows[pl.ds(expert * 2 * slots + slots, slots), columns] = grads[part]
+
+    @pl.when(step == 0)
+    def _():
+        gather(place_ref[1])
+
+    @pl.when(step == count)
+    def _():
+        gather(place_ref[2])
+
+    def product(inner):
+        index = lax.rem(step, count)
+        both = pl.ds(pl.multiple_of(index * 2 * slots, 2 * slots), 2 * slots)
+        for start in range(0, width, CHUNK):
+            columns = pl.ds(start, CHUNK)
+            out_ref[0, columns, :] = lax.dot_general(
+                rows[both, columns],
+                inner,
+                (((0,), (0,)), ((), ())),
+                preferred_element_type=jnp.float32,
+            ).astype(out_ref.dtype)
+
+    @pl.when(step < count)
+    def _():
+        product(own_ref[0])
+
+    @pl.when(step >= count)
+    def _():
+        product(other_ref[0])
+
+
+def gathered_plan(
+    section_inputs,
+    saved_inputs,
+    output_grads,
+    forward_routes,
+    backward_routes,
+    forward_gates,
+    backward_gates,
+    expert_weights,
+):
+    token_count = section_inputs.shape[1]
+    top = forward_routes.shape[2]
+    _, local_count, width, inner_width = expert_weights.shape
+    groups, pair = lax.axis_size("expert"), lax.axis_size("dp")
+    count = local_count // pair
+    total = groups * pair * token_count
+    slots = -(-groups * pair * CAP // 16) * 16
+    half = width // pair
+    weights = expert_weights[0]
+
+    notes = jnp.concatenate(
+        [
+            backward_routes[0].astype(jnp.float32),
+            backward_gates[0],
+            forward_routes[0].astype(jnp.float32),
+            forward_gates[0],
+            jnp.zeros((token_count, LANES - 4 * top), jnp.float32),
+        ],
+        axis=1,
+    )
+    everyone = functools.partial(lax.all_gather, axis_name=("expert", "dp"), axis=0, tiled=True)
+    notes_all = everyone(notes)
+    inputs_all = everyone(section_inputs[0])
+    saved_all = everyone(saved_inputs[0])
+    grads_all = everyone(output_grads[0])
+
+    side = lax.axis_index("dp")
+    base = lax.axis_index("expert") * local_count
+    place = jnp.stack([side, base + side * count, base + (1 - side) * count]).astype(jnp.int32)
+
+    def whole(array):
+        return pl.BlockSpec(array.shape, lambda step, place: (0,) * array.ndim)
+
+    weight_spec = pl.BlockSpec(
+        (1, width, inner_width), lambda step, place: (place[0] * count + step, 0, 0)
+    )
+    sums = jax.ShapeDtypeStruct((total, width), jnp.bfloat16)
+    params = pltpu.CompilerParams(vmem_limit_bytes=VMEM_LIMIT, dimension_semantics=("arbitrary",))
+    pass_flops = 2 * 2 * count * CHUNK * width * inner_width
+    weight_bytes = count * width * inner_width * 2
+
+    layer_part = pl.pallas_call(
+        functools.partial(forward_kernel, count, top, slots),
+        grid_spec=pltpu.PrefetchScalarGridSpec(
+            num_scalar_prefetch=1,
+            grid=(count,),
+            in_specs=[whole(notes_all), whole(inputs_all), weight_spec],
+            out_specs=whole(sums),
+            scratch_shapes=[
+                pltpu.VMEM((count * slots, total), jnp.bfloat16),
+                pltpu.VMEM((count * slots, LANES), jnp.float32),
+                pltpu.VMEM((count * slots, width), jnp.bfloat16),
+                pltpu.VMEM((count * slots, width), jnp.bfloat16),
+            ],
+        ),
+        out_shape=sums,
+        compiler_params=params,
+        cost_estimate=pl.CostEstimate(
+            flops=pass_flops, bytes_accessed=weight_bytes, transcendentals=0
+        ),
+        name="expert_forward",
+    )(place, notes_all, inputs_all, weights)
+
+    inner = jax.ShapeDtypeStruct((count, 2 * slots, inner_width), jnp.bfloat16)
+    grad_part, inner_own = pl.pallas_call(
+        functools.partial(backward_kernel, count, top, slots),
+        grid_spec=pltpu.PrefetchScalarGridSpec(
+            num_scalar_prefetch=1,
+            grid=(count,),
+            in_specs=[whole(notes_all), whole(saved_all), whole(grads_all), weight_spec],
+            out_specs=[
+                whole(sums),
+                pl.BlockSpec((1, 2 * slots, inner_width), lambda step, place: (step, 0, 0)),
+            ],
+            scratch_shapes=[
+                pltpu.VMEM((count * slots, total), jnp.bfloat16),
+                pltpu.VMEM((count * slots, LANES), jnp.float32),
+                pltpu.VMEM((count * 2 * slots, width), jnp.bfloat16),
+                pltpu.VMEM((count * slots, width), jnp.bfloat16),
+            ],
+        ),
+        out_shape=[sums, inner],
+        compiler_params=params,
+        cost_estimate=pl.CostEstimate(
+            flops=pass_flops, bytes_accessed=weight_bytes, transcendentals=0
+        ),
+        name="expert_backward",
+    )(place, notes_all, saved_all, grads_all, weights)
+    inner_other = shifted(inner_own, "dp", 1)
+
+    def own_block(step, place):
+        return (jnp.minimum(step, count - 1), 0, 0)
+
+    def other_block(step, place):
+        return (jnp.maximum(step - count, 0), 0, 0)
+
+    def out_block(step, place):
+        side = jnp.where(step < count, place[0], 1 - place[0])
+        return (side * count + lax.rem(step, count), 0, 0)
+
+    half_spec = pl.BlockSpec((total, half), lambda step, place: (0, place[0]))
+    weight_grads = pl.pallas_call(
+        functools.partial(weight_kernel, count, top, slots),
+        grid_spec=pltpu.PrefetchScalarGridSpec(
+            num_scalar_prefetch=1,
+            grid=(2 * count,),
+            in_specs=[
+                whole(notes_all),
+                half_spec,
+                half_spec,
+                pl.BlockSpec((1, 2 * slots, inner_width), own_block),
+                pl.BlockSpec((1, 2 * slots, inner_width), other_block),
+            ],
+            out_specs=pl.BlockSpec((1, half, inner_width), out_block),
+            scratch_shapes=[
+                pltpu.VMEM((count * slots, total), jnp.bfloat16),
+                pltpu.VMEM((count * slots, LANES), jnp.float32),
+                pltpu.VMEM((count * 2 * slots, half), jnp.bfloat16),
+            ],
+        ),
+        out_shape=jax.ShapeDtypeStruct((local_count, half, inner_width), jnp.bfloat16),
+        compiler_params=params,
+        cost_estimate=pl.CostEstimate(
+            flops=pass_flops // 2, bytes_accessed=weight_bytes, transcendentals=0
+        ),
+        name="weight_gradient",
+    )(place, notes_all, saved_all, grads_all, inner_own, inner_other)
+
+    def home(part, own):
+        mine = lax.psum_scatter(part, ("expert", "dp"), scatter_dimension=0, tiled=True)
+        return (own.astype(jnp.float32) + mine.astype(jnp.float32)).astype(jnp.bfloat16)
+
+    next_inputs = shifted(home(layer_part, section_inputs[0]), "pipe", 1)[None]
+    prior_grads = shifted(home(grad_part, output_grads[0]), "pipe", -1)[None]
+    return (next_inputs, prior_grads, weight_grads[None])
+
+
+def on_device(*arrays):
+    token_count = arrays[0].shape[1]
+    local_count = arrays[-1].shape[1]
+    groups, pair = lax.axis_size("expert"), lax.axis_size("dp")
+    gathered = groups * token_count
+    packed = groups * local_count * CAP
+    if gathered <= packed and pair == 2 and local_count % pair == 0:
+        return gathered_plan(*arrays)
+    return packed_plan(*arrays)
+
+
 def solution(mesh):
     placed = (
         P("pipe", ("expert", "dp"), None),

time: 327 us -> 197 us (0.60); the launches traced: 321 us -> 196 us
  matrix products: 200 us -> 0 us
  waiting for transfers between devices: 32.5 us -> 97.7 us
  Pallas kernels: 0 us -> 56.9 us
  local copies, waits for them, and re-layouts: 36.5 us -> 9.08 us
  starting transfers between devices: 27.8 us -> 5.42 us
  blocking collectives: 0 us -> 10.7 us
  other arithmetic: 9.55 us -> 2.67 us
    dot_general x6 -> x0, matrix products: 200 us -> none  [the longest x1 50.6 us: expert_forward(): jnp.einsum('nlch,ldh->nlcd', active, weights, preferred_element_type=jnp....]
    pallas_call x0 -> x3, Pallas kernels: none -> 56.9 us  [the longest x1 19.3 us: gathered_plan(): pl.pallas_call(functools.partial(forward_kernel, count, top, slots), grid...]
    reduce_scatter x1 -> x2, waiting for transfers between devices: 0.01 us -> 52.5 us  [home(): lax.psum_scatter(part, ('expert', 'dp'), scatter_dimension=0, tiled=True)]
    all_gather x0 -> x3, waiting for transfers between devices: none -> 43 us  [the longest x1 25.4 us: gathered_plan(): grads_all = everyone(output_grads[0])]
    all_to_all x5 -> x0, waiting for transfers between devices: 30 us -> none  [the longest x1 14.1 us: on_device(): lax.all_to_all(forward_rows, 'expert', split_axis=0, concat_axis=0, tiled...]
    all_to_all x5 -> x0, starting transfers between devices: 21.9 us -> none  [the longest x1 5.29 us: on_device(): lax.all_to_all(saved_rows, 'expert', split_axis=0, concat_axis=0, tiled=T...]
    gather x6 -> x0, local copies, waits for them, and re-layouts: 13.4 us -> none  [the longest x4 10.2 us: pack_rows(): picked = jnp.take(source, jnp.maximum(owner_row - 1, 0) // spread, axis=0)]
    all_gather x0 -> x1, blocking collectives: none -> 10.7 us  [gathered_plan(): notes_all = everyone(notes)]
  transfers between devices with their start and end apart: 8 -> 8, of which waited for: 4 -> 5; matrix products, arithmetic and copies ran while one was open for 39% -> 3% of each run, Pallas kernels for 0% -> 29%
where the time goes in v1:
time: 197 us; the launch traced here: 196 us
  waiting for transfers between devices  97.7 us (50%)
  Pallas kernels  56.9 us (29%)
  between operations  13.8 us (7%)
  blocking collectives  10.7 us (5%)
  local copies, waits for them, and re-layouts  9.08 us (5%)
  starting transfers between devices  5.42 us (3%)
  other arithmetic  2.67 us (1%)
    reduce_scatter x2, waiting for transfers between devices, home(): lax.psum_scatter(part, ('expert', 'dp'), scatter_dimension=0, tiled=True)  52.5 us
    all_gather x1, waiting for transfers between devices, gathered_plan(): grads_all = everyone(output_grads[0])  25.4 us
    pallas_call x1, Pallas kernels, gathered_plan(): pl.pallas_call(functools.partial(forward_kernel, count, top, slots), grid...  19.3 us
    pallas_call x1, Pallas kernels, gathered_plan(): pl.pallas_call(functools.partial(backward_kernel, count, top, slots), gri...  19.3 us
    pallas_call x1, Pallas kernels, gathered_plan(): pl.pallas_call(functools.partial(weight_kernel, count, top, slots), grid_...  18.2 us
    all_gather x1, waiting for transfers between devices, gathered_plan(): inputs_all = everyone(section_inputs[0])  12.8 us
    all_gather x1, blocking collectives, gathered_plan(): notes_all = everyone(notes)  10.7 us
    unnamed x20, local copies, waits for them, and re-layouts  8.99 us
  transfers between devices with their start and end apart: 8, of which 5 were waited for; matrix products, arithmetic and copies ran while one was open for 3% of the time, Pallas kernels for 29%

profile of v1, /device:TPU:0, one launch (start us, length us, event | category | flops | bytes accessed | tf_op | source)
XLA Modules:
  0.0 196.2 jit_solution(2028256343072468169)
XLA Ops:
  7.2 0.0 all-gather.7.cloned.1.call-start
  7.2 0.7 all-gather.7.cloned.1.call-update
  7.9 0.0 all-gather.9.cloned.1.call-start
  7.9 0.7 all-gather.9.cloned.1.call-update
  8.6 0.0 all-gather.11.cloned.1.call-start
  8.7 0.7 all-gather.11.cloned.1.call-update
  9.4 0.0 reduce-scatter.3.cloned.1.call-start
  9.4 0.8 copy.13
  10.2 0.8 copy.11
  11.0 0.8 copy.14
  11.7 0.8 copy.12
  12.5 0.1 concatenate.3
  12.6 10.7 %all_gather.12.notes_ref = f32[256,128]{1,0:T(8,128)S(1)} all-gather(f32[32,128]{1,0:T(8,128)S(1)} %concatenate.3), channel_id=1, replica_groups=mesh['pipe'=4,'expert'=4,'dp'=2] {'expert','dp'}, dimensions={0}, use_global_device_ids=true | all-gather | bytes 147456 | tf_op jit(solution)/shard_map/all_gather | solution.py:346
  23.3 0.1 pad_add_fusion.place_ref
  23.3 12.8 %all-gather.7.cloned.1.call-done = bf16[1,256,2048]{2,1,0:T(8,128)(2,1)} async-done(((bf16[1,32,2048]{2,1,0:T(8,128)(2,1)}), bf16[1,256,2048]{2,1,0:T(8,128)(2,1)}) %all-gather.7.cloned.1.call-update) | async-done | bytes 1048592 | tf_op jit(solution)/shard_map/all_gather | solution.py:347
  36.1 0.0 copy-start.4
  36.1 1.2 copy-done.4
  37.4 19.3 %expert_forward.1 = bf16[256,2048]{1,0:T(8,128)(2,1)} custom-call(s32[3]{0:T(128)S(1)} %pad_add_fusion.place_ref, f32[256,128]{1,0:T(8,128)S(1)} %all_gather.12.notes_ref, bf16[256,2048]{1,0:T(8,128)(2,1)S(1)} %bitcast.26, bf16[16,2048,768]{2,1,0:T(8,128)(2,1)} %bitcast.27), custom_call_target="tpu_custom_call" | custom-call | flops 12884901888 | bytes 25165824 | tf_op jit(solution)/shard_map/expert_forward/pallas_call | solution.py:366
  56.7 0.0 reduce-scatter.3.cloned.1.call-update
  56.7 0.0 reduce-scatter.5.cloned.1.call-start
  56.7 4.8 %all-gather.9.cloned.1.call-done = bf16[1,256,2048]{2,1,0:T(8,128)(2,1)} async-done(((bf16[1,32,2048]{2,1,0:T(8,128)(2,1)}), bf16[1,256,2048]{2,1,0:T(8,128)(2,1)}) %all-gather.9.cloned.1.call-update) | async-done | bytes 1048592 | tf_op jit(solution)/shard_map/all_gather | solution.py:348
  61.6 25.4 %all-gather.11.cloned.1.call-done = bf16[1,256,2048]{2,1,0:T(8,128)(2,1)} async-done(((bf16[1,32,2048]{2,1,0:T(8,128)(2,1)}), bf16[1,256,2048]{2,1,0:T(8,128)(2,1)}) %all-gather.11.cloned.1.call-update) | async-done | bytes 1048592 | tf_op jit(solution)/shard_map/all_gather | solution.py:349
  87.0 0.0 copy-start
  87.0 1.2 copy-done
  88.2 0.0 copy-start.2
  88.2 1.2 copy-done.2
  89.4 0.0 copy-start.6
  89.4 0.0 copy-start.1
  89.4 0.0 copy-start.3
  89.4 19.3 %expert_backward.1 = (bf16[256,2048]{1,0:T(8,128)(2,1)S(1)}, bf16[8,96,768]{2,1,0:T(8,128)(2,1)S(1)}) custom-call(s32[3]{0:T(128)S(1)} %pad_add_fusion.place_ref, f32[256,128]{1,0:T(8,128)S(1)} %all_gather.12.notes_ref, bf16[256,2048]{1,0:T(8,128)(2,1)S(1)} %bitcast.22, bf16[256,2048]{1,0:T(8,128)(2,1)S(1)} %bitcast.24, bf16[16,2048,768]{2,1,0:T(8,128)(2,1)} %bitcast.28), custom_call_target="tpu_custom_call" | custom-call | flops 12884901888 | bytes 25165824 | tf_op jit(solution)/shard_map/expert_backward/pallas_call | solution.py:389
  108.8 0.0 copy-start.5
  108.8 0.9 copy-done.5
  109.7 0.0 reduce-scatter.5.cloned.1.call-update
  109.7 0.4 collective-permute-start.2
  110.1 16.6 %reduce-scatter.3.cloned.1.call-done = bf16[32,2048]{1,0:T(8,128)(2,1)} async-done(((bf16[256,2048]{1,0:T(8,128)(2,1)}), bf16[32,2048]{1,0:T(8,128)(2,1)}) %reduce-scatter.3.cloned.1.call-update) | async-done | bytes 131088 | tf_op jit(solution)/shard_map/reduce_scatter | solution.py:454
  126.7 0.0 copy-done.6
  126.7 1.6 fusion.1
  128.3 1.5 collective-permute-start
  129.7 36.0 %reduce-scatter.5.cloned.1.call-done = bf16[32,2048]{1,0:T(8,128)(2,1)} async-done(((bf16[256,2048]{1,0:T(8,128)(2,1)}), bf16[32,2048]{1,0:T(8,128)(2,1)}) %reduce-scatter.5.cloned.1.call-update) | async-done | bytes 131088 | tf_op jit(solution)/shard_map/reduce_scatter | solution.py:454
  165.7 1.0 fusion
  166.7 3.4 %collective-permute-start.1 = (bf16[32,2048]{1,0:T(8,128)(2,1)S(1)}, bf16[32,2048]{1,0:T(8,128)(2,1)S(1)}, u32[]{:S(2)}, u32[]{:S(2)}) collective-permute-start(bf16[32,2048]{1,0:T(8,128)(2,1)S(1)} %fusion), channel_id=1, source_target_pairs={{0,24},{8,0},{16,8},{24,16},{1,25},{9,1},{17,9},{25,17},{2,26},{10... | collective-permute-start | bytes 393224 | tf_op jit(solution)/shard_map/ppermute | solution.py:19
  170.1 0.0 collective-permute-done.2.other_ref
  170.1 0.0 copy-done.1
  170.1 0.0 copy-done.3
  170.1 18.2 %weight_gradient.1 = bf16[16,1024,768]{2,1,0:T(8,128)(2,1)} custom-call(s32[3]{0:T(128)S(1)} %pad_add_fusion.place_ref, f32[256,128]{1,0:T(8,128)S(1)} %all_gather.12.notes_ref, bf16[256,2048]{1,0:T(8,128)(2,1)S(1)} %bitcast.23, bf16[256,2048]{1,0:T(8,128)(2,1)S(1)} %bitcast.25, bf16[8,96,768]{2,1,0:T(8,128)(2,1)S(1)} %get-tuple-element.6.own_ref, ...), custom_call_target="tpu_custom_call" | custom-call | flops 6442450944 | bytes 25165824 | tf_op jit(solution)/shard_map/weight_gradient/pallas_call | solution.py:426
  188.3 0.0 collective-permute-done
  188.3 0.0 collective-permute-done.1
  188.3 0.7 copy.17
  189.0 0.7 copy.18
  (2 shorter events, 0.0 us)
Async XLA Ops:
  7.2 29.0 %all-gather.7.cloned.1.call-start = ((), (), s32[]{:S(2)}) async-start(), calls=%async_computation.4 | async-start | bytes 1179648 | tf_op jit(solution)/shard_map/all_gather | solution.py:347
  7.9 53.7 %all-gather.9.cloned.1.call-start = ((), (), s32[]{:S(2)}) async-start(), calls=%async_computation.5 | async-start | bytes 1179648 | tf_op jit(solution)/shard_map/all_gather | solution.py:348
  8.6 78.3 %all-gather.11.cloned.1.call-start = ((), (), s32[]{:S(2)}) async-start(), calls=%async_computation.6 | async-start | bytes 1179648 | tf_op jit(solution)/shard_map/all_gather | solution.py:349
  9.4 117.3 %reduce-scatter.3.cloned.1.call-start = ((), (), s32[]{:S(2)}) async-start(), calls=%async_computation.2 | async-start | bytes 1179648 | tf_op jit(solution)/shard_map/reduce_scatter | solution.py:454
  36.1 1.2 copy-start.4
  56.7 109.0 %reduce-scatter.5.cloned.1.call-start = ((), (), s32[]{:S(2)}) async-start(), calls=%async_computation.3 | async-start | bytes 1179648 | tf_op jit(solution)/shard_map/reduce_scatter | solution.py:454
  87.0 1.2 copy-start
  88.2 1.2 copy-start.2
  89.4 37.2 %copy-start.6 = (bf16[1,32,2048]{2,1,0:T(8,128)(2,1)S(1)}, bf16[1,32,2048]{2,1,0:T(8,128)(2,1)}, u32[]{:S(2)}) copy-start(bf16[1,32,2048]{2,1,0:T(8,128)(2,1)} %param.8) | copy-start | bytes 393220
  89.4 80.7 %copy-start.1 = (bf16[1,256,2048]{2,1,0:T(8,128)(2,1)S(1)}, bf16[1,256,2048]{2,1,0:T(8,128)(2,1)}, u32[]{:S(2)}) copy-start(bf16[1,256,2048]{2,1,0:T(8,128)(2,1)} %all-gather.9.cloned.1.call-done) | copy-start | bytes 3145732
  89.4 80.7 %copy-start.3 = (bf16[1,256,2048]{2,1,0:T(8,128)(2,1)S(1)}, bf16[1,256,2048]{2,1,0:T(8,128)(2,1)}, u32[]{:S(2)}) copy-start(bf16[1,256,2048]{2,1,0:T(8,128)(2,1)} %all-gather.11.cloned.1.call-done) | copy-start | bytes 3145732
  108.8 1.0 copy-start.5
  109.7 60.4 %collective-permute-start.2 = (bf16[8,96,768]{2,1,0:T(8,128)(2,1)S(1)}, bf16[8,96,768]{2,1,0:T(8,128)(2,1)}, u32[]{:S(2)}, u32[]{:S(2)}) collective-permute-start(bf16[8,96,768]{2,1,0:T(8,128)(2,1)S(1)} %get-tuple-element.6.own_ref), channel_id=1, source_target_pairs={{0,1},{1,0},{2,3},{3,2},{4,5},{5,4},{6,7},{7,6},{8,9},{9,8},{10,11... | collective-permute-start | bytes 3538952 | tf_op jit(solution)/shard_map/ppermute | solution.py:19
  128.3 60.1 %collective-permute-start = (bf16[32,2048]{1,0:T(8,128)(2,1)}, bf16[32,2048]{1,0:T(8,128)(2,1)S(1)}, u32[]{:S(2)}, u32[]{:S(2)}) collective-permute-start(bf16[32,2048]{1,0:T(8,128)(2,1)} %fusion.1), channel_id=1, source_target_pairs={{0,8},{8,16},{16,24},{24,0},{1,9},{9,17},{17,25},{25,1},{2,10},{10... | collective-permute-start | bytes 393224 | tf_op jit(solution)/shard_map/ppermute | solution.py:19
  166.7 21.6 %collective-permute-start.1 = (bf16[32,2048]{1,0:T(8,128)(2,1)S(1)}, bf16[32,2048]{1,0:T(8,128)(2,1)S(1)}, u32[]{:S(2)}, u32[]{:S(2)}) collective-permute-start(bf16[32,2048]{1,0:T(8,128)(2,1)S(1)} %fusion), channel_id=1, source_target_pairs={{0,24},{8,0},{16,8},{24,16},{1,25},{9,1},{17,9},{25,17},{2,26},{10... | collective-permute-start | bytes 393224 | tf_op jit(solution)/shard_map/ppermute | solution.py:19
Sparse Core Ops, SparseCore 0:
  9.9 26.1 all-gather.6
  38.0 23.4 all-gather.8
  63.4 23.4 all-gather.10
  90.6 36.0 reduce-scatter.2
  129.7 35.9 reduce-scatter.4

commit v2 on v0

--- a/solution.py
+++ b/solution.py
@@ -1,9 +1,16 @@
+import functools
+
 import jax
 import jax.numpy as jnp
 from jax import lax
+from jax.experimental import pallas as pl
+from jax.experimental.pallas import tpu as pltpu
 from jax.sharding import PartitionSpec as P
 
 CAP = 5
+LANES = 128
+CHUNK = 256
+VMEM_LIMIT = 48 * 1024 * 1024
 
 
 def shifted(value, axis, steps):
@@ -58,7 +65,7 @@
     return (row_grads, weight_part)
 
 
-def on_device(
+def packed_plan(
     section_inputs,
     saved_inputs,
     output_grads,
@@ -123,6 +130,400 @@
     return (next_inputs, prior_grads, weight_grads)
 
 
+def swapped(value, code):
+    axes = ("expert", "dp")
+    count = lax.axis_size(axes[0]) * lax.axis_size(axes[1])
+    return lax.ppermute(value, axes, [(source, source ^ code) for source in range(count)])
+
+
+def notes_kernel(place_ref, back_routes, back_gates, fore_routes, fore_gates, out_ref, spare):
+    top, size = back_routes.shape
+    spare[...] = jnp.zeros_like(spare)
+    for place, ref in enumerate((back_routes, back_gates, fore_routes, fore_gates)):
+        spare[pl.ds(place * top, top), 0:size] = ref[...].astype(jnp.float32)
+    out_ref[...] = pltpu.roll(spare[...], place_ref[3], axis=1)
+
+
+def picks_kernel(count, top, slots, place_ref, near_ref, far_ref, *refs):
+    outs, turned = refs[:-1], refs[-1]
+    tokens = turned.shape[1]
+    turned[...] = near_ref[...] + far_ref[...]
+    row = lax.broadcasted_iota(jnp.int32, (tokens, tokens), 0)
+    column = lax.broadcasted_iota(jnp.int32, (tokens, tokens), 1)
+    earlier = jnp.where(row < column, 1.0, 0.0).astype(jnp.bfloat16)
+    slot = lax.broadcasted_iota(jnp.int32, (slots, tokens), 0).astype(jnp.float32)
+
+    def fill(first, start, picks, gates, flipped):
+        ids = (first + lax.broadcasted_iota(jnp.int32, (count, tokens), 0)).astype(jnp.float32)
+        named = jnp.zeros((count, tokens), jnp.float32)
+        gated = jnp.zeros((count, tokens), jnp.float32)
+        for column in range(start, start + top):
+            same = turned[column : column + 1, :] == ids
+            named = named + jnp.where(same, 1.0, 0.0)
+            gated = gated + jnp.where(same, turned[column + top : column + top + 1, :], 0.0)
+        place = jnp.dot(named.astype(jnp.bfloat16), earlier, preferred_element_type=jnp.float32)
+        place = jnp.where(named > 0.0, place, -1.0)
+        for expert in range(count):
+            rows = pl.ds(expert * slots, slots)
+            hit = place[expert : expert + 1, :] == slot
+            picks[rows, :] = jnp.where(hit, 1.0, 0.0).astype(jnp.bfloat16)
+            own = jnp.sum(jnp.where(hit, gated[expert : expert + 1, :], 0.0), axis=1, keepdims=True)
+            gates[rows, :] = jnp.broadcast_to(own, (slots, LANES))
+        if flipped is not None:
+            flipped[...] = picks[...].T
+
+    fill(place_ref[1], 2 * top, outs[0], outs[1], outs[2])
+    fill(place_ref[1], 0, outs[3], outs[4], outs[5])
+    fill(place_ref[2], 0, outs[6], outs[7], None)
+
+
+def spread_gate(gates, rows, width):
+    gate = gates[rows, 0:1]
+    return jnp.broadcast_to(gate, (gate.shape[0], width))
+
+
+def assemble(place_ref, blocks, tokens, lead):
+    for code, block in enumerate(blocks):
+        size = block.shape[-2]
+        rows = pl.ds(pl.multiple_of(place_ref[3 + code], size), size)
+        if lead is None:
+            tokens[rows, :] = block[...]
+        else:
+            tokens[rows, :] = block[lead]
+
+
+def combine(place_ref, flipped, results, sums, outs):
+    width = sums.shape[1]
+    for start in range(0, width, CHUNK):
+        columns = pl.ds(start, CHUNK)
+        sums[:, columns] = jnp.dot(
+            flipped[...], results[:, columns], preferred_element_type=jnp.float32
+        ).astype(sums.dtype)
+    for out, codes in outs:
+        size = out.shape[1]
+        for lead, code in enumerate(codes):
+            rows = pl.ds(pl.multiple_of(place_ref[3 + code], size), size)
+            out[lead] = sums[rows, :]
+
+
+def gather_pairs(count, slots, picks, gates, saved_ref, grads_ref, rows):
+    width = saved_ref.shape[1]
+    gate = spread_gate(gates, pl.ds(0, count * slots), CHUNK)
+    for start in range(0, width, CHUNK):
+        columns = pl.ds(start, CHUNK)
+        saved = jnp.dot(
+            picks[...], saved_ref[:, columns], preferred_element_type=jnp.float32
+        ).astype(rows.dtype)
+        grads = jnp.dot(picks[...], grads_ref[:, columns], preferred_element_type=jnp.float32)
+        grads = (grads * gate).astype(rows.dtype)
+        for expert in range(count):
+            part = slice(expert * slots, (expert + 1) * slots)
+            rows[pl.ds(expert * 2 * slots, slots), columns] = saved[part]
+            rows[pl.ds(expert * 2 * slots + slots, slots), columns] = grads[part]
+
+
+def forward_kernel(count, slots, devices, out_codes, place_ref, *refs):
+    picks, gates, flipped, weights_ref = refs[:4]
+    blocks = refs[4 : 4 + devices]
+    outs = list(zip(refs[4 + devices :], out_codes))
+    tokens, rows, results = refs[-3:]
+    step = pl.program_id(0)
+    width = tokens.shape[1]
+
+    @pl.when(step == 0)
+    def _():
+        assemble(place_ref, blocks, tokens, None)
+        for start in range(0, width, CHUNK):
+            columns = pl.ds(start, CHUNK)
+            rows[:, columns] = jnp.dot(
+                picks[...], tokens[:, columns], preferred_element_type=jnp.float32
+            ).astype(rows.dtype)
+
+    mine = pl.ds(pl.multiple_of(step * slots, slots), slots)
+    hidden = jnp.dot(rows[mine, :], weights_ref[0], preferred_element_type=jnp.float32)
+    active = (hidden * jax.nn.sigmoid(hidden)).astype(jnp.bfloat16)
+    result = lax.dot_general(
+        active, weights_ref[0], (((1,), (1,)), ((), ())), preferred_element_type=jnp.float32
+    )
+    results[mine, :] = (result * spread_gate(gates, mine, width)).astype(results.dtype)
+
+    @pl.when(step == count - 1)
+    def _():
+        combine(place_ref, flipped, results, tokens, outs)
+
+
+def backward_kernel(count, slots, devices, out_codes, place_ref, *refs):
+    picks, gates, flipped, weights_ref = refs[:4]
+    blocks = refs[4 : 4 + devices]
+    outs = list(zip(refs[4 + devices :], out_codes))
+    inner_ref, saved_ref, grads_ref, rows, results = refs[-5:]
+    step = pl.program_id(0)
+
+    @pl.when(step == 0)
+    def _():
+        assemble(place_ref, blocks, saved_ref, 0)
+        assemble(place_ref, blocks, grads_ref, 1)
+        gather_pairs(count, slots, picks, gates, saved_ref, grads_ref, rows)
+
+    mine = pl.ds(pl.multiple_of(step * slots, slots), slots)
+    both = pl.ds(pl.multiple_of(step * 2 * slots, 2 * slots), 2 * slots)
+    product = jnp.dot(rows[both, :], weights_ref[0], preferred_element_type=jnp.float32)
+    hidden, active_grads = product[:slots], product[slots:]
+    sigma = jax.nn.sigmoid(hidden)
+    hidden_grads = (active_grads * sigma * (1.0 + hidden * (1.0 - sigma))).astype(jnp.bfloat16)
+    inner_ref[0, :slots, :] = hidden_grads
+    inner_ref[0, slots:, :] = (hidden * sigma).astype(jnp.bfloat16)
+    results[mine, :] = lax.dot_general(
+        hidden_grads, weights_ref[0], (((1,), (1,)), ((), ())), preferred_element_type=jnp.float32
+    ).astype(results.dtype)
+
+    @pl.when(step == count - 1)
+    def _():
+        combine(place_ref, flipped, results, saved_ref, outs)
+
+
+def weight_kernel(count, slots, devices, place_ref, *refs):
+    picks, gates, inner_ref = refs[:3]
+    blocks = refs[3 : 3 + devices]
+    out_ref, saved_ref, grads_ref, rows = refs[-4:]
+    step = pl.program_id(0)
+
+    @pl.when(step == 0)
+    def _():
+        assemble(place_ref, blocks, saved_ref, 0)
+        assemble(place_ref, blocks, grads_ref, 1)
+        gather_pairs(count, slots, picks, gates, saved_ref, grads_ref, rows)
+
+    both = pl.ds(pl.multiple_of(step * 2 * slots, 2 * slots), 2 * slots)
+    flat = rows[both, :].T
+    for start in range(0, inner_ref.shape[-1], CHUNK):
+        columns = pl.ds(start, CHUNK)
+        out_ref[0, :, columns] = jnp.dot(
+            flat, inner_ref[0, :, columns], preferred_element_type=jnp.float32
+        ).astype(out_ref.dtype)
+
+
+def gathered_plan(
+    section_inputs,
+    saved_inputs,
+    output_grads,
+    forward_routes,
+    backward_routes,
+    forward_gates,
+    backward_gates,
+    expert_weights,
+):
+    token_count = section_inputs.shape[1]
+    top = forward_routes.shape[2]
+    _, local_count, width, inner_width = expert_weights.shape
+    groups, pair = lax.axis_size("expert"), lax.axis_size("dp")
+    devices = groups * pair
+    count = local_count // pair
+    total = devices * token_count
+    slots = -(-devices * CAP // 16) * 16
+    rows = count * slots
+    half = width // pair
+    weights = expert_weights[0]
+
+    side, group = lax.axis_index("dp"), lax.axis_index("expert")
+    index = group * pair + side
+    base = group * local_count
+    place = jnp.stack(
+        [side, base + side * count, base + (1 - side) * count]
+        + [(index ^ code) * token_count for code in range(devices)]
+    ).astype(jnp.int32)
+    params = pltpu.CompilerParams(vmem_limit_bytes=VMEM_LIMIT, dimension_semantics=("arbitrary",))
+
+    def whole(shape):
+        return pl.BlockSpec(shape, lambda *_: (0,) * len(shape))
+
+    def call(kernel, name, steps, in_specs, out_specs, out_shape, scratch, flops=0, aliases=()):
+        return pl.pallas_call(
+            kernel,
+            grid_spec=pltpu.PrefetchScalarGridSpec(
+                num_scalar_prefetch=1,
+                grid=(steps,),
+                in_specs=in_specs,
+                out_specs=out_specs,
+                scratch_shapes=scratch,
+            ),
+            out_shape=out_shape,
+            compiler_params=params,
+            cost_estimate=pl.CostEstimate(
+                flops=flops, bytes_accessed=flops // 512 + 1024, transcendentals=0
+            ),
+            input_output_aliases=dict(aliases),
+            name=name,
+        )
+
+    def onward(block):
+        return swapped(block, 1)
+
+    def across(block):
+        return [swapped(block, code) for code in range(pair, devices, pair)]
+
+    def after(first, then):
+        then, _ = lax.optimization_barrier((then, first))
+        return then
+
+    forward_near = [section_inputs[0]] + across(section_inputs[0])
+    forward_far = [onward(block) for block in forward_near]
+    inputs_all = [block for both in zip(forward_near, forward_far) for block in both]
+
+    table = jax.ShapeDtypeStruct((4 * top, total), jnp.float32)
+    small = whole((top, token_count))
+    notes = call(
+        notes_kernel,
+        "notes",
+        1,
+        [small] * 4,
+        whole(table.shape),
+        table,
+        [pltpu.VMEM(table.shape, jnp.float32)],
+    )(place, backward_routes[0].T, backward_gates[0].T, forward_routes[0].T, forward_gates[0].T)
+    code = pair
+    while code < devices:
+        notes = notes + swapped(notes, code)
+        code *= 2
+    notes_far = onward(notes)
+
+    pick = jax.ShapeDtypeStruct((rows, total), jnp.bfloat16)
+    flip = jax.ShapeDtypeStruct((total, rows), jnp.bfloat16)
+    gate = jax.ShapeDtypeStruct((rows, LANES), jnp.float32)
+    pick_outs = [pick, gate, flip, pick, gate, flip, pick, gate]
+    picks = call(
+        functools.partial(picks_kernel, count, top, slots),
+        "slot_picks",
+        1,
+        [whole(table.shape)] * 2,
+        [whole(out.shape) for out in pick_outs],
+        pick_outs,
+        [pltpu.VMEM(table.shape, jnp.float32)],
+    )(place, notes, notes_far)
+    forward_picks, own_picks, other_picks = picks[:3], picks[3:6], picks[6:]
+
+    backward_own = after(forward_near, jnp.stack([saved_inputs[0], output_grads[0]]))
+    backward_near = across(backward_own)
+
+    pick_specs = [whole(pick.shape), whole(gate.shape), whole(flip.shape)]
+    weight_spec = pl.BlockSpec(
+        (1, width, inner_width), lambda step, place: (place[0] * count + step, 0, 0)
+    )
+    pass_flops = 2 * 2 * count * CHUNK * width * inner_width
+    codes = range(devices)
+    tokens = pltpu.VMEM((total, width), jnp.bfloat16)
+    slot_rows = pltpu.VMEM((rows, width), jnp.bfloat16)
+
+    chip_block = jax.ShapeDtypeStruct((pair, token_count, width), jnp.bfloat16)
+    forward_codes = [codes[first : first + pair] for first in range(0, devices, pair)]
+    layer_parts = call(
+        functools.partial(forward_kernel, count, slots, devices, forward_codes),
+        "expert_forward",
+        count,
+        pick_specs + [weight_spec] + [whole((token_count, width))] * devices,
+        [whole(chip_block.shape)] * groups,
+        [chip_block] * groups,
+        [tokens, slot_rows, slot_rows],
+        pass_flops,
+    )(place, *forward_picks, weights, *inputs_all)
+    layer_near = [
+        swapped(part, code) for part, code in zip(layer_parts[1:], range(pair, devices, pair))
+    ]
+
+    backward_near = [backward_own] + after(layer_parts, backward_near)
+    backward_far = [onward(block) for block in backward_near]
+    backward_all = [block for both in zip(backward_near, backward_far) for block in both]
+
+    inner = jax.ShapeDtypeStruct((count, 2 * slots, inner_width), jnp.bfloat16)
+    own_block = jax.ShapeDtypeStruct((1, token_count, width), jnp.bfloat16)
+    far_block = jax.ShapeDtypeStruct((groups, token_count, width), jnp.bfloat16)
+    backward_codes = [codes[first : first + 1] for first in range(0, devices, pair)]
+    backward_codes.append(codes[1::pair])
+    *grad_parts, grad_far, inner_own = call(
+        functools.partial(backward_kernel, count, slots, devices, backward_codes),
+        "expert_backward",
+        count,
+        pick_specs + [weight_spec] + [whole(backward_own.shape)] * devices,
+        [whole(own_block.shape)] * groups
+        + [whole(far_block.shape)]
+        + [pl.BlockSpec((1, 2 * slots, inner_width), lambda step, place: (step, 0, 0))],
+        [own_block] * groups + [far_block, inner],
+        [tokens, tokens, pltpu.VMEM((2 * rows, width), jnp.bfloat16), slot_rows],
+        pass_flops,
+    )(place, *own_picks, weights, *backward_all)
+    inner_other = onward(inner_own)
+    grad_far = onward(grad_far)
+
+    def summed(*blocks):
+        return functools.reduce(jnp.add, [block.astype(jnp.float32) for block in blocks])
+
+    layer_near = after(grad_parts, layer_near)
+    layer_mine = summed(layer_parts[0][0], *[block[0] for block in layer_near])
+    layer_other = summed(layer_parts[0][1], *[block[1] for block in layer_near])
+    layer_other = onward(layer_other.astype(jnp.bfloat16))
+
+    def gradient(whose, inner_rows, picked, earlier):
+        out = jax.ShapeDtypeStruct((local_count, half, inner_width), jnp.bfloat16)
+        earlier = [] if earlier is None else [earlier]
+
+        def out_block(step, place):
+            owner = place[0] if whose == 0 else 1 - place[0]
+            return (owner * count + step, 0, 0)
+
+        specs = [
+            pick_specs[0],
+            pick_specs[1],
+            pl.BlockSpec((1, 2 * slots, inner_width), lambda step, place: (step, 0, 0)),
+        ]
+        specs += [
+            pl.BlockSpec((2, token_count, half), lambda step, place: (0, 0, place[0]))
+        ] * devices
+        specs += [pl.BlockSpec(memory_space=pl.ANY)] * len(earlier)
+        half_tokens = pltpu.VMEM((total, half), jnp.bfloat16)
+        return call(
+            functools.partial(weight_kernel, count, slots, devices),
+            "weight_gradient_" + ("own", "other")[whose],
+            count,
+            specs,
+            pl.BlockSpec((1, half, inner_width), out_block),
+            out,
+            [half_tokens, half_tokens, pltpu.VMEM((2 * rows, half), jnp.bfloat16)],
+            pass_flops // 2,
+            [(len(specs), 0)] if earlier else [],
+        )(place, *picked[:2], inner_rows, *backward_all, *earlier)
+
+    own_done = gradient(0, inner_own, own_picks, None)
+
+    layer_other, grad_far = after(own_done, (layer_other, grad_far))
+    layer_out = (summed(section_inputs[0], layer_other) + layer_mine).astype(jnp.bfloat16)
+    next_inputs = shifted(layer_out, "pipe", 1)[None]
+    grad_sums = [
+        summed(part[0], grad_far[place_]).astype(jnp.bfloat16)
+        for place_, part in enumerate(grad_parts)
+    ]
+    grad_near = [
+        swapped(part, code) for part, code in zip(grad_sums[1:], range(pair, devices, pair))
+    ]
+    weight_grads = gradient(1, inner_other, other_picks, own_done)
+
+    grad_near = after(weight_grads, grad_near)
+    input_grads = summed(output_grads[0], grad_sums[0], *grad_near).astype(jnp.bfloat16)
+    prior_grads = shifted(input_grads, "pipe", -1)[None]
+    return (next_inputs, prior_grads, weight_grads[None])
+
+
+def on_device(*arrays):
+    token_count = arrays[0].shape[1]
+    local_count = arrays[-1].shape[1]
+    groups, pair = lax.axis_size("expert"), lax.axis_size("dp")
+    gathered = groups * token_count
+    packed = groups * local_count * CAP
+    paired = pair == 2 and local_count % pair == 0 and groups & (groups - 1) == 0
+    if gathered <= packed and paired and gathered * pair % LANES == 0:
+        return gathered_plan(*arrays)
+    return packed_plan(*arrays)
+
+
 def solution(mesh):
     placed = (
         P("pipe", ("expert", "dp"), None),

time: 327 us -> 97.7 us (0.30); the launches traced: 321 us -> 97.1 us
  matrix products: 200 us -> 0 us
  Pallas kernels: 0 us -> 56.9 us
  local copies, waits for them, and re-layouts: 36.5 us -> 5.05 us
  waiting for transfers between devices: 32.5 us -> 6.98 us
  between operations: 15.1 us -> 0.81 us
  other arithmetic: 9.55 us -> 1.39 us
    dot_general x6 -> x0, matrix products: 200 us -> none  [the longest x1 50.6 us: expert_forward(): jnp.einsum('nlch,ldh->nlcd', active, weights, preferred_element_type=jnp....]
    pallas_call x0 -> x6, Pallas kernels: none -> 56.9 us  [the longest x1 18.9 us: gathered_plan(): call(functools.partial(backward_kernel, count, slots, devices, backward_c...]
    all_to_all x5 -> x0, waiting for transfers between devices: 30 us -> none  [the longest x1 14.1 us: on_device(): lax.all_to_all(forward_rows, 'expert', split_axis=0, concat_axis=0, tiled...]
    all_to_all x5 -> x0, starting transfers between devices: 21.9 us -> none  [the longest x1 5.29 us: on_device(): lax.all_to_all(saved_rows, 'expert', split_axis=0, concat_axis=0, tiled=T...]
    ppermute x0 -> x26, starting transfers between devices: none -> 21.8 us  [swapped(): lax.ppermute(value, axes, [(source, source ^ code) for source in range(co...]
    gather x6 -> x0, local copies, waits for them, and re-layouts: 13.4 us -> none  [the longest x4 10.2 us: pack_rows(): picked = jnp.take(source, jnp.maximum(owner_row - 1, 0) // spread, axis=0)]
    reshape x6 -> x0, local copies, waits for them, and re-layouts: 6.12 us -> none  [the longest x2 2.48 us: on_device(): pack_rows(section_inputs[0], forward_slot, slot_total, route_count)]
    ppermute x0 -> x26, waiting for transfers between devices: none -> 4.08 us  [swapped(): lax.ppermute(value, axes, [(source, source ^ code) for source in range(co...]
  transfers between devices with their start and end apart: 8 -> 28, of which waited for: 4 -> 3; matrix products, arithmetic and copies ran while one was open for 39% -> 1% of each run, Pallas kernels for 0% -> 59%
where the time goes in v2:
time: 97.7 us; the launch traced here: 97.1 us
  Pallas kernels  56.9 us (58%)
  starting transfers between devices  25.9 us (27%)
  waiting for transfers between devices  6.98 us (7%)
  local copies, waits for them, and re-layouts  5.05 us (5%)
  other arithmetic  1.39 us (1%)
    ppermute x26, starting transfers between devices, swapped(): lax.ppermute(value, axes, [(source, source ^ code) for source in range(co...  21.8 us
    pallas_call x1, Pallas kernels, gathered_plan(): call(functools.partial(backward_kernel, count, slots, devices, backward_c...  18.9 us
    pallas_call x1, Pallas kernels, gathered_plan(): call(functools.partial(forward_kernel, count, slots, devices, forward_cod...  18.2 us
    pallas_call x2, Pallas kernels, gradient(): call(functools.partial(weight_kernel, count, slots, devices), 'weight_gra...  18.1 us
    unnamed x16, local copies, waits for them, and re-layouts  4.97 us
    ppermute x2, starting transfers between devices, shifted(): return lax.ppermute(value, axis, pairs)  4.12 us
    ppermute x26, waiting for transfers between devices, swapped(): lax.ppermute(value, axes, [(source, source ^ code) for source in range(co...  4.08 us
    ppermute x2, waiting for transfers between devices, shifted(): return lax.ppermute(value, axis, pairs)  2.9 us
  transfers between devices with their start and end apart: 28, of which 3 were waited for; matrix products, arithmetic and copies ran while one was open for 1% of the time, Pallas kernels for 59%

profile of v2, /device:TPU:0, one launch (start us, length us, event | category | flops | bytes accessed | tf_op | source)
XLA Modules:
  0.0 97.1 jit_solution(17722070604134147066)
XLA Ops:
  0.6 4.0 %collective-permute-start.8 = (bf16[32,2048]{1,0:T(8,128)(2,1)}, bf16[32,2048]{1,0:T(8,128)(2,1)S(1)}, u32[]{:S(2)}, u32[]{:S(2)}) collective-permute-start(bf16[32,2048]{1,0:T(8,128)(2,1)} %bitcast.49), channel_id=1, source_target_pairs={{0,6},{1,7},{2,4},{3,5},{4,2},{5,3},{6,0},{7,1},{8,14},{9,15},{10,... | collective-permute-start | bytes 393224 | tf_op jit(solution)/shard_map/ppermute | solution.py:136
  4.6 0.5 collective-permute-start.6
  5.1 0.1 collective-permute-start.4
  5.2 0.1 stack.50.place_ref
  5.3 0.7 copy-done.2
  6.0 0.7 copy-done.3
  6.7 0.7 copy-done.4
  7.4 0.7 copy-done.5
  8.1 0.6 notes.1
  8.7 1.9 %collective-permute-start = (f32[32,256]{1,0:T(8,128)S(1)}, f32[32,256]{1,0:T(8,128)S(1)}, u32[]{:S(2)}, u32[]{:S(2)}) collective-permute-start(f32[32,256]{1,0:T(8,128)S(1)} %notes.1), channel_id=1, source_target_pairs={{0,2},{1,3},{2,0},{3,1},{4,6},{5,7},{6,4},{7,5},{8,10},{9,11},{10,... | collective-permute-start | bytes 98312 | tf_op jit(solution)/shard_map/ppermute | solution.py:136
  10.6 2.0 %collective-permute-done = f32[32,256]{1,0:T(8,128)S(1)} collective-permute-done((f32[32,256]{1,0:T(8,128)S(1)}, f32[32,256]{1,0:T(8,128)S(1)}, u32[]{:S(2)}, u32[]{:S(2)}) %collective-permute-start) | collective-permute-done | bytes 32800 | tf_op jit(solution)/shard_map/ppermute | solution.py:136
  12.6 1.9 %collective-permute-start.1 = (f32[32,256]{1,0:T(8,128)S(1)}, f32[32,256]{1,0:T(8,128)S(1)}, u32[]{:S(2)}, u32[]{:S(2)}) collective-permute-start(f32[32,256]{1,0:T(8,128)S(1)} %add.80), channel_id=1, source_target_pairs={{0,4},{1,5},{2,6},{3,7},{4,0},{5,1},{6,2},{7,3},{8,12},{9,13},{10,... | collective-permute-start | bytes 98312 | tf_op jit(solution)/shard_map/ppermute | solution.py:136
  14.5 0.0 collective-permute-start.3
  14.5 2.0 %collective-permute-done.1 = f32[32,256]{1,0:T(8,128)S(1)} collective-permute-done((f32[32,256]{1,0:T(8,128)S(1)}, f32[32,256]{1,0:T(8,128)S(1)}, u32[]{:S(2)}, u32[]{:S(2)}) %collective-permute-start.1) | collective-permute-done | bytes 32800 | tf_op jit(solution)/shard_map/ppermute | solution.py:136
  16.5 0.0 collective-permute-start.2
  16.6 0.0 collective-permute-done.8.refs_10_
  16.6 0.5 collective-permute-start.9
  17.1 0.0 collective-permute-done.6.refs_8_
  17.1 0.1 collective-permute-start.7
  17.1 0.0 collective-permute-done.4.refs_6_
  17.1 0.4 collective-permute-start.5
  17.6 1.0 %pad_maximum_fusion.refs_4_.refs_3_ = bf16[2,32,2048]{2,1,0:T(8,128)(2,1)S(1)} fusion(bf16[1,32,2048]{2,1,0:T(8,128)(2,1)} %param.10, bf16[1,32,2048]{2,1,0:T(8,128)(2,1)} %param.9), kind=kLoop, calls=%fused_computation | loop fusion | flops 131072 | bytes 524288 | tf_op jit(solution)/shard_map/stack | solution.py:405
  18.6 0.0 collective-permute-done.2.far_ref
  18.6 1.1 %slot_picks.1 = (bf16[384,256]{1,0:T(8,128)(2,1)S(1)}, f32[384,128]{1,0:T(8,128)S(1)}, bf16[256,384]{1,0:T(8,128)(2,1)S(1)}, bf16[384,256]{1,0:T(8,128)(2,1)S(1)...) custom-call(s32[11]{0:T(128)S(1)} %stack.50.place_ref, ...), custom_call_target="tpu_custom_call" | custom-call | bytes 1024 | tf_op jit(solution)/shard_map/slot_picks/pallas_call | solution.py:394
  19.7 2.9 %collective-permute-start.16 = (bf16[2,32,2048]{2,1,0:T(8,128)(2,1)S(1)}, bf16[2,32,2048]{2,1,0:T(8,128)(2,1)S(1)}, u32[]{:S(2)}, u32[]{:S(2)}) collective-permute-start(bf16[2,32,2048]{2,1,0:T(8,128)(2,1)S(1)} %pad_maximum_fusion.refs_4_.refs_3_), channel_id=1, source_target_pairs={{0,6},{1,7},{2,4},{3,5},{4,2},{5,3},{6,0},{7,1},{8,14},{9,15},{10,... | collective-permute-start | bytes 786440 | tf_op jit(solution)/shard_map/ppermute | solution.py:136
  22.6 0.0 collective-permute-done.3.refs_5_
  22.6 0.5 collective-permute-start.15
  23.1 0.0 collective-permute-done.9.refs_11_
  23.1 0.1 collective-permute-start.14
  23.2 0.0 collective-permute-done.7.refs_9_
  23.2 0.0 collective-permute-start.13
  23.2 0.0 copy-start
  23.3 0.9 copy-done
  24.2 18.2 %expert_forward.1 = (bf16[2,32,2048]{2,1,0:T(8,128)(2,1)S(1)}, bf16[2,32,2048]{2,1,0:T(8,128)(2,1)S(1)}, bf16[2,32,2048]{2,1,0:T(8,128)(2,1)S(1)}, bf16[2,32,2048]{2,1,0:T(8,128)(2,1)S(1)}) custom-call(s32[11]{0:T(128)S(1)} %stack.50.place_ref, bf16[384,256]{1,0:T(8,128)(2,1)S(1)} %get-tuple-element.33.refs_0_, f32[384,128]{1,0:T(8,128)S(1)} %get-tuple-element.34.refs_1_, ...), custom_call_target="tpu_custom_call" | custom-call | flops 12884901888 | bytes 25166848 | tf_op jit(solution)/shard_map/expert_forward/pallas_call | solution.py:419
  42.4 0.0 collective-permute-done.16.refs_10_.refs_9_
  42.4 0.0 collective-permute-done.14.refs_6_.refs_5_
  42.4 0.6 collective-permute-start.17
  43.0 0.1 collective-permute-start.18
  43.1 0.4 collective-permute-start.19
  43.5 1.9 %collective-permute-start.10 = (bf16[2,32,2048]{2,1,0:T(8,128)(2,1)S(1)}, bf16[2,32,2048]{2,1,0:T(8,128)(2,1)S(1)}, u32[]{:S(2)}, u32[]{:S(2)}) collective-permute-start(bf16[2,32,2048]{2,1,0:T(8,128)(2,1)S(1)} %get-tuple-element.37), channel_id=1, source_target_pairs={{0,2},{1,3},{2,0},{3,1},{4,6},{5,7},{6,4},{7,5},{8,10},{9,11},{10,... | collective-permute-start | bytes 786440 | tf_op jit(solution)/shard_map/ppermute | solution.py:136
  45.4 0.0 collective-permute-done.13.refs_5_.refs_4_
  45.4 1.5 %collective-permute-start.11 = (bf16[2,32,2048]{2,1,0:T(8,128)(2,1)S(1)}, bf16[2,32,2048]{2,1,0:T(8,128)(2,1)S(1)}, u32[]{:S(2)}, u32[]{:S(2)}) collective-permute-start(bf16[2,32,2048]{2,1,0:T(8,128)(2,1)S(1)} %get-tuple-element.38), channel_id=1, source_target_pairs={{0,4},{1,5},{2,6},{3,7},{4,0},{5,1},{6,2},{7,3},{8,12},{9,13},{10,... | collective-permute-start | bytes 786440 | tf_op jit(solution)/shard_map/ppermute | solution.py:136
  46.9 0.1 collective-permute-start.12
  47.0 18.9 %expert_backward.1 = (bf16[1,32,2048]{2,1,0:T(8,128)(2,1)S(1)}, bf16[1,32,2048]{2,1,0:T(8,128)(2,1)S(1)}, bf16[1,32,2048]{2,1,0:T(8,128)(2,1)S(1)}, bf16[1,32,20...) custom-call(s32[11]{0:T(128)S(1)} %stack.50.place_ref, ...), custom_call_target="tpu_custom_call" | custom-call | flops 12884901888 | bytes 25166848 | tf_op jit(solution)/shard_map/expert_backward/pallas_call | solution.py:442
  65.9 0.0 copy-start.1
  66.0 0.0 collective-permute-done.10
  66.0 0.1 fusion.4
  66.1 0.1 collective-permute-start.20
  66.2 0.4 collective-permute-start.21
  66.6 0.1 collective-permute-start.26
  66.7 9.0 %weight_gradient_own.1.refs_11_ = bf16[16,1024,768]{2,1,0:T(8,128)(2,1)} custom-call(s32[11]{0:T(128)S(1)} %stack.50.place_ref, bf16[384,256]{1,0:T(8,128)(2,1)S(1)} %get-tuple-element.40.refs_0_, f32[384,128]{1,0:T(8,128)S(1)} %get-tuple-element.41.refs_1_, bf16[8,96,768]{2,1,0:T(8,128)(2,1)S(1)} %get-tuple-element.55.refs_2_, ...), custom_call_target="tpu_custom_call" | custom-call | flops 6442450944 | bytes 12583936 | tf_op jit(solution)/shard_map/weight_gradient_own/pallas_call | solution.py:483
  75.8 0.1 fusion.7
  75.9 2.9 %collective-permute-start.25 = (bf16[32,2048]{1,0:T(8,128)(2,1)S(1)}, bf16[32,2048]{1,0:T(8,128)(2,1)S(1)}, u32[]{:S(2)}, u32[]{:S(2)}) collective-permute-start(bf16[32,2048]{1,0:T(8,128)(2,1)S(1)} %get-tuple-element.63), channel_id=1, source_target_pairs={{0,6},{1,7},{2,4},{3,5},{4,2},{5,3},{6,0},{7,1},{8,14},{9,15},{10,... | collective-permute-start | bytes 393224 | tf_op jit(solution)/shard_map/ppermute | solution.py:136
  78.8 0.5 collective-permute-start.24
  79.3 0.2 collective-permute-start.23
  79.4 0.1 fusion.3
  79.5 2.0 %collective-permute-start.22 = (bf16[32,2048]{1,0:T(8,128)(2,1)S(1)}, bf16[32,2048]{1,0:T(8,128)(2,1)S(1)}, u32[]{:S(2)}, u32[]{:S(2)}) collective-permute-start(bf16[32,2048]{1,0:T(8,128)(2,1)S(1)} %fusion.3), channel_id=1, source_target_pairs={{0,8},{8,16},{16,24},{24,0},{1,9},{9,17},{17,25},{25,1},{2,10},{10... | collective-permute-start | bytes 393224 | tf_op jit(solution)/shard_map/ppermute | solution.py:19
  81.5 9.0 %weight_gradient_other.1 = bf16[16,1024,768]{2,1,0:T(8,128)(2,1)} custom-call(s32[11]{0:T(128)S(1)} %stack.50.place_ref, bf16[384,256]{1,0:T(8,128)(2,1)S(1)} %get-tuple-element.58.refs_0_, f32[384,128]{1,0:T(8,128)S(1)} %get-tuple-element.59.refs_1_, bf16[8,96,768]{2,1,0:T(8,128)(2,1)S(1)} %collective-permute-done.26.refs_2_, ...), custom_call_target="tpu_custom_call", output_to_operand_aliasing={{}: (12, {})} | custom-call | flops 6442450944 | bytes 12583936 | tf_op jit(solution)/shard_map/weight_gradient_other/pallas_call | solution.py:483
  90.6 0.0 collective-permute-done.23
  90.6 0.1 fusion.2
  90.7 2.1 %collective-permute-start.27 = (bf16[32,2048]{1,0:T(8,128)(2,1)S(1)}, bf16[32,2048]{1,0:T(8,128)(2,1)S(1)}, u32[]{:S(2)}, u32[]{:S(2)}) collective-permute-start(bf16[32,2048]{1,0:T(8,128)(2,1)S(1)} %fusion.2), channel_id=1, source_target_pairs={{0,24},{8,0},{16,8},{24,16},{1,25},{9,1},{17,9},{25,17},{2,26},{10... | collective-permute-start | bytes 393224 | tf_op jit(solution)/shard_map/ppermute | solution.py:19
  92.8 2.9 %collective-permute-done.27 = bf16[32,2048]{1,0:T(8,128)(2,1)S(1)} collective-permute-done((bf16[32,2048]{1,0:T(8,128)(2,1)S(1)}, bf16[32,2048]{1,0:T(8,128)(2,1)S(1)}, u32[]{:S(2)}, u32[]{:S(2)}) %collective-permute-start.27) | collective-permute-done | bytes 131104 | tf_op jit(solution)/shard_map/ppermute | solution.py:19
  95.7 0.7 copy.15
  96.4 0.7 copy.16
  (22 shorter events, 0.1 us)
Async XLA Ops:
  0.6 15.9 %collective-permute-start.8 = (bf16[32,2048]{1,0:T(8,128)(2,1)}, bf16[32,2048]{1,0:T(8,128)(2,1)S(1)}, u32[]{:S(2)}, u32[]{:S(2)}) collective-permute-start(bf16[32,2048]{1,0:T(8,128)(2,1)} %bitcast.49), channel_id=1, source_target_pairs={{0,6},{1,7},{2,4},{3,5},{4,2},{5,3},{6,0},{7,1},{8,14},{9,15},{10,... | collective-permute-start | bytes 393224 | tf_op jit(solution)/shard_map/ppermute | solution.py:136
  4.6 12.5 %collective-permute-start.6 = (bf16[32,2048]{1,0:T(8,128)(2,1)}, bf16[32,2048]{1,0:T(8,128)(2,1)S(1)}, u32[]{:S(2)}, u32[]{:S(2)}) collective-permute-start(bf16[32,2048]{1,0:T(8,128)(2,1)} %bitcast.50), channel_id=1, source_target_pairs={{0,4},{1,5},{2,6},{3,7},{4,0},{5,1},{6,2},{7,3},{8,12},{9,13},{10,... | collective-permute-start | bytes 393224 | tf_op jit(solution)/shard_map/ppermute | solution.py:136
  5.1 12.1 %collective-permute-start.4 = (bf16[32,2048]{1,0:T(8,128)(2,1)}, bf16[32,2048]{1,0:T(8,128)(2,1)S(1)}, u32[]{:S(2)}, u32[]{:S(2)}) collective-permute-start(bf16[32,2048]{1,0:T(8,128)(2,1)} %bitcast.51), channel_id=1, source_target_pairs={{0,2},{1,3},{2,0},{3,1},{4,6},{5,7},{6,4},{7,5},{8,10},{9,11},{10,... | collective-permute-start | bytes 393224 | tf_op jit(solution)/shard_map/ppermute | solution.py:136
  5.3 0.7 copy-start.2
  6.0 0.7 copy-start.3
  6.7 0.7 copy-start.4
  7.4 0.7 copy-start.5
  8.7 3.9 %collective-permute-start = (f32[32,256]{1,0:T(8,128)S(1)}, f32[32,256]{1,0:T(8,128)S(1)}, u32[]{:S(2)}, u32[]{:S(2)}) collective-permute-start(f32[32,256]{1,0:T(8,128)S(1)} %notes.1), channel_id=1, source_target_pairs={{0,2},{1,3},{2,0},{3,1},{4,6},{5,7},{6,4},{7,5},{8,10},{9,11},{10,... | collective-permute-start | bytes 98312 | tf_op jit(solution)/shard_map/ppermute | solution.py:136
  12.6 3.9 %collective-permute-start.1 = (f32[32,256]{1,0:T(8,128)S(1)}, f32[32,256]{1,0:T(8,128)S(1)}, u32[]{:S(2)}, u32[]{:S(2)}) collective-permute-start(f32[32,256]{1,0:T(8,128)S(1)} %add.80), channel_id=1, source_target_pairs={{0,4},{1,5},{2,6},{3,7},{4,0},{5,1},{6,2},{7,3},{8,12},{9,13},{10,... | collective-permute-start | bytes 98312 | tf_op jit(solution)/shard_map/ppermute | solution.py:136
  14.5 8.0 %collective-permute-start.3 = (bf16[32,2048]{1,0:T(8,128)(2,1)}, bf16[32,2048]{1,0:T(8,128)(2,1)S(1)}, u32[]{:S(2)}, u32[]{:S(2)}) collective-permute-start(bf16[32,2048]{1,0:T(8,128)(2,1)} %bitcast.52), channel_id=1, source_target_pairs={{0,1},{1,0},{2,3},{3,2},{4,5},{5,4},{6,7},{7,6},{8,9},{9,8},{10,11... | collective-permute-start | bytes 393224 | tf_op jit(solution)/shard_map/ppermute | solution.py:136
  16.5 2.0 %collective-permute-start.2 = (f32[32,256]{1,0:T(8,128)S(1)}, f32[32,256]{1,0:T(8,128)S(1)}, u32[]{:S(2)}, u32[]{:S(2)}) collective-permute-start(f32[32,256]{1,0:T(8,128)S(1)} %add.81.near_ref), channel_id=1, source_target_pairs={{0,1},{1,0},{2,3},{3,2},{4,5},{5,4},{6,7},{7,6},{8,9},{9,8},{10,11... | collective-permute-start | bytes 98312 | tf_op jit(solution)/shard_map/ppermute | solution.py:136
  16.6 6.5 %collective-permute-start.9 = (bf16[32,2048]{1,0:T(8,128)(2,1)S(1)}, bf16[32,2048]{1,0:T(8,128)(2,1)S(1)}, u32[]{:S(2)}, u32[]{:S(2)}) collective-permute-start(bf16[32,2048]{1,0:T(8,128)(2,1)S(1)} %collective-permute-done.8.refs_10_), channel_id=1, source_target_pairs={{0,1},{1,0},{2,3},{3,2},{4,5},{5,4},{6,7},{7,6},{8,9},{9,8},{10,11... | collective-permute-start | bytes 393224 | tf_op jit(solution)/shard_map/ppermute | solution.py:136
  17.1 6.2 %collective-permute-start.7 = (bf16[32,2048]{1,0:T(8,128)(2,1)S(1)}, bf16[32,2048]{1,0:T(8,128)(2,1)S(1)}, u32[]{:S(2)}, u32[]{:S(2)}) collective-permute-start(bf16[32,2048]{1,0:T(8,128)(2,1)S(1)} %collective-permute-done.6.refs_8_), channel_id=1, source_target_pairs={{0,1},{1,0},{2,3},{3,2},{4,5},{5,4},{6,7},{7,6},{8,9},{9,8},{10,11... | collective-permute-start | bytes 393224 | tf_op jit(solution)/shard_map/ppermute | solution.py:136
  17.1 6.1 %collective-permute-start.5 = (bf16[32,2048]{1,0:T(8,128)(2,1)S(1)}, bf16[32,2048]{1,0:T(8,128)(2,1)S(1)}, u32[]{:S(2)}, u32[]{:S(2)}) collective-permute-start(bf16[32,2048]{1,0:T(8,128)(2,1)S(1)} %collective-permute-done.4.refs_6_), channel_id=1, source_target_pairs={{0,1},{1,0},{2,3},{3,2},{4,5},{5,4},{6,7},{7,6},{8,9},{9,8},{10,11... | collective-permute-start | bytes 393224 | tf_op jit(solution)/shard_map/ppermute | solution.py:136
  19.7 22.7 %collective-permute-start.16 = (bf16[2,32,2048]{2,1,0:T(8,128)(2,1)S(1)}, bf16[2,32,2048]{2,1,0:T(8,128)(2,1)S(1)}, u32[]{:S(2)}, u32[]{:S(2)}) collective-permute-start(bf16[2,32,2048]{2,1,0:T(8,128)(2,1)S(1)} %pad_maximum_fusion.refs_4_.refs_3_), channel_id=1, source_target_pairs={{0,6},{1,7},{2,4},{3,5},{4,2},{5,3},{6,0},{7,1},{8,14},{9,15},{10,... | collective-permute-start | bytes 786440 | tf_op jit(solution)/shard_map/ppermute | solution.py:136
  22.6 19.8 %collective-permute-start.15 = (bf16[2,32,2048]{2,1,0:T(8,128)(2,1)S(1)}, bf16[2,32,2048]{2,1,0:T(8,128)(2,1)S(1)}, u32[]{:S(2)}, u32[]{:S(2)}) collective-permute-start(bf16[2,32,2048]{2,1,0:T(8,128)(2,1)S(1)} %pad_maximum_fusion.refs_4_.refs_3_), channel_id=1, source_target_pairs={{0,4},{1,5},{2,6},{3,7},{4,0},{5,1},{6,2},{7,3},{8,12},{9,13},{10,... | collective-permute-start | bytes 786440 | tf_op jit(solution)/shard_map/ppermute | solution.py:136
  23.1 19.3 %collective-permute-start.14 = (bf16[2,32,2048]{2,1,0:T(8,128)(2,1)S(1)}, bf16[2,32,2048]{2,1,0:T(8,128)(2,1)S(1)}, u32[]{:S(2)}, u32[]{:S(2)}) collective-permute-start(bf16[2,32,2048]{2,1,0:T(8,128)(2,1)S(1)} %pad_maximum_fusion.refs_4_.refs_3_), channel_id=1, source_target_pairs={{0,2},{1,3},{2,0},{3,1},{4,6},{5,7},{6,4},{7,5},{8,10},{9,11},{10,... | collective-permute-start | bytes 786440 | tf_op jit(solution)/shard_map/ppermute | solution.py:136
  23.2 22.2 %collective-permute-start.13 = (bf16[2,32,2048]{2,1,0:T(8,128)(2,1)S(1)}, bf16[2,32,2048]{2,1,0:T(8,128)(2,1)S(1)}, u32[]{:S(2)}, u32[]{:S(2)}) collective-permute-start(bf16[2,32,2048]{2,1,0:T(8,128)(2,1)S(1)} %pad_maximum_fusion.refs_4_.refs_3_), channel_id=1, source_target_pairs={{0,1},{1,0},{2,3},{3,2},{4,5},{5,4},{6,7},{7,6},{8,9},{9,8},{10,11... | collective-permute-start | bytes 786440 | tf_op jit(solution)/shard_map/ppermute | solution.py:136
  23.2 0.9 copy-start
  42.4 4.5 %collective-permute-start.17 = (bf16[2,32,2048]{2,1,0:T(8,128)(2,1)S(1)}, bf16[2,32,2048]{2,1,0:T(8,128)(2,1)S(1)}, u32[]{:S(2)}, u32[]{:S(2)}) collective-permute-start(bf16[2,32,2048]{2,1,0:T(8,128)(2,1)S(1)} %collective-permute-done.14.refs_6_.refs_5_), channel_id=1, source_target_pairs={{0,1},{1,0},{2,3},{3,2},{4,5},{5,4},{6,7},{7,6},{8,9},{9,8},{10,11... | collective-permute-start | bytes 786440 | tf_op jit(solution)/shard_map/ppermute | solution.py:136
  43.0 4.0 %collective-permute-start.18 = (bf16[2,32,2048]{2,1,0:T(8,128)(2,1)S(1)}, bf16[2,32,2048]{2,1,0:T(8,128)(2,1)S(1)}, u32[]{:S(2)}, u32[]{:S(2)}) collective-permute-start(bf16[2,32,2048]{2,1,0:T(8,128)(2,1)S(1)} %collective-permute-done.15.refs_8_.refs_7_), channel_id=1, source_target_pairs={{0,1},{1,0},{2,3},{3,2},{4,5},{5,4},{6,7},{7,6},{8,9},{9,8},{10,11... | collective-permute-start | bytes 786440 | tf_op jit(solution)/shard_map/ppermute | solution.py:136
  43.1 3.9 %collective-permute-start.19 = (bf16[2,32,2048]{2,1,0:T(8,128)(2,1)S(1)}, bf16[2,32,2048]{2,1,0:T(8,128)(2,1)S(1)}, u32[]{:S(2)}, u32[]{:S(2)}) collective-permute-start(bf16[2,32,2048]{2,1,0:T(8,128)(2,1)S(1)} %collective-permute-done.16.refs_10_.refs_9_), channel_id=1, source_target_pairs={{0,1},{1,0},{2,3},{3,2},{4,5},{5,4},{6,7},{7,6},{8,9},{9,8},{10,11... | collective-permute-start | bytes 786440 | tf_op jit(solution)/shard_map/ppermute | solution.py:136
  43.5 22.5 %collective-permute-start.10 = (bf16[2,32,2048]{2,1,0:T(8,128)(2,1)S(1)}, bf16[2,32,2048]{2,1,0:T(8,128)(2,1)S(1)}, u32[]{:S(2)}, u32[]{:S(2)}) collective-permute-start(bf16[2,32,2048]{2,1,0:T(8,128)(2,1)S(1)} %get-tuple-element.37), channel_id=1, source_target_pairs={{0,2},{1,3},{2,0},{3,1},{4,6},{5,7},{6,4},{7,5},{8,10},{9,11},{10,... | collective-permute-start | bytes 786440 | tf_op jit(solution)/shard_map/ppermute | solution.py:136
  45.4 20.6 %collective-permute-start.11 = (bf16[2,32,2048]{2,1,0:T(8,128)(2,1)S(1)}, bf16[2,32,2048]{2,1,0:T(8,128)(2,1)S(1)}, u32[]{:S(2)}, u32[]{:S(2)}) collective-permute-start(bf16[2,32,2048]{2,1,0:T(8,128)(2,1)S(1)} %get-tuple-element.38), channel_id=1, source_target_pairs={{0,4},{1,5},{2,6},{3,7},{4,0},{5,1},{6,2},{7,3},{8,12},{9,13},{10,... | collective-permute-start | bytes 786440 | tf_op jit(solution)/shard_map/ppermute | solution.py:136
  46.9 19.1 %collective-permute-start.12 = (bf16[2,32,2048]{2,1,0:T(8,128)(2,1)S(1)}, bf16[2,32,2048]{2,1,0:T(8,128)(2,1)S(1)}, u32[]{:S(2)}, u32[]{:S(2)}) collective-permute-start(bf16[2,32,2048]{2,1,0:T(8,128)(2,1)S(1)} %get-tuple-element.39), channel_id=1, source_target_pairs={{0,6},{1,7},{2,4},{3,5},{4,2},{5,3},{6,0},{7,1},{8,14},{9,15},{10,... | collective-permute-start | bytes 786440 | tf_op jit(solution)/shard_map/ppermute | solution.py:136
  65.9 13.5 %copy-start.1 = (bf16[1,32,2048]{2,1,0:T(8,128)(2,1)S(1)}, bf16[1,32,2048]{2,1,0:T(8,128)(2,1)}, u32[]{:S(2)}) copy-start(bf16[1,32,2048]{2,1,0:T(8,128)(2,1)} %param.8) | copy-start | bytes 393220
  66.1 9.7 %collective-permute-start.20 = (bf16[32,2048]{1,0:T(8,128)(2,1)S(1)}, bf16[32,2048]{1,0:T(8,128)(2,1)S(1)}, u32[]{:S(2)}, u32[]{:S(2)}) collective-permute-start(bf16[32,2048]{1,0:T(8,128)(2,1)S(1)} %fusion.4), channel_id=1, source_target_pairs={{0,1},{1,0},{2,3},{3,2},{4,5},{5,4},{6,7},{7,6},{8,9},{9,8},{10,11... | collective-permute-start | bytes 393224 | tf_op jit(solution)/shard_map/ppermute | solution.py:136
  66.2 9.6 %collective-permute-start.21 = (bf16[4,32,2048]{2,1,0:T(8,128)(2,1)S(1)}, bf16[4,32,2048]{2,1,0:T(8,128)(2,1)S(1)}, u32[]{:S(2)}, u32[]{:S(2)}) collective-permute-start(bf16[4,32,2048]{2,1,0:T(8,128)(2,1)S(1)} %get-tuple-element.54), channel_id=1, source_target_pairs={{0,1},{1,0},{2,3},{3,2},{4,5},{5,4},{6,7},{7,6},{8,9},{9,8},{10,11... | collective-permute-start | bytes 1572872 | tf_op jit(solution)/shard_map/ppermute | solution.py:136
  66.6 14.9 %collective-permute-start.26 = (bf16[8,96,768]{2,1,0:T(8,128)(2,1)S(1)}, bf16[8,96,768]{2,1,0:T(8,128)(2,1)S(1)}, u32[]{:S(2)}, u32[]{:S(2)}) collective-permute-start(bf16[8,96,768]{2,1,0:T(8,128)(2,1)S(1)} %get-tuple-element.55.refs_2_), channel_id=1, source_target_pairs={{0,1},{1,0},{2,3},{3,2},{4,5},{5,4},{6,7},{7,6},{8,9},{9,8},{10,11... | collective-permute-start | bytes 3538952 | tf_op jit(solution)/shard_map/ppermute | solution.py:136
  75.9 14.7 %collective-permute-start.25 = (bf16[32,2048]{1,0:T(8,128)(2,1)S(1)}, bf16[32,2048]{1,0:T(8,128)(2,1)S(1)}, u32[]{:S(2)}, u32[]{:S(2)}) collective-permute-start(bf16[32,2048]{1,0:T(8,128)(2,1)S(1)} %get-tuple-element.63), channel_id=1, source_target_pairs={{0,6},{1,7},{2,4},{3,5},{4,2},{5,3},{6,0},{7,1},{8,14},{9,15},{10,... | collective-permute-start | bytes 393224 | tf_op jit(solution)/shard_map/ppermute | solution.py:136
  78.8 11.8 %collective-permute-start.24 = (bf16[32,2048]{1,0:T(8,128)(2,1)S(1)}, bf16[32,2048]{1,0:T(8,128)(2,1)S(1)}, u32[]{:S(2)}, u32[]{:S(2)}) collective-permute-start(bf16[32,2048]{1,0:T(8,128)(2,1)S(1)} %get-tuple-element.64), channel_id=1, source_target_pairs={{0,4},{1,5},{2,6},{3,7},{4,0},{5,1},{6,2},{7,3},{8,12},{9,13},{10,... | collective-permute-start | bytes 393224 | tf_op jit(solution)/shard_map/ppermute | solution.py:136
  79.3 11.3 %collective-permute-start.23 = (bf16[32,2048]{1,0:T(8,128)(2,1)S(1)}, bf16[32,2048]{1,0:T(8,128)(2,1)S(1)}, u32[]{:S(2)}, u32[]{:S(2)}) collective-permute-start(bf16[32,2048]{1,0:T(8,128)(2,1)S(1)} %get-tuple-element.65), channel_id=1, source_target_pairs={{0,2},{1,3},{2,0},{3,1},{4,6},{5,7},{6,4},{7,5},{8,10},{9,11},{10,... | collective-permute-start | bytes 393224 | tf_op jit(solution)/shard_map/ppermute | solution.py:136
  79.5 13.3 %collective-permute-start.22 = (bf16[32,2048]{1,0:T(8,128)(2,1)S(1)}, bf16[32,2048]{1,0:T(8,128)(2,1)S(1)}, u32[]{:S(2)}, u32[]{:S(2)}) collective-permute-start(bf16[32,2048]{1,0:T(8,128)(2,1)S(1)} %fusion.3), channel_id=1, source_target_pairs={{0,8},{8,16},{16,24},{24,0},{1,9},{9,17},{17,25},{25,1},{2,10},{10... | collective-permute-start | bytes 393224 | tf_op jit(solution)/shard_map/ppermute | solution.py:19
  81.5 9.1 %copy-start.6 = (bf16[1,32,2048]{2,1,0:T(8,128)(2,1)S(1)}, bf16[1,32,2048]{2,1,0:T(8,128)(2,1)}, u32[]{:S(2)}) copy-start(bf16[1,32,2048]{2,1,0:T(8,128)(2,1)} %param.10) | copy-start | bytes 393220
  90.7 5.0 %collective-permute-start.27 = (bf16[32,2048]{1,0:T(8,128)(2,1)S(1)}, bf16[32,2048]{1,0:T(8,128)(2,1)S(1)}, u32[]{:S(2)}, u32[]{:S(2)}) collective-permute-start(bf16[32,2048]{1,0:T(8,128)(2,1)S(1)} %fusion.2), channel_id=1, source_target_pairs={{0,24},{8,0},{16,8},{24,16},{1,25},{9,1},{17,9},{25,17},{2,26},{10... | collective-permute-start | bytes 393224 | tf_op jit(solution)/shard_map/ppermute | solution.py:19

commit v3 on v0

--- a/solution.py
+++ b/solution.py
@@ -1,9 +1,16 @@
+import functools
+
 import jax
 import jax.numpy as jnp
 from jax import lax
+from jax.experimental import pallas as pl
+from jax.experimental.pallas import tpu as pltpu
 from jax.sharding import PartitionSpec as P
 
 CAP = 5
+LANES = 128
+CHUNK = 256
+VMEM_LIMIT = 48 * 1024 * 1024
 
 
 def shifted(value, axis, steps):
@@ -58,7 +65,7 @@
     return (row_grads, weight_part)
 
 
-def on_device(
+def packed_plan(
     section_inputs,
     saved_inputs,
     output_grads,
@@ -123,6 +130,348 @@
     return (next_inputs, prior_grads, weight_grads)
 
 
+def swapped(value, code):
+    axes = ("expert", "dp")
+    count = lax.axis_size(axes[0]) * lax.axis_size(axes[1])
+    return lax.ppermute(value, axes, [(source, source ^ code) for source in range(count)])
+
+
+def pack_kernel(fore_tokens, saved, grads, back_routes, back_gates, fore_routes, fore_gates, out_ref, notes):
+    size, width = fore_tokens.shape
+    top = back_routes.shape[0]
+    for place, ref in enumerate((fore_tokens, saved, grads)):
+        out_ref[:, pl.ds(place * width, width)] = ref[...]
+    notes[...] = jnp.zeros_like(notes)
+    for place, (routes, gates) in enumerate(((back_routes, back_gates), (fore_routes, fore_gates))):
+        first = place * 4 * top
+        notes[pl.ds(first, top), 0:size] = routes[...].astype(jnp.float32)
+        rest = gates[...]
+        for term in range(1, 4):
+            part = rest.astype(jnp.bfloat16).astype(jnp.float32)
+            notes[pl.ds(first + term * top, top), 0:size] = part
+            rest = rest - part
+    out_ref[:, pl.ds(3 * width, LANES)] = notes[...].T[:size, :].astype(jnp.bfloat16)
+
+
+def picks_kernel(count, top, slots, devices, place_ref, *refs):
+    blocks, outs, (notes, turned) = refs[:devices], refs[devices:-2], refs[-2:]
+    tokens = notes.shape[0]
+    for code, block in enumerate(blocks):
+        size = block.shape[0]
+        rows = pl.ds(pl.multiple_of(place_ref[3 + code], size), size)
+        notes[rows, :] = block[...].astype(jnp.float32)
+    turned[...] = notes[...].T
+    row = lax.broadcasted_iota(jnp.int32, (tokens, tokens), 0)
+    column = lax.broadcasted_iota(jnp.int32, (tokens, tokens), 1)
+    earlier = jnp.where(row < column, 1.0, 0.0).astype(jnp.bfloat16)
+    slot = lax.broadcasted_iota(jnp.int32, (slots, tokens), 0).astype(jnp.float32)
+
+    def fill(first, start, picks, gates, flipped):
+        ids = (first + lax.broadcasted_iota(jnp.int32, (count, tokens), 0)).astype(jnp.float32)
+        named = jnp.zeros((count, tokens), jnp.float32)
+        gated = jnp.zeros((count, tokens), jnp.float32)
+        for column in range(start, start + top):
+            same = turned[column : column + 1, :] == ids
+            terms = [turned[column + term * top : column + term * top + 1, :] for term in (1, 2, 3)]
+            named = named + jnp.where(same, 1.0, 0.0)
+            gated = gated + jnp.where(same, terms[0] + terms[1] + terms[2], 0.0)
+        place = jnp.dot(named.astype(jnp.bfloat16), earlier, preferred_element_type=jnp.float32)
+        place = jnp.where(named > 0.0, place, -1.0)
+        for expert in range(count):
+            rows = pl.ds(expert * slots, slots)
+            hit = place[expert : expert + 1, :] == slot
+            picks[rows, :] = jnp.where(hit, 1.0, 0.0).astype(jnp.bfloat16)
+            own = jnp.sum(jnp.where(hit, gated[expert : expert + 1, :], 0.0), axis=1, keepdims=True)
+            gates[rows, :] = jnp.broadcast_to(own, (slots, LANES))
+        if flipped is not None:
+            flipped[...] = picks[...].T
+
+    fill(place_ref[1], 4 * top, outs[0], outs[1], outs[2])
+    fill(place_ref[1], 0, outs[3], outs[4], outs[5])
+    fill(place_ref[2], 0, outs[6], outs[7], None)
+
+
+def spread_gate(gates, rows, width):
+    gate = gates[rows, 0:1]
+    return jnp.broadcast_to(gate, (gate.shape[0], width))
+
+
+def assemble(place_ref, blocks, columns, tokens):
+    for code, block in enumerate(blocks):
+        size = block.shape[0]
+        rows = pl.ds(pl.multiple_of(place_ref[3 + code], size), size)
+        tokens[rows, :] = block[:, columns]
+
+
+def combine(place_ref, flipped, results, sums, outs):
+    width = sums.shape[1]
+    for start in range(0, width, CHUNK):
+        columns = pl.ds(start, CHUNK)
+        sums[:, columns] = jnp.dot(
+            flipped[...], results[:, columns], preferred_element_type=jnp.float32
+        ).astype(sums.dtype)
+    for out, lead, code in outs:
+        size = out.shape[-2]
+        rows = pl.ds(pl.multiple_of(place_ref[3 + code], size), size)
+        out[lead] = sums[rows, :]
+
+
+def gather(count, slots, picks, gates, tokens_ref, rows, first, stride):
+    width = tokens_ref.shape[1]
+    for start in range(0, width, CHUNK):
+        columns = pl.ds(start, CHUNK)
+        taken = jnp.dot(picks[...], tokens_ref[:, columns], preferred_element_type=jnp.float32)
+        if gates is not None:
+            taken = taken * spread_gate(gates, pl.ds(0, count * slots), CHUNK)
+        taken = taken.astype(rows.dtype)
+        for expert in range(count):
+            part = slice(expert * slots, (expert + 1) * slots)
+            rows[pl.ds(first + expert * stride, slots), columns] = taken[part]
+
+
+def expert_kernel(count, slots, devices, pair, place_ref, *refs):
+    fore_picks, fore_gates, fore_flip, back_picks, back_gates, back_flip, weights_ref = refs[:7]
+    blocks = refs[7 : 7 + devices]
+    near_outs = refs[7 + devices : 7 + devices + devices // pair]
+    far_out, inner_ref, tokens, rows, fore_results, back_results, second = refs[-7:]
+    step = pl.program_id(0)
+    width = tokens.shape[1]
+
+    @pl.when(step == 0)
+    def _():
+        taken = ((fore_picks, None), (back_picks, None), (back_picks, back_gates))
+        for place, (picks, gates) in enumerate(taken):
+            assemble(place_ref, blocks, pl.ds(place * width, width), tokens)
+            gather(count, slots, picks, gates, tokens, rows, place * slots, 3 * slots)
+
+    mine = pl.ds(pl.multiple_of(step * slots, slots), slots)
+    three = pl.ds(pl.multiple_of(step * 3 * slots, 3 * slots), 3 * slots)
+    product = jnp.dot(rows[three, :], weights_ref[0], preferred_element_type=jnp.float32)
+    ahead, hidden, active_grads = product[:slots], product[slots : 2 * slots], product[2 * slots :]
+    sigma = jax.nn.sigmoid(hidden)
+    hidden_grads = (active_grads * sigma * (1.0 + hidden * (1.0 - sigma))).astype(jnp.bfloat16)
+    inner_ref[0, :slots, :] = hidden_grads
+    inner_ref[0, slots:, :] = (hidden * sigma).astype(jnp.bfloat16)
+    second[:slots, :] = (ahead * jax.nn.sigmoid(ahead)).astype(jnp.bfloat16)
+    second[slots:, :] = hidden_grads
+    result = lax.dot_general(
+        second[...], weights_ref[0], (((1,), (1,)), ((), ())), preferred_element_type=jnp.float32
+    )
+    fore_results[mine, :] = (result[:slots] * spread_gate(fore_gates, mine, width)).astype(
+        fore_results.dtype
+    )
+    back_results[mine, :] = result[slots:].astype(back_results.dtype)
+
+    @pl.when(step == count - 1)
+    def _():
+        for lead, (flipped, results) in enumerate(((fore_flip, fore_results), (back_flip, back_results))):
+            outs = [(out, lead, pair * group) for group, out in enumerate(near_outs)]
+            outs += [(far_out, (group, lead), pair * group + 1) for group in range(len(near_outs))]
+            combine(place_ref, flipped, results, tokens, outs)
+
+
+def weight_kernel(count, slots, devices, place_ref, *refs):
+    picks, gates, inner_ref = refs[:3]
+    saved, grads = refs[3 : 3 + devices], refs[3 + devices : 3 + 2 * devices]
+    out_ref, tokens, rows = refs[-3:]
+    step = pl.program_id(0)
+    half = tokens.shape[1]
+
+    @pl.when(step == 0)
+    def _():
+        for place, (blocks, scale) in enumerate(((saved, None), (grads, gates))):
+            assemble(place_ref, blocks, pl.ds(0, half), tokens)
+            gather(count, slots, picks, scale, tokens, rows, place * slots, 2 * slots)
+
+    both = pl.ds(pl.multiple_of(step * 2 * slots, 2 * slots), 2 * slots)
+    flat = rows[both, :].T
+    for start in range(0, inner_ref.shape[-1], CHUNK):
+        columns = pl.ds(start, CHUNK)
+        out_ref[0, :, columns] = jnp.dot(
+            flat, inner_ref[0, :, columns], preferred_element_type=jnp.float32
+        ).astype(out_ref.dtype)
+
+
+def gathered_plan(
+    section_inputs,
+    saved_inputs,
+    output_grads,
+    forward_routes,
+    backward_routes,
+    forward_gates,
+    backward_gates,
+    expert_weights,
+):
+    token_count = section_inputs.shape[1]
+    top = forward_routes.shape[2]
+    _, local_count, width, inner_width = expert_weights.shape
+    groups, pair = lax.axis_size("expert"), lax.axis_size("dp")
+    devices = groups * pair
+    count = local_count // pair
+    total = devices * token_count
+    slots = -(-devices * CAP // 16) * 16
+    rows = count * slots
+    half = width // pair
+    weights = expert_weights[0]
+
+    side, group = lax.axis_index("dp"), lax.axis_index("expert")
+    index = group * pair + side
+    base = group * local_count
+    place = jnp.stack(
+        [side, base + side * count, base + (1 - side) * count]
+        + [(index ^ code) * token_count for code in range(devices)]
+    ).astype(jnp.int32)
+    params = pltpu.CompilerParams(vmem_limit_bytes=VMEM_LIMIT, dimension_semantics=("arbitrary",))
+
+    def whole(shape):
+        return pl.BlockSpec(shape, lambda *_: (0,) * len(shape))
+
+    def call(kernel, name, steps, in_specs, out_specs, out_shape, scratch, flops=0, aliases=()):
+        return pl.pallas_call(
+            kernel,
+            grid_spec=pltpu.PrefetchScalarGridSpec(
+                num_scalar_prefetch=1,
+                grid=(steps,),
+                in_specs=in_specs,
+                out_specs=out_specs,
+                scratch_shapes=scratch,
+            ),
+            out_shape=out_shape,
+            compiler_params=params,
+            cost_estimate=pl.CostEstimate(
+                flops=flops, bytes_accessed=flops // 512 + 1024, transcendentals=0
+            ),
+            input_output_aliases=dict(aliases),
+            name=name,
+        )
+
+    def onward(block):
+        return swapped(block, 1)
+
+    def across(parts):
+        return [swapped(part, code) for part, code in zip(parts, range(pair, devices, pair))]
+
+    def after(first, then):
+        then, _ = lax.optimization_barrier((then, first))
+        return then
+
+    def summed(*blocks):
+        return functools.reduce(jnp.add, [block.astype(jnp.float32) for block in blocks])
+
+    packed = jax.ShapeDtypeStruct((token_count, 3 * width + LANES), jnp.bfloat16)
+    own = pl.pallas_call(
+        pack_kernel,
+        in_specs=[pl.BlockSpec(memory_space=pltpu.VMEM)] * 7,
+        out_specs=pl.BlockSpec(memory_space=pltpu.VMEM),
+        out_shape=packed,
+        scratch_shapes=[pltpu.VMEM((LANES, LANES), jnp.float32)],
+        compiler_params=pltpu.CompilerParams(vmem_limit_bytes=VMEM_LIMIT),
+        name="pack",
+    )(
+        section_inputs[0],
+        saved_inputs[0],
+        output_grads[0],
+        backward_routes[0].T,
+        backward_gates[0].T,
+        forward_routes[0].T,
+        forward_gates[0].T,
+    )
+    near = [own] + across([own] * (groups - 1))
+    blocks = [block for one in near for block in (one, onward(one))]
+
+    pick = jax.ShapeDtypeStruct((rows, total), jnp.bfloat16)
+    flip = jax.ShapeDtypeStruct((total, rows), jnp.bfloat16)
+    gate = jax.ShapeDtypeStruct((rows, LANES), jnp.float32)
+    pick_outs = [pick, gate, flip, pick, gate, flip, pick, gate]
+    picks = call(
+        functools.partial(picks_kernel, count, top, slots, devices),
+        "slot_picks",
+        1,
+        [pl.BlockSpec((token_count, LANES), lambda *_: (0, 3 * width // LANES))] * devices,
+        [whole(out.shape) for out in pick_outs],
+        pick_outs,
+        [pltpu.VMEM((total, LANES), jnp.float32), pltpu.VMEM((LANES, total), jnp.float32)],
+    )(place, *blocks)
+
+    pass_flops = 2 * 2 * count * CHUNK * width * inner_width
+    near_part = jax.ShapeDtypeStruct((2, token_count, width), jnp.bfloat16)
+    far_part = jax.ShapeDtypeStruct((groups, 2, token_count, width), jnp.bfloat16)
+    inner = jax.ShapeDtypeStruct((count, 2 * slots, inner_width), jnp.bfloat16)
+    inner_spec = pl.BlockSpec((1, 2 * slots, inner_width), lambda step, place: (step, 0, 0))
+    *near_parts, far_sums, inner_own = call(
+        functools.partial(expert_kernel, count, slots, devices, pair),
+        "experts",
+        count,
+        [whole(array.shape) for array in picks[:6]]
+        + [pl.BlockSpec((1, width, inner_width), lambda step, place: (place[0] * count + step, 0, 0))]
+        + [whole(packed.shape)] * devices,
+        [whole(near_part.shape)] * groups + [whole(far_part.shape), inner_spec],
+        [near_part] * groups + [far_part, inner],
+        [
+            pltpu.VMEM((total, width), jnp.bfloat16),
+            pltpu.VMEM((3 * rows, width), jnp.bfloat16),
+            pltpu.VMEM((rows, width), jnp.bfloat16),
+            pltpu.VMEM((rows, width), jnp.bfloat16),
+            pltpu.VMEM((2 * slots, inner_width), jnp.bfloat16),
+        ],
+        pass_flops,
+    )(place, *picks[:6], weights, *blocks)
+    far_sums = onward(far_sums)
+    inner_other = onward(inner_own)
+
+    def gradient(whose, inner_rows, picked, earlier):
+        earlier = [] if earlier is None else [earlier]
+
+        def out_block(step, place):
+            owner = place[0] if whose == 0 else 1 - place[0]
+            return (owner * count + step, 0, 0)
+
+        specs = [whole(pick.shape), whole(gate.shape), inner_spec]
+        for first in (pair, 2 * pair):
+            specs += [
+                pl.BlockSpec((token_count, half), lambda step, place, first=first: (0, first + place[0]))
+            ] * devices
+        specs += [pl.BlockSpec(memory_space=pl.ANY)] * len(earlier)
+        return call(
+            functools.partial(weight_kernel, count, slots, devices),
+            "weight_gradient_" + ("own", "other")[whose],
+            count,
+            specs,
+            pl.BlockSpec((1, half, inner_width), out_block),
+            jax.ShapeDtypeStruct((local_count, half, inner_width), jnp.bfloat16),
+            [pltpu.VMEM((total, half), jnp.bfloat16), pltpu.VMEM((2 * rows, half), jnp.bfloat16)],
+            pass_flops // 2,
+            [(len(specs), 0)] if earlier else [],
+        )(place, *picked, inner_rows, *blocks, *blocks, *earlier)
+
+    own_done = gradient(0, inner_own, picks[3:5], None)
+    far_sums = after(own_done, far_sums)
+    sums = [
+        summed(part, far_sums[group]).astype(jnp.bfloat16) for group, part in enumerate(near_parts)
+    ]
+    near_sums = across(sums[1:])
+    weight_grads = gradient(1, inner_other, picks[6:8], own_done)
+    near_sums = after(weight_grads, near_sums)
+    moved = summed(sums[0], *near_sums)
+    layer_out = (section_inputs[0].astype(jnp.float32) + moved[0]).astype(jnp.bfloat16)
+    input_grads = (output_grads[0].astype(jnp.float32) + moved[1]).astype(jnp.bfloat16)
+    next_inputs = shifted(layer_out, "pipe", 1)[None]
+    prior_grads = shifted(input_grads, "pipe", -1)[None]
+    return (next_inputs, prior_grads, weight_grads[None])
+
+
+def on_device(*arrays):
+    token_count = arrays[0].shape[1]
+    local_count = arrays[-1].shape[1]
+    groups, pair = lax.axis_size("expert"), lax.axis_size("dp")
+    gathered = groups * token_count
+    packed = groups * local_count * CAP
+    paired = pair == 2 and local_count % pair == 0 and groups & (groups - 1) == 0
+    if gathered <= packed and paired and gathered * pair % LANES == 0:
+        return gathered_plan(*arrays)
+    return packed_plan(*arrays)
+
+
 def solution(mesh):
     placed = (
         P("pipe", ("expert", "dp"), None),

time: 327 us -> 92.8 us (0.28); the launches traced: 321 us -> 92.2 us
  matrix products: 200 us -> 0 us
  Pallas kernels: 0 us -> 42.5 us
  local copies, waits for them, and re-layouts: 36.5 us -> 8.13 us
  starting transfers between devices: 27.8 us -> 12.5 us
  between operations: 15.1 us -> 0.72 us
  other arithmetic: 9.55 us -> 0.47 us
  waiting for transfers between devices: 32.5 us -> 27.8 us
    dot_general x6 -> x0, matrix products: 200 us -> none  [the longest x1 50.6 us: expert_forward(): jnp.einsum('nlch,ldh->nlcd', active, weights, preferred_element_type=jnp....]
    pallas_call x0 -> x5, Pallas kernels: none -> 42.5 us  [the longest x1 21.5 us: gathered_plan(): call(functools.partial(expert_kernel, count, slots, devices, pair), 'expe...]
    all_to_all x5 -> x0, waiting for transfers between devices: 30 us -> none  [the longest x1 14.1 us: on_device(): lax.all_to_all(forward_rows, 'expert', split_axis=0, concat_axis=0, tiled...]
    all_to_all x5 -> x0, starting transfers between devices: 21.9 us -> none  [the longest x1 5.29 us: on_device(): lax.all_to_all(saved_rows, 'expert', split_axis=0, concat_axis=0, tiled=T...]
    ppermute x0 -> x12, waiting for transfers between devices: none -> 21 us  [swapped(): lax.ppermute(value, axes, [(source, source ^ code) for source in range(co...]
    gather x6 -> x0, local copies, waits for them, and re-layouts: 13.4 us -> none  [the longest x4 10.2 us: pack_rows(): picked = jnp.take(source, jnp.maximum(owner_row - 1, 0) // spread, axis=0)]
    ppermute x0 -> x12, starting transfers between devices: none -> 8.88 us  [swapped(): lax.ppermute(value, axes, [(source, source ^ code) for source in range(co...]
    reshape x6 -> x0, local copies, waits for them, and re-layouts: 6.12 us -> none  [the longest x2 2.48 us: on_device(): pack_rows(section_inputs[0], forward_slot, slot_total, route_count)]
  transfers between devices with their start and end apart: 8 -> 14, of which waited for: 4 -> 9; matrix products, arithmetic and copies ran while one was open for 39% -> 0% of each run, Pallas kernels for 0% -> 21%
where the time goes in v3:
time: 92.8 us; the launch traced here: 92.2 us
  Pallas kernels  42.5 us (46%)
  waiting for transfers between devices  27.8 us (30%)
  starting transfers between devices  12.5 us (13%)
  local copies, waits for them, and re-layouts  8.13 us (9%)
    pallas_call x1, Pallas kernels, gathered_plan(): call(functools.partial(expert_kernel, count, slots, devices, pair), 'expe...  21.5 us
    ppermute x12, waiting for transfers between devices, swapped(): lax.ppermute(value, axes, [(source, source ^ code) for source in range(co...  21 us
    pallas_call x2, Pallas kernels, gradient(): call(functools.partial(weight_kernel, count, slots, devices), 'weight_gra...  19.8 us
    ppermute x12, starting transfers between devices, swapped(): lax.ppermute(value, axes, [(source, source ^ code) for source in range(co...  8.88 us
    unnamed x22, local copies, waits for them, and re-layouts  8.04 us
    ppermute x2, waiting for transfers between devices, shifted(): return lax.ppermute(value, axis, pairs)  6.83 us
    ppermute x2, starting transfers between devices, shifted(): return lax.ppermute(value, axis, pairs)  3.64 us
  transfers between devices with their start and end apart: 14, of which 9 were waited for; matrix products, arithmetic and copies ran while one was open for 0% of the time, Pallas kernels for 21%

profile of v3, /device:TPU:0, one launch (start us, length us, event | category | flops | bytes accessed | tf_op | source)
XLA Modules:
  0.0 92.2 jit_solution(10658138648224927185)
XLA Ops:
  0.6 0.0 copy-start.1
  0.6 0.9 copy-done.1
  1.5 0.0 copy-start.3
  1.5 0.9 copy-done.3
  2.4 0.0 copy-start.5
  2.4 0.9 copy-done.5
  3.3 0.0 copy-start.6
  3.4 0.7 copy-done.6
  4.0 0.0 copy-start.7
  4.0 0.7 copy-done.7
  4.7 0.0 copy-start.8
  4.7 0.7 copy-done.8
  5.4 0.0 copy-start.9
  5.4 0.7 copy-done.9
  6.1 0.1 pack.1.refs_0_.refs_7_.refs_3_.refs_11_
  6.2 3.9 %collective-permute-start.5 = (bf16[32,6272]{1,0:T(8,128)(2,1)S(1)}, bf16[32,6272]{1,0:T(8,128)(2,1)S(1)}, u32[]{:S(2)}, u32[]{:S(2)}) collective-permute-start(bf16[32,6272]{1,0:T(8,128)(2,1)S(1)} %pack.1.refs_0_.refs_7_.refs_3_.refs_11_), channel_id=1, source_target_pairs={{0,6},{1,7},{2,4},{3,5},{4,2},{5,3},{6,0},{7,1},{8,14},{9,15},{10,... | collective-permute-start | bytes 1204232 | tf_op jit(solution)/shard_map/ppermute | solution.py:136
  10.1 0.5 collective-permute-start.3
  10.6 0.1 collective-permute-start.1
  10.8 0.0 collective-permute-start
  10.8 9.5 %collective-permute-done.5.refs_6_.refs_13_.refs_9_.refs_17_ = bf16[32,6272]{1,0:T(8,128)(2,1)S(1)} collective-permute-done((bf16[32,6272]{1,0:T(8,128)(2,1)S(1)}, bf16[32,6272]{1,0:T(8,128)(2,1)S(1)}, u32[]{:S(2)}, u32[]{:S(2)}) %collective-permute-start.5) | collective-permute-done | bytes 401440 | tf_op jit(solution)/shard_map/ppermute | solution.py:136
  20.3 0.0 collective-permute-start.6
  20.3 7.7 %collective-permute-done.3.refs_4_.refs_11_.refs_7_.refs_15_ = bf16[32,6272]{1,0:T(8,128)(2,1)S(1)} collective-permute-done((bf16[32,6272]{1,0:T(8,128)(2,1)S(1)}, bf16[32,6272]{1,0:T(8,128)(2,1)S(1)}, u32[]{:S(2)}, u32[]{:S(2)}) %collective-permute-start.3) | collective-permute-done | bytes 401440 | tf_op jit(solution)/shard_map/ppermute | solution.py:136
  28.0 0.0 collective-permute-start.4
  28.0 0.3 collective-permute-done.1.refs_2_.refs_9_.refs_5_.refs_13_
  28.3 0.2 collective-permute-start.2
  28.5 0.1 stack.47.place_ref
  28.6 0.0 collective-permute-done.refs_1_.refs_8_.refs_4_.refs_12_
  28.6 0.0 collective-permute-done.6.refs_7_.refs_14_.refs_10_.refs_18_
  28.6 1.1 %collective-permute-done.4.refs_5_.refs_12_.refs_8_.refs_16_ = bf16[32,6272]{1,0:T(8,128)(2,1)S(1)} collective-permute-done((bf16[32,6272]{1,0:T(8,128)(2,1)S(1)}, bf16[32,6272]{1,0:T(8,128)(2,1)S(1)}, u32[]{:S(2)}, u32[]{:S(2)}) %collective-permute-start.4) | collective-permute-done | bytes 401440 | tf_op jit(solution)/shard_map/ppermute | solution.py:136
  29.7 0.6 collective-permute-done.2.refs_3_.refs_10_.refs_6_.refs_14_
  30.3 1.2 %slot_picks.1 = (bf16[384,256]{1,0:T(8,128)(2,1)S(1)}, f32[384,128]{1,0:T(8,128)S(1)}, bf16[256,384]{1,0:T(8,128)(2,1)S(1)}, bf16[384,256]{1,0:T(8,128)(2,1)S(1)...) custom-call(s32[11]{0:T(128)S(1)} %stack.47.place_ref, ...), custom_call_target="tpu_custom_call" | custom-call | bytes 1024 | tf_op jit(solution)/shard_map/slot_picks/pallas_call | solution.py:386
  31.5 21.5 %experts.1 = (bf16[2,32,2048]{2,1,0:T(8,128)(2,1)S(1)}, bf16[2,32,2048]{2,1,0:T(8,128)(2,1)S(1)}, bf16[2,32,2048]{2,1,0:T(8,128)(2,1)S(1)}, bf16[2,32,2048]{2,1,...) custom-call(s32[11]{0:T(128)S(1)} %stack.47.place_ref, ...), custom_call_target="tpu_custom_call" | custom-call | flops 12884901888 | bytes 25166848 | tf_op jit(solution)/shard_map/experts/pallas_call | solution.py:401
  53.0 0.1 collective-permute-start.7
  53.1 0.4 collective-permute-start.11
  53.5 0.0 copy-start
  53.5 1.3 %copy-done = bf16[8,96,768]{2,1,0:T(8,128)(2,1)S(1)} copy-done((bf16[8,96,768]{2,1,0:T(8,128)(2,1)S(1)}, bf16[8,96,768]{2,1,0:T(8,128)(2,1)}, u32[]{:S(2)}) %copy-start) | copy-done | bytes 1179672
  54.8 9.9 %weight_gradient_own.1.refs_19_ = bf16[16,1024,768]{2,1,0:T(8,128)(2,1)} custom-call(s32[11]{0:T(128)S(1)} %stack.47.place_ref, bf16[384,256]{1,0:T(8,128)(2,1)S(1)} %get-tuple-element.24.refs_3_.refs_0_, f32[384,128]{1,0:T(8,128)S(1)} %get-tuple-element.25.refs_4_.refs_1_, bf16[8,96,768]{2,1,0:T(8,128)(2,1)S(1)} %copy-done, ...), custom_call_target="tpu_custom_call" | custom-call | flops 6442450944 | bytes 12583936 | tf_op jit(solution)/shard_map/weight_gradient_own/pallas_call | solution.py:435
  64.7 0.0 collective-permute-done.7
  64.7 0.3 fusion
  64.9 1.9 %collective-permute-start.10 = (bf16[2,32,2048]{2,1,0:T(8,128)(2,1)S(1)}, bf16[2,32,2048]{2,1,0:T(8,128)(2,1)S(1)}, u32[]{:S(2)}, u32[]{:S(2)}) collective-permute-start(bf16[2,32,2048]{2,1,0:T(8,128)(2,1)S(1)} %get-tuple-element.39), channel_id=1, source_target_pairs={{0,6},{1,7},{2,4},{3,5},{4,2},{5,3},{6,0},{7,1},{8,14},{9,15},{10,... | collective-permute-start | bytes 786440 | tf_op jit(solution)/shard_map/ppermute | solution.py:136
  66.8 1.3 %collective-permute-start.9 = (bf16[2,32,2048]{2,1,0:T(8,128)(2,1)S(1)}, bf16[2,32,2048]{2,1,0:T(8,128)(2,1)S(1)}, u32[]{:S(2)}, u32[]{:S(2)}) collective-permute-start(bf16[2,32,2048]{2,1,0:T(8,128)(2,1)S(1)} %get-tuple-element.40), channel_id=1, source_target_pairs={{0,4},{1,5},{2,6},{3,7},{4,0},{5,1},{6,2},{7,3},{8,12},{9,13},{10,... | collective-permute-start | bytes 786440 | tf_op jit(solution)/shard_map/ppermute | solution.py:136
  68.1 0.4 collective-permute-start.8
  68.5 0.0 collective-permute-done.11.refs_2_
  68.5 0.0 copy-start.2
  68.5 0.0 copy-start.4
  68.5 9.9 %weight_gradient_other.1 = bf16[16,1024,768]{2,1,0:T(8,128)(2,1)} custom-call(s32[11]{0:T(128)S(1)} %stack.47.place_ref, bf16[384,256]{1,0:T(8,128)(2,1)S(1)} %get-tuple-element.34.refs_0_, f32[384,128]{1,0:T(8,128)S(1)} %get-tuple-element.35.refs_1_, bf16[8,96,768]{2,1,0:T(8,128)(2,1)S(1)} %collective-permute-done.11.refs_2_, ...), custom_call_target="tpu_custom_call", output_to_operand_aliasing={{}: (20, {})} | custom-call | flops 6442450944 | bytes 12583936 | tf_op jit(solution)/shard_map/weight_gradient_other/pallas_call | solution.py:435
  78.4 0.0 collective-permute-done.10
  78.4 1.5 %collective-permute-done.9 = bf16[2,32,2048]{2,1,0:T(8,128)(2,1)S(1)} collective-permute-done((bf16[2,32,2048]{2,1,0:T(8,128)(2,1)S(1)}, bf16[2,32,2048]{2,1,0:T(8,128)(2,1)S(1)}, u32[]{:S(2)}, u32[]{:S(2)}) %collective-permute-start.9) | collective-permute-done | bytes 262176 | tf_op jit(solution)/shard_map/ppermute | solution.py:136
  79.9 0.3 collective-permute-done.8
  80.2 0.2 convert_add_fusion.4
  80.3 0.0 copy-done.2
  80.3 0.0 copy-done.4
  80.4 3.6 %collective-permute-start.13 = (bf16[32,2048]{1,0:T(8,128)(2,1)S(1)}, bf16[32,2048]{1,0:T(8,128)(2,1)S(1)}, u32[]{:S(2)}, u32[]{:S(2)}) collective-permute-start(bf16[32,2048]{1,0:T(8,128)(2,1)S(1)} %get-tuple-element.42), channel_id=1, source_target_pairs={{0,24},{8,0},{16,8},{24,16},{1,25},{9,1},{17,9},{25,17},{2,26},{10... | collective-permute-start | bytes 393224 | tf_op jit(solution)/shard_map/ppermute | solution.py:19
  84.0 0.0 collective-permute-start.12
  84.0 3.9 %collective-permute-done.13 = bf16[32,2048]{1,0:T(8,128)(2,1)S(1)} collective-permute-done((bf16[32,2048]{1,0:T(8,128)(2,1)S(1)}, bf16[32,2048]{1,0:T(8,128)(2,1)S(1)}, u32[]{:S(2)}, u32[]{:S(2)}) %collective-permute-start.13) | collective-permute-done | bytes 131104 | tf_op jit(solution)/shard_map/ppermute | solution.py:19
  87.9 2.9 %collective-permute-done.12 = bf16[32,2048]{1,0:T(8,128)(2,1)S(1)} collective-permute-done((bf16[32,2048]{1,0:T(8,128)(2,1)S(1)}, bf16[32,2048]{1,0:T(8,128)(2,1)S(1)}, u32[]{:S(2)}, u32[]{:S(2)}) %collective-permute-start.12) | collective-permute-done | bytes 131104 | tf_op jit(solution)/shard_map/ppermute | solution.py:19
  90.9 0.7 copy.15
  91.5 0.7 copy.16
  (1 shorter events, 0.0 us)
Async XLA Ops:
  0.6 0.9 copy-start.1
  1.5 0.9 copy-start.3
  2.4 0.9 copy-start.5
  3.3 0.7 copy-start.6
  4.0 0.7 copy-start.7
  4.7 0.7 copy-start.8
  5.4 0.7 copy-start.9
  6.2 14.1 %collective-permute-start.5 = (bf16[32,6272]{1,0:T(8,128)(2,1)S(1)}, bf16[32,6272]{1,0:T(8,128)(2,1)S(1)}, u32[]{:S(2)}, u32[]{:S(2)}) collective-permute-start(bf16[32,6272]{1,0:T(8,128)(2,1)S(1)} %pack.1.refs_0_.refs_7_.refs_3_.refs_11_), channel_id=1, source_target_pairs={{0,6},{1,7},{2,4},{3,5},{4,2},{5,3},{6,0},{7,1},{8,14},{9,15},{10,... | collective-permute-start | bytes 1204232 | tf_op jit(solution)/shard_map/ppermute | solution.py:136
  10.1 17.9 %collective-permute-start.3 = (bf16[32,6272]{1,0:T(8,128)(2,1)S(1)}, bf16[32,6272]{1,0:T(8,128)(2,1)S(1)}, u32[]{:S(2)}, u32[]{:S(2)}) collective-permute-start(bf16[32,6272]{1,0:T(8,128)(2,1)S(1)} %pack.1.refs_0_.refs_7_.refs_3_.refs_11_), channel_id=1, source_target_pairs={{0,4},{1,5},{2,6},{3,7},{4,0},{5,1},{6,2},{7,3},{8,12},{9,13},{10,... | collective-permute-start | bytes 1204232 | tf_op jit(solution)/shard_map/ppermute | solution.py:136
  10.6 17.7 %collective-permute-start.1 = (bf16[32,6272]{1,0:T(8,128)(2,1)S(1)}, bf16[32,6272]{1,0:T(8,128)(2,1)S(1)}, u32[]{:S(2)}, u32[]{:S(2)}) collective-permute-start(bf16[32,6272]{1,0:T(8,128)(2,1)S(1)} %pack.1.refs_0_.refs_7_.refs_3_.refs_11_), channel_id=1, source_target_pairs={{0,2},{1,3},{2,0},{3,1},{4,6},{5,7},{6,4},{7,5},{8,10},{9,11},{10,... | collective-permute-start | bytes 1204232 | tf_op jit(solution)/shard_map/ppermute | solution.py:136
  10.8 17.9 %collective-permute-start = (bf16[32,6272]{1,0:T(8,128)(2,1)S(1)}, bf16[32,6272]{1,0:T(8,128)(2,1)S(1)}, u32[]{:S(2)}, u32[]{:S(2)}) collective-permute-start(bf16[32,6272]{1,0:T(8,128)(2,1)S(1)} %pack.1.refs_0_.refs_7_.refs_3_.refs_11_), channel_id=1, source_target_pairs={{0,1},{1,0},{2,3},{3,2},{4,5},{5,4},{6,7},{7,6},{8,9},{9,8},{10,11... | collective-permute-start | bytes 1204232 | tf_op jit(solution)/shard_map/ppermute | solution.py:136
  20.3 8.3 %collective-permute-start.6 = (bf16[32,6272]{1,0:T(8,128)(2,1)S(1)}, bf16[32,6272]{1,0:T(8,128)(2,1)S(1)}, u32[]{:S(2)}, u32[]{:S(2)}) collective-permute-start(bf16[32,6272]{1,0:T(8,128)(2,1)S(1)} %collective-permute-done.5.refs_6_.refs_13_.refs_9_.refs_17_), channel_id=1, source_target_pairs={{0,1},{1,0},{2,3},{3,2},{4,5},{5,4},{6,7},{7,6},{8,9},{9,8},{10,11... | collective-permute-start | bytes 1204232 | tf_op jit(solution)/shard_map/ppermute | solution.py:136
  28.0 1.7 %collective-permute-start.4 = (bf16[32,6272]{1,0:T(8,128)(2,1)S(1)}, bf16[32,6272]{1,0:T(8,128)(2,1)S(1)}, u32[]{:S(2)}, u32[]{:S(2)}) collective-permute-start(bf16[32,6272]{1,0:T(8,128)(2,1)S(1)} %collective-permute-done.3.refs_4_.refs_11_.refs_7_.refs_15_), channel_id=1, source_target_pairs={{0,1},{1,0},{2,3},{3,2},{4,5},{5,4},{6,7},{7,6},{8,9},{9,8},{10,11... | collective-permute-start | bytes 1204232 | tf_op jit(solution)/shard_map/ppermute | solution.py:136
  28.3 2.0 %collective-permute-start.2 = (bf16[32,6272]{1,0:T(8,128)(2,1)S(1)}, bf16[32,6272]{1,0:T(8,128)(2,1)S(1)}, u32[]{:S(2)}, u32[]{:S(2)}) collective-permute-start(bf16[32,6272]{1,0:T(8,128)(2,1)S(1)} %collective-permute-done.1.refs_2_.refs_9_.refs_5_.refs_13_), channel_id=1, source_target_pairs={{0,1},{1,0},{2,3},{3,2},{4,5},{5,4},{6,7},{7,6},{8,9},{9,8},{10,11... | collective-permute-start | bytes 1204232 | tf_op jit(solution)/shard_map/ppermute | solution.py:136
  53.0 11.7 %collective-permute-start.7 = (bf16[4,2,32,2048]{3,2,1,0:T(8,128)(2,1)}, bf16[4,2,32,2048]{3,2,1,0:T(8,128)(2,1)S(1)}, u32[]{:S(2)}, u32[]{:S(2)}) collective-permute-start(bf16[4,2,32,2048]{3,2,1,0:T(8,128)(2,1)} %get-tuple-element.28), channel_id=1, source_target_pairs={{0,1},{1,0},{2,3},{3,2},{4,5},{5,4},{6,7},{7,6},{8,9},{9,8},{10,11... | collective-permute-start | bytes 3145736 | tf_op jit(solution)/shard_map/ppermute | solution.py:136
  53.1 15.4 %collective-permute-start.11 = (bf16[8,96,768]{2,1,0:T(8,128)(2,1)}, bf16[8,96,768]{2,1,0:T(8,128)(2,1)S(1)}, u32[]{:S(2)}, u32[]{:S(2)}) collective-permute-start(bf16[8,96,768]{2,1,0:T(8,128)(2,1)} %get-tuple-element.29.refs_2_), channel_id=1, source_target_pairs={{0,1},{1,0},{2,3},{3,2},{4,5},{5,4},{6,7},{7,6},{8,9},{9,8},{10,11... | collective-permute-start | bytes 3538952 | tf_op jit(solution)/shard_map/ppermute | solution.py:136
  53.5 1.3 %copy-start = (bf16[8,96,768]{2,1,0:T(8,128)(2,1)S(1)}, bf16[8,96,768]{2,1,0:T(8,128)(2,1)}, u32[]{:S(2)}) copy-start(bf16[8,96,768]{2,1,0:T(8,128)(2,1)} %get-tuple-element.29.refs_2_) | copy-start | bytes 3538948
  64.9 13.4 %collective-permute-start.10 = (bf16[2,32,2048]{2,1,0:T(8,128)(2,1)S(1)}, bf16[2,32,2048]{2,1,0:T(8,128)(2,1)S(1)}, u32[]{:S(2)}, u32[]{:S(2)}) collective-permute-start(bf16[2,32,2048]{2,1,0:T(8,128)(2,1)S(1)} %get-tuple-element.39), channel_id=1, source_target_pairs={{0,6},{1,7},{2,4},{3,5},{4,2},{5,3},{6,0},{7,1},{8,14},{9,15},{10,... | collective-permute-start | bytes 786440 | tf_op jit(solution)/shard_map/ppermute | solution.py:136
  66.8 13.0 %collective-permute-start.9 = (bf16[2,32,2048]{2,1,0:T(8,128)(2,1)S(1)}, bf16[2,32,2048]{2,1,0:T(8,128)(2,1)S(1)}, u32[]{:S(2)}, u32[]{:S(2)}) collective-permute-start(bf16[2,32,2048]{2,1,0:T(8,128)(2,1)S(1)} %get-tuple-element.40), channel_id=1, source_target_pairs={{0,4},{1,5},{2,6},{3,7},{4,0},{5,1},{6,2},{7,3},{8,12},{9,13},{10,... | collective-permute-start | bytes 786440 | tf_op jit(solution)/shard_map/ppermute | solution.py:136
  68.1 12.0 %collective-permute-start.8 = (bf16[2,32,2048]{2,1,0:T(8,128)(2,1)S(1)}, bf16[2,32,2048]{2,1,0:T(8,128)(2,1)S(1)}, u32[]{:S(2)}, u32[]{:S(2)}) collective-permute-start(bf16[2,32,2048]{2,1,0:T(8,128)(2,1)S(1)} %get-tuple-element.41), channel_id=1, source_target_pairs={{0,2},{1,3},{2,0},{3,1},{4,6},{5,7},{6,4},{7,5},{8,10},{9,11},{10,... | collective-permute-start | bytes 786440 | tf_op jit(solution)/shard_map/ppermute | solution.py:136
  68.5 11.8 %copy-start.2 = (bf16[1,32,2048]{2,1,0:T(8,128)(2,1)S(1)}, bf16[1,32,2048]{2,1,0:T(8,128)(2,1)}, u32[]{:S(2)}) copy-start(bf16[1,32,2048]{2,1,0:T(8,128)(2,1)} %param.8) | copy-start | bytes 393220
  68.5 11.8 %copy-start.4 = (bf16[1,32,2048]{2,1,0:T(8,128)(2,1)S(1)}, bf16[1,32,2048]{2,1,0:T(8,128)(2,1)}, u32[]{:S(2)}) copy-start(bf16[1,32,2048]{2,1,0:T(8,128)(2,1)} %param.10) | copy-start | bytes 393220
  80.4 7.5 %collective-permute-start.13 = (bf16[32,2048]{1,0:T(8,128)(2,1)S(1)}, bf16[32,2048]{1,0:T(8,128)(2,1)S(1)}, u32[]{:S(2)}, u32[]{:S(2)}) collective-permute-start(bf16[32,2048]{1,0:T(8,128)(2,1)S(1)} %get-tuple-element.42), channel_id=1, source_target_pairs={{0,24},{8,0},{16,8},{24,16},{1,25},{9,1},{17,9},{25,17},{2,26},{10... | collective-permute-start | bytes 393224 | tf_op jit(solution)/shard_map/ppermute | solution.py:19
  84.0 6.8 %collective-permute-start.12 = (bf16[32,2048]{1,0:T(8,128)(2,1)S(1)}, bf16[32,2048]{1,0:T(8,128)(2,1)S(1)}, u32[]{:S(2)}, u32[]{:S(2)}) collective-permute-start(bf16[32,2048]{1,0:T(8,128)(2,1)S(1)} %get-tuple-element.43), channel_id=1, source_target_pairs={{0,8},{8,16},{16,24},{24,0},{1,9},{9,17},{17,25},{25,1},{2,10},{10... | collective-permute-start | bytes 393224 | tf_op jit(solution)/shard_map/ppermute | solution.py:19

commit v4 on v3

--- a/solution.py
+++ b/solution.py
@@ -10,7 +10,10 @@
 CAP = 5
 LANES = 128
 CHUNK = 256
-VMEM_LIMIT = 48 * 1024 * 1024
+VMEM_LIMIT = 24 * 1024 * 1024
+EXPERTS_LIMIT = 44 * 1024 * 1024
+WIDE_LIMIT = 60 * 1024 * 1024
+WEIGHT_CUTS = 4
 
 
 def shifted(value, axis, steps):
@@ -136,11 +139,20 @@
     return lax.ppermute(value, axes, [(source, source ^ code) for source in range(count)])
 
 
-def pack_kernel(fore_tokens, saved, grads, back_routes, back_gates, fore_routes, fore_gates, out_ref, notes):
-    size, width = fore_tokens.shape
-    top = back_routes.shape[0]
-    for place, ref in enumerate((fore_tokens, saved, grads)):
-        out_ref[:, pl.ds(place * width, width)] = ref[...]
+def pack_kernel(*refs):
+    sources, out_ref, (*held, notes, done) = refs[:7], refs[7], refs[8:]
+    size, width = sources[0].shape
+    top = sources[3].shape[0]
+    targets = [out_ref.at[:, pl.ds(place * width, width)] for place in range(3)] + held
+    copies = [
+        pltpu.make_async_copy(source, target, done.at[place])
+        for place, (source, target) in enumerate(zip(sources, targets))
+    ]
+    for copy in copies:
+        copy.start()
+    for copy in copies:
+        copy.wait()
+    back_routes, back_gates, fore_routes, fore_gates = held
     notes[...] = jnp.zeros_like(notes)
     for place, (routes, gates) in enumerate(((back_routes, back_gates), (fore_routes, fore_gates))):
         first = place * 4 * top
@@ -203,17 +215,13 @@
         tokens[rows, :] = block[:, columns]
 
 
-def combine(place_ref, flipped, results, sums, outs):
+def combine(flipped, results, sums):
     width = sums.shape[1]
     for start in range(0, width, CHUNK):
         columns = pl.ds(start, CHUNK)
         sums[:, columns] = jnp.dot(
             flipped[...], results[:, columns], preferred_element_type=jnp.float32
         ).astype(sums.dtype)
-    for out, lead, code in outs:
-        size = out.shape[-2]
-        rows = pl.ds(pl.multiple_of(place_ref[3 + code], size), size)
-        out[lead] = sums[rows, :]
 
 
 def gather(count, slots, picks, gates, tokens_ref, rows, first, stride):
@@ -230,44 +238,106 @@
 
 
 def expert_kernel(count, slots, devices, pair, place_ref, *refs):
-    fore_picks, fore_gates, fore_flip, back_picks, back_gates, back_flip, weights_ref = refs[:7]
-    blocks = refs[7 : 7 + devices]
-    near_outs = refs[7 + devices : 7 + devices + devices // pair]
-    far_out, inner_ref, tokens, rows, fore_results, back_results, second = refs[-7:]
-    step = pl.program_id(0)
-    width = tokens.shape[1]
-
-    @pl.when(step == 0)
-    def _():
-        taken = ((fore_picks, None), (back_picks, None), (back_picks, back_gates))
-        for place, (picks, gates) in enumerate(taken):
-            assemble(place_ref, blocks, pl.ds(place * width, width), tokens)
-            gather(count, slots, picks, gates, tokens, rows, place * slots, 3 * slots)
-
-    mine = pl.ds(pl.multiple_of(step * slots, slots), slots)
-    three = pl.ds(pl.multiple_of(step * 3 * slots, 3 * slots), 3 * slots)
-    product = jnp.dot(rows[three, :], weights_ref[0], preferred_element_type=jnp.float32)
-    ahead, hidden, active_grads = product[:slots], product[slots : 2 * slots], product[2 * slots :]
-    sigma = jax.nn.sigmoid(hidden)
-    hidden_grads = (active_grads * sigma * (1.0 + hidden * (1.0 - sigma))).astype(jnp.bfloat16)
-    inner_ref[0, :slots, :] = hidden_grads
-    inner_ref[0, slots:, :] = (hidden * sigma).astype(jnp.bfloat16)
-    second[:slots, :] = (ahead * jax.nn.sigmoid(ahead)).astype(jnp.bfloat16)
-    second[slots:, :] = hidden_grads
-    result = lax.dot_general(
-        second[...], weights_ref[0], (((1,), (1,)), ((), ())), preferred_element_type=jnp.float32
-    )
-    fore_results[mine, :] = (result[:slots] * spread_gate(fore_gates, mine, width)).astype(
-        fore_results.dtype
-    )
-    back_results[mine, :] = result[slots:].astype(back_results.dtype)
-
-    @pl.when(step == count - 1)
-    def _():
-        for lead, (flipped, results) in enumerate(((fore_flip, fore_results), (back_flip, back_results))):
-            outs = [(out, lead, pair * group) for group, out in enumerate(near_outs)]
-            outs += [(far_out, (group, lead), pair * group + 1) for group in range(len(near_outs))]
-            combine(place_ref, flipped, results, tokens, outs)
+    picks_in, weights_in, blocks = refs[:6], refs[6], refs[7 : 7 + devices]
+    groups = devices // pair
+    near_outs, far_out, inner_out = refs[7 + devices : 7 + devices + groups], *refs[7 + devices + groups :][:2]
+    scratch = refs[9 + devices + groups :]
+    held, tokens = scratch[:6], scratch[6:9]
+    rows, fore_results, back_results, second, inner, weights_ref = scratch[9:15]
+    weights_done, in_done, out_done, inner_done = scratch[15:]
+    fore_picks, fore_gates, fore_flip, back_picks, back_gates, back_flip = held
+    size, width = blocks[0].shape[0], tokens[0].shape[1]
+
+    def home(code):
+        return pl.ds(pl.multiple_of(place_ref[3 + code], size), size)
+
+    arriving = [
+        pltpu.make_async_copy(source, target, in_done.at[3 * devices + place])
+        for place, (source, target) in enumerate(zip(picks_in, held))
+    ]
+    coming = [
+        [
+            pltpu.make_async_copy(
+                block.at[:, pl.ds(place * width, width)],
+                tokens[place].at[home(code), :],
+                in_done.at[place * devices + code],
+            )
+            for code, block in enumerate(blocks)
+        ]
+        for place in range(3)
+    ]
+    for copy in arriving + coming[0] + coming[1] + coming[2]:
+        copy.start()
+
+    def weight_copies(step):
+        cut = width // WEIGHT_CUTS
+        return [
+            pltpu.make_async_copy(
+                weights_in.at[place_ref[0] * count + step, pl.ds(place * cut, cut), :],
+                weights_ref.at[step, pl.ds(place * cut, cut), :],
+                weights_done.at[step, place],
+            )
+            for place in range(WEIGHT_CUTS)
+        ]
+
+    for step in range(count):
+        for copy in weight_copies(step):
+            copy.start()
+    for copy in arriving:
+        copy.wait()
+    taken = ((fore_picks, None), (back_picks, None), (back_picks, back_gates))
+    for place, (picks, gates) in enumerate(taken):
+        for copy in coming[place]:
+            copy.wait()
+        gather(count, slots, picks, gates, tokens[place], rows, place * slots, 3 * slots)
+
+    def inner_copy(step):
+        return pltpu.make_async_copy(inner.at[step], inner_out.at[step], inner_done.at[step])
+
+    @pl.loop(0, count)
+    def _(step):
+        mine = pl.ds(pl.multiple_of(step * slots, slots), slots)
+        three = pl.ds(pl.multiple_of(step * 3 * slots, 3 * slots), 3 * slots)
+        for copy in weight_copies(step):
+            copy.wait()
+        product = jnp.dot(rows[three, :], weights_ref[step], preferred_element_type=jnp.float32)
+        ahead, hidden, active_grads = (
+            product[:slots],
+            product[slots : 2 * slots],
+            product[2 * slots :],
+        )
+        sigma = jax.nn.sigmoid(hidden)
+        hidden_grads = (active_grads * sigma * (1.0 + hidden * (1.0 - sigma))).astype(jnp.bfloat16)
+        inner[step, :slots, :] = hidden_grads
+        inner[step, slots:, :] = (hidden * sigma).astype(jnp.bfloat16)
+        inner_copy(step).start()
+        second[:slots, :] = (ahead * jax.nn.sigmoid(ahead)).astype(jnp.bfloat16)
+        second[slots:, :] = hidden_grads
+        result = lax.dot_general(
+            second[...],
+            weights_ref[step],
+            (((1,), (1,)), ((), ())),
+            preferred_element_type=jnp.float32,
+        )
+        fore_results[mine, :] = (result[:slots] * spread_gate(fore_gates, mine, width)).astype(
+            fore_results.dtype
+        )
+        back_results[mine, :] = result[slots:].astype(back_results.dtype)
+
+    leaving = []
+    for lead, (flipped, results) in enumerate(((fore_flip, fore_results), (back_flip, back_results))):
+        sums = tokens[lead]
+        combine(flipped, results, sums)
+        targets = [(out.at[lead], pair * group) for group, out in enumerate(near_outs)]
+        targets += [(far_out.at[group, lead], pair * group + 1) for group in range(groups)]
+        for target, code in targets:
+            done = out_done.at[lead * devices + code]
+            leaving.append(pltpu.make_async_copy(sums.at[home(code), :], target, done))
+            leaving[-1].start()
+    for copy in leaving:
+        copy.wait()
+    for step in range(count):
+        inner_copy(step).wait()
 
 
 def weight_kernel(count, slots, devices, place_ref, *refs):
@@ -361,11 +431,18 @@
     packed = jax.ShapeDtypeStruct((token_count, 3 * width + LANES), jnp.bfloat16)
     own = pl.pallas_call(
         pack_kernel,
-        in_specs=[pl.BlockSpec(memory_space=pltpu.VMEM)] * 7,
+        in_specs=[pl.BlockSpec(memory_space=pl.ANY)] * 7,
         out_specs=pl.BlockSpec(memory_space=pltpu.VMEM),
         out_shape=packed,
-        scratch_shapes=[pltpu.VMEM((LANES, LANES), jnp.float32)],
-        compiler_params=pltpu.CompilerParams(vmem_limit_bytes=VMEM_LIMIT),
+        scratch_shapes=[
+            pltpu.VMEM((top, token_count), jnp.int32),
+            pltpu.VMEM((top, token_count), jnp.float32),
+            pltpu.VMEM((top, token_count), jnp.int32),
+            pltpu.VMEM((top, token_count), jnp.float32),
+            pltpu.VMEM((LANES, LANES), jnp.float32),
+            pltpu.SemaphoreType.DMA((7,)),
+        ],
+        compiler_params=pltpu.CompilerParams(vmem_limit_bytes=WIDE_LIMIT),
         name="pack",
     )(
         section_inputs[0],
@@ -398,24 +475,38 @@
     far_part = jax.ShapeDtypeStruct((groups, 2, token_count, width), jnp.bfloat16)
     inner = jax.ShapeDtypeStruct((count, 2 * slots, inner_width), jnp.bfloat16)
     inner_spec = pl.BlockSpec((1, 2 * slots, inner_width), lambda step, place: (step, 0, 0))
-    *near_parts, far_sums, inner_own = call(
+    in_smem, anywhere = (pl.BlockSpec(memory_space=space) for space in (pltpu.SMEM, pl.ANY))
+    tokens = pltpu.VMEM((total, width), jnp.bfloat16)
+    *near_parts, far_sums, inner_own = pl.pallas_call(
         functools.partial(expert_kernel, count, slots, devices, pair),
-        "experts",
-        count,
-        [whole(array.shape) for array in picks[:6]]
-        + [pl.BlockSpec((1, width, inner_width), lambda step, place: (place[0] * count + step, 0, 0))]
-        + [whole(packed.shape)] * devices,
-        [whole(near_part.shape)] * groups + [whole(far_part.shape), inner_spec],
-        [near_part] * groups + [far_part, inner],
-        [
-            pltpu.VMEM((total, width), jnp.bfloat16),
+        in_specs=[in_smem] + [anywhere] * (7 + devices),
+        out_specs=[anywhere] * (groups + 2),
+        out_shape=[near_part] * groups + [far_part, inner],
+        scratch_shapes=[pltpu.VMEM(array.shape, array.dtype) for array in pick_outs[:6]]
+        + [tokens] * 3
+        + [
             pltpu.VMEM((3 * rows, width), jnp.bfloat16),
             pltpu.VMEM((rows, width), jnp.bfloat16),
             pltpu.VMEM((rows, width), jnp.bfloat16),
             pltpu.VMEM((2 * slots, inner_width), jnp.bfloat16),
+            pltpu.VMEM(inner.shape, inner.dtype),
+            pltpu.VMEM((count, width, inner_width), jnp.bfloat16),
+            pltpu.SemaphoreType.DMA((count, WEIGHT_CUTS)),
+            pltpu.SemaphoreType.DMA((3 * devices + 6,)),
+            pltpu.SemaphoreType.DMA((2 * devices,)),
+            pltpu.SemaphoreType.DMA((count,)),
         ],
-        pass_flops,
-    )(place, *picks[:6], weights, *blocks)
+        compiler_params=pltpu.CompilerParams(vmem_limit_bytes=EXPERTS_LIMIT),
+        cost_estimate=pl.CostEstimate(
+            flops=pass_flops, bytes_accessed=pass_flops // 512, transcendentals=0
+        ),
+        name="experts",
+    )(
+        place,
+        *picks[:6],
+        weights,
+        *blocks,
+    )
     far_sums = onward(far_sums)
     inner_other = onward(inner_own)
 

time: 92.8 us -> 97.1 us (1.046)
  Pallas kernels: 42.5 us -> 51.7 us
  local copies, waits for them, and re-layouts: 8.13 us -> 3.4 us
    pallas_call x2, Pallas kernels: 21.6 us -> 30.7 us  [the longest x1 28.8 us: gathered_plan(): pl.pallas_call(functools.partial(expert_kernel, count, slots, devices, pa...]
    unnamed x22 -> x10, local copies, waits for them, and re-layouts: 8.04 us -> 3.31 us
  transfers between devices with their start and end apart: 14 -> 14, of which waited for: 9 -> 9; matrix products, arithmetic and copies ran while one was open for 0% -> 0% of each run, Pallas kernels for 21% -> 20%
where the time goes in v4:
time: 97.1 us; the launch traced here: 96.9 us
  Pallas kernels  51.7 us (53%)
  waiting for transfers between devices  28.1 us (29%)
  starting transfers between devices  12.6 us (13%)
  local copies, waits for them, and re-layouts  3.4 us (4%)
    pallas_call x1, Pallas kernels, gathered_plan(): pl.pallas_call(functools.partial(expert_kernel, count, slots, devices, pa...  28.8 us
    ppermute x12, waiting for transfers between devices, swapped(): lax.ppermute(value, axes, [(source, source ^ code) for source in range(co...  21.2 us
    pallas_call x2, Pallas kernels, gradient(): call(functools.partial(weight_kernel, count, slots, devices), 'weight_gra...  19.7 us
    ppermute x12, starting transfers between devices, swapped(): lax.ppermute(value, axes, [(source, source ^ code) for source in range(co...  8.97 us
    ppermute x2, waiting for transfers between devices, shifted(): return lax.ppermute(value, axis, pairs)  6.83 us
    ppermute x2, starting transfers between devices, shifted(): return lax.ppermute(value, axis, pairs)  3.66 us
    unnamed x10, local copies, waits for them, and re-layouts  3.31 us
  transfers between devices with their start and end apart: 14, of which 9 were waited for; matrix products, arithmetic and copies ran while one was open for 0% of the time, Pallas kernels for 20%

profile of v4, /device:TPU:0, one launch (start us, length us, event | category | flops | bytes accessed | tf_op | source)
XLA Modules:
  0.0 96.9 jit_solution(490005775528939008)
XLA Ops:
  0.6 1.9 %pack.1.refs_0_.refs_7_.refs_3_.refs_11_ = bf16[32,6272]{1,0:T(8,128)(2,1)} custom-call(bf16[32,2048]{1,0:T(8,128)(2,1)} %bitcast.58, bf16[32,2048]{1,0:T(8,128)(2,1)} %bitcast.60, bf16[32,2048]{1,0:T(8,128)(2,1)} %bitcast.59, s32[8,32]{1,0:T(8,128)} %bitcast.63, f32[8,32]{1,0:T(8,128)} %bitcast.64, s32[8,32]{1,0:T(8,128)} %bitcast.65, f32[8,32]{1,0:T(8,128)} %bitcast.66), custom_call_target="tpu_custom_call" | custom-call | tf_op jit(solution)/shard_map/pack/pallas_call | solution.py:432
  2.6 4.0 %collective-permute-start.5 = (bf16[32,6272]{1,0:T(8,128)(2,1)}, bf16[32,6272]{1,0:T(8,128)(2,1)S(1)}, u32[]{:S(2)}, u32[]{:S(2)}) collective-permute-start(bf16[32,6272]{1,0:T(8,128)(2,1)} %pack.1.refs_0_.refs_7_.refs_3_.refs_11_), channel_id=1, source_target_pairs={{0,6},{1,7},{2,4},{3,5},{4,2},{5,3},{6,0},{7,1},{8,14},{9,15},{10,... | collective-permute-start | bytes 1204232 | tf_op jit(solution)/shard_map/ppermute | solution.py:139
  6.5 0.5 collective-permute-start.3
  7.0 0.1 collective-permute-start.1
  7.2 0.0 collective-permute-start
  7.2 9.7 %collective-permute-done.5.refs_6_.refs_13_.refs_9_.refs_17_ = bf16[32,6272]{1,0:T(8,128)(2,1)S(1)} collective-permute-done((bf16[32,6272]{1,0:T(8,128)(2,1)}, bf16[32,6272]{1,0:T(8,128)(2,1)S(1)}, u32[]{:S(2)}, u32[]{:S(2)}) %collective-permute-start.5) | collective-permute-done | bytes 401440 | tf_op jit(solution)/shard_map/ppermute | solution.py:139
  16.9 0.0 collective-permute-start.6
  16.9 7.7 %collective-permute-done.3.refs_4_.refs_11_.refs_7_.refs_15_ = bf16[32,6272]{1,0:T(8,128)(2,1)S(1)} collective-permute-done((bf16[32,6272]{1,0:T(8,128)(2,1)}, bf16[32,6272]{1,0:T(8,128)(2,1)S(1)}, u32[]{:S(2)}, u32[]{:S(2)}) %collective-permute-start.3) | collective-permute-done | bytes 401440 | tf_op jit(solution)/shard_map/ppermute | solution.py:139
  24.6 0.0 collective-permute-start.4
  24.7 0.3 collective-permute-done.1.refs_2_.refs_9_.refs_5_.refs_13_
  24.9 0.2 collective-permute-start.2
  25.1 0.1 stack.47.place_ref
  25.2 0.0 collective-permute-done.refs_1_.refs_8_.refs_4_.refs_12_
  25.2 0.0 collective-permute-done.6.refs_7_.refs_14_.refs_10_.refs_18_
  25.3 1.1 %collective-permute-done.4.refs_5_.refs_12_.refs_8_.refs_16_ = bf16[32,6272]{1,0:T(8,128)(2,1)S(1)} collective-permute-done((bf16[32,6272]{1,0:T(8,128)(2,1)S(1)}, bf16[32,6272]{1,0:T(8,128)(2,1)S(1)}, u32[]{:S(2)}, u32[]{:S(2)}) %collective-permute-start.4) | collective-permute-done | bytes 401440 | tf_op jit(solution)/shard_map/ppermute | solution.py:139
  26.4 0.6 collective-permute-done.2.refs_3_.refs_10_.refs_6_.refs_14_
  26.9 0.0 copy-start
  26.9 1.0 %copy-done = bf16[32,6272]{1,0:T(8,128)(2,1)S(1)} copy-done((bf16[32,6272]{1,0:T(8,128)(2,1)S(1)}, bf16[32,6272]{1,0:T(8,128)(2,1)}, u32[]{:S(2)}) %copy-start) | copy-done | bytes 401432
  27.9 1.2 %slot_picks.1 = (bf16[384,256]{1,0:T(8,128)(2,1)S(1)}, f32[384,128]{1,0:T(8,128)S(1)}, bf16[256,384]{1,0:T(8,128)(2,1)S(1)}, bf16[384,256]{1,0:T(8,128)(2,1)S(1)...) custom-call(s32[11]{0:T(128)S(1)} %stack.47.place_ref, ...), custom_call_target="tpu_custom_call" | custom-call | bytes 1024 | tf_op jit(solution)/shard_map/slot_picks/pallas_call | solution.py:463
  29.1 0.0 copy-start.1
  29.1 1.0 %copy-done.1 = bf16[32,6272]{1,0:T(8,128)(2,1)S(1)} copy-done((bf16[32,6272]{1,0:T(8,128)(2,1)S(1)}, bf16[32,6272]{1,0:T(8,128)(2,1)}, u32[]{:S(2)}) %copy-start.1) | copy-done | bytes 401432
  30.1 28.8 %experts.1 = (bf16[2,32,2048]{2,1,0:T(8,128)(2,1)S(1)}, bf16[2,32,2048]{2,1,0:T(8,128)(2,1)S(1)}, bf16[2,32,2048]{2,1,0:T(8,128)(2,1)S(1)}, bf16[2,32,2048]{2,1,...) custom-call(s32[11]{0:T(128)S(1)} %stack.47.place_ref, ...), custom_call_target="tpu_custom_call" | custom-call | flops 12884901888 | bytes 25165824 | tf_op jit(solution)/shard_map/experts/pallas_call | solution.py:480
  58.9 0.2 collective-permute-start.7
  59.2 0.4 collective-permute-start.11
  59.5 9.9 %weight_gradient_own.1.refs_19_ = bf16[16,1024,768]{2,1,0:T(8,128)(2,1)} custom-call(s32[11]{0:T(128)S(1)} %stack.47.place_ref, bf16[384,256]{1,0:T(8,128)(2,1)S(1)} %get-tuple-element.24.refs_3_.refs_0_, f32[384,128]{1,0:T(8,128)S(1)} %get-tuple-element.25.refs_4_.refs_1_, bf16[8,96,768]{2,1,0:T(8,128)(2,1)S(1)} %get-tuple-element.29.refs_2_, ...), custom_call_target="tpu_custom_call" | custom-call | flops 6442450944 | bytes 12583936 | tf_op jit(solution)/shard_map/weight_gradient_own/pallas_call | solution.py:526
  69.4 0.0 collective-permute-done.7
  69.4 0.3 fusion
  69.7 1.9 %collective-permute-start.10 = (bf16[2,32,2048]{2,1,0:T(8,128)(2,1)S(1)}, bf16[2,32,2048]{2,1,0:T(8,128)(2,1)S(1)}, u32[]{:S(2)}, u32[]{:S(2)}) collective-permute-start(bf16[2,32,2048]{2,1,0:T(8,128)(2,1)S(1)} %get-tuple-element.39), channel_id=1, source_target_pairs={{0,6},{1,7},{2,4},{3,5},{4,2},{5,3},{6,0},{7,1},{8,14},{9,15},{10,... | collective-permute-start | bytes 786440 | tf_op jit(solution)/shard_map/ppermute | solution.py:139
  71.5 1.3 %collective-permute-start.9 = (bf16[2,32,2048]{2,1,0:T(8,128)(2,1)S(1)}, bf16[2,32,2048]{2,1,0:T(8,128)(2,1)S(1)}, u32[]{:S(2)}, u32[]{:S(2)}) collective-permute-start(bf16[2,32,2048]{2,1,0:T(8,128)(2,1)S(1)} %get-tuple-element.40), channel_id=1, source_target_pairs={{0,4},{1,5},{2,6},{3,7},{4,0},{5,1},{6,2},{7,3},{8,12},{9,13},{10,... | collective-permute-start | bytes 786440 | tf_op jit(solution)/shard_map/ppermute | solution.py:139
  72.9 0.3 collective-permute-start.8
  73.2 0.0 collective-permute-done.11.refs_2_
  73.2 0.0 copy-start.2
  73.2 0.0 copy-start.3
  73.2 9.9 %weight_gradient_other.1 = bf16[16,1024,768]{2,1,0:T(8,128)(2,1)} custom-call(s32[11]{0:T(128)S(1)} %stack.47.place_ref, bf16[384,256]{1,0:T(8,128)(2,1)S(1)} %get-tuple-element.34.refs_0_, f32[384,128]{1,0:T(8,128)S(1)} %get-tuple-element.35.refs_1_, bf16[8,96,768]{2,1,0:T(8,128)(2,1)S(1)} %collective-permute-done.11.refs_2_, ...), custom_call_target="tpu_custom_call", output_to_operand_aliasing={{}: (20, {})} | custom-call | flops 6442450944 | bytes 12583936 | tf_op jit(solution)/shard_map/weight_gradient_other/pallas_call | solution.py:526
  83.1 0.0 collective-permute-done.10
  83.1 1.5 %collective-permute-done.9 = bf16[2,32,2048]{2,1,0:T(8,128)(2,1)S(1)} collective-permute-done((bf16[2,32,2048]{2,1,0:T(8,128)(2,1)S(1)}, bf16[2,32,2048]{2,1,0:T(8,128)(2,1)S(1)}, u32[]{:S(2)}, u32[]{:S(2)}) %collective-permute-start.9) | collective-permute-done | bytes 262176 | tf_op jit(solution)/shard_map/ppermute | solution.py:139
  84.6 0.3 collective-permute-done.8
  84.9 0.2 convert_add_fusion.4
  85.1 0.0 copy-done.2
  85.1 0.0 copy-done.3
  85.1 3.7 %collective-permute-start.13 = (bf16[32,2048]{1,0:T(8,128)(2,1)S(1)}, bf16[32,2048]{1,0:T(8,128)(2,1)S(1)}, u32[]{:S(2)}, u32[]{:S(2)}) collective-permute-start(bf16[32,2048]{1,0:T(8,128)(2,1)S(1)} %get-tuple-element.42), channel_id=1, source_target_pairs={{0,24},{8,0},{16,8},{24,16},{1,25},{9,1},{17,9},{25,17},{2,26},{10... | collective-permute-start | bytes 393224 | tf_op jit(solution)/shard_map/ppermute | solution.py:22
  88.8 0.0 collective-permute-start.12
  88.8 3.9 %collective-permute-done.13 = bf16[32,2048]{1,0:T(8,128)(2,1)S(1)} collective-permute-done((bf16[32,2048]{1,0:T(8,128)(2,1)S(1)}, bf16[32,2048]{1,0:T(8,128)(2,1)S(1)}, u32[]{:S(2)}, u32[]{:S(2)}) %collective-permute-start.13) | collective-permute-done | bytes 131104 | tf_op jit(solution)/shard_map/ppermute | solution.py:22
  92.7 2.9 %collective-permute-done.12 = bf16[32,2048]{1,0:T(8,128)(2,1)S(1)} collective-permute-done((bf16[32,2048]{1,0:T(8,128)(2,1)S(1)}, bf16[32,2048]{1,0:T(8,128)(2,1)S(1)}, u32[]{:S(2)}, u32[]{:S(2)}) %collective-permute-start.12) | collective-permute-done | bytes 131104 | tf_op jit(solution)/shard_map/ppermute | solution.py:22
  95.6 0.7 copy.15
  96.3 0.7 copy.16
  (1 shorter events, 0.0 us)
Async XLA Ops:
  2.6 14.3 %collective-permute-start.5 = (bf16[32,6272]{1,0:T(8,128)(2,1)}, bf16[32,6272]{1,0:T(8,128)(2,1)S(1)}, u32[]{:S(2)}, u32[]{:S(2)}) collective-permute-start(bf16[32,6272]{1,0:T(8,128)(2,1)} %pack.1.refs_0_.refs_7_.refs_3_.refs_11_), channel_id=1, source_target_pairs={{0,6},{1,7},{2,4},{3,5},{4,2},{5,3},{6,0},{7,1},{8,14},{9,15},{10,... | collective-permute-start | bytes 1204232 | tf_op jit(solution)/shard_map/ppermute | solution.py:139
  6.5 18.1 %collective-permute-start.3 = (bf16[32,6272]{1,0:T(8,128)(2,1)}, bf16[32,6272]{1,0:T(8,128)(2,1)S(1)}, u32[]{:S(2)}, u32[]{:S(2)}) collective-permute-start(bf16[32,6272]{1,0:T(8,128)(2,1)} %pack.1.refs_0_.refs_7_.refs_3_.refs_11_), channel_id=1, source_target_pairs={{0,4},{1,5},{2,6},{3,7},{4,0},{5,1},{6,2},{7,3},{8,12},{9,13},{10,... | collective-permute-start | bytes 1204232 | tf_op jit(solution)/shard_map/ppermute | solution.py:139
  7.0 17.9 %collective-permute-start.1 = (bf16[32,6272]{1,0:T(8,128)(2,1)}, bf16[32,6272]{1,0:T(8,128)(2,1)S(1)}, u32[]{:S(2)}, u32[]{:S(2)}) collective-permute-start(bf16[32,6272]{1,0:T(8,128)(2,1)} %pack.1.refs_0_.refs_7_.refs_3_.refs_11_), channel_id=1, source_target_pairs={{0,2},{1,3},{2,0},{3,1},{4,6},{5,7},{6,4},{7,5},{8,10},{9,11},{10,... | collective-permute-start | bytes 1204232 | tf_op jit(solution)/shard_map/ppermute | solution.py:139
  7.2 18.1 %collective-permute-start = (bf16[32,6272]{1,0:T(8,128)(2,1)}, bf16[32,6272]{1,0:T(8,128)(2,1)S(1)}, u32[]{:S(2)}, u32[]{:S(2)}) collective-permute-start(bf16[32,6272]{1,0:T(8,128)(2,1)} %pack.1.refs_0_.refs_7_.refs_3_.refs_11_), channel_id=1, source_target_pairs={{0,1},{1,0},{2,3},{3,2},{4,5},{5,4},{6,7},{7,6},{8,9},{9,8},{10,11... | collective-permute-start | bytes 1204232 | tf_op jit(solution)/shard_map/ppermute | solution.py:139
  16.9 8.3 %collective-permute-start.6 = (bf16[32,6272]{1,0:T(8,128)(2,1)S(1)}, bf16[32,6272]{1,0:T(8,128)(2,1)S(1)}, u32[]{:S(2)}, u32[]{:S(2)}) collective-permute-start(bf16[32,6272]{1,0:T(8,128)(2,1)S(1)} %collective-permute-done.5.refs_6_.refs_13_.refs_9_.refs_17_), channel_id=1, source_target_pairs={{0,1},{1,0},{2,3},{3,2},{4,5},{5,4},{6,7},{7,6},{8,9},{9,8},{10,11... | collective-permute-start | bytes 1204232 | tf_op jit(solution)/shard_map/ppermute | solution.py:139
  24.6 1.7 %collective-permute-start.4 = (bf16[32,6272]{1,0:T(8,128)(2,1)S(1)}, bf16[32,6272]{1,0:T(8,128)(2,1)S(1)}, u32[]{:S(2)}, u32[]{:S(2)}) collective-permute-start(bf16[32,6272]{1,0:T(8,128)(2,1)S(1)} %collective-permute-done.3.refs_4_.refs_11_.refs_7_.refs_15_), channel_id=1, source_target_pairs={{0,1},{1,0},{2,3},{3,2},{4,5},{5,4},{6,7},{7,6},{8,9},{9,8},{10,11... | collective-permute-start | bytes 1204232 | tf_op jit(solution)/shard_map/ppermute | solution.py:139
  24.9 2.0 %collective-permute-start.2 = (bf16[32,6272]{1,0:T(8,128)(2,1)S(1)}, bf16[32,6272]{1,0:T(8,128)(2,1)S(1)}, u32[]{:S(2)}, u32[]{:S(2)}) collective-permute-start(bf16[32,6272]{1,0:T(8,128)(2,1)S(1)} %collective-permute-done.1.refs_2_.refs_9_.refs_5_.refs_13_), channel_id=1, source_target_pairs={{0,1},{1,0},{2,3},{3,2},{4,5},{5,4},{6,7},{7,6},{8,9},{9,8},{10,11... | collective-permute-start | bytes 1204232 | tf_op jit(solution)/shard_map/ppermute | solution.py:139
  26.9 1.0 %copy-start = (bf16[32,6272]{1,0:T(8,128)(2,1)S(1)}, bf16[32,6272]{1,0:T(8,128)(2,1)}, u32[]{:S(2)}) copy-start(bf16[32,6272]{1,0:T(8,128)(2,1)} %pack.1.refs_0_.refs_7_.refs_3_.refs_11_) | copy-start | bytes 1204228
  29.1 1.0 %copy-start.1 = (bf16[32,6272]{1,0:T(8,128)(2,1)S(1)}, bf16[32,6272]{1,0:T(8,128)(2,1)}, u32[]{:S(2)}) copy-start(bf16[32,6272]{1,0:T(8,128)(2,1)} %pack.1.refs_0_.refs_7_.refs_3_.refs_11_) | copy-start | bytes 1204228
  58.9 10.4 %collective-permute-start.7 = (bf16[4,2,32,2048]{3,2,1,0:T(8,128)(2,1)S(1)}, bf16[4,2,32,2048]{3,2,1,0:T(8,128)(2,1)S(1)}, u32[]{:S(2)}, u32[]{:S(2)}) collective-permute-start(bf16[4,2,32,2048]{3,2,1,0:T(8,128)(2,1)S(1)} %get-tuple-element.28), channel_id=1, source_target_pairs={{0,1},{1,0},{2,3},{3,2},{4,5},{5,4},{6,7},{7,6},{8,9},{9,8},{10,11... | collective-permute-start | bytes 3145736 | tf_op jit(solution)/shard_map/ppermute | solution.py:139
  59.2 14.1 %collective-permute-start.11 = (bf16[8,96,768]{2,1,0:T(8,128)(2,1)S(1)}, bf16[8,96,768]{2,1,0:T(8,128)(2,1)S(1)}, u32[]{:S(2)}, u32[]{:S(2)}) collective-permute-start(bf16[8,96,768]{2,1,0:T(8,128)(2,1)S(1)} %get-tuple-element.29.refs_2_), channel_id=1, source_target_pairs={{0,1},{1,0},{2,3},{3,2},{4,5},{5,4},{6,7},{7,6},{8,9},{9,8},{10,11... | collective-permute-start | bytes 3538952 | tf_op jit(solution)/shard_map/ppermute | solution.py:139
  69.7 13.4 %collective-permute-start.10 = (bf16[2,32,2048]{2,1,0:T(8,128)(2,1)S(1)}, bf16[2,32,2048]{2,1,0:T(8,128)(2,1)S(1)}, u32[]{:S(2)}, u32[]{:S(2)}) collective-permute-start(bf16[2,32,2048]{2,1,0:T(8,128)(2,1)S(1)} %get-tuple-element.39), channel_id=1, source_target_pairs={{0,6},{1,7},{2,4},{3,5},{4,2},{5,3},{6,0},{7,1},{8,14},{9,15},{10,... | collective-permute-start | bytes 786440 | tf_op jit(solution)/shard_map/ppermute | solution.py:139
  71.5 13.0 %collective-permute-start.9 = (bf16[2,32,2048]{2,1,0:T(8,128)(2,1)S(1)}, bf16[2,32,2048]{2,1,0:T(8,128)(2,1)S(1)}, u32[]{:S(2)}, u32[]{:S(2)}) collective-permute-start(bf16[2,32,2048]{2,1,0:T(8,128)(2,1)S(1)} %get-tuple-element.40), channel_id=1, source_target_pairs={{0,4},{1,5},{2,6},{3,7},{4,0},{5,1},{6,2},{7,3},{8,12},{9,13},{10,... | collective-permute-start | bytes 786440 | tf_op jit(solution)/shard_map/ppermute | solution.py:139
  72.9 12.0 %collective-permute-start.8 = (bf16[2,32,2048]{2,1,0:T(8,128)(2,1)S(1)}, bf16[2,32,2048]{2,1,0:T(8,128)(2,1)S(1)}, u32[]{:S(2)}, u32[]{:S(2)}) collective-permute-start(bf16[2,32,2048]{2,1,0:T(8,128)(2,1)S(1)} %get-tuple-element.41), channel_id=1, source_target_pairs={{0,2},{1,3},{2,0},{3,1},{4,6},{5,7},{6,4},{7,5},{8,10},{9,11},{10,... | collective-permute-start | bytes 786440 | tf_op jit(solution)/shard_map/ppermute | solution.py:139
  73.2 11.8 %copy-start.2 = (bf16[1,32,2048]{2,1,0:T(8,128)(2,1)S(1)}, bf16[1,32,2048]{2,1,0:T(8,128)(2,1)}, u32[]{:S(2)}) copy-start(bf16[1,32,2048]{2,1,0:T(8,128)(2,1)} %param.8) | copy-start | bytes 393220
  73.2 11.8 %copy-start.3 = (bf16[1,32,2048]{2,1,0:T(8,128)(2,1)S(1)}, bf16[1,32,2048]{2,1,0:T(8,128)(2,1)}, u32[]{:S(2)}) copy-start(bf16[1,32,2048]{2,1,0:T(8,128)(2,1)} %param.10) | copy-start | bytes 393220
  85.1 7.5 %collective-permute-start.13 = (bf16[32,2048]{1,0:T(8,128)(2,1)S(1)}, bf16[32,2048]{1,0:T(8,128)(2,1)S(1)}, u32[]{:S(2)}, u32[]{:S(2)}) collective-permute-start(bf16[32,2048]{1,0:T(8,128)(2,1)S(1)} %get-tuple-element.42), channel_id=1, source_target_pairs={{0,24},{8,0},{16,8},{24,16},{1,25},{9,1},{17,9},{25,17},{2,26},{10... | collective-permute-start | bytes 393224 | tf_op jit(solution)/shard_map/ppermute | solution.py:22
  88.8 6.8 %collective-permute-start.12 = (bf16[32,2048]{1,0:T(8,128)(2,1)S(1)}, bf16[32,2048]{1,0:T(8,128)(2,1)S(1)}, u32[]{:S(2)}, u32[]{:S(2)}) collective-permute-start(bf16[32,2048]{1,0:T(8,128)(2,1)S(1)} %get-tuple-element.43), channel_id=1, source_target_pairs={{0,8},{8,16},{16,24},{24,0},{1,9},{9,17},{17,25},{25,1},{2,10},{10... | collective-permute-start | bytes 393224 | tf_op jit(solution)/shard_map/ppermute | solution.py:22

commit v5 on v4

--- a/solution.py
+++ b/solution.py
@@ -11,9 +11,9 @@
 LANES = 128
 CHUNK = 256
 VMEM_LIMIT = 24 * 1024 * 1024
-EXPERTS_LIMIT = 44 * 1024 * 1024
-WIDE_LIMIT = 60 * 1024 * 1024
+EXPERTS_LIMIT = 36 * 1024 * 1024
 WEIGHT_CUTS = 4
+WEIGHT_SLOTS = 3
 
 
 def shifted(value, axis, steps):
@@ -240,8 +240,8 @@
 def expert_kernel(count, slots, devices, pair, place_ref, *refs):
     picks_in, weights_in, blocks = refs[:6], refs[6], refs[7 : 7 + devices]
     groups = devices // pair
-    near_outs, far_out, inner_out = refs[7 + devices : 7 + devices + groups], *refs[7 + devices + groups :][:2]
-    scratch = refs[9 + devices + groups :]
+    outs, inner_out = refs[7 + devices : 9 + devices + 2 * groups], refs[9 + devices + 2 * groups]
+    scratch = refs[10 + devices + 2 * groups :]
     held, tokens = scratch[:6], scratch[6:9]
     rows, fore_results, back_results, second, inner, weights_ref = scratch[9:15]
     weights_done, in_done, out_done, inner_done = scratch[15:]
@@ -274,13 +274,13 @@
         return [
             pltpu.make_async_copy(
                 weights_in.at[place_ref[0] * count + step, pl.ds(place * cut, cut), :],
-                weights_ref.at[step, pl.ds(place * cut, cut), :],
-                weights_done.at[step, place],
+                weights_ref.at[lax.rem(step, WEIGHT_SLOTS), pl.ds(place * cut, cut), :],
+                weights_done.at[lax.rem(step, WEIGHT_SLOTS), place],
             )
             for place in range(WEIGHT_CUTS)
         ]
 
-    for step in range(count):
+    for step in range(min(count, WEIGHT_SLOTS - 1)):
         for copy in weight_copies(step):
             copy.start()
     for copy in arriving:
@@ -298,9 +298,16 @@
     def _(step):
         mine = pl.ds(pl.multiple_of(step * slots, slots), slots)
         three = pl.ds(pl.multiple_of(step * 3 * slots, 3 * slots), 3 * slots)
+        slot = lax.rem(step, WEIGHT_SLOTS)
+
+        @pl.when(step + WEIGHT_SLOTS - 1 < count)
+        def _():
+            for copy in weight_copies(step + WEIGHT_SLOTS - 1):
+                copy.start()
+
         for copy in weight_copies(step):
             copy.wait()
-        product = jnp.dot(rows[three, :], weights_ref[step], preferred_element_type=jnp.float32)
+        product = jnp.dot(rows[three, :], weights_ref[slot], preferred_element_type=jnp.float32)
         ahead, hidden, active_grads = (
             product[:slots],
             product[slots : 2 * slots],
@@ -315,7 +322,7 @@
         second[slots:, :] = hidden_grads
         result = lax.dot_general(
             second[...],
-            weights_ref[step],
+            weights_ref[slot],
             (((1,), (1,)), ((), ())),
             preferred_element_type=jnp.float32,
         )
@@ -328,8 +335,9 @@
     for lead, (flipped, results) in enumerate(((fore_flip, fore_results), (back_flip, back_results))):
         sums = tokens[lead]
         combine(flipped, results, sums)
-        targets = [(out.at[lead], pair * group) for group, out in enumerate(near_outs)]
-        targets += [(far_out.at[group, lead], pair * group + 1) for group in range(groups)]
+        *near_outs, far_out = outs[lead * (groups + 1) : (lead + 1) * (groups + 1)]
+        targets = [(far_out.at[group], pair * group + 1) for group in range(groups)]
+        targets += [(out, pair * group) for group, out in enumerate(near_outs)]
         for target, code in targets:
             done = out_done.at[lead * devices + code]
             leaving.append(pltpu.make_async_copy(sums.at[home(code), :], target, done))
@@ -340,26 +348,62 @@
         inner_copy(step).wait()
 
 
-def weight_kernel(count, slots, devices, place_ref, *refs):
-    picks, gates, inner_ref = refs[:3]
-    saved, grads = refs[3 : 3 + devices], refs[3 + devices : 3 + 2 * devices]
-    out_ref, tokens, rows = refs[-3:]
-    step = pl.program_id(0)
-    half = tokens.shape[1]
-
-    @pl.when(step == 0)
-    def _():
-        for place, (blocks, scale) in enumerate(((saved, None), (grads, gates))):
-            assemble(place_ref, blocks, pl.ds(0, half), tokens)
-            gather(count, slots, picks, scale, tokens, rows, place * slots, 2 * slots)
-
-    both = pl.ds(pl.multiple_of(step * 2 * slots, 2 * slots), 2 * slots)
-    flat = rows[both, :].T
-    for start in range(0, inner_ref.shape[-1], CHUNK):
-        columns = pl.ds(start, CHUNK)
-        out_ref[0, :, columns] = jnp.dot(
-            flat, inner_ref[0, :, columns], preferred_element_type=jnp.float32
-        ).astype(out_ref.dtype)
+def weight_kernel(whose, first, number, count, slots, devices, place_ref, *refs):
+    held_in, blocks = refs[:3], refs[3 : 3 + devices]
+    out_ref, picks, gates, inner, saved, grads, rows, staged, in_done, out_done = refs[-10:]
+    size, half = blocks[0].shape[0], saved.shape[1]
+    side = place_ref[0]
+    owner = side if whose == 0 else 1 - side
+    part = pl.ds(first * slots, number * slots)
+
+    arriving = [
+        pltpu.make_async_copy(source, target, in_done.at[2 * devices + place])
+        for place, (source, target) in enumerate(
+            (
+                (held_in[0].at[part, :], picks),
+                (held_in[1].at[part, :], gates),
+                (held_in[2].at[pl.ds(first, number)], inner),
+            )
+        )
+    ]
+    coming = [
+        [
+            pltpu.make_async_copy(
+                block.at[:, pl.ds(pl.multiple_of((2 * place + 2 + side) * half, half), half)],
+                target.at[pl.ds(pl.multiple_of(place_ref[3 + code], size), size), :],
+                in_done.at[place * devices + code],
+            )
+            for code, block in enumerate(blocks)
+        ]
+        for place, target in enumerate((saved, grads))
+    ]
+    for copy in arriving + coming[0] + coming[1]:
+        copy.start()
+    for copy in arriving:
+        copy.wait()
+    for place, (tokens, scale) in enumerate(((saved, None), (grads, gates))):
+        for copy in coming[place]:
+            copy.wait()
+        gather(number, slots, picks, scale, tokens, rows, place * slots, 2 * slots)
+
+    leaving = []
+    for step in range(number):
+        flat = rows[pl.ds(step * 2 * slots, 2 * slots), :].T
+        for start in range(0, half, CHUNK):
+            chunk = pl.ds(start, CHUNK)
+            staged[step, chunk, :] = jnp.dot(
+                flat[start : start + CHUNK], inner[step], preferred_element_type=jnp.float32
+            ).astype(staged.dtype)
+            leaving.append(
+                pltpu.make_async_copy(
+                    staged.at[step, chunk, :],
+                    out_ref.at[owner * count + first + step, chunk, :],
+                    out_done.at[step, start // CHUNK],
+                )
+            )
+            leaving[-1].start()
+    for copy in leaving:
+        copy.wait()
 
 
 def gathered_plan(
@@ -442,16 +486,21 @@
             pltpu.VMEM((LANES, LANES), jnp.float32),
             pltpu.SemaphoreType.DMA((7,)),
         ],
-        compiler_params=pltpu.CompilerParams(vmem_limit_bytes=WIDE_LIMIT),
+        compiler_params=pltpu.CompilerParams(vmem_limit_bytes=VMEM_LIMIT),
         name="pack",
     )(
-        section_inputs[0],
-        saved_inputs[0],
-        output_grads[0],
-        backward_routes[0].T,
-        backward_gates[0].T,
-        forward_routes[0].T,
-        forward_gates[0].T,
+        *[
+            pltpu.with_memory_space_constraint(array, pltpu.HBM)
+            for array in (
+                section_inputs[0],
+                saved_inputs[0],
+                output_grads[0],
+                backward_routes[0].T,
+                backward_gates[0].T,
+                forward_routes[0].T,
+                forward_gates[0].T,
+            )
+        ]
     )
     near = [own] + across([own] * (groups - 1))
     blocks = [block for one in near for block in (one, onward(one))]
@@ -471,17 +520,16 @@
     )(place, *blocks)
 
     pass_flops = 2 * 2 * count * CHUNK * width * inner_width
-    near_part = jax.ShapeDtypeStruct((2, token_count, width), jnp.bfloat16)
-    far_part = jax.ShapeDtypeStruct((groups, 2, token_count, width), jnp.bfloat16)
+    near_part = jax.ShapeDtypeStruct((token_count, width), jnp.bfloat16)
+    far_part = jax.ShapeDtypeStruct((groups, token_count, width), jnp.bfloat16)
     inner = jax.ShapeDtypeStruct((count, 2 * slots, inner_width), jnp.bfloat16)
-    inner_spec = pl.BlockSpec((1, 2 * slots, inner_width), lambda step, place: (step, 0, 0))
     in_smem, anywhere = (pl.BlockSpec(memory_space=space) for space in (pltpu.SMEM, pl.ANY))
     tokens = pltpu.VMEM((total, width), jnp.bfloat16)
-    *near_parts, far_sums, inner_own = pl.pallas_call(
+    *parts, inner_own = pl.pallas_call(
         functools.partial(expert_kernel, count, slots, devices, pair),
         in_specs=[in_smem] + [anywhere] * (7 + devices),
-        out_specs=[anywhere] * (groups + 2),
-        out_shape=[near_part] * groups + [far_part, inner],
+        out_specs=[anywhere] * (2 * groups + 3),
+        out_shape=([near_part] * groups + [far_part]) * 2 + [inner],
         scratch_shapes=[pltpu.VMEM(array.shape, array.dtype) for array in pick_outs[:6]]
         + [tokens] * 3
         + [
@@ -490,8 +538,8 @@
             pltpu.VMEM((rows, width), jnp.bfloat16),
             pltpu.VMEM((2 * slots, inner_width), jnp.bfloat16),
             pltpu.VMEM(inner.shape, inner.dtype),
-            pltpu.VMEM((count, width, inner_width), jnp.bfloat16),
-            pltpu.SemaphoreType.DMA((count, WEIGHT_CUTS)),
+            pltpu.VMEM((WEIGHT_SLOTS, width, inner_width), jnp.bfloat16),
+            pltpu.SemaphoreType.DMA((WEIGHT_SLOTS, WEIGHT_CUTS)),
             pltpu.SemaphoreType.DMA((3 * devices + 6,)),
             pltpu.SemaphoreType.DMA((2 * devices,)),
             pltpu.SemaphoreType.DMA((count,)),
@@ -507,48 +555,64 @@
         weights,
         *blocks,
     )
-    far_sums = onward(far_sums)
-    inner_other = onward(inner_own)
-
-    def gradient(whose, inner_rows, picked, earlier):
+    *layer_parts, layer_far = parts[: groups + 1]
+    *grad_parts, grad_far = parts[groups + 1 :]
+    layer_far, grad_far, inner_other = onward(layer_far), onward(grad_far), onward(inner_own)
+
+    def gradient(whose, first, number, inner_rows, earlier):
         earlier = [] if earlier is None else [earlier]
-
-        def out_block(step, place):
-            owner = place[0] if whose == 0 else 1 - place[0]
-            return (owner * count + step, 0, 0)
-
-        specs = [whole(pick.shape), whole(gate.shape), inner_spec]
-        for first in (pair, 2 * pair):
-            specs += [
-                pl.BlockSpec((token_count, half), lambda step, place, first=first: (0, first + place[0]))
-            ] * devices
-        specs += [pl.BlockSpec(memory_space=pl.ANY)] * len(earlier)
-        return call(
-            functools.partial(weight_kernel, count, slots, devices),
-            "weight_gradient_" + ("own", "other")[whose],
-            count,
-            specs,
-            pl.BlockSpec((1, half, inner_width), out_block),
-            jax.ShapeDtypeStruct((local_count, half, inner_width), jnp.bfloat16),
-            [pltpu.VMEM((total, half), jnp.bfloat16), pltpu.VMEM((2 * rows, half), jnp.bfloat16)],
-            pass_flops // 2,
-            [(len(specs), 0)] if earlier else [],
-        )(place, *picked, inner_rows, *blocks, *blocks, *earlier)
-
-    own_done = gradient(0, inner_own, picks[3:5], None)
-    far_sums = after(own_done, far_sums)
-    sums = [
-        summed(part, far_sums[group]).astype(jnp.bfloat16) for group, part in enumerate(near_parts)
-    ]
-    near_sums = across(sums[1:])
-    weight_grads = gradient(1, inner_other, picks[6:8], own_done)
-    near_sums = after(weight_grads, near_sums)
-    moved = summed(sums[0], *near_sums)
-    layer_out = (section_inputs[0].astype(jnp.float32) + moved[0]).astype(jnp.bfloat16)
-    input_grads = (output_grads[0].astype(jnp.float32) + moved[1]).astype(jnp.bfloat16)
+        held = list(picks[3:5] if whose == 0 else picks[6:8]) + [inner_rows]
+        operands = held + blocks + earlier
+        half_tokens = pltpu.VMEM((total, half), jnp.bfloat16)
+        return pl.pallas_call(
+            functools.partial(weight_kernel, whose, first, number, count, slots, devices),
+            in_specs=[in_smem] + [anywhere] * len(operands),
+            out_specs=anywhere,
+            out_shape=jax.ShapeDtypeStruct((local_count, half, inner_width), jnp.bfloat16),
+            scratch_shapes=[
+                pltpu.VMEM((number * slots, total), jnp.bfloat16),
+                pltpu.VMEM((number * slots, LANES), jnp.float32),
+                pltpu.VMEM((number, 2 * slots, inner_width), jnp.bfloat16),
+                half_tokens,
+                half_tokens,
+                pltpu.VMEM((number * 2 * slots, half), jnp.bfloat16),
+                pltpu.VMEM((number, half, inner_width), jnp.bfloat16),
+                pltpu.SemaphoreType.DMA((2 * devices + 3,)),
+                pltpu.SemaphoreType.DMA((number, half // CHUNK)),
+            ],
+            compiler_params=pltpu.CompilerParams(vmem_limit_bytes=VMEM_LIMIT),
+            cost_estimate=pl.CostEstimate(
+                flops=number * pass_flops // count // 2,
+                bytes_accessed=number * half * inner_width * 4,
+                transcendentals=0,
+            ),
+            input_output_aliases={len(operands): 0} if earlier else {},
+            name=f"weight_gradient_{whose}_{first}",
+        )(place, *operands)
+
+    def pair_sums(near_parts, far):
+        return [summed(part, far[group]).astype(jnp.bfloat16) for group, part in enumerate(near_parts)]
+
+    piece = -(-count // 2)
+    done = gradient(0, 0, piece, inner_own, None)
+    layer_sums = pair_sums(layer_parts, after(done, layer_far))
+    layer_near = across(layer_sums[1:])
+    grad_sums = pair_sums(grad_parts, after((layer_sums, inner_other), grad_far))
+    grad_near = across(grad_sums[1:])
+    done = after(grad_sums, done)
+    if piece < count:
+        done = gradient(0, piece, count - piece, inner_own, done)
+    done = gradient(1, 0, piece, inner_other, after(layer_near[0], done))
+    layer_near = after(done, layer_near)
+    layer_out = summed(section_inputs[0], layer_sums[0], *layer_near).astype(jnp.bfloat16)
     next_inputs = shifted(layer_out, "pipe", 1)[None]
+    done = after(layer_out, done)
+    if piece < count:
+        done = gradient(1, piece, count - piece, inner_other, done)
+    grad_near = after((done, next_inputs), grad_near)
+    input_grads = summed(output_grads[0], grad_sums[0], *grad_near).astype(jnp.bfloat16)
     prior_grads = shifted(input_grads, "pipe", -1)[None]
-    return (next_inputs, prior_grads, weight_grads[None])
+    return (next_inputs, prior_grads, done[None])
 
 
 def on_device(*arrays):

time: 97.1 us -> 92.9 us (0.957)
  waiting for transfers between devices: 28.1 us -> 22.2 us
  starting transfers between devices: 12.6 us -> 16.7 us
  local copies, waits for them, and re-layouts: 3.4 us -> 1.41 us
    ppermute x2, waiting for transfers between devices: 6.83 us -> 2.93 us  [shifted(): return lax.ppermute(value, axis, pairs)]
    ppermute x12 -> x16, starting transfers between devices: 8.97 us -> 12.7 us  [swapped(): lax.ppermute(value, axes, [(source, source ^ code) for source in range(co...]
    unnamed x10 -> x6, local copies, waits for them, and re-layouts: 3.31 us -> 1.32 us
    ppermute x12 -> x16, waiting for transfers between devices: 21.2 us -> 19.2 us  [swapped(): lax.ppermute(value, axes, [(source, source ^ code) for source in range(co...]
    pallas_call x2 -> x4, Pallas kernels: 19.7 us -> 20.3 us  [gradient(): pl.pallas_call(functools.partial(weight_kernel, whose, first, number, cou...]
  transfers between devices with their start and end apart: 14 -> 18, of which waited for: 9 -> 6; matrix products, arithmetic and copies ran while one was open for 0% -> 0% of each run, Pallas kernels for 20% -> 22%
where the time goes in v5:
time: 92.9 us; the launch traced here: 92.8 us
  Pallas kernels  51.3 us (55%)
  waiting for transfers between devices  22.2 us (24%)
  starting transfers between devices  16.7 us (18%)
  local copies, waits for them, and re-layouts  1.41 us (2%)
    pallas_call x1, Pallas kernels, gathered_plan(): pl.pallas_call(functools.partial(expert_kernel, count, slots, devices, pa...  28.6 us
    pallas_call x4, Pallas kernels, gradient(): pl.pallas_call(functools.partial(weight_kernel, whose, first, number, cou...  20.3 us
    ppermute x16, waiting for transfers between devices, swapped(): lax.ppermute(value, axes, [(source, source ^ code) for source in range(co...  19.2 us
    ppermute x16, starting transfers between devices, swapped(): lax.ppermute(value, axes, [(source, source ^ code) for source in range(co...  12.7 us
    ppermute x2, starting transfers between devices, shifted(): return lax.ppermute(value, axis, pairs)  3.92 us
    ppermute x2, waiting for transfers between devices, shifted(): return lax.ppermute(value, axis, pairs)  2.93 us
  transfers between devices with their start and end apart: 18, of which 6 were waited for; matrix products, arithmetic and copies ran while one was open for 0% of the time, Pallas kernels for 22%

profile of v5, /device:TPU:0, one launch (start us, length us, event | category | flops | bytes accessed | tf_op | source)
XLA Modules:
  0.0 92.8 jit_solution(17647247013529140507)
XLA Ops:
  0.6 1.2 %pack.1.refs_0_.refs_7_.refs_3_ = bf16[32,6272]{1,0:T(8,128)(2,1)S(1)} custom-call(bf16[32,2048]{1,0:T(8,128)(2,1)} %bitcast.58, bf16[32,2048]{1,0:T(8,128)(2,1)} %bitcast.60, bf16[32,2048]{1,0:T(8,128)(2,1)} %bitcast.59, s32[8,32]{1,0:T(8,128)} %bitcast.63, f32[8,32]{1,0:T(8,128)} %bitcast.64, s32[8,32]{1,0:T(8,128)} %bitcast.65, f32[8,32]{1,0:T(8,128)} %bitcast.66), custom_call_target="tpu_custom_call" | custom-call | tf_op jit(solution)/shard_map/pack/pallas_call | solution.py:476
  1.8 4.0 %collective-permute-start.5 = (bf16[32,6272]{1,0:T(8,128)(2,1)S(1)}, bf16[32,6272]{1,0:T(8,128)(2,1)S(1)}, u32[]{:S(2)}, u32[]{:S(2)}) collective-permute-start(bf16[32,6272]{1,0:T(8,128)(2,1)S(1)} %pack.1.refs_0_.refs_7_.refs_3_), channel_id=1, source_target_pairs={{0,6},{1,7},{2,4},{3,5},{4,2},{5,3},{6,0},{7,1},{8,14},{9,15},{10,... | collective-permute-start | bytes 1204232 | tf_op jit(solution)/shard_map/ppermute | solution.py:139
  5.8 0.5 collective-permute-start.3
  6.3 0.1 collective-permute-start.1
  6.4 0.0 collective-permute-start
  6.4 9.5 %collective-permute-done.5.refs_6_.refs_13_.refs_9_ = bf16[32,6272]{1,0:T(8,128)(2,1)S(1)} collective-permute-done((bf16[32,6272]{1,0:T(8,128)(2,1)S(1)}, bf16[32,6272]{1,0:T(8,128)(2,1)S(1)}, u32[]{:S(2)}, u32[]{:S(2)}) %collective-permute-start.5) | collective-permute-done | bytes 401440 | tf_op jit(solution)/shard_map/ppermute | solution.py:139
  15.9 0.0 collective-permute-start.6
  16.0 7.7 %collective-permute-done.3.refs_4_.refs_11_.refs_7_ = bf16[32,6272]{1,0:T(8,128)(2,1)S(1)} collective-permute-done((bf16[32,6272]{1,0:T(8,128)(2,1)S(1)}, bf16[32,6272]{1,0:T(8,128)(2,1)S(1)}, u32[]{:S(2)}, u32[]{:S(2)}) %collective-permute-start.3) | collective-permute-done | bytes 401440 | tf_op jit(solution)/shard_map/ppermute | solution.py:139
  23.7 0.0 collective-permute-start.4
  23.7 0.3 collective-permute-done.1.refs_2_.refs_9_.refs_5_
  24.0 0.2 collective-permute-start.2
  24.2 0.1 stack.47.place_ref
  24.3 0.0 collective-permute-done.refs_1_.refs_8_.refs_4_
  24.3 0.0 collective-permute-done.6.refs_7_.refs_14_.refs_10_
  24.3 1.1 %collective-permute-done.4.refs_5_.refs_12_.refs_8_ = bf16[32,6272]{1,0:T(8,128)(2,1)S(1)} collective-permute-done((bf16[32,6272]{1,0:T(8,128)(2,1)S(1)}, bf16[32,6272]{1,0:T(8,128)(2,1)S(1)}, u32[]{:S(2)}, u32[]{:S(2)}) %collective-permute-start.4) | collective-permute-done | bytes 401440 | tf_op jit(solution)/shard_map/ppermute | solution.py:139
  25.4 0.6 collective-permute-done.2.refs_3_.refs_10_.refs_6_
  26.0 1.2 %slot_picks.1 = (bf16[384,256]{1,0:T(8,128)(2,1)S(1)}, f32[384,128]{1,0:T(8,128)S(1)}, bf16[256,384]{1,0:T(8,128)(2,1)S(1)}, bf16[384,256]{1,0:T(8,128)(2,1)S(1)...) custom-call(s32[11]{0:T(128)S(1)} %stack.47.place_ref, ...), custom_call_target="tpu_custom_call" | custom-call | bytes 1024 | tf_op jit(solution)/shard_map/slot_picks/pallas_call | solution.py:512
  27.2 28.6 %experts.1 = (bf16[32,2048]{1,0:T(8,128)(2,1)S(1)}, bf16[32,2048]{1,0:T(8,128)(2,1)S(1)}, bf16[32,2048]{1,0:T(8,128)(2,1)S(1)}, bf16[32,2048]{1,0:T(8,128)(2,1)S...) custom-call(s32[11]{0:T(128)S(1)} %stack.47.place_ref, ...), custom_call_target="tpu_custom_call" | custom-call | flops 12884901888 | bytes 25165824 | tf_op jit(solution)/shard_map/experts/pallas_call | solution.py:528
  55.8 0.2 collective-permute-start.11
  56.0 0.4 collective-permute-start.7
  56.4 0.1 collective-permute-start.12
  56.5 5.0 %weight_gradient_0_0.1.refs_11_ = bf16[16,1024,768]{2,1,0:T(8,128)(2,1)} custom-call(s32[11]{0:T(128)S(1)} %stack.47.place_ref, bf16[384,256]{1,0:T(8,128)(2,1)S(1)} %get-tuple-element.36.refs_3_.refs_0_, f32[384,128]{1,0:T(8,128)S(1)} %get-tuple-element.37.refs_4_.refs_1_, bf16[8,96,768]{2,1,0:T(8,128)(2,1)S(1)} %get-tuple-element.41.refs_2_, ...), custom_call_target="tpu_custom_call" | custom-call | flops 3221225472 | bytes 12582912 | tf_op jit(solution)/shard_map/weight_gradient_0_0/pallas_call | solution.py:567
  61.6 0.0 collective-permute-done.7
  61.6 0.1 fusion.7
  61.7 1.9 %collective-permute-start.10 = (bf16[32,2048]{1,0:T(8,128)(2,1)S(1)}, bf16[32,2048]{1,0:T(8,128)(2,1)S(1)}, u32[]{:S(2)}, u32[]{:S(2)}) collective-permute-start(bf16[32,2048]{1,0:T(8,128)(2,1)S(1)} %get-tuple-element.68), channel_id=1, source_target_pairs={{0,6},{1,7},{2,4},{3,5},{4,2},{5,3},{6,0},{7,1},{8,14},{9,15},{10,... | collective-permute-start | bytes 393224 | tf_op jit(solution)/shard_map/ppermute | solution.py:139
  63.6 1.3 %collective-permute-start.9 = (bf16[32,2048]{1,0:T(8,128)(2,1)S(1)}, bf16[32,2048]{1,0:T(8,128)(2,1)S(1)}, u32[]{:S(2)}, u32[]{:S(2)}) collective-permute-start(bf16[32,2048]{1,0:T(8,128)(2,1)S(1)} %get-tuple-element.69), channel_id=1, source_target_pairs={{0,4},{1,5},{2,6},{3,7},{4,0},{5,1},{6,2},{7,3},{8,12},{9,13},{10,... | collective-permute-start | bytes 393224 | tf_op jit(solution)/shard_map/ppermute | solution.py:139
  64.9 0.3 collective-permute-start.8
  65.3 0.0 collective-permute-done.12
  65.3 0.0 collective-permute-done.11.refs_2_
  65.3 0.1 fusion
  65.4 1.9 %collective-permute-start.16 = (bf16[32,2048]{1,0:T(8,128)(2,1)S(1)}, bf16[32,2048]{1,0:T(8,128)(2,1)S(1)}, u32[]{:S(2)}, u32[]{:S(2)}) collective-permute-start(bf16[32,2048]{1,0:T(8,128)(2,1)S(1)} %get-tuple-element.63), channel_id=1, source_target_pairs={{0,6},{1,7},{2,4},{3,5},{4,2},{5,3},{6,0},{7,1},{8,14},{9,15},{10,... | collective-permute-start | bytes 393224 | tf_op jit(solution)/shard_map/ppermute | solution.py:139
  67.3 1.3 %collective-permute-start.15 = (bf16[32,2048]{1,0:T(8,128)(2,1)S(1)}, bf16[32,2048]{1,0:T(8,128)(2,1)S(1)}, u32[]{:S(2)}, u32[]{:S(2)}) collective-permute-start(bf16[32,2048]{1,0:T(8,128)(2,1)S(1)} %get-tuple-element.64), channel_id=1, source_target_pairs={{0,4},{1,5},{2,6},{3,7},{4,0},{5,1},{6,2},{7,3},{8,12},{9,13},{10,... | collective-permute-start | bytes 393224 | tf_op jit(solution)/shard_map/ppermute | solution.py:139
  68.6 5.0 %weight_gradient_0_4.1.refs_11_ = bf16[16,1024,768]{2,1,0:T(8,128)(2,1)} custom-call(s32[11]{0:T(128)S(1)} %stack.47.place_ref, bf16[384,256]{1,0:T(8,128)(2,1)S(1)} %get-tuple-element.36.refs_3_.refs_0_, f32[384,128]{1,0:T(8,128)S(1)} %get-tuple-element.37.refs_4_.refs_1_, ...), custom_call_target="tpu_custom_call", output_to_operand_aliasing={{}: (12, {})} | custom-call | flops 3221225472 | bytes 12582912 | tf_op jit(solution)/shard_map/weight_gradient_0_4/pallas_call | solution.py:567
  73.6 0.0 collective-permute-done.8
  73.7 0.4 collective-permute-start.14
  74.1 0.0 copy-start
  74.1 5.2 %weight_gradient_1_0.1.refs_11_ = bf16[16,1024,768]{2,1,0:T(8,128)(2,1)} custom-call(s32[11]{0:T(128)S(1)} %stack.47.place_ref, bf16[384,256]{1,0:T(8,128)(2,1)S(1)} %get-tuple-element.46.refs_0_, f32[384,128]{1,0:T(8,128)S(1)} %get-tuple-element.47.refs_1_, ...), custom_call_target="tpu_custom_call", output_to_operand_aliasing={{}: (12, {})} | custom-call | flops 3221225472 | bytes 12582912 | tf_op jit(solution)/shard_map/weight_gradient_1_0/pallas_call | solution.py:567
  79.3 0.0 collective-permute-done.10
  79.3 0.0 collective-permute-done.9
  79.3 0.0 copy-done
  79.3 0.1 add_convert_fusion.1
  79.4 0.0 copy-start.1
  79.4 1.8 %collective-permute-start.13 = (bf16[32,2048]{1,0:T(8,128)(2,1)S(1)}, bf16[32,2048]{1,0:T(8,128)(2,1)S(1)}, u32[]{:S(2)}, u32[]{:S(2)}) collective-permute-start(bf16[32,2048]{1,0:T(8,128)(2,1)S(1)} %add_convert_fusion.1), channel_id=1, source_target_pairs={{0,8},{8,16},{16,24},{24,0},{1,9},{9,17},{17,25},{25,1},{2,10},{10... | collective-permute-start | bytes 393224 | tf_op jit(solution)/shard_map/ppermute | solution.py:22
  81.2 5.0 %weight_gradient_1_4.1 = bf16[16,1024,768]{2,1,0:T(8,128)(2,1)} custom-call(s32[11]{0:T(128)S(1)} %stack.47.place_ref, bf16[384,256]{1,0:T(8,128)(2,1)S(1)} %get-tuple-element.46.refs_0_, f32[384,128]{1,0:T(8,128)S(1)} %get-tuple-element.47.refs_1_, bf16[8,96,768]{2,1,0:T(8,128)(2,1)S(1)} %collective-permute-done.11.refs_2_, ...), custom_call_target="tpu_custom_call", output_to_operand_aliasing={{}: (12, {})} | custom-call | flops 3221225472 | bytes 12582912 | tf_op jit(solution)/shard_map/weight_gradient_1_4/pallas_call | solution.py:567
  86.3 0.0 collective-permute-done.16
  86.3 0.0 collective-permute-done.15
  86.3 0.0 collective-permute-done.14
  86.3 0.0 collective-permute-done.13
  86.3 0.0 copy-done.1
  86.3 0.1 add_convert_fusion
  86.4 2.1 %collective-permute-start.17 = (bf16[32,2048]{1,0:T(8,128)(2,1)S(1)}, bf16[32,2048]{1,0:T(8,128)(2,1)S(1)}, u32[]{:S(2)}, u32[]{:S(2)}) collective-permute-start(bf16[32,2048]{1,0:T(8,128)(2,1)S(1)} %add_convert_fusion), channel_id=1, source_target_pairs={{0,24},{8,0},{16,8},{24,16},{1,25},{9,1},{17,9},{25,17},{2,26},{10... | collective-permute-start | bytes 393224 | tf_op jit(solution)/shard_map/ppermute | solution.py:22
  88.5 2.9 %collective-permute-done.17 = bf16[32,2048]{1,0:T(8,128)(2,1)S(1)} collective-permute-done((bf16[32,2048]{1,0:T(8,128)(2,1)S(1)}, bf16[32,2048]{1,0:T(8,128)(2,1)S(1)}, u32[]{:S(2)}, u32[]{:S(2)}) %collective-permute-start.17) | collective-permute-done | bytes 131104 | tf_op jit(solution)/shard_map/ppermute | solution.py:22
  91.5 0.7 copy.19
  92.1 0.7 copy.20
Async XLA Ops:
  1.8 14.1 %collective-permute-start.5 = (bf16[32,6272]{1,0:T(8,128)(2,1)S(1)}, bf16[32,6272]{1,0:T(8,128)(2,1)S(1)}, u32[]{:S(2)}, u32[]{:S(2)}) collective-permute-start(bf16[32,6272]{1,0:T(8,128)(2,1)S(1)} %pack.1.refs_0_.refs_7_.refs_3_), channel_id=1, source_target_pairs={{0,6},{1,7},{2,4},{3,5},{4,2},{5,3},{6,0},{7,1},{8,14},{9,15},{10,... | collective-permute-start | bytes 1204232 | tf_op jit(solution)/shard_map/ppermute | solution.py:139
  5.8 17.9 %collective-permute-start.3 = (bf16[32,6272]{1,0:T(8,128)(2,1)S(1)}, bf16[32,6272]{1,0:T(8,128)(2,1)S(1)}, u32[]{:S(2)}, u32[]{:S(2)}) collective-permute-start(bf16[32,6272]{1,0:T(8,128)(2,1)S(1)} %pack.1.refs_0_.refs_7_.refs_3_), channel_id=1, source_target_pairs={{0,4},{1,5},{2,6},{3,7},{4,0},{5,1},{6,2},{7,3},{8,12},{9,13},{10,... | collective-permute-start | bytes 1204232 | tf_op jit(solution)/shard_map/ppermute | solution.py:139
  6.3 17.7 %collective-permute-start.1 = (bf16[32,6272]{1,0:T(8,128)(2,1)S(1)}, bf16[32,6272]{1,0:T(8,128)(2,1)S(1)}, u32[]{:S(2)}, u32[]{:S(2)}) collective-permute-start(bf16[32,6272]{1,0:T(8,128)(2,1)S(1)} %pack.1.refs_0_.refs_7_.refs_3_), channel_id=1, source_target_pairs={{0,2},{1,3},{2,0},{3,1},{4,6},{5,7},{6,4},{7,5},{8,10},{9,11},{10,... | collective-permute-start | bytes 1204232 | tf_op jit(solution)/shard_map/ppermute | solution.py:139
  6.4 17.9 %collective-permute-start = (bf16[32,6272]{1,0:T(8,128)(2,1)S(1)}, bf16[32,6272]{1,0:T(8,128)(2,1)S(1)}, u32[]{:S(2)}, u32[]{:S(2)}) collective-permute-start(bf16[32,6272]{1,0:T(8,128)(2,1)S(1)} %pack.1.refs_0_.refs_7_.refs_3_), channel_id=1, source_target_pairs={{0,1},{1,0},{2,3},{3,2},{4,5},{5,4},{6,7},{7,6},{8,9},{9,8},{10,11... | collective-permute-start | bytes 1204232 | tf_op jit(solution)/shard_map/ppermute | solution.py:139
  15.9 8.3 %collective-permute-start.6 = (bf16[32,6272]{1,0:T(8,128)(2,1)S(1)}, bf16[32,6272]{1,0:T(8,128)(2,1)S(1)}, u32[]{:S(2)}, u32[]{:S(2)}) collective-permute-start(bf16[32,6272]{1,0:T(8,128)(2,1)S(1)} %collective-permute-done.5.refs_6_.refs_13_.refs_9_), channel_id=1, source_target_pairs={{0,1},{1,0},{2,3},{3,2},{4,5},{5,4},{6,7},{7,6},{8,9},{9,8},{10,11... | collective-permute-start | bytes 1204232 | tf_op jit(solution)/shard_map/ppermute | solution.py:139
  23.7 1.7 %collective-permute-start.4 = (bf16[32,6272]{1,0:T(8,128)(2,1)S(1)}, bf16[32,6272]{1,0:T(8,128)(2,1)S(1)}, u32[]{:S(2)}, u32[]{:S(2)}) collective-permute-start(bf16[32,6272]{1,0:T(8,128)(2,1)S(1)} %collective-permute-done.3.refs_4_.refs_11_.refs_7_), channel_id=1, source_target_pairs={{0,1},{1,0},{2,3},{3,2},{4,5},{5,4},{6,7},{7,6},{8,9},{9,8},{10,11... | collective-permute-start | bytes 1204232 | tf_op jit(solution)/shard_map/ppermute | solution.py:139
  24.0 2.0 %collective-permute-start.2 = (bf16[32,6272]{1,0:T(8,128)(2,1)S(1)}, bf16[32,6272]{1,0:T(8,128)(2,1)S(1)}, u32[]{:S(2)}, u32[]{:S(2)}) collective-permute-start(bf16[32,6272]{1,0:T(8,128)(2,1)S(1)} %collective-permute-done.1.refs_2_.refs_9_.refs_5_), channel_id=1, source_target_pairs={{0,1},{1,0},{2,3},{3,2},{4,5},{5,4},{6,7},{7,6},{8,9},{9,8},{10,11... | collective-permute-start | bytes 1204232 | tf_op jit(solution)/shard_map/ppermute | solution.py:139
  55.8 9.5 %collective-permute-start.11 = (bf16[8,96,768]{2,1,0:T(8,128)(2,1)S(1)}, bf16[8,96,768]{2,1,0:T(8,128)(2,1)S(1)}, u32[]{:S(2)}, u32[]{:S(2)}) collective-permute-start(bf16[8,96,768]{2,1,0:T(8,128)(2,1)S(1)} %get-tuple-element.41.refs_2_), channel_id=1, source_target_pairs={{0,1},{1,0},{2,3},{3,2},{4,5},{5,4},{6,7},{7,6},{8,9},{9,8},{10,11... | collective-permute-start | bytes 3538952 | tf_op jit(solution)/shard_map/ppermute | solution.py:139
  56.0 5.5 %collective-permute-start.7 = (bf16[4,32,2048]{2,1,0:T(8,128)(2,1)S(1)}, bf16[4,32,2048]{2,1,0:T(8,128)(2,1)S(1)}, u32[]{:S(2)}, u32[]{:S(2)}) collective-permute-start(bf16[4,32,2048]{2,1,0:T(8,128)(2,1)S(1)} %get-tuple-element.40), channel_id=1, source_target_pairs={{0,1},{1,0},{2,3},{3,2},{4,5},{5,4},{6,7},{7,6},{8,9},{9,8},{10,11... | collective-permute-start | bytes 1572872 | tf_op jit(solution)/shard_map/ppermute | solution.py:139
  56.4 8.9 %collective-permute-start.12 = (bf16[4,32,2048]{2,1,0:T(8,128)(2,1)S(1)}, bf16[4,32,2048]{2,1,0:T(8,128)(2,1)S(1)}, u32[]{:S(2)}, u32[]{:S(2)}) collective-permute-start(bf16[4,32,2048]{2,1,0:T(8,128)(2,1)S(1)} %get-tuple-element.49), channel_id=1, source_target_pairs={{0,1},{1,0},{2,3},{3,2},{4,5},{5,4},{6,7},{7,6},{8,9},{9,8},{10,11... | collective-permute-start | bytes 1572872 | tf_op jit(solution)/shard_map/ppermute | solution.py:139
  61.7 17.6 %collective-permute-start.10 = (bf16[32,2048]{1,0:T(8,128)(2,1)S(1)}, bf16[32,2048]{1,0:T(8,128)(2,1)S(1)}, u32[]{:S(2)}, u32[]{:S(2)}) collective-permute-start(bf16[32,2048]{1,0:T(8,128)(2,1)S(1)} %get-tuple-element.68), channel_id=1, source_target_pairs={{0,6},{1,7},{2,4},{3,5},{4,2},{5,3},{6,0},{7,1},{8,14},{9,15},{10,... | collective-permute-start | bytes 393224 | tf_op jit(solution)/shard_map/ppermute | solution.py:139
  63.6 15.7 %collective-permute-start.9 = (bf16[32,2048]{1,0:T(8,128)(2,1)S(1)}, bf16[32,2048]{1,0:T(8,128)(2,1)S(1)}, u32[]{:S(2)}, u32[]{:S(2)}) collective-permute-start(bf16[32,2048]{1,0:T(8,128)(2,1)S(1)} %get-tuple-element.69), channel_id=1, source_target_pairs={{0,4},{1,5},{2,6},{3,7},{4,0},{5,1},{6,2},{7,3},{8,12},{9,13},{10,... | collective-permute-start | bytes 393224 | tf_op jit(solution)/shard_map/ppermute | solution.py:139
  64.9 8.7 %collective-permute-start.8 = (bf16[32,2048]{1,0:T(8,128)(2,1)S(1)}, bf16[32,2048]{1,0:T(8,128)(2,1)S(1)}, u32[]{:S(2)}, u32[]{:S(2)}) collective-permute-start(bf16[32,2048]{1,0:T(8,128)(2,1)S(1)} %get-tuple-element.70), channel_id=1, source_target_pairs={{0,2},{1,3},{2,0},{3,1},{4,6},{5,7},{6,4},{7,5},{8,10},{9,11},{10,... | collective-permute-start | bytes 393224 | tf_op jit(solution)/shard_map/ppermute | solution.py:139
  65.4 20.9 %collective-permute-start.16 = (bf16[32,2048]{1,0:T(8,128)(2,1)S(1)}, bf16[32,2048]{1,0:T(8,128)(2,1)S(1)}, u32[]{:S(2)}, u32[]{:S(2)}) collective-permute-start(bf16[32,2048]{1,0:T(8,128)(2,1)S(1)} %get-tuple-element.63), channel_id=1, source_target_pairs={{0,6},{1,7},{2,4},{3,5},{4,2},{5,3},{6,0},{7,1},{8,14},{9,15},{10,... | collective-permute-start | bytes 393224 | tf_op jit(solution)/shard_map/ppermute | solution.py:139
  67.3 19.0 %collective-permute-start.15 = (bf16[32,2048]{1,0:T(8,128)(2,1)S(1)}, bf16[32,2048]{1,0:T(8,128)(2,1)S(1)}, u32[]{:S(2)}, u32[]{:S(2)}) collective-permute-start(bf16[32,2048]{1,0:T(8,128)(2,1)S(1)} %get-tuple-element.64), channel_id=1, source_target_pairs={{0,4},{1,5},{2,6},{3,7},{4,0},{5,1},{6,2},{7,3},{8,12},{9,13},{10,... | collective-permute-start | bytes 393224 | tf_op jit(solution)/shard_map/ppermute | solution.py:139
  73.7 12.6 %collective-permute-start.14 = (bf16[32,2048]{1,0:T(8,128)(2,1)S(1)}, bf16[32,2048]{1,0:T(8,128)(2,1)S(1)}, u32[]{:S(2)}, u32[]{:S(2)}) collective-permute-start(bf16[32,2048]{1,0:T(8,128)(2,1)S(1)} %get-tuple-element.65), channel_id=1, source_target_pairs={{0,2},{1,3},{2,0},{3,1},{4,6},{5,7},{6,4},{7,5},{8,10},{9,11},{10,... | collective-permute-start | bytes 393224 | tf_op jit(solution)/shard_map/ppermute | solution.py:139
  74.1 5.2 %copy-start = (bf16[1,32,2048]{2,1,0:T(8,128)(2,1)S(1)}, bf16[1,32,2048]{2,1,0:T(8,128)(2,1)}, u32[]{:S(2)}) copy-start(bf16[1,32,2048]{2,1,0:T(8,128)(2,1)} %param.8) | copy-start | bytes 393220
  79.4 6.9 %copy-start.1 = (bf16[1,32,2048]{2,1,0:T(8,128)(2,1)S(1)}, bf16[1,32,2048]{2,1,0:T(8,128)(2,1)}, u32[]{:S(2)}) copy-start(bf16[1,32,2048]{2,1,0:T(8,128)(2,1)} %param.10) | copy-start | bytes 393220
  79.4 6.9 %collective-permute-start.13 = (bf16[32,2048]{1,0:T(8,128)(2,1)S(1)}, bf16[32,2048]{1,0:T(8,128)(2,1)S(1)}, u32[]{:S(2)}, u32[]{:S(2)}) collective-permute-start(bf16[32,2048]{1,0:T(8,128)(2,1)S(1)} %add_convert_fusion.1), channel_id=1, source_target_pairs={{0,8},{8,16},{16,24},{24,0},{1,9},{9,17},{17,25},{25,1},{2,10},{10... | collective-permute-start | bytes 393224 | tf_op jit(solution)/shard_map/ppermute | solution.py:22
  86.4 5.0 %collective-permute-start.17 = (bf16[32,2048]{1,0:T(8,128)(2,1)S(1)}, bf16[32,2048]{1,0:T(8,128)(2,1)S(1)}, u32[]{:S(2)}, u32[]{:S(2)}) collective-permute-start(bf16[32,2048]{1,0:T(8,128)(2,1)S(1)} %add_convert_fusion), channel_id=1, source_target_pairs={{0,24},{8,0},{16,8},{24,16},{1,25},{9,1},{17,9},{25,17},{2,26},{10... | collective-permute-start | bytes 393224 | tf_op jit(solution)/shard_map/ppermute | solution.py:22

commit v6 on v5

--- a/solution.py
+++ b/solution.py
@@ -11,9 +11,8 @@
 LANES = 128
 CHUNK = 256
 VMEM_LIMIT = 24 * 1024 * 1024
-EXPERTS_LIMIT = 36 * 1024 * 1024
+EXPERTS_LIMIT = 40 * 1024 * 1024
 WEIGHT_CUTS = 4
-WEIGHT_SLOTS = 3
 
 
 def shifted(value, axis, steps):
@@ -178,7 +177,7 @@
     earlier = jnp.where(row < column, 1.0, 0.0).astype(jnp.bfloat16)
     slot = lax.broadcasted_iota(jnp.int32, (slots, tokens), 0).astype(jnp.float32)
 
-    def fill(first, start, picks, gates, flipped):
+    def find(first, start):
         ids = (first + lax.broadcasted_iota(jnp.int32, (count, tokens), 0)).astype(jnp.float32)
         named = jnp.zeros((count, tokens), jnp.float32)
         gated = jnp.zeros((count, tokens), jnp.float32)
@@ -188,19 +187,26 @@
             named = named + jnp.where(same, 1.0, 0.0)
             gated = gated + jnp.where(same, terms[0] + terms[1] + terms[2], 0.0)
         place = jnp.dot(named.astype(jnp.bfloat16), earlier, preferred_element_type=jnp.float32)
-        place = jnp.where(named > 0.0, place, -1.0)
+        return jnp.where(named > 0.0, place, -1.0), gated
+
+    def fill(place, gated, picks, gates, flipped):
         for expert in range(count):
             rows = pl.ds(expert * slots, slots)
             hit = place[expert : expert + 1, :] == slot
             picks[rows, :] = jnp.where(hit, 1.0, 0.0).astype(jnp.bfloat16)
             own = jnp.sum(jnp.where(hit, gated[expert : expert + 1, :], 0.0), axis=1, keepdims=True)
             gates[rows, :] = jnp.broadcast_to(own, (slots, LANES))
-        if flipped is not None:
-            flipped[...] = picks[...].T
-
-    fill(place_ref[1], 4 * top, outs[0], outs[1], outs[2])
-    fill(place_ref[1], 0, outs[3], outs[4], outs[5])
-    fill(place_ref[2], 0, outs[6], outs[7], None)
+        flipped[...] = picks[...].T
+
+    places, gated = find(place_ref[1], 4 * top)
+    fill(places, gated, outs[0], outs[1], outs[2])
+    places, gated = find(place_ref[1], 0)
+    fill(places, gated, outs[3], outs[4], outs[5])
+    other_places, other_gated = find(place_ref[2], 0)
+    turned[...] = jnp.zeros_like(turned)
+    for row, value in enumerate((places, other_places, gated, other_gated)):
+        turned[pl.ds(row * count, count), :] = value
+    outs[6][...] = turned[...].T
 
 
 def spread_gate(gates, rows, width):
@@ -238,161 +244,154 @@
 
 
 def expert_kernel(count, slots, devices, pair, place_ref, *refs):
-    picks_in, weights_in, blocks = refs[:6], refs[6], refs[7 : 7 + devices]
+    picks_in, weights, blocks = refs[:6], refs[6 : 6 + WEIGHT_CUTS], refs[6 + WEIGHT_CUTS :][:devices]
     groups = devices // pair
-    outs, inner_out = refs[7 + devices : 9 + devices + 2 * groups], refs[9 + devices + 2 * groups]
-    scratch = refs[10 + devices + 2 * groups :]
+    outs = refs[6 + WEIGHT_CUTS + devices :][: 2 * groups + 2]
+    inner, turned, *scratch = refs[8 + WEIGHT_CUTS + devices + 2 * groups :]
     held, tokens = scratch[:6], scratch[6:9]
-    rows, fore_results, back_results, second, inner, weights_ref = scratch[9:15]
-    weights_done, in_done, out_done, inner_done = scratch[15:]
+    rows, fore_results, back_results, second, in_done, out_done = scratch[9:]
     fore_picks, fore_gates, fore_flip, back_picks, back_gates, back_flip = held
-    size, width = blocks[0].shape[0], tokens[0].shape[1]
+    size, (total, width) = blocks[0].shape[0], tokens[0].shape
+    step = pl.program_id(0)
 
     def home(code):
         return pl.ds(pl.multiple_of(place_ref[3 + code], size), size)
 
-    arriving = [
-        pltpu.make_async_copy(source, target, in_done.at[3 * devices + place])
-        for place, (source, target) in enumerate(zip(picks_in, held))
-    ]
-    coming = [
+    @pl.when(step == 0)
+    def _():
+        arriving = [
+            pltpu.make_async_copy(source, target, in_done.at[3 * devices + place])
+            for place, (source, target) in enumerate(zip(picks_in, held))
+        ]
+        coming = [
+            [
+                pltpu.make_async_copy(
+                    block.at[:, pl.ds(place * width, width)],
+                    tokens[place].at[home(code), :],
+                    in_done.at[place * devices + code],
+                )
+                for code, block in enumerate(blocks)
+            ]
+            for place in range(3)
+        ]
+        for copy in arriving + coming[0] + coming[1] + coming[2]:
+            copy.start()
+        for copy in arriving:
+            copy.wait()
+        taken = ((fore_picks, None), (back_picks, None), (back_picks, back_gates))
+        for place, (picks, gates) in enumerate(taken):
+            for copy in coming[place]:
+                copy.wait()
+            gather(count, slots, picks, gates, tokens[place], rows, place * slots, 3 * slots)
+
+    mine = pl.ds(pl.multiple_of(step * slots, slots), slots)
+    three = pl.ds(pl.multiple_of(step * 3 * slots, 3 * slots), 3 * slots)
+    cut = width // WEIGHT_CUTS
+    product = functools.reduce(
+        jnp.add,
         [
-            pltpu.make_async_copy(
-                block.at[:, pl.ds(place * width, width)],
-                tokens[place].at[home(code), :],
-                in_done.at[place * devices + code],
+            jnp.dot(
+                rows[three, pl.ds(place * cut, cut)],
+                weight[0],
+                preferred_element_type=jnp.float32,
             )
-            for code, block in enumerate(blocks)
-        ]
-        for place in range(3)
-    ]
-    for copy in arriving + coming[0] + coming[1] + coming[2]:
-        copy.start()
-
-    def weight_copies(step):
-        cut = width // WEIGHT_CUTS
-        return [
-            pltpu.make_async_copy(
-                weights_in.at[place_ref[0] * count + step, pl.ds(place * cut, cut), :],
-                weights_ref.at[lax.rem(step, WEIGHT_SLOTS), pl.ds(place * cut, cut), :],
-                weights_done.at[lax.rem(step, WEIGHT_SLOTS), place],
-            )
-            for place in range(WEIGHT_CUTS)
-        ]
-
-    for step in range(min(count, WEIGHT_SLOTS - 1)):
-        for copy in weight_copies(step):
-            copy.start()
-    for copy in arriving:
-        copy.wait()
-    taken = ((fore_picks, None), (back_picks, None), (back_picks, back_gates))
-    for place, (picks, gates) in enumerate(taken):
-        for copy in coming[place]:
-            copy.wait()
-        gather(count, slots, picks, gates, tokens[place], rows, place * slots, 3 * slots)
-
-    def inner_copy(step):
-        return pltpu.make_async_copy(inner.at[step], inner_out.at[step], inner_done.at[step])
-
-    @pl.loop(0, count)
-    def _(step):
-        mine = pl.ds(pl.multiple_of(step * slots, slots), slots)
-        three = pl.ds(pl.multiple_of(step * 3 * slots, 3 * slots), 3 * slots)
-        slot = lax.rem(step, WEIGHT_SLOTS)
-
-        @pl.when(step + WEIGHT_SLOTS - 1 < count)
-        def _():
-            for copy in weight_copies(step + WEIGHT_SLOTS - 1):
-                copy.start()
-
-        for copy in weight_copies(step):
-            copy.wait()
-        product = jnp.dot(rows[three, :], weights_ref[slot], preferred_element_type=jnp.float32)
-        ahead, hidden, active_grads = (
-            product[:slots],
-            product[slots : 2 * slots],
-            product[2 * slots :],
+            for place, weight in enumerate(weights)
+        ],
+    )
+    ahead, hidden, active_grads = product[:slots], product[slots : 2 * slots], product[2 * slots :]
+    sigma = jax.nn.sigmoid(hidden)
+    hidden_grads = (active_grads * sigma * (1.0 + hidden * (1.0 - sigma))).astype(jnp.bfloat16)
+    inner[0, :slots, :] = hidden_grads
+    inner[0, slots:, :] = (hidden * sigma).astype(jnp.bfloat16)
+    second[:slots, :] = (ahead * jax.nn.sigmoid(ahead)).astype(jnp.bfloat16)
+    second[slots:, :] = hidden_grads
+    for place, weight in enumerate(weights):
+        columns = pl.ds(place * cut, cut)
+        result = lax.dot_general(
+            second[...], weight[0], (((1,), (1,)), ((), ())), preferred_element_type=jnp.float32
         )
-        sigma = jax.nn.sigmoid(hidden)
-        hidden_grads = (active_grads * sigma * (1.0 + hidden * (1.0 - sigma))).astype(jnp.bfloat16)
-        inner[step, :slots, :] = hidden_grads
-        inner[step, slots:, :] = (hidden * sigma).astype(jnp.bfloat16)
-        inner_copy(step).start()
-        second[:slots, :] = (ahead * jax.nn.sigmoid(ahead)).astype(jnp.bfloat16)
-        second[slots:, :] = hidden_grads
-        result = lax.dot_general(
-            second[...],
-            weights_ref[slot],
-            (((1,), (1,)), ((), ())),
-            preferred_element_type=jnp.float32,
-        )
-        fore_results[mine, :] = (result[:slots] * spread_gate(fore_gates, mine, width)).astype(
+        fore_results[mine, columns] = (result[:slots] * spread_gate(fore_gates, mine, cut)).astype(
             fore_results.dtype
         )
-        back_results[mine, :] = result[slots:].astype(back_results.dtype)
-
-    leaving = []
-    for lead, (flipped, results) in enumerate(((fore_flip, fore_results), (back_flip, back_results))):
-        sums = tokens[lead]
-        combine(flipped, results, sums)
-        *near_outs, far_out = outs[lead * (groups + 1) : (lead + 1) * (groups + 1)]
-        targets = [(far_out.at[group], pair * group + 1) for group in range(groups)]
-        targets += [(out, pair * group) for group, out in enumerate(near_outs)]
-        for target, code in targets:
-            done = out_done.at[lead * devices + code]
-            leaving.append(pltpu.make_async_copy(sums.at[home(code), :], target, done))
-            leaving[-1].start()
-    for copy in leaving:
-        copy.wait()
-    for step in range(count):
-        inner_copy(step).wait()
-
-
-def weight_kernel(whose, first, number, count, slots, devices, place_ref, *refs):
-    held_in, blocks = refs[:3], refs[3 : 3 + devices]
-    out_ref, picks, gates, inner, saved, grads, rows, staged, in_done, out_done = refs[-10:]
-    size, half = blocks[0].shape[0], saved.shape[1]
+        back_results[mine, columns] = result[slots:].astype(back_results.dtype)
+
+    span = turned.shape[0]
+    first = place_ref[0] * (width // pair) + step * span
+    for place in range(2):
+        some = tokens[1 + place][:, pl.ds(pl.multiple_of(first, LANES), span)]
+        turned[:, pl.ds(place * total, total)] = some.T
+
+    @pl.when(step == count - 1)
+    def _():
+        leaving = []
+        for lead, (flipped, results) in enumerate(
+            ((fore_flip, fore_results), (back_flip, back_results))
+        ):
+            sums = tokens[lead]
+            combine(flipped, results, sums)
+            *near_outs, far_out = outs[lead * (groups + 1) : (lead + 1) * (groups + 1)]
+            targets = [(far_out.at[group], pair * group + 1) for group in range(groups)]
+            targets += [(out, pair * group) for group, out in enumerate(near_outs)]
+            for target, code in targets:
+                done = out_done.at[lead * devices + code]
+                leaving.append(pltpu.make_async_copy(sums.at[home(code), :], target, done))
+                leaving[-1].start()
+        for copy in leaving:
+            copy.wait()
+
+
+def weight_kernel(whose, first, number, count, slots, place_ref, *refs):
+    columns_in, inner_in, turned_in = refs[:3]
+    out_ref, columns, inner, turned, picks, rows, staged, in_done, out_done = refs[-9:]
+    total, half = columns.shape[0], turned.shape[0]
     side = place_ref[0]
     owner = side if whose == 0 else 1 - side
-    part = pl.ds(first * slots, number * slots)
-
     arriving = [
-        pltpu.make_async_copy(source, target, in_done.at[2 * devices + place])
-        for place, (source, target) in enumerate(
-            (
-                (held_in[0].at[part, :], picks),
-                (held_in[1].at[part, :], gates),
-                (held_in[2].at[pl.ds(first, number)], inner),
-            )
-        )
+        pltpu.make_async_copy(columns_in, columns, in_done.at[0]),
+        pltpu.make_async_copy(
+            inner_in.at[pl.ds(first, number)], inner.at[:, pl.ds(0, 2 * slots), :], in_done.at[1]
+        ),
+        pltpu.make_async_copy(turned_in, turned, in_done.at[2]),
     ]
-    coming = [
-        [
-            pltpu.make_async_copy(
-                block.at[:, pl.ds(pl.multiple_of((2 * place + 2 + side) * half, half), half)],
-                target.at[pl.ds(pl.multiple_of(place_ref[3 + code], size), size), :],
-                in_done.at[place * devices + code],
-            )
-            for code, block in enumerate(blocks)
-        ]
-        for place, target in enumerate((saved, grads))
-    ]
-    for copy in arriving + coming[0] + coming[1]:
+    for copy in arriving:
         copy.start()
-    for copy in arriving:
+    inner[:, pl.ds(2 * slots, LANES - 2 * slots), :] = jnp.zeros(
+        (number, LANES - 2 * slots, inner.shape[2]), inner.dtype
+    )
+    arriving[0].wait()
+    lane = lax.broadcasted_iota(jnp.int32, (total, LANES), 1).astype(jnp.float32)
+    is_saved = lax.broadcasted_iota(jnp.int32, (1, LANES), 1) < slots
+    scales = []
+    for step in range(number):
+        column = whose * count + first + step
+        slot = jnp.broadcast_to(columns[:, column : column + 1], (total, LANES))
+        column += 2 * count
+        gate = jnp.broadcast_to(columns[:, column : column + 1], (total, LANES))
+        saved, grads = slot == lane, slot == lane - slots
+        lanes = pl.ds(step * LANES, LANES)
+        picks[pl.ds(0, total), lanes] = jnp.where(saved, 1.0, 0.0).astype(picks.dtype)
+        picks[pl.ds(total, total), lanes] = jnp.where(
+            jnp.logical_and(grads, lane >= slots), 1.0, 0.0
+        ).astype(picks.dtype)
+        scale = jnp.sum(jnp.where(grads, gate, 0.0), axis=0, keepdims=True)
+        scales.append(jnp.where(is_saved, 1.0, scale))
+    for copy in arriving[1:]:
         copy.wait()
-    for place, (tokens, scale) in enumerate(((saved, None), (grads, gates))):
-        for copy in coming[place]:
-            copy.wait()
-        gather(number, slots, picks, scale, tokens, rows, place * slots, 2 * slots)
+    for step in range(0, number, 2):
+        lanes = pl.ds(step * LANES, 2 * LANES)
+        scale = jnp.concatenate(scales[step : step + 2], axis=1)
+        rows[:, lanes] = (
+            jnp.dot(turned[...], picks[:, lanes], preferred_element_type=jnp.float32) * scale
+        ).astype(rows.dtype)
 
     leaving = []
     for step in range(number):
-        flat = rows[pl.ds(step * 2 * slots, 2 * slots), :].T
         for start in range(0, half, CHUNK):
             chunk = pl.ds(start, CHUNK)
             staged[step, chunk, :] = jnp.dot(
-                flat[start : start + CHUNK], inner[step], preferred_element_type=jnp.float32
+                rows[chunk, pl.ds(step * LANES, LANES)],
+                inner[step],
+                preferred_element_type=jnp.float32,
             ).astype(staged.dtype)
             leaving.append(
                 pltpu.make_async_copy(
@@ -508,7 +507,8 @@
     pick = jax.ShapeDtypeStruct((rows, total), jnp.bfloat16)
     flip = jax.ShapeDtypeStruct((total, rows), jnp.bfloat16)
     gate = jax.ShapeDtypeStruct((rows, LANES), jnp.float32)
-    pick_outs = [pick, gate, flip, pick, gate, flip, pick, gate]
+    columns = jax.ShapeDtypeStruct((total, LANES), jnp.float32)
+    pick_outs = [pick, gate, flip, pick, gate, flip, columns]
     picks = call(
         functools.partial(picks_kernel, count, top, slots, devices),
         "slot_picks",
@@ -523,61 +523,69 @@
     near_part = jax.ShapeDtypeStruct((token_count, width), jnp.bfloat16)
     far_part = jax.ShapeDtypeStruct((groups, token_count, width), jnp.bfloat16)
     inner = jax.ShapeDtypeStruct((count, 2 * slots, inner_width), jnp.bfloat16)
+    turned = jax.ShapeDtypeStruct((half, 2 * total), jnp.bfloat16)
     in_smem, anywhere = (pl.BlockSpec(memory_space=space) for space in (pltpu.SMEM, pl.ANY))
     tokens = pltpu.VMEM((total, width), jnp.bfloat16)
-    *parts, inner_own = pl.pallas_call(
+    cut = width // WEIGHT_CUTS
+    *parts, inner_own, tokens_turned = pl.pallas_call(
         functools.partial(expert_kernel, count, slots, devices, pair),
-        in_specs=[in_smem] + [anywhere] * (7 + devices),
-        out_specs=[anywhere] * (2 * groups + 3),
-        out_shape=([near_part] * groups + [far_part]) * 2 + [inner],
-        scratch_shapes=[pltpu.VMEM(array.shape, array.dtype) for array in pick_outs[:6]]
-        + [tokens] * 3
-        + [
-            pltpu.VMEM((3 * rows, width), jnp.bfloat16),
-            pltpu.VMEM((rows, width), jnp.bfloat16),
-            pltpu.VMEM((rows, width), jnp.bfloat16),
-            pltpu.VMEM((2 * slots, inner_width), jnp.bfloat16),
-            pltpu.VMEM(inner.shape, inner.dtype),
-            pltpu.VMEM((WEIGHT_SLOTS, width, inner_width), jnp.bfloat16),
-            pltpu.SemaphoreType.DMA((WEIGHT_SLOTS, WEIGHT_CUTS)),
-            pltpu.SemaphoreType.DMA((3 * devices + 6,)),
-            pltpu.SemaphoreType.DMA((2 * devices,)),
-            pltpu.SemaphoreType.DMA((count,)),
-        ],
-        compiler_params=pltpu.CompilerParams(vmem_limit_bytes=EXPERTS_LIMIT),
+        grid_spec=pltpu.PrefetchScalarGridSpec(
+            num_scalar_prefetch=1,
+            grid=(count,),
+            in_specs=[anywhere] * 6
+            + [
+                pl.BlockSpec(
+                    (1, cut, inner_width),
+                    lambda step, place, part=part: (place[0] * count + step, part, 0),
+                )
+                for part in range(WEIGHT_CUTS)
+            ]
+            + [anywhere] * devices,
+            out_specs=[anywhere] * (2 * groups + 2)
+            + [
+                pl.BlockSpec((1, 2 * slots, inner_width), lambda step, place: (step, 0, 0)),
+                pl.BlockSpec((half // count, 2 * total), lambda step, place: (step, 0)),
+            ],
+            scratch_shapes=[pltpu.VMEM(array.shape, array.dtype) for array in pick_outs[:6]]
+            + [tokens] * 3
+            + [
+                pltpu.VMEM((3 * rows, width), jnp.bfloat16),
+                pltpu.VMEM((rows, width), jnp.bfloat16),
+                pltpu.VMEM((rows, width), jnp.bfloat16),
+                pltpu.VMEM((2 * slots, inner_width), jnp.bfloat16),
+                pltpu.SemaphoreType.DMA((3 * devices + 6,)),
+                pltpu.SemaphoreType.DMA((2 * devices,)),
+            ],
+        ),
+        out_shape=([near_part] * groups + [far_part]) * 2 + [inner, turned],
+        compiler_params=pltpu.CompilerParams(
+            vmem_limit_bytes=EXPERTS_LIMIT, dimension_semantics=("arbitrary",)
+        ),
         cost_estimate=pl.CostEstimate(
             flops=pass_flops, bytes_accessed=pass_flops // 512, transcendentals=0
         ),
         name="experts",
-    )(
-        place,
-        *picks[:6],
-        weights,
-        *blocks,
-    )
+    )(place, *picks[:6], *[weights] * WEIGHT_CUTS, *blocks)
     *layer_parts, layer_far = parts[: groups + 1]
     *grad_parts, grad_far = parts[groups + 1 :]
     layer_far, grad_far, inner_other = onward(layer_far), onward(grad_far), onward(inner_own)
 
     def gradient(whose, first, number, inner_rows, earlier):
         earlier = [] if earlier is None else [earlier]
-        held = list(picks[3:5] if whose == 0 else picks[6:8]) + [inner_rows]
-        operands = held + blocks + earlier
-        half_tokens = pltpu.VMEM((total, half), jnp.bfloat16)
+        operands = [picks[6], inner_rows, tokens_turned] + earlier
         return pl.pallas_call(
-            functools.partial(weight_kernel, whose, first, number, count, slots, devices),
+            functools.partial(weight_kernel, whose, first, number, count, slots),
             in_specs=[in_smem] + [anywhere] * len(operands),
             out_specs=anywhere,
             out_shape=jax.ShapeDtypeStruct((local_count, half, inner_width), jnp.bfloat16),
             scratch_shapes=[
-                pltpu.VMEM((number * slots, total), jnp.bfloat16),
-                pltpu.VMEM((number * slots, LANES), jnp.float32),
-                pltpu.VMEM((number, 2 * slots, inner_width), jnp.bfloat16),
-                half_tokens,
-                half_tokens,
-                pltpu.VMEM((number * 2 * slots, half), jnp.bfloat16),
+                pltpu.VMEM(columns.shape, columns.dtype),
+                pltpu.VMEM((number, LANES, inner_width), jnp.bfloat16),
+                pltpu.VMEM(turned.shape, turned.dtype),
+                pltpu.VMEM((2 * total, number * LANES), jnp.bfloat16),
+                pltpu.VMEM((half, number * LANES), jnp.bfloat16),
                 pltpu.VMEM((number, half, inner_width), jnp.bfloat16),
-                pltpu.SemaphoreType.DMA((2 * devices + 3,)),
+                pltpu.SemaphoreType.DMA((3,)),
                 pltpu.SemaphoreType.DMA((number, half // CHUNK)),
             ],
             compiler_params=pltpu.CompilerParams(vmem_limit_bytes=VMEM_LIMIT),
@@ -621,7 +629,7 @@
     groups, pair = lax.axis_size("expert"), lax.axis_size("dp")
     gathered = groups * token_count
     packed = groups * local_count * CAP
-    paired = pair == 2 and local_count % pair == 0 and groups & (groups - 1) == 0
+    paired = pair == 2 and local_count % 8 == 0 and groups & (groups - 1) == 0
     if gathered <= packed and paired and gathered * pair % LANES == 0:
         return gathered_plan(*arrays)
     return packed_plan(*arrays)

time: 92.9 us -> 91.2 us (0.982)
  Pallas kernels: 51.3 us -> 49.4 us
    pallas_call x1, Pallas kernels: 28.6 us -> 27.5 us  [gathered_plan(): pl.pallas_call(functools.partial(expert_kernel, count, slots, devices, pa...]
  transfers between devices with their start and end apart: 18 -> 18, of which waited for: 6 -> 7; matrix products, arithmetic and copies ran while one was open for 0% -> 0% of each run, Pallas kernels for 22% -> 22%
where the time goes in v6:
time: 91.2 us; the launch traced here: 91 us
  Pallas kernels  49.4 us (54%)
  waiting for transfers between devices  22.3 us (24%)
  starting transfers between devices  16.6 us (18%)
  local copies, waits for them, and re-layouts  1.41 us (2%)
    pallas_call x1, Pallas kernels, gathered_plan(): pl.pallas_call(functools.partial(expert_kernel, count, slots, devices, pa...  27.5 us
    pallas_call x4, Pallas kernels, gradient(): pl.pallas_call(functools.partial(weight_kernel, whose, first, number, cou...  19.6 us
    ppermute x16, waiting for transfers between devices, swapped(): lax.ppermute(value, axes, [(source, source ^ code) for source in range(co...  19.2 us
    ppermute x16, starting transfers between devices, swapped(): lax.ppermute(value, axes, [(source, source ^ code) for source in range(co...  12.8 us
    ppermute x2, starting transfers between devices, shifted(): return lax.ppermute(value, axis, pairs)  3.86 us
    ppermute x2, waiting for transfers between devices, shifted(): return lax.ppermute(value, axis, pairs)  3.08 us
  transfers between devices with their start and end apart: 18, of which 7 were waited for; matrix products, arithmetic and copies ran while one was open for 0% of the time, Pallas kernels for 22%

profile of v6, /device:TPU:0, one launch (start us, length us, event | category | flops | bytes accessed | tf_op | source)
XLA Modules:
  0.0 91.0 jit_solution(15857178901244743038)
XLA Ops:
  0.6 1.2 %pack.1.refs_0_.refs_10_ = bf16[32,6272]{1,0:T(8,128)(2,1)S(1)} custom-call(bf16[32,2048]{1,0:T(8,128)(2,1)} %bitcast.61, bf16[32,2048]{1,0:T(8,128)(2,1)} %bitcast.63, bf16[32,2048]{1,0:T(8,128)(2,1)} %bitcast.62, s32[8,32]{1,0:T(8,128)} %bitcast.66, f32[8,32]{1,0:T(8,128)} %bitcast.67, s32[8,32]{1,0:T(8,128)} %bitcast.68, f32[8,32]{1,0:T(8,128)} %bitcast.69), custom_call_target="tpu_custom_call" | custom-call | tf_op jit(solution)/shard_map/pack/pallas_call | solution.py:475
  1.8 4.0 %collective-permute-start.5 = (bf16[32,6272]{1,0:T(8,128)(2,1)S(1)}, bf16[32,6272]{1,0:T(8,128)(2,1)S(1)}, u32[]{:S(2)}, u32[]{:S(2)}) collective-permute-start(bf16[32,6272]{1,0:T(8,128)(2,1)S(1)} %pack.1.refs_0_.refs_10_), channel_id=1, source_target_pairs={{0,6},{1,7},{2,4},{3,5},{4,2},{5,3},{6,0},{7,1},{8,14},{9,15},{10,... | collective-permute-start | bytes 1204232 | tf_op jit(solution)/shard_map/ppermute | solution.py:138
  5.8 0.5 collective-permute-start.3
  6.3 0.1 collective-permute-start.1
  6.4 0.0 collective-permute-start
  6.4 9.5 %collective-permute-done.5.refs_6_.refs_16_ = bf16[32,6272]{1,0:T(8,128)(2,1)S(1)} collective-permute-done((bf16[32,6272]{1,0:T(8,128)(2,1)S(1)}, bf16[32,6272]{1,0:T(8,128)(2,1)S(1)}, u32[]{:S(2)}, u32[]{:S(2)}) %collective-permute-start.5) | collective-permute-done | bytes 401440 | tf_op jit(solution)/shard_map/ppermute | solution.py:138
  15.9 0.0 collective-permute-start.6
  16.0 7.7 %collective-permute-done.3.refs_4_.refs_14_ = bf16[32,6272]{1,0:T(8,128)(2,1)S(1)} collective-permute-done((bf16[32,6272]{1,0:T(8,128)(2,1)S(1)}, bf16[32,6272]{1,0:T(8,128)(2,1)S(1)}, u32[]{:S(2)}, u32[]{:S(2)}) %collective-permute-start.3) | collective-permute-done | bytes 401440 | tf_op jit(solution)/shard_map/ppermute | solution.py:138
  23.7 0.0 collective-permute-start.4
  23.7 0.3 collective-permute-done.1.refs_2_.refs_12_
  24.0 0.2 collective-permute-start.2
  24.2 0.1 stack.47.place_ref
  24.3 0.0 collective-permute-done.refs_1_.refs_11_
  24.3 0.0 collective-permute-done.6.refs_7_.refs_17_
  24.3 1.1 %collective-permute-done.4.refs_5_.refs_15_ = bf16[32,6272]{1,0:T(8,128)(2,1)S(1)} collective-permute-done((bf16[32,6272]{1,0:T(8,128)(2,1)S(1)}, bf16[32,6272]{1,0:T(8,128)(2,1)S(1)}, u32[]{:S(2)}, u32[]{:S(2)}) %collective-permute-start.4) | collective-permute-done | bytes 401440 | tf_op jit(solution)/shard_map/ppermute | solution.py:138
  25.4 0.6 collective-permute-done.2.refs_3_.refs_13_
  26.0 1.1 %slot_picks.1 = (bf16[384,256]{1,0:T(8,128)(2,1)S(1)}, f32[384,128]{1,0:T(8,128)S(1)}, bf16[256,384]{1,0:T(8,128)(2,1)S(1)}, bf16[384,256]{1,0:T(8,128)(2,1)S(1)...) custom-call(s32[11]{0:T(128)S(1)} %stack.47.place_ref, ...), custom_call_target="tpu_custom_call" | custom-call | bytes 1024 | tf_op jit(solution)/shard_map/slot_picks/pallas_call | solution.py:512
  27.1 27.5 %experts.1 = (bf16[32,2048]{1,0:T(8,128)(2,1)S(1)}, bf16[32,2048]{1,0:T(8,128)(2,1)S(1)}, bf16[32,2048]{1,0:T(8,128)(2,1)S(1)}, bf16[32,2048]{1,0:T(8,128)(2,1)S...) custom-call(s32[11]{0:T(128)S(1)} %stack.47.place_ref, ...), custom_call_target="tpu_custom_call" | custom-call | flops 12884901888 | bytes 25165824 | tf_op jit(solution)/shard_map/experts/pallas_call | solution.py:530
  54.6 0.2 collective-permute-start.11
  54.8 0.4 collective-permute-start.7
  55.2 0.1 collective-permute-start.12
  55.3 4.9 %weight_gradient_0_0.1.refs_3_ = bf16[16,1024,768]{2,1,0:T(8,128)(2,1)} custom-call(s32[11]{0:T(128)S(1)} %stack.47.place_ref, f32[256,128]{1,0:T(8,128)S(1)} %get-tuple-element.41.refs_0_, bf16[8,96,768]{2,1,0:T(8,128)(2,1)S(1)} %get-tuple-element.42.refs_1_, bf16[1024,512]{1,0:T(8,128)(2,1)S(1)} %get-tuple-element.43.refs_2_), custom_call_target="tpu_custom_call" | custom-call | flops 3221225472 | bytes 12582912 | tf_op jit(solution)/shard_map/weight_gradient_0_0/pallas_call | solution.py:576
  60.2 0.0 collective-permute-done.7
  60.2 0.1 fusion.7
  60.3 1.9 %collective-permute-start.10 = (bf16[32,2048]{1,0:T(8,128)(2,1)S(1)}, bf16[32,2048]{1,0:T(8,128)(2,1)S(1)}, u32[]{:S(2)}, u32[]{:S(2)}) collective-permute-start(bf16[32,2048]{1,0:T(8,128)(2,1)S(1)} %get-tuple-element.68), channel_id=1, source_target_pairs={{0,6},{1,7},{2,4},{3,5},{4,2},{5,3},{6,0},{7,1},{8,14},{9,15},{10,... | collective-permute-start | bytes 393224 | tf_op jit(solution)/shard_map/ppermute | solution.py:138
  62.2 1.3 %collective-permute-start.9 = (bf16[32,2048]{1,0:T(8,128)(2,1)S(1)}, bf16[32,2048]{1,0:T(8,128)(2,1)S(1)}, u32[]{:S(2)}, u32[]{:S(2)}) collective-permute-start(bf16[32,2048]{1,0:T(8,128)(2,1)S(1)} %get-tuple-element.69), channel_id=1, source_target_pairs={{0,4},{1,5},{2,6},{3,7},{4,0},{5,1},{6,2},{7,3},{8,12},{9,13},{10,... | collective-permute-start | bytes 393224 | tf_op jit(solution)/shard_map/ppermute | solution.py:138
  63.6 0.4 collective-permute-start.8
  63.9 0.0 collective-permute-done.12
  63.9 0.0 collective-permute-done.11.refs_1_
  63.9 0.1 fusion
  64.1 1.9 %collective-permute-start.16 = (bf16[32,2048]{1,0:T(8,128)(2,1)S(1)}, bf16[32,2048]{1,0:T(8,128)(2,1)S(1)}, u32[]{:S(2)}, u32[]{:S(2)}) collective-permute-start(bf16[32,2048]{1,0:T(8,128)(2,1)S(1)} %get-tuple-element.63), channel_id=1, source_target_pairs={{0,6},{1,7},{2,4},{3,5},{4,2},{5,3},{6,0},{7,1},{8,14},{9,15},{10,... | collective-permute-start | bytes 393224 | tf_op jit(solution)/shard_map/ppermute | solution.py:138
  65.9 1.3 %collective-permute-start.15 = (bf16[32,2048]{1,0:T(8,128)(2,1)S(1)}, bf16[32,2048]{1,0:T(8,128)(2,1)S(1)}, u32[]{:S(2)}, u32[]{:S(2)}) collective-permute-start(bf16[32,2048]{1,0:T(8,128)(2,1)S(1)} %get-tuple-element.64), channel_id=1, source_target_pairs={{0,4},{1,5},{2,6},{3,7},{4,0},{5,1},{6,2},{7,3},{8,12},{9,13},{10,... | collective-permute-start | bytes 393224 | tf_op jit(solution)/shard_map/ppermute | solution.py:138
  67.3 4.9 %weight_gradient_0_4.1.refs_3_ = bf16[16,1024,768]{2,1,0:T(8,128)(2,1)} custom-call(s32[11]{0:T(128)S(1)} %stack.47.place_ref, f32[256,128]{1,0:T(8,128)S(1)} %get-tuple-element.41.refs_0_, bf16[8,96,768]{2,1,0:T(8,128)(2,1)S(1)} %get-tuple-element.42.refs_1_, bf16[1024,512]{1,0:T(8,128)(2,1)S(1)} %get-tuple-element.43.refs_2_, ...), custom_call_target="tpu_custom_call", output_to_operand_aliasing={{}: (4, {})} | custom-call | flops 3221225472 | bytes 12582912 | tf_op jit(solution)/shard_map/weight_gradient_0_4/pallas_call | solution.py:576
  72.1 0.0 copy-start
  72.1 0.0 collective-permute-done.8
  72.1 0.4 collective-permute-start.14
  72.6 5.0 %weight_gradient_1_0.1.refs_3_ = bf16[16,1024,768]{2,1,0:T(8,128)(2,1)} custom-call(s32[11]{0:T(128)S(1)} %stack.47.place_ref, f32[256,128]{1,0:T(8,128)S(1)} %get-tuple-element.41.refs_0_, bf16[8,96,768]{2,1,0:T(8,128)(2,1)S(1)} %collective-permute-done.11.refs_1_, bf16[1024,512]{1,0:T(8,128)(2,1)S(1)} %get-tuple-element.43.refs_2_, ...), custom_call_target="tpu_custom_call", output_to_operand_aliasing={{}: (4, {})} | custom-call | flops 3221225472 | bytes 12582912 | tf_op jit(solution)/shard_map/weight_gradient_1_0/pallas_call | solution.py:576
  77.6 0.0 collective-permute-done.10
  77.6 0.0 collective-permute-done.9
  77.6 0.0 copy-done
  77.6 0.1 add_convert_fusion.1
  77.7 0.0 copy-start.1
  77.8 1.8 %collective-permute-start.13 = (bf16[32,2048]{1,0:T(8,128)(2,1)S(1)}, bf16[32,2048]{1,0:T(8,128)(2,1)S(1)}, u32[]{:S(2)}, u32[]{:S(2)}) collective-permute-start(bf16[32,2048]{1,0:T(8,128)(2,1)S(1)} %add_convert_fusion.1), channel_id=1, source_target_pairs={{0,8},{8,16},{16,24},{24,0},{1,9},{9,17},{17,25},{25,1},{2,10},{10... | collective-permute-start | bytes 393224 | tf_op jit(solution)/shard_map/ppermute | solution.py:21
  79.6 4.9 %weight_gradient_1_4.1 = bf16[16,1024,768]{2,1,0:T(8,128)(2,1)} custom-call(s32[11]{0:T(128)S(1)} %stack.47.place_ref, f32[256,128]{1,0:T(8,128)S(1)} %get-tuple-element.41.refs_0_, bf16[8,96,768]{2,1,0:T(8,128)(2,1)S(1)} %collective-permute-done.11.refs_1_, bf16[1024,512]{1,0:T(8,128)(2,1)S(1)} %get-tuple-element.43.refs_2_, ...), custom_call_target="tpu_custom_call", output_to_operand_aliasing={{}: (4, {})} | custom-call | flops 3221225472 | bytes 12582912 | tf_op jit(solution)/shard_map/weight_gradient_1_4/pallas_call | solution.py:576
  84.4 0.0 collective-permute-done.16
  84.4 0.0 collective-permute-done.15
  84.5 0.0 collective-permute-done.14
  84.5 0.1 collective-permute-done.13
  84.6 0.0 copy-done.1
  84.6 0.1 add_convert_fusion
  84.7 2.0 %collective-permute-start.17 = (bf16[32,2048]{1,0:T(8,128)(2,1)S(1)}, bf16[32,2048]{1,0:T(8,128)(2,1)S(1)}, u32[]{:S(2)}, u32[]{:S(2)}) collective-permute-start(bf16[32,2048]{1,0:T(8,128)(2,1)S(1)} %add_convert_fusion), channel_id=1, source_target_pairs={{0,24},{8,0},{16,8},{24,16},{1,25},{9,1},{17,9},{25,17},{2,26},{10... | collective-permute-start | bytes 393224 | tf_op jit(solution)/shard_map/ppermute | solution.py:21
  86.7 3.0 %collective-permute-done.17 = bf16[32,2048]{1,0:T(8,128)(2,1)S(1)} collective-permute-done((bf16[32,2048]{1,0:T(8,128)(2,1)S(1)}, bf16[32,2048]{1,0:T(8,128)(2,1)S(1)}, u32[]{:S(2)}, u32[]{:S(2)}) %collective-permute-start.17) | collective-permute-done | bytes 131104 | tf_op jit(solution)/shard_map/ppermute | solution.py:21
  89.7 0.7 copy.19
  90.3 0.7 copy.20
Async XLA Ops:
  1.8 14.1 %collective-permute-start.5 = (bf16[32,6272]{1,0:T(8,128)(2,1)S(1)}, bf16[32,6272]{1,0:T(8,128)(2,1)S(1)}, u32[]{:S(2)}, u32[]{:S(2)}) collective-permute-start(bf16[32,6272]{1,0:T(8,128)(2,1)S(1)} %pack.1.refs_0_.refs_10_), channel_id=1, source_target_pairs={{0,6},{1,7},{2,4},{3,5},{4,2},{5,3},{6,0},{7,1},{8,14},{9,15},{10,... | collective-permute-start | bytes 1204232 | tf_op jit(solution)/shard_map/ppermute | solution.py:138
  5.8 17.9 %collective-permute-start.3 = (bf16[32,6272]{1,0:T(8,128)(2,1)S(1)}, bf16[32,6272]{1,0:T(8,128)(2,1)S(1)}, u32[]{:S(2)}, u32[]{:S(2)}) collective-permute-start(bf16[32,6272]{1,0:T(8,128)(2,1)S(1)} %pack.1.refs_0_.refs_10_), channel_id=1, source_target_pairs={{0,4},{1,5},{2,6},{3,7},{4,0},{5,1},{6,2},{7,3},{8,12},{9,13},{10,... | collective-permute-start | bytes 1204232 | tf_op jit(solution)/shard_map/ppermute | solution.py:138
  6.3 17.7 %collective-permute-start.1 = (bf16[32,6272]{1,0:T(8,128)(2,1)S(1)}, bf16[32,6272]{1,0:T(8,128)(2,1)S(1)}, u32[]{:S(2)}, u32[]{:S(2)}) collective-permute-start(bf16[32,6272]{1,0:T(8,128)(2,1)S(1)} %pack.1.refs_0_.refs_10_), channel_id=1, source_target_pairs={{0,2},{1,3},{2,0},{3,1},{4,6},{5,7},{6,4},{7,5},{8,10},{9,11},{10,... | collective-permute-start | bytes 1204232 | tf_op jit(solution)/shard_map/ppermute | solution.py:138
  6.4 17.9 %collective-permute-start = (bf16[32,6272]{1,0:T(8,128)(2,1)S(1)}, bf16[32,6272]{1,0:T(8,128)(2,1)S(1)}, u32[]{:S(2)}, u32[]{:S(2)}) collective-permute-start(bf16[32,6272]{1,0:T(8,128)(2,1)S(1)} %pack.1.refs_0_.refs_10_), channel_id=1, source_target_pairs={{0,1},{1,0},{2,3},{3,2},{4,5},{5,4},{6,7},{7,6},{8,9},{9,8},{10,11... | collective-permute-start | bytes 1204232 | tf_op jit(solution)/shard_map/ppermute | solution.py:138
  15.9 8.3 %collective-permute-start.6 = (bf16[32,6272]{1,0:T(8,128)(2,1)S(1)}, bf16[32,6272]{1,0:T(8,128)(2,1)S(1)}, u32[]{:S(2)}, u32[]{:S(2)}) collective-permute-start(bf16[32,6272]{1,0:T(8,128)(2,1)S(1)} %collective-permute-done.5.refs_6_.refs_16_), channel_id=1, source_target_pairs={{0,1},{1,0},{2,3},{3,2},{4,5},{5,4},{6,7},{7,6},{8,9},{9,8},{10,11... | collective-permute-start | bytes 1204232 | tf_op jit(solution)/shard_map/ppermute | solution.py:138
  23.7 1.7 %collective-permute-start.4 = (bf16[32,6272]{1,0:T(8,128)(2,1)S(1)}, bf16[32,6272]{1,0:T(8,128)(2,1)S(1)}, u32[]{:S(2)}, u32[]{:S(2)}) collective-permute-start(bf16[32,6272]{1,0:T(8,128)(2,1)S(1)} %collective-permute-done.3.refs_4_.refs_14_), channel_id=1, source_target_pairs={{0,1},{1,0},{2,3},{3,2},{4,5},{5,4},{6,7},{7,6},{8,9},{9,8},{10,11... | collective-permute-start | bytes 1204232 | tf_op jit(solution)/shard_map/ppermute | solution.py:138
  24.0 2.0 %collective-permute-start.2 = (bf16[32,6272]{1,0:T(8,128)(2,1)S(1)}, bf16[32,6272]{1,0:T(8,128)(2,1)S(1)}, u32[]{:S(2)}, u32[]{:S(2)}) collective-permute-start(bf16[32,6272]{1,0:T(8,128)(2,1)S(1)} %collective-permute-done.1.refs_2_.refs_12_), channel_id=1, source_target_pairs={{0,1},{1,0},{2,3},{3,2},{4,5},{5,4},{6,7},{7,6},{8,9},{9,8},{10,11... | collective-permute-start | bytes 1204232 | tf_op jit(solution)/shard_map/ppermute | solution.py:138
  54.6 9.3 %collective-permute-start.11 = (bf16[8,96,768]{2,1,0:T(8,128)(2,1)S(1)}, bf16[8,96,768]{2,1,0:T(8,128)(2,1)S(1)}, u32[]{:S(2)}, u32[]{:S(2)}) collective-permute-start(bf16[8,96,768]{2,1,0:T(8,128)(2,1)S(1)} %get-tuple-element.42.refs_1_), channel_id=1, source_target_pairs={{0,1},{1,0},{2,3},{3,2},{4,5},{5,4},{6,7},{7,6},{8,9},{9,8},{10,11... | collective-permute-start | bytes 3538952 | tf_op jit(solution)/shard_map/ppermute | solution.py:138
  54.8 5.4 %collective-permute-start.7 = (bf16[4,32,2048]{2,1,0:T(8,128)(2,1)S(1)}, bf16[4,32,2048]{2,1,0:T(8,128)(2,1)S(1)}, u32[]{:S(2)}, u32[]{:S(2)}) collective-permute-start(bf16[4,32,2048]{2,1,0:T(8,128)(2,1)S(1)} %get-tuple-element.40), channel_id=1, source_target_pairs={{0,1},{1,0},{2,3},{3,2},{4,5},{5,4},{6,7},{7,6},{8,9},{9,8},{10,11... | collective-permute-start | bytes 1572872 | tf_op jit(solution)/shard_map/ppermute | solution.py:138
  55.2 8.7 %collective-permute-start.12 = (bf16[4,32,2048]{2,1,0:T(8,128)(2,1)S(1)}, bf16[4,32,2048]{2,1,0:T(8,128)(2,1)S(1)}, u32[]{:S(2)}, u32[]{:S(2)}) collective-permute-start(bf16[4,32,2048]{2,1,0:T(8,128)(2,1)S(1)} %get-tuple-element.49), channel_id=1, source_target_pairs={{0,1},{1,0},{2,3},{3,2},{4,5},{5,4},{6,7},{7,6},{8,9},{9,8},{10,11... | collective-permute-start | bytes 1572872 | tf_op jit(solution)/shard_map/ppermute | solution.py:138
  60.3 17.3 %collective-permute-start.10 = (bf16[32,2048]{1,0:T(8,128)(2,1)S(1)}, bf16[32,2048]{1,0:T(8,128)(2,1)S(1)}, u32[]{:S(2)}, u32[]{:S(2)}) collective-permute-start(bf16[32,2048]{1,0:T(8,128)(2,1)S(1)} %get-tuple-element.68), channel_id=1, source_target_pairs={{0,6},{1,7},{2,4},{3,5},{4,2},{5,3},{6,0},{7,1},{8,14},{9,15},{10,... | collective-permute-start | bytes 393224 | tf_op jit(solution)/shard_map/ppermute | solution.py:138
  62.2 15.4 %collective-permute-start.9 = (bf16[32,2048]{1,0:T(8,128)(2,1)S(1)}, bf16[32,2048]{1,0:T(8,128)(2,1)S(1)}, u32[]{:S(2)}, u32[]{:S(2)}) collective-permute-start(bf16[32,2048]{1,0:T(8,128)(2,1)S(1)} %get-tuple-element.69), channel_id=1, source_target_pairs={{0,4},{1,5},{2,6},{3,7},{4,0},{5,1},{6,2},{7,3},{8,12},{9,13},{10,... | collective-permute-start | bytes 393224 | tf_op jit(solution)/shard_map/ppermute | solution.py:138
  63.6 8.6 %collective-permute-start.8 = (bf16[32,2048]{1,0:T(8,128)(2,1)S(1)}, bf16[32,2048]{1,0:T(8,128)(2,1)S(1)}, u32[]{:S(2)}, u32[]{:S(2)}) collective-permute-start(bf16[32,2048]{1,0:T(8,128)(2,1)S(1)} %get-tuple-element.70), channel_id=1, source_target_pairs={{0,2},{1,3},{2,0},{3,1},{4,6},{5,7},{6,4},{7,5},{8,10},{9,11},{10,... | collective-permute-start | bytes 393224 | tf_op jit(solution)/shard_map/ppermute | solution.py:138
  64.1 20.4 %collective-permute-start.16 = (bf16[32,2048]{1,0:T(8,128)(2,1)S(1)}, bf16[32,2048]{1,0:T(8,128)(2,1)S(1)}, u32[]{:S(2)}, u32[]{:S(2)}) collective-permute-start(bf16[32,2048]{1,0:T(8,128)(2,1)S(1)} %get-tuple-element.63), channel_id=1, source_target_pairs={{0,6},{1,7},{2,4},{3,5},{4,2},{5,3},{6,0},{7,1},{8,14},{9,15},{10,... | collective-permute-start | bytes 393224 | tf_op jit(solution)/shard_map/ppermute | solution.py:138
  65.9 18.5 %collective-permute-start.15 = (bf16[32,2048]{1,0:T(8,128)(2,1)S(1)}, bf16[32,2048]{1,0:T(8,128)(2,1)S(1)}, u32[]{:S(2)}, u32[]{:S(2)}) collective-permute-start(bf16[32,2048]{1,0:T(8,128)(2,1)S(1)} %get-tuple-element.64), channel_id=1, source_target_pairs={{0,4},{1,5},{2,6},{3,7},{4,0},{5,1},{6,2},{7,3},{8,12},{9,13},{10,... | collective-permute-start | bytes 393224 | tf_op jit(solution)/shard_map/ppermute | solution.py:138
  72.1 5.5 %copy-start = (bf16[1,32,2048]{2,1,0:T(8,128)(2,1)S(1)}, bf16[1,32,2048]{2,1,0:T(8,128)(2,1)}, u32[]{:S(2)}) copy-start(bf16[1,32,2048]{2,1,0:T(8,128)(2,1)} %param.8) | copy-start | bytes 393220
  72.1 12.3 %collective-permute-start.14 = (bf16[32,2048]{1,0:T(8,128)(2,1)S(1)}, bf16[32,2048]{1,0:T(8,128)(2,1)S(1)}, u32[]{:S(2)}, u32[]{:S(2)}) collective-permute-start(bf16[32,2048]{1,0:T(8,128)(2,1)S(1)} %get-tuple-element.65), channel_id=1, source_target_pairs={{0,2},{1,3},{2,0},{3,1},{4,6},{5,7},{6,4},{7,5},{8,10},{9,11},{10,... | collective-permute-start | bytes 393224 | tf_op jit(solution)/shard_map/ppermute | solution.py:138
  77.7 6.8 %copy-start.1 = (bf16[1,32,2048]{2,1,0:T(8,128)(2,1)S(1)}, bf16[1,32,2048]{2,1,0:T(8,128)(2,1)}, u32[]{:S(2)}) copy-start(bf16[1,32,2048]{2,1,0:T(8,128)(2,1)} %param.10) | copy-start | bytes 393220
  77.8 6.8 %collective-permute-start.13 = (bf16[32,2048]{1,0:T(8,128)(2,1)S(1)}, bf16[32,2048]{1,0:T(8,128)(2,1)S(1)}, u32[]{:S(2)}, u32[]{:S(2)}) collective-permute-start(bf16[32,2048]{1,0:T(8,128)(2,1)S(1)} %add_convert_fusion.1), channel_id=1, source_target_pairs={{0,8},{8,16},{16,24},{24,0},{1,9},{9,17},{17,25},{25,1},{2,10},{10... | collective-permute-start | bytes 393224 | tf_op jit(solution)/shard_map/ppermute | solution.py:21
  84.7 5.0 %collective-permute-start.17 = (bf16[32,2048]{1,0:T(8,128)(2,1)S(1)}, bf16[32,2048]{1,0:T(8,128)(2,1)S(1)}, u32[]{:S(2)}, u32[]{:S(2)}) collective-permute-start(bf16[32,2048]{1,0:T(8,128)(2,1)S(1)} %add_convert_fusion), channel_id=1, source_target_pairs={{0,24},{8,0},{16,8},{24,16},{1,25},{9,1},{17,9},{25,17},{2,26},{10... | collective-permute-start | bytes 393224 | tf_op jit(solution)/shard_map/ppermute | solution.py:21

commit v7 on v6

--- a/solution.py
+++ b/solution.py
@@ -244,44 +244,20 @@
 
 
 def expert_kernel(count, slots, devices, pair, place_ref, *refs):
-    picks_in, weights, blocks = refs[:6], refs[6 : 6 + WEIGHT_CUTS], refs[6 + WEIGHT_CUTS :][:devices]
+    fore_picks, fore_gates, fore_flip, back_picks, back_gates, back_flip = refs[:6]
+    weights, blocks = refs[6 : 6 + WEIGHT_CUTS], refs[6 + WEIGHT_CUTS :][:devices]
     groups = devices // pair
     outs = refs[6 + WEIGHT_CUTS + devices :][: 2 * groups + 2]
     inner, turned, *scratch = refs[8 + WEIGHT_CUTS + devices + 2 * groups :]
-    held, tokens = scratch[:6], scratch[6:9]
-    rows, fore_results, back_results, second, in_done, out_done = scratch[9:]
-    fore_picks, fore_gates, fore_flip, back_picks, back_gates, back_flip = held
-    size, (total, width) = blocks[0].shape[0], tokens[0].shape
+    tokens, (rows, fore_results, back_results, second) = scratch[:3], scratch[3:]
+    total, width = tokens[0].shape
     step = pl.program_id(0)
-
-    def home(code):
-        return pl.ds(pl.multiple_of(place_ref[3 + code], size), size)
 
     @pl.when(step == 0)
     def _():
-        arriving = [
-            pltpu.make_async_copy(source, target, in_done.at[3 * devices + place])
-            for place, (source, target) in enumerate(zip(picks_in, held))
-        ]
-        coming = [
-            [
-                pltpu.make_async_copy(
-                    block.at[:, pl.ds(place * width, width)],
-                    tokens[place].at[home(code), :],
-                    in_done.at[place * devices + code],
-                )
-                for code, block in enumerate(blocks)
-            ]
-            for place in range(3)
-        ]
-        for copy in arriving + coming[0] + coming[1] + coming[2]:
-            copy.start()
-        for copy in arriving:
-            copy.wait()
         taken = ((fore_picks, None), (back_picks, None), (back_picks, back_gates))
         for place, (picks, gates) in enumerate(taken):
-            for copy in coming[place]:
-                copy.wait()
+            assemble(place_ref, blocks, pl.ds(place * width, width), tokens[place])
             gather(count, slots, picks, gates, tokens[place], rows, place * slots, 3 * slots)
 
     mine = pl.ds(pl.multiple_of(step * slots, slots), slots)
@@ -303,17 +279,16 @@
     hidden_grads = (active_grads * sigma * (1.0 + hidden * (1.0 - sigma))).astype(jnp.bfloat16)
     inner[0, :slots, :] = hidden_grads
     inner[0, slots:, :] = (hidden * sigma).astype(jnp.bfloat16)
-    second[:slots, :] = (ahead * jax.nn.sigmoid(ahead)).astype(jnp.bfloat16)
+    gate = spread_gate(fore_gates, mine, ahead.shape[1])
+    second[:slots, :] = (ahead * jax.nn.sigmoid(ahead) * gate).astype(jnp.bfloat16)
     second[slots:, :] = hidden_grads
     for place, weight in enumerate(weights):
         columns = pl.ds(place * cut, cut)
         result = lax.dot_general(
             second[...], weight[0], (((1,), (1,)), ((), ())), preferred_element_type=jnp.float32
-        )
-        fore_results[mine, columns] = (result[:slots] * spread_gate(fore_gates, mine, cut)).astype(
-            fore_results.dtype
-        )
-        back_results[mine, columns] = result[slots:].astype(back_results.dtype)
+        ).astype(fore_results.dtype)
+        fore_results[mine, columns] = result[:slots]
+        back_results[mine, columns] = result[slots:]
 
     span = turned.shape[0]
     first = place_ref[0] * (width // pair) + step * span
@@ -323,42 +298,28 @@
 
     @pl.when(step == count - 1)
     def _():
-        leaving = []
         for lead, (flipped, results) in enumerate(
             ((fore_flip, fore_results), (back_flip, back_results))
         ):
             sums = tokens[lead]
             combine(flipped, results, sums)
             *near_outs, far_out = outs[lead * (groups + 1) : (lead + 1) * (groups + 1)]
-            targets = [(far_out.at[group], pair * group + 1) for group in range(groups)]
-            targets += [(out, pair * group) for group, out in enumerate(near_outs)]
-            for target, code in targets:
-                done = out_done.at[lead * devices + code]
-                leaving.append(pltpu.make_async_copy(sums.at[home(code), :], target, done))
-                leaving[-1].start()
-        for copy in leaving:
-            copy.wait()
+            size = far_out.shape[1]
+            for group, out in enumerate(near_outs):
+                near, far = (
+                    pl.ds(pl.multiple_of(place_ref[3 + pair * group + code], size), size)
+                    for code in range(pair)
+                )
+                out[...] = sums[near, :]
+                far_out[group] = sums[far, :]
 
 
 def weight_kernel(whose, first, number, count, slots, place_ref, *refs):
-    columns_in, inner_in, turned_in = refs[:3]
-    out_ref, columns, inner, turned, picks, rows, staged, in_done, out_done = refs[-9:]
+    columns, inner, turned = refs[:3]
+    out_ref, picks, rows, staged, out_done = refs[-5:]
     total, half = columns.shape[0], turned.shape[0]
     side = place_ref[0]
     owner = side if whose == 0 else 1 - side
-    arriving = [
-        pltpu.make_async_copy(columns_in, columns, in_done.at[0]),
-        pltpu.make_async_copy(
-            inner_in.at[pl.ds(first, number)], inner.at[:, pl.ds(0, 2 * slots), :], in_done.at[1]
-        ),
-        pltpu.make_async_copy(turned_in, turned, in_done.at[2]),
-    ]
-    for copy in arriving:
-        copy.start()
-    inner[:, pl.ds(2 * slots, LANES - 2 * slots), :] = jnp.zeros(
-        (number, LANES - 2 * slots, inner.shape[2]), inner.dtype
-    )
-    arriving[0].wait()
     lane = lax.broadcasted_iota(jnp.int32, (total, LANES), 1).astype(jnp.float32)
     is_saved = lax.broadcasted_iota(jnp.int32, (1, LANES), 1) < slots
     scales = []
@@ -375,8 +336,6 @@
         ).astype(picks.dtype)
         scale = jnp.sum(jnp.where(grads, gate, 0.0), axis=0, keepdims=True)
         scales.append(jnp.where(is_saved, 1.0, scale))
-    for copy in arriving[1:]:
-        copy.wait()
     for step in range(0, number, 2):
         lanes = pl.ds(step * LANES, 2 * LANES)
         scale = jnp.concatenate(scales[step : step + 2], axis=1)
@@ -389,8 +348,8 @@
         for start in range(0, half, CHUNK):
             chunk = pl.ds(start, CHUNK)
             staged[step, chunk, :] = jnp.dot(
-                rows[chunk, pl.ds(step * LANES, LANES)],
-                inner[step],
+                rows[chunk, pl.ds(step * LANES, 2 * slots)],
+                inner[first + step],
                 preferred_element_type=jnp.float32,
             ).astype(staged.dtype)
             leaving.append(
@@ -524,7 +483,9 @@
     far_part = jax.ShapeDtypeStruct((groups, token_count, width), jnp.bfloat16)
     inner = jax.ShapeDtypeStruct((count, 2 * slots, inner_width), jnp.bfloat16)
     turned = jax.ShapeDtypeStruct((half, 2 * total), jnp.bfloat16)
-    in_smem, anywhere = (pl.BlockSpec(memory_space=space) for space in (pltpu.SMEM, pl.ANY))
+    in_smem, in_vmem, anywhere = (
+        pl.BlockSpec(memory_space=space) for space in (pltpu.SMEM, pltpu.VMEM, pl.ANY)
+    )
     tokens = pltpu.VMEM((total, width), jnp.bfloat16)
     cut = width // WEIGHT_CUTS
     *parts, inner_own, tokens_turned = pl.pallas_call(
@@ -532,7 +493,7 @@
         grid_spec=pltpu.PrefetchScalarGridSpec(
             num_scalar_prefetch=1,
             grid=(count,),
-            in_specs=[anywhere] * 6
+            in_specs=[whole(array.shape) for array in pick_outs[:6]]
             + [
                 pl.BlockSpec(
                     (1, cut, inner_width),
@@ -540,21 +501,18 @@
                 )
                 for part in range(WEIGHT_CUTS)
             ]
-            + [anywhere] * devices,
-            out_specs=[anywhere] * (2 * groups + 2)
+            + [whole(packed.shape)] * devices,
+            out_specs=([whole(near_part.shape)] * groups + [whole(far_part.shape)]) * 2
             + [
                 pl.BlockSpec((1, 2 * slots, inner_width), lambda step, place: (step, 0, 0)),
                 pl.BlockSpec((half // count, 2 * total), lambda step, place: (step, 0)),
             ],
-            scratch_shapes=[pltpu.VMEM(array.shape, array.dtype) for array in pick_outs[:6]]
-            + [tokens] * 3
+            scratch_shapes=[tokens] * 3
             + [
                 pltpu.VMEM((3 * rows, width), jnp.bfloat16),
                 pltpu.VMEM((rows, width), jnp.bfloat16),
                 pltpu.VMEM((rows, width), jnp.bfloat16),
                 pltpu.VMEM((2 * slots, inner_width), jnp.bfloat16),
-                pltpu.SemaphoreType.DMA((3 * devices + 6,)),
-                pltpu.SemaphoreType.DMA((2 * devices,)),
             ],
         ),
         out_shape=([near_part] * groups + [far_part]) * 2 + [inner, turned],
@@ -575,17 +533,13 @@
         operands = [picks[6], inner_rows, tokens_turned] + earlier
         return pl.pallas_call(
             functools.partial(weight_kernel, whose, first, number, count, slots),
-            in_specs=[in_smem] + [anywhere] * len(operands),
+            in_specs=[in_smem, in_vmem, in_vmem, in_vmem] + [anywhere] * len(earlier),
             out_specs=anywhere,
             out_shape=jax.ShapeDtypeStruct((local_count, half, inner_width), jnp.bfloat16),
             scratch_shapes=[
-                pltpu.VMEM(columns.shape, columns.dtype),
-                pltpu.VMEM((number, LANES, inner_width), jnp.bfloat16),
-                pltpu.VMEM(turned.shape, turned.dtype),
                 pltpu.VMEM((2 * total, number * LANES), jnp.bfloat16),
                 pltpu.VMEM((half, number * LANES), jnp.bfloat16),
                 pltpu.VMEM((number, half, inner_width), jnp.bfloat16),
-                pltpu.SemaphoreType.DMA((3,)),
                 pltpu.SemaphoreType.DMA((number, half // CHUNK)),
             ],
             compiler_params=pltpu.CompilerParams(vmem_limit_bytes=VMEM_LIMIT),

time: 91.2 us -> 83.1 us (0.911)
  Pallas kernels: 49.4 us -> 40.9 us
    pallas_call x1, Pallas kernels: 27.5 us -> 20.7 us  [gathered_plan(): pl.pallas_call(functools.partial(expert_kernel, count, slots, devices, pa...]
    pallas_call x4, Pallas kernels: 19.6 us -> 17.9 us  [gradient(): pl.pallas_call(functools.partial(weight_kernel, whose, first, number, cou...]
  transfers between devices with their start and end apart: 18 -> 18, of which waited for: 7 -> 7; matrix products, arithmetic and copies ran while one was open for 0% -> 1% of each run, Pallas kernels for 22% -> 22%
where the time goes in v7:
time: 83.1 us; the launch traced here: 82.9 us
  Pallas kernels  40.9 us (49%)
  waiting for transfers between devices  22.7 us (27%)
  starting transfers between devices  16.6 us (20%)
  local copies, waits for them, and re-layouts  1.41 us (2%)
    pallas_call x1, Pallas kernels, gathered_plan(): pl.pallas_call(functools.partial(expert_kernel, count, slots, devices, pa...  20.7 us
    ppermute x16, waiting for transfers between devices, swapped(): lax.ppermute(value, axes, [(source, source ^ code) for source in range(co...  19.2 us
    pallas_call x4, Pallas kernels, gradient(): pl.pallas_call(functools.partial(weight_kernel, whose, first, number, cou...  17.9 us
    ppermute x16, starting transfers between devices, swapped(): lax.ppermute(value, axes, [(source, source ^ code) for source in range(co...  12.8 us
    ppermute x2, starting transfers between devices, shifted(): return lax.ppermute(value, axis, pairs)  3.89 us
    ppermute x2, waiting for transfers between devices, shifted(): return lax.ppermute(value, axis, pairs)  3.45 us
  transfers between devices with their start and end apart: 18, of which 7 were waited for; matrix products, arithmetic and copies ran while one was open for 1% of the time, Pallas kernels for 22%

profile of v7, /device:TPU:0, one launch (start us, length us, event | category | flops | bytes accessed | tf_op | source)
XLA Modules:
  0.0 82.9 jit_solution(11646926368362635232)
XLA Ops:
  0.6 1.2 %pack.1.refs_0_.refs_10_ = bf16[32,6272]{1,0:T(8,128)(2,1)S(1)} custom-call(bf16[32,2048]{1,0:T(8,128)(2,1)} %bitcast.61, bf16[32,2048]{1,0:T(8,128)(2,1)} %bitcast.63, bf16[32,2048]{1,0:T(8,128)(2,1)} %bitcast.62, s32[8,32]{1,0:T(8,128)} %bitcast.66, f32[8,32]{1,0:T(8,128)} %bitcast.67, s32[8,32]{1,0:T(8,128)} %bitcast.68, f32[8,32]{1,0:T(8,128)} %bitcast.69), custom_call_target="tpu_custom_call" | custom-call | tf_op jit(solution)/shard_map/pack/pallas_call | solution.py:434
  1.8 4.0 %collective-permute-start.5 = (bf16[32,6272]{1,0:T(8,128)(2,1)S(1)}, bf16[32,6272]{1,0:T(8,128)(2,1)S(1)}, u32[]{:S(2)}, u32[]{:S(2)}) collective-permute-start(bf16[32,6272]{1,0:T(8,128)(2,1)S(1)} %pack.1.refs_0_.refs_10_), channel_id=1, source_target_pairs={{0,6},{1,7},{2,4},{3,5},{4,2},{5,3},{6,0},{7,1},{8,14},{9,15},{10,... | collective-permute-start | bytes 1204232 | tf_op jit(solution)/shard_map/ppermute | solution.py:138
  5.8 0.5 collective-permute-start.3
  6.3 0.1 collective-permute-start.1
  6.4 0.0 collective-permute-start
  6.4 9.5 %collective-permute-done.5.refs_6_.refs_16_ = bf16[32,6272]{1,0:T(8,128)(2,1)S(1)} collective-permute-done((bf16[32,6272]{1,0:T(8,128)(2,1)S(1)}, bf16[32,6272]{1,0:T(8,128)(2,1)S(1)}, u32[]{:S(2)}, u32[]{:S(2)}) %collective-permute-start.5) | collective-permute-done | bytes 401440 | tf_op jit(solution)/shard_map/ppermute | solution.py:138
  15.9 0.0 collective-permute-start.6
  16.0 7.7 %collective-permute-done.3.refs_4_.refs_14_ = bf16[32,6272]{1,0:T(8,128)(2,1)S(1)} collective-permute-done((bf16[32,6272]{1,0:T(8,128)(2,1)S(1)}, bf16[32,6272]{1,0:T(8,128)(2,1)S(1)}, u32[]{:S(2)}, u32[]{:S(2)}) %collective-permute-start.3) | collective-permute-done | bytes 401440 | tf_op jit(solution)/shard_map/ppermute | solution.py:138
  23.7 0.0 collective-permute-start.4
  23.7 0.3 collective-permute-done.1.refs_2_.refs_12_
  24.0 0.2 collective-permute-start.2
  24.2 0.1 stack.47.place_ref
  24.3 0.0 collective-permute-done.refs_1_.refs_11_
  24.3 0.0 collective-permute-done.6.refs_7_.refs_17_
  24.3 1.1 %collective-permute-done.4.refs_5_.refs_15_ = bf16[32,6272]{1,0:T(8,128)(2,1)S(1)} collective-permute-done((bf16[32,6272]{1,0:T(8,128)(2,1)S(1)}, bf16[32,6272]{1,0:T(8,128)(2,1)S(1)}, u32[]{:S(2)}, u32[]{:S(2)}) %collective-permute-start.4) | collective-permute-done | bytes 401440 | tf_op jit(solution)/shard_map/ppermute | solution.py:138
  25.4 0.6 collective-permute-done.2.refs_3_.refs_13_
  26.0 1.1 %slot_picks.1 = (bf16[384,256]{1,0:T(8,128)(2,1)S(1)}, f32[384,128]{1,0:T(8,128)S(1)}, bf16[256,384]{1,0:T(8,128)(2,1)S(1)}, bf16[384,256]{1,0:T(8,128)(2,1)S(1)...) custom-call(s32[11]{0:T(128)S(1)} %stack.47.place_ref, ...), custom_call_target="tpu_custom_call" | custom-call | bytes 1024 | tf_op jit(solution)/shard_map/slot_picks/pallas_call | solution.py:471
  27.1 20.7 %experts.1 = (bf16[32,2048]{1,0:T(8,128)(2,1)S(1)}, bf16[32,2048]{1,0:T(8,128)(2,1)S(1)}, bf16[32,2048]{1,0:T(8,128)(2,1)S(1)}, bf16[32,2048]{1,0:T(8,128)(2,1)S...) custom-call(s32[11]{0:T(128)S(1)} %stack.47.place_ref, ...), custom_call_target="tpu_custom_call" | custom-call | flops 12884901888 | bytes 25165824 | tf_op jit(solution)/shard_map/experts/pallas_call | solution.py:491
  47.9 0.2 collective-permute-start.11
  48.1 0.4 collective-permute-start.7
  48.4 0.1 collective-permute-start.12
  48.6 4.5 %weight_gradient_0_0.1.refs_3_ = bf16[16,1024,768]{2,1,0:T(8,128)(2,1)} custom-call(s32[11]{0:T(128)S(1)} %stack.47.place_ref, f32[256,128]{1,0:T(8,128)S(1)} %get-tuple-element.41.refs_0_, bf16[8,96,768]{2,1,0:T(8,128)(2,1)S(1)} %get-tuple-element.42.refs_1_, bf16[1024,512]{1,0:T(8,128)(2,1)S(1)} %get-tuple-element.43.refs_2_), custom_call_target="tpu_custom_call" | custom-call | flops 3221225472 | bytes 12582912 | tf_op jit(solution)/shard_map/weight_gradient_0_0/pallas_call | solution.py:534
  53.1 0.0 collective-permute-done.7
  53.1 0.1 fusion.7
  53.2 1.9 %collective-permute-start.10 = (bf16[32,2048]{1,0:T(8,128)(2,1)S(1)}, bf16[32,2048]{1,0:T(8,128)(2,1)S(1)}, u32[]{:S(2)}, u32[]{:S(2)}) collective-permute-start(bf16[32,2048]{1,0:T(8,128)(2,1)S(1)} %get-tuple-element.68), channel_id=1, source_target_pairs={{0,6},{1,7},{2,4},{3,5},{4,2},{5,3},{6,0},{7,1},{8,14},{9,15},{10,... | collective-permute-start | bytes 393224 | tf_op jit(solution)/shard_map/ppermute | solution.py:138
  55.1 1.3 %collective-permute-start.9 = (bf16[32,2048]{1,0:T(8,128)(2,1)S(1)}, bf16[32,2048]{1,0:T(8,128)(2,1)S(1)}, u32[]{:S(2)}, u32[]{:S(2)}) collective-permute-start(bf16[32,2048]{1,0:T(8,128)(2,1)S(1)} %get-tuple-element.69), channel_id=1, source_target_pairs={{0,4},{1,5},{2,6},{3,7},{4,0},{5,1},{6,2},{7,3},{8,12},{9,13},{10,... | collective-permute-start | bytes 393224 | tf_op jit(solution)/shard_map/ppermute | solution.py:138
  56.4 0.3 collective-permute-start.8
  56.8 0.0 collective-permute-done.12
  56.8 0.0 collective-permute-done.11.refs_1_
  56.8 0.1 fusion
  56.9 1.9 %collective-permute-start.16 = (bf16[32,2048]{1,0:T(8,128)(2,1)S(1)}, bf16[32,2048]{1,0:T(8,128)(2,1)S(1)}, u32[]{:S(2)}, u32[]{:S(2)}) collective-permute-start(bf16[32,2048]{1,0:T(8,128)(2,1)S(1)} %get-tuple-element.63), channel_id=1, source_target_pairs={{0,6},{1,7},{2,4},{3,5},{4,2},{5,3},{6,0},{7,1},{8,14},{9,15},{10,... | collective-permute-start | bytes 393224 | tf_op jit(solution)/shard_map/ppermute | solution.py:138
  58.8 1.3 %collective-permute-start.15 = (bf16[32,2048]{1,0:T(8,128)(2,1)S(1)}, bf16[32,2048]{1,0:T(8,128)(2,1)S(1)}, u32[]{:S(2)}, u32[]{:S(2)}) collective-permute-start(bf16[32,2048]{1,0:T(8,128)(2,1)S(1)} %get-tuple-element.64), channel_id=1, source_target_pairs={{0,4},{1,5},{2,6},{3,7},{4,0},{5,1},{6,2},{7,3},{8,12},{9,13},{10,... | collective-permute-start | bytes 393224 | tf_op jit(solution)/shard_map/ppermute | solution.py:138
  60.1 4.5 %weight_gradient_0_4.1.refs_3_ = bf16[16,1024,768]{2,1,0:T(8,128)(2,1)} custom-call(s32[11]{0:T(128)S(1)} %stack.47.place_ref, f32[256,128]{1,0:T(8,128)S(1)} %get-tuple-element.41.refs_0_, bf16[8,96,768]{2,1,0:T(8,128)(2,1)S(1)} %get-tuple-element.42.refs_1_, bf16[1024,512]{1,0:T(8,128)(2,1)S(1)} %get-tuple-element.43.refs_2_, ...), custom_call_target="tpu_custom_call", output_to_operand_aliasing={{}: (4, {})} | custom-call | flops 3221225472 | bytes 12582912 | tf_op jit(solution)/shard_map/weight_gradient_0_4/pallas_call | solution.py:534
  64.6 0.0 copy-start
  64.6 0.0 collective-permute-done.8
  64.6 0.4 collective-permute-start.14
  65.0 4.5 %weight_gradient_1_0.1.refs_3_ = bf16[16,1024,768]{2,1,0:T(8,128)(2,1)} custom-call(s32[11]{0:T(128)S(1)} %stack.47.place_ref, f32[256,128]{1,0:T(8,128)S(1)} %get-tuple-element.41.refs_0_, bf16[8,96,768]{2,1,0:T(8,128)(2,1)S(1)} %collective-permute-done.11.refs_1_, bf16[1024,512]{1,0:T(8,128)(2,1)S(1)} %get-tuple-element.43.refs_2_, ...), custom_call_target="tpu_custom_call", output_to_operand_aliasing={{}: (4, {})} | custom-call | flops 3221225472 | bytes 12582912 | tf_op jit(solution)/shard_map/weight_gradient_1_0/pallas_call | solution.py:534
  69.5 0.0 collective-permute-done.10
  69.5 0.0 collective-permute-done.9
  69.5 0.0 copy-done
  69.5 0.1 add_convert_fusion.1
  69.6 0.0 copy-start.1
  69.7 1.8 %collective-permute-start.13 = (bf16[32,2048]{1,0:T(8,128)(2,1)S(1)}, bf16[32,2048]{1,0:T(8,128)(2,1)S(1)}, u32[]{:S(2)}, u32[]{:S(2)}) collective-permute-start(bf16[32,2048]{1,0:T(8,128)(2,1)S(1)} %add_convert_fusion.1), channel_id=1, source_target_pairs={{0,8},{8,16},{16,24},{24,0},{1,9},{9,17},{17,25},{25,1},{2,10},{10... | collective-permute-start | bytes 393224 | tf_op jit(solution)/shard_map/ppermute | solution.py:21
  71.5 4.5 %weight_gradient_1_4.1 = bf16[16,1024,768]{2,1,0:T(8,128)(2,1)} custom-call(s32[11]{0:T(128)S(1)} %stack.47.place_ref, f32[256,128]{1,0:T(8,128)S(1)} %get-tuple-element.41.refs_0_, bf16[8,96,768]{2,1,0:T(8,128)(2,1)S(1)} %collective-permute-done.11.refs_1_, bf16[1024,512]{1,0:T(8,128)(2,1)S(1)} %get-tuple-element.43.refs_2_, ...), custom_call_target="tpu_custom_call", output_to_operand_aliasing={{}: (4, {})} | custom-call | flops 3221225472 | bytes 12582912 | tf_op jit(solution)/shard_map/weight_gradient_1_4/pallas_call | solution.py:534
  76.0 0.0 collective-permute-done.16
  76.0 0.0 collective-permute-done.15
  76.0 0.0 collective-permute-done.14
  76.0 0.5 collective-permute-done.13
  76.5 0.0 copy-done.1
  76.5 0.1 add_convert_fusion
  76.6 2.1 %collective-permute-start.17 = (bf16[32,2048]{1,0:T(8,128)(2,1)S(1)}, bf16[32,2048]{1,0:T(8,128)(2,1)S(1)}, u32[]{:S(2)}, u32[]{:S(2)}) collective-permute-start(bf16[32,2048]{1,0:T(8,128)(2,1)S(1)} %add_convert_fusion), channel_id=1, source_target_pairs={{0,24},{8,0},{16,8},{24,16},{1,25},{9,1},{17,9},{25,17},{2,26},{10... | collective-permute-start | bytes 393224 | tf_op jit(solution)/shard_map/ppermute | solution.py:21
  78.6 3.0 %collective-permute-done.17 = bf16[32,2048]{1,0:T(8,128)(2,1)S(1)} collective-permute-done((bf16[32,2048]{1,0:T(8,128)(2,1)S(1)}, bf16[32,2048]{1,0:T(8,128)(2,1)S(1)}, u32[]{:S(2)}, u32[]{:S(2)}) %collective-permute-start.17) | collective-permute-done | bytes 131104 | tf_op jit(solution)/shard_map/ppermute | solution.py:21
  81.6 0.7 copy.19
  82.2 0.7 copy.20
Async XLA Ops:
  1.8 14.1 %collective-permute-start.5 = (bf16[32,6272]{1,0:T(8,128)(2,1)S(1)}, bf16[32,6272]{1,0:T(8,128)(2,1)S(1)}, u32[]{:S(2)}, u32[]{:S(2)}) collective-permute-start(bf16[32,6272]{1,0:T(8,128)(2,1)S(1)} %pack.1.refs_0_.refs_10_), channel_id=1, source_target_pairs={{0,6},{1,7},{2,4},{3,5},{4,2},{5,3},{6,0},{7,1},{8,14},{9,15},{10,... | collective-permute-start | bytes 1204232 | tf_op jit(solution)/shard_map/ppermute | solution.py:138
  5.8 17.9 %collective-permute-start.3 = (bf16[32,6272]{1,0:T(8,128)(2,1)S(1)}, bf16[32,6272]{1,0:T(8,128)(2,1)S(1)}, u32[]{:S(2)}, u32[]{:S(2)}) collective-permute-start(bf16[32,6272]{1,0:T(8,128)(2,1)S(1)} %pack.1.refs_0_.refs_10_), channel_id=1, source_target_pairs={{0,4},{1,5},{2,6},{3,7},{4,0},{5,1},{6,2},{7,3},{8,12},{9,13},{10,... | collective-permute-start | bytes 1204232 | tf_op jit(solution)/shard_map/ppermute | solution.py:138
  6.3 17.7 %collective-permute-start.1 = (bf16[32,6272]{1,0:T(8,128)(2,1)S(1)}, bf16[32,6272]{1,0:T(8,128)(2,1)S(1)}, u32[]{:S(2)}, u32[]{:S(2)}) collective-permute-start(bf16[32,6272]{1,0:T(8,128)(2,1)S(1)} %pack.1.refs_0_.refs_10_), channel_id=1, source_target_pairs={{0,2},{1,3},{2,0},{3,1},{4,6},{5,7},{6,4},{7,5},{8,10},{9,11},{10,... | collective-permute-start | bytes 1204232 | tf_op jit(solution)/shard_map/ppermute | solution.py:138
  6.4 17.9 %collective-permute-start = (bf16[32,6272]{1,0:T(8,128)(2,1)S(1)}, bf16[32,6272]{1,0:T(8,128)(2,1)S(1)}, u32[]{:S(2)}, u32[]{:S(2)}) collective-permute-start(bf16[32,6272]{1,0:T(8,128)(2,1)S(1)} %pack.1.refs_0_.refs_10_), channel_id=1, source_target_pairs={{0,1},{1,0},{2,3},{3,2},{4,5},{5,4},{6,7},{7,6},{8,9},{9,8},{10,11... | collective-permute-start | bytes 1204232 | tf_op jit(solution)/shard_map/ppermute | solution.py:138
  15.9 8.3 %collective-permute-start.6 = (bf16[32,6272]{1,0:T(8,128)(2,1)S(1)}, bf16[32,6272]{1,0:T(8,128)(2,1)S(1)}, u32[]{:S(2)}, u32[]{:S(2)}) collective-permute-start(bf16[32,6272]{1,0:T(8,128)(2,1)S(1)} %collective-permute-done.5.refs_6_.refs_16_), channel_id=1, source_target_pairs={{0,1},{1,0},{2,3},{3,2},{4,5},{5,4},{6,7},{7,6},{8,9},{9,8},{10,11... | collective-permute-start | bytes 1204232 | tf_op jit(solution)/shard_map/ppermute | solution.py:138
  23.7 1.7 %collective-permute-start.4 = (bf16[32,6272]{1,0:T(8,128)(2,1)S(1)}, bf16[32,6272]{1,0:T(8,128)(2,1)S(1)}, u32[]{:S(2)}, u32[]{:S(2)}) collective-permute-start(bf16[32,6272]{1,0:T(8,128)(2,1)S(1)} %collective-permute-done.3.refs_4_.refs_14_), channel_id=1, source_target_pairs={{0,1},{1,0},{2,3},{3,2},{4,5},{5,4},{6,7},{7,6},{8,9},{9,8},{10,11... | collective-permute-start | bytes 1204232 | tf_op jit(solution)/shard_map/ppermute | solution.py:138
  24.0 2.0 %collective-permute-start.2 = (bf16[32,6272]{1,0:T(8,128)(2,1)S(1)}, bf16[32,6272]{1,0:T(8,128)(2,1)S(1)}, u32[]{:S(2)}, u32[]{:S(2)}) collective-permute-start(bf16[32,6272]{1,0:T(8,128)(2,1)S(1)} %collective-permute-done.1.refs_2_.refs_12_), channel_id=1, source_target_pairs={{0,1},{1,0},{2,3},{3,2},{4,5},{5,4},{6,7},{7,6},{8,9},{9,8},{10,11... | collective-permute-start | bytes 1204232 | tf_op jit(solution)/shard_map/ppermute | solution.py:138
  47.9 8.9 %collective-permute-start.11 = (bf16[8,96,768]{2,1,0:T(8,128)(2,1)S(1)}, bf16[8,96,768]{2,1,0:T(8,128)(2,1)S(1)}, u32[]{:S(2)}, u32[]{:S(2)}) collective-permute-start(bf16[8,96,768]{2,1,0:T(8,128)(2,1)S(1)} %get-tuple-element.42.refs_1_), channel_id=1, source_target_pairs={{0,1},{1,0},{2,3},{3,2},{4,5},{5,4},{6,7},{7,6},{8,9},{9,8},{10,11... | collective-permute-start | bytes 3538952 | tf_op jit(solution)/shard_map/ppermute | solution.py:138
  48.1 5.0 %collective-permute-start.7 = (bf16[4,32,2048]{2,1,0:T(8,128)(2,1)S(1)}, bf16[4,32,2048]{2,1,0:T(8,128)(2,1)S(1)}, u32[]{:S(2)}, u32[]{:S(2)}) collective-permute-start(bf16[4,32,2048]{2,1,0:T(8,128)(2,1)S(1)} %get-tuple-element.40), channel_id=1, source_target_pairs={{0,1},{1,0},{2,3},{3,2},{4,5},{5,4},{6,7},{7,6},{8,9},{9,8},{10,11... | collective-permute-start | bytes 1572872 | tf_op jit(solution)/shard_map/ppermute | solution.py:138
  48.4 8.3 %collective-permute-start.12 = (bf16[4,32,2048]{2,1,0:T(8,128)(2,1)S(1)}, bf16[4,32,2048]{2,1,0:T(8,128)(2,1)S(1)}, u32[]{:S(2)}, u32[]{:S(2)}) collective-permute-start(bf16[4,32,2048]{2,1,0:T(8,128)(2,1)S(1)} %get-tuple-element.49), channel_id=1, source_target_pairs={{0,1},{1,0},{2,3},{3,2},{4,5},{5,4},{6,7},{7,6},{8,9},{9,8},{10,11... | collective-permute-start | bytes 1572872 | tf_op jit(solution)/shard_map/ppermute | solution.py:138
  53.2 16.3 %collective-permute-start.10 = (bf16[32,2048]{1,0:T(8,128)(2,1)S(1)}, bf16[32,2048]{1,0:T(8,128)(2,1)S(1)}, u32[]{:S(2)}, u32[]{:S(2)}) collective-permute-start(bf16[32,2048]{1,0:T(8,128)(2,1)S(1)} %get-tuple-element.68), channel_id=1, source_target_pairs={{0,6},{1,7},{2,4},{3,5},{4,2},{5,3},{6,0},{7,1},{8,14},{9,15},{10,... | collective-permute-start | bytes 393224 | tf_op jit(solution)/shard_map/ppermute | solution.py:138
  55.1 14.4 %collective-permute-start.9 = (bf16[32,2048]{1,0:T(8,128)(2,1)S(1)}, bf16[32,2048]{1,0:T(8,128)(2,1)S(1)}, u32[]{:S(2)}, u32[]{:S(2)}) collective-permute-start(bf16[32,2048]{1,0:T(8,128)(2,1)S(1)} %get-tuple-element.69), channel_id=1, source_target_pairs={{0,4},{1,5},{2,6},{3,7},{4,0},{5,1},{6,2},{7,3},{8,12},{9,13},{10,... | collective-permute-start | bytes 393224 | tf_op jit(solution)/shard_map/ppermute | solution.py:138
  56.4 8.2 %collective-permute-start.8 = (bf16[32,2048]{1,0:T(8,128)(2,1)S(1)}, bf16[32,2048]{1,0:T(8,128)(2,1)S(1)}, u32[]{:S(2)}, u32[]{:S(2)}) collective-permute-start(bf16[32,2048]{1,0:T(8,128)(2,1)S(1)} %get-tuple-element.70), channel_id=1, source_target_pairs={{0,2},{1,3},{2,0},{3,1},{4,6},{5,7},{6,4},{7,5},{8,10},{9,11},{10,... | collective-permute-start | bytes 393224 | tf_op jit(solution)/shard_map/ppermute | solution.py:138
  56.9 19.0 %collective-permute-start.16 = (bf16[32,2048]{1,0:T(8,128)(2,1)S(1)}, bf16[32,2048]{1,0:T(8,128)(2,1)S(1)}, u32[]{:S(2)}, u32[]{:S(2)}) collective-permute-start(bf16[32,2048]{1,0:T(8,128)(2,1)S(1)} %get-tuple-element.63), channel_id=1, source_target_pairs={{0,6},{1,7},{2,4},{3,5},{4,2},{5,3},{6,0},{7,1},{8,14},{9,15},{10,... | collective-permute-start | bytes 393224 | tf_op jit(solution)/shard_map/ppermute | solution.py:138
  58.8 17.2 %collective-permute-start.15 = (bf16[32,2048]{1,0:T(8,128)(2,1)S(1)}, bf16[32,2048]{1,0:T(8,128)(2,1)S(1)}, u32[]{:S(2)}, u32[]{:S(2)}) collective-permute-start(bf16[32,2048]{1,0:T(8,128)(2,1)S(1)} %get-tuple-element.64), channel_id=1, source_target_pairs={{0,4},{1,5},{2,6},{3,7},{4,0},{5,1},{6,2},{7,3},{8,12},{9,13},{10,... | collective-permute-start | bytes 393224 | tf_op jit(solution)/shard_map/ppermute | solution.py:138
  64.6 4.9 %copy-start = (bf16[1,32,2048]{2,1,0:T(8,128)(2,1)S(1)}, bf16[1,32,2048]{2,1,0:T(8,128)(2,1)}, u32[]{:S(2)}) copy-start(bf16[1,32,2048]{2,1,0:T(8,128)(2,1)} %param.8) | copy-start | bytes 393220
  64.6 11.4 %collective-permute-start.14 = (bf16[32,2048]{1,0:T(8,128)(2,1)S(1)}, bf16[32,2048]{1,0:T(8,128)(2,1)S(1)}, u32[]{:S(2)}, u32[]{:S(2)}) collective-permute-start(bf16[32,2048]{1,0:T(8,128)(2,1)S(1)} %get-tuple-element.65), channel_id=1, source_target_pairs={{0,2},{1,3},{2,0},{3,1},{4,6},{5,7},{6,4},{7,5},{8,10},{9,11},{10,... | collective-permute-start | bytes 393224 | tf_op jit(solution)/shard_map/ppermute | solution.py:138
  69.6 6.8 %copy-start.1 = (bf16[1,32,2048]{2,1,0:T(8,128)(2,1)S(1)}, bf16[1,32,2048]{2,1,0:T(8,128)(2,1)}, u32[]{:S(2)}) copy-start(bf16[1,32,2048]{2,1,0:T(8,128)(2,1)} %param.10) | copy-start | bytes 393220
  69.7 6.8 %collective-permute-start.13 = (bf16[32,2048]{1,0:T(8,128)(2,1)S(1)}, bf16[32,2048]{1,0:T(8,128)(2,1)S(1)}, u32[]{:S(2)}, u32[]{:S(2)}) collective-permute-start(bf16[32,2048]{1,0:T(8,128)(2,1)S(1)} %add_convert_fusion.1), channel_id=1, source_target_pairs={{0,8},{8,16},{16,24},{24,0},{1,9},{9,17},{17,25},{25,1},{2,10},{10... | collective-permute-start | bytes 393224 | tf_op jit(solution)/shard_map/ppermute | solution.py:21
  76.6 5.0 %collective-permute-start.17 = (bf16[32,2048]{1,0:T(8,128)(2,1)S(1)}, bf16[32,2048]{1,0:T(8,128)(2,1)S(1)}, u32[]{:S(2)}, u32[]{:S(2)}) collective-permute-start(bf16[32,2048]{1,0:T(8,128)(2,1)S(1)} %add_convert_fusion), channel_id=1, source_target_pairs={{0,24},{8,0},{16,8},{24,16},{1,25},{9,1},{17,9},{25,17},{2,26},{10... | collective-permute-start | bytes 393224 | tf_op jit(solution)/shard_map/ppermute | solution.py:21

commit v8 on v7

--- a/solution.py
+++ b/solution.py
@@ -263,29 +263,38 @@
     mine = pl.ds(pl.multiple_of(step * slots, slots), slots)
     three = pl.ds(pl.multiple_of(step * 3 * slots, 3 * slots), 3 * slots)
     cut = width // WEIGHT_CUTS
-    product = functools.reduce(
-        jnp.add,
-        [
-            jnp.dot(
-                rows[three, pl.ds(place * cut, cut)],
-                weight[0],
-                preferred_element_type=jnp.float32,
-            )
-            for place, weight in enumerate(weights)
-        ],
-    )
-    ahead, hidden, active_grads = product[:slots], product[slots : 2 * slots], product[2 * slots :]
-    sigma = jax.nn.sigmoid(hidden)
-    hidden_grads = (active_grads * sigma * (1.0 + hidden * (1.0 - sigma))).astype(jnp.bfloat16)
-    inner[0, :slots, :] = hidden_grads
-    inner[0, slots:, :] = (hidden * sigma).astype(jnp.bfloat16)
-    gate = spread_gate(fore_gates, mine, ahead.shape[1])
-    second[:slots, :] = (ahead * jax.nn.sigmoid(ahead) * gate).astype(jnp.bfloat16)
-    second[slots:, :] = hidden_grads
-    for place, weight in enumerate(weights):
-        columns = pl.ds(place * cut, cut)
+    for start in range(0, inner.shape[2], CHUNK):
+        lanes = pl.ds(start, CHUNK)
+        product = functools.reduce(
+            jnp.add,
+            [
+                jnp.dot(
+                    rows[three, pl.ds(place * cut, cut)],
+                    weight[0, :, lanes],
+                    preferred_element_type=jnp.float32,
+                )
+                for place, weight in enumerate(weights)
+            ],
+        )
+        ahead, hidden, active_grads = (
+            product[:slots],
+            product[slots : 2 * slots],
+            product[2 * slots :],
+        )
+        sigma = jax.nn.sigmoid(hidden)
+        hidden_grads = (active_grads * sigma * (1.0 + hidden * (1.0 - sigma))).astype(jnp.bfloat16)
+        inner[0, :slots, lanes] = hidden_grads
+        inner[0, slots:, lanes] = (hidden * sigma).astype(jnp.bfloat16)
+        gate = spread_gate(fore_gates, mine, CHUNK)
+        second[:slots, lanes] = (ahead * jax.nn.sigmoid(ahead) * gate).astype(jnp.bfloat16)
+        second[slots:, lanes] = hidden_grads
+    for start in range(0, width, CHUNK):
+        columns = pl.ds(start, CHUNK)
         result = lax.dot_general(
-            second[...], weight[0], (((1,), (1,)), ((), ())), preferred_element_type=jnp.float32
+            second[...],
+            weights[start // cut][0, pl.ds(start % cut, CHUNK), :],
+            (((1,), (1,)), ((), ())),
+            preferred_element_type=jnp.float32,
         ).astype(fore_results.dtype)
         fore_results[mine, columns] = result[:slots]
         back_results[mine, columns] = result[slots:]
@@ -347,11 +356,14 @@
     for step in range(number):
         for start in range(0, half, CHUNK):
             chunk = pl.ds(start, CHUNK)
-            staged[step, chunk, :] = jnp.dot(
-                rows[chunk, pl.ds(step * LANES, 2 * slots)],
-                inner[first + step],
-                preferred_element_type=jnp.float32,
-            ).astype(staged.dtype)
+            for corner in range(start, start + CHUNK, LANES):
+                for column in range(0, inner.shape[2], CHUNK):
+                    tile = (step, pl.ds(corner, LANES), pl.ds(column, CHUNK))
+                    staged[tile] = jnp.dot(
+                        rows[tile[1], pl.ds(step * LANES, 2 * slots)],
+                        inner[first + step, :, tile[2]],
+                        preferred_element_type=jnp.float32,
+                    ).astype(staged.dtype)
             leaving.append(
                 pltpu.make_async_copy(
                     staged.at[step, chunk, :],

time: 83.1 us -> 82.8 us (level)
  no operation moved by 1% of the time
where the time goes in v8:
time: 82.8 us; the launch traced here: 82.6 us
  Pallas kernels  40.6 us (49%)
  waiting for transfers between devices  22.7 us (27%)
  starting transfers between devices  16.6 us (20%)
  local copies, waits for them, and re-layouts  1.41 us (2%)
    pallas_call x1, Pallas kernels, gathered_plan(): pl.pallas_call(functools.partial(expert_kernel, count, slots, devices, pa...  20.5 us
    ppermute x16, waiting for transfers between devices, swapped(): lax.ppermute(value, axes, [(source, source ^ code) for source in range(co...  19.2 us
    pallas_call x4, Pallas kernels, gradient(): pl.pallas_call(functools.partial(weight_kernel, whose, first, number, cou...  17.8 us
    ppermute x16, starting transfers between devices, swapped(): lax.ppermute(value, axes, [(source, source ^ code) for source in range(co...  12.8 us
    ppermute x2, starting transfers between devices, shifted(): return lax.ppermute(value, axis, pairs)  3.86 us
    ppermute x2, waiting for transfers between devices, shifted(): return lax.ppermute(value, axis, pairs)  3.49 us
  transfers between devices with their start and end apart: 18, of which 7 were waited for; matrix products, arithmetic and copies ran while one was open for 1% of the time, Pallas kernels for 22%

profile of v8, /device:TPU:0, one launch (start us, length us, event | category | flops | bytes accessed | tf_op | source)
XLA Modules:
  0.0 82.6 jit_solution(17185812972403101838)
XLA Ops:
  0.6 1.2 %pack.1.refs_0_.refs_10_ = bf16[32,6272]{1,0:T(8,128)(2,1)S(1)} custom-call(bf16[32,2048]{1,0:T(8,128)(2,1)} %bitcast.61, bf16[32,2048]{1,0:T(8,128)(2,1)} %bitcast.63, bf16[32,2048]{1,0:T(8,128)(2,1)} %bitcast.62, s32[8,32]{1,0:T(8,128)} %bitcast.66, f32[8,32]{1,0:T(8,128)} %bitcast.67, s32[8,32]{1,0:T(8,128)} %bitcast.68, f32[8,32]{1,0:T(8,128)} %bitcast.69), custom_call_target="tpu_custom_call" | custom-call | tf_op jit(solution)/shard_map/pack/pallas_call | solution.py:446
  1.8 4.0 %collective-permute-start.5 = (bf16[32,6272]{1,0:T(8,128)(2,1)S(1)}, bf16[32,6272]{1,0:T(8,128)(2,1)S(1)}, u32[]{:S(2)}, u32[]{:S(2)}) collective-permute-start(bf16[32,6272]{1,0:T(8,128)(2,1)S(1)} %pack.1.refs_0_.refs_10_), channel_id=1, source_target_pairs={{0,6},{1,7},{2,4},{3,5},{4,2},{5,3},{6,0},{7,1},{8,14},{9,15},{10,... | collective-permute-start | bytes 1204232 | tf_op jit(solution)/shard_map/ppermute | solution.py:138
  5.8 0.5 collective-permute-start.3
  6.3 0.1 collective-permute-start.1
  6.4 0.0 collective-permute-start
  6.4 9.5 %collective-permute-done.5.refs_6_.refs_16_ = bf16[32,6272]{1,0:T(8,128)(2,1)S(1)} collective-permute-done((bf16[32,6272]{1,0:T(8,128)(2,1)S(1)}, bf16[32,6272]{1,0:T(8,128)(2,1)S(1)}, u32[]{:S(2)}, u32[]{:S(2)}) %collective-permute-start.5) | collective-permute-done | bytes 401440 | tf_op jit(solution)/shard_map/ppermute | solution.py:138
  15.9 0.0 collective-permute-start.6
  16.0 7.7 %collective-permute-done.3.refs_4_.refs_14_ = bf16[32,6272]{1,0:T(8,128)(2,1)S(1)} collective-permute-done((bf16[32,6272]{1,0:T(8,128)(2,1)S(1)}, bf16[32,6272]{1,0:T(8,128)(2,1)S(1)}, u32[]{:S(2)}, u32[]{:S(2)}) %collective-permute-start.3) | collective-permute-done | bytes 401440 | tf_op jit(solution)/shard_map/ppermute | solution.py:138
  23.7 0.0 collective-permute-start.4
  23.7 0.3 collective-permute-done.1.refs_2_.refs_12_
  24.0 0.2 collective-permute-start.2
  24.2 0.1 stack.47.place_ref
  24.3 0.0 collective-permute-done.refs_1_.refs_11_
  24.3 0.0 collective-permute-done.6.refs_7_.refs_17_
  24.3 1.1 %collective-permute-done.4.refs_5_.refs_15_ = bf16[32,6272]{1,0:T(8,128)(2,1)S(1)} collective-permute-done((bf16[32,6272]{1,0:T(8,128)(2,1)S(1)}, bf16[32,6272]{1,0:T(8,128)(2,1)S(1)}, u32[]{:S(2)}, u32[]{:S(2)}) %collective-permute-start.4) | collective-permute-done | bytes 401440 | tf_op jit(solution)/shard_map/ppermute | solution.py:138
  25.4 0.6 collective-permute-done.2.refs_3_.refs_13_
  26.0 1.1 %slot_picks.1 = (bf16[384,256]{1,0:T(8,128)(2,1)S(1)}, f32[384,128]{1,0:T(8,128)S(1)}, bf16[256,384]{1,0:T(8,128)(2,1)S(1)}, bf16[384,256]{1,0:T(8,128)(2,1)S(1)...) custom-call(s32[11]{0:T(128)S(1)} %stack.47.place_ref, ...), custom_call_target="tpu_custom_call" | custom-call | bytes 1024 | tf_op jit(solution)/shard_map/slot_picks/pallas_call | solution.py:483
  27.1 20.5 %experts.1 = (bf16[32,2048]{1,0:T(8,128)(2,1)S(1)}, bf16[32,2048]{1,0:T(8,128)(2,1)S(1)}, bf16[32,2048]{1,0:T(8,128)(2,1)S(1)}, bf16[32,2048]{1,0:T(8,128)(2,1)S...) custom-call(s32[11]{0:T(128)S(1)} %stack.47.place_ref, ...), custom_call_target="tpu_custom_call" | custom-call | flops 12884901888 | bytes 25165824 | tf_op jit(solution)/shard_map/experts/pallas_call | solution.py:503
  47.6 0.2 collective-permute-start.11
  47.8 0.4 collective-permute-start.7
  48.2 0.1 collective-permute-start.12
  48.3 4.5 %weight_gradient_0_0.1.refs_3_ = bf16[16,1024,768]{2,1,0:T(8,128)(2,1)} custom-call(s32[11]{0:T(128)S(1)} %stack.47.place_ref, f32[256,128]{1,0:T(8,128)S(1)} %get-tuple-element.41.refs_0_, bf16[8,96,768]{2,1,0:T(8,128)(2,1)S(1)} %get-tuple-element.42.refs_1_, bf16[1024,512]{1,0:T(8,128)(2,1)S(1)} %get-tuple-element.43.refs_2_), custom_call_target="tpu_custom_call" | custom-call | flops 3221225472 | bytes 12582912 | tf_op jit(solution)/shard_map/weight_gradient_0_0/pallas_call | solution.py:546
  52.8 0.0 collective-permute-done.7
  52.8 0.1 fusion.7
  52.9 1.9 %collective-permute-start.10 = (bf16[32,2048]{1,0:T(8,128)(2,1)S(1)}, bf16[32,2048]{1,0:T(8,128)(2,1)S(1)}, u32[]{:S(2)}, u32[]{:S(2)}) collective-permute-start(bf16[32,2048]{1,0:T(8,128)(2,1)S(1)} %get-tuple-element.68), channel_id=1, source_target_pairs={{0,6},{1,7},{2,4},{3,5},{4,2},{5,3},{6,0},{7,1},{8,14},{9,15},{10,... | collective-permute-start | bytes 393224 | tf_op jit(solution)/shard_map/ppermute | solution.py:138
  54.8 1.3 %collective-permute-start.9 = (bf16[32,2048]{1,0:T(8,128)(2,1)S(1)}, bf16[32,2048]{1,0:T(8,128)(2,1)S(1)}, u32[]{:S(2)}, u32[]{:S(2)}) collective-permute-start(bf16[32,2048]{1,0:T(8,128)(2,1)S(1)} %get-tuple-element.69), channel_id=1, source_target_pairs={{0,4},{1,5},{2,6},{3,7},{4,0},{5,1},{6,2},{7,3},{8,12},{9,13},{10,... | collective-permute-start | bytes 393224 | tf_op jit(solution)/shard_map/ppermute | solution.py:138
  56.1 0.4 collective-permute-start.8
  56.5 0.0 collective-permute-done.12
  56.5 0.0 collective-permute-done.11.refs_1_
  56.5 0.1 fusion
  56.6 1.9 %collective-permute-start.16 = (bf16[32,2048]{1,0:T(8,128)(2,1)S(1)}, bf16[32,2048]{1,0:T(8,128)(2,1)S(1)}, u32[]{:S(2)}, u32[]{:S(2)}) collective-permute-start(bf16[32,2048]{1,0:T(8,128)(2,1)S(1)} %get-tuple-element.63), channel_id=1, source_target_pairs={{0,6},{1,7},{2,4},{3,5},{4,2},{5,3},{6,0},{7,1},{8,14},{9,15},{10,... | collective-permute-start | bytes 393224 | tf_op jit(solution)/shard_map/ppermute | solution.py:138
  58.5 1.3 %collective-permute-start.15 = (bf16[32,2048]{1,0:T(8,128)(2,1)S(1)}, bf16[32,2048]{1,0:T(8,128)(2,1)S(1)}, u32[]{:S(2)}, u32[]{:S(2)}) collective-permute-start(bf16[32,2048]{1,0:T(8,128)(2,1)S(1)} %get-tuple-element.64), channel_id=1, source_target_pairs={{0,4},{1,5},{2,6},{3,7},{4,0},{5,1},{6,2},{7,3},{8,12},{9,13},{10,... | collective-permute-start | bytes 393224 | tf_op jit(solution)/shard_map/ppermute | solution.py:138
  59.8 4.4 %weight_gradient_0_4.1.refs_3_ = bf16[16,1024,768]{2,1,0:T(8,128)(2,1)} custom-call(s32[11]{0:T(128)S(1)} %stack.47.place_ref, f32[256,128]{1,0:T(8,128)S(1)} %get-tuple-element.41.refs_0_, bf16[8,96,768]{2,1,0:T(8,128)(2,1)S(1)} %get-tuple-element.42.refs_1_, bf16[1024,512]{1,0:T(8,128)(2,1)S(1)} %get-tuple-element.43.refs_2_, ...), custom_call_target="tpu_custom_call", output_to_operand_aliasing={{}: (4, {})} | custom-call | flops 3221225472 | bytes 12582912 | tf_op jit(solution)/shard_map/weight_gradient_0_4/pallas_call | solution.py:546
  64.3 0.0 copy-start
  64.3 0.0 collective-permute-done.8
  64.3 0.4 collective-permute-start.14
  64.7 4.5 %weight_gradient_1_0.1.refs_3_ = bf16[16,1024,768]{2,1,0:T(8,128)(2,1)} custom-call(s32[11]{0:T(128)S(1)} %stack.47.place_ref, f32[256,128]{1,0:T(8,128)S(1)} %get-tuple-element.41.refs_0_, bf16[8,96,768]{2,1,0:T(8,128)(2,1)S(1)} %collective-permute-done.11.refs_1_, bf16[1024,512]{1,0:T(8,128)(2,1)S(1)} %get-tuple-element.43.refs_2_, ...), custom_call_target="tpu_custom_call", output_to_operand_aliasing={{}: (4, {})} | custom-call | flops 3221225472 | bytes 12582912 | tf_op jit(solution)/shard_map/weight_gradient_1_0/pallas_call | solution.py:546
  69.2 0.0 collective-permute-done.10
  69.2 0.0 collective-permute-done.9
  69.2 0.0 copy-done
  69.2 0.1 add_convert_fusion.1
  69.3 0.0 copy-start.1
  69.3 1.8 %collective-permute-start.13 = (bf16[32,2048]{1,0:T(8,128)(2,1)S(1)}, bf16[32,2048]{1,0:T(8,128)(2,1)S(1)}, u32[]{:S(2)}, u32[]{:S(2)}) collective-permute-start(bf16[32,2048]{1,0:T(8,128)(2,1)S(1)} %add_convert_fusion.1), channel_id=1, source_target_pairs={{0,8},{8,16},{16,24},{24,0},{1,9},{9,17},{17,25},{25,1},{2,10},{10... | collective-permute-start | bytes 393224 | tf_op jit(solution)/shard_map/ppermute | solution.py:21
  71.1 4.4 %weight_gradient_1_4.1 = bf16[16,1024,768]{2,1,0:T(8,128)(2,1)} custom-call(s32[11]{0:T(128)S(1)} %stack.47.place_ref, f32[256,128]{1,0:T(8,128)S(1)} %get-tuple-element.41.refs_0_, bf16[8,96,768]{2,1,0:T(8,128)(2,1)S(1)} %collective-permute-done.11.refs_1_, bf16[1024,512]{1,0:T(8,128)(2,1)S(1)} %get-tuple-element.43.refs_2_, ...), custom_call_target="tpu_custom_call", output_to_operand_aliasing={{}: (4, {})} | custom-call | flops 3221225472 | bytes 12582912 | tf_op jit(solution)/shard_map/weight_gradient_1_4/pallas_call | solution.py:546
  75.6 0.0 collective-permute-done.16
  75.6 0.0 collective-permute-done.15
  75.6 0.0 collective-permute-done.14
  75.6 0.5 collective-permute-done.13
  76.1 0.0 copy-done.1
  76.2 0.1 add_convert_fusion
  76.2 2.0 %collective-permute-start.17 = (bf16[32,2048]{1,0:T(8,128)(2,1)S(1)}, bf16[32,2048]{1,0:T(8,128)(2,1)S(1)}, u32[]{:S(2)}, u32[]{:S(2)}) collective-permute-start(bf16[32,2048]{1,0:T(8,128)(2,1)S(1)} %add_convert_fusion), channel_id=1, source_target_pairs={{0,24},{8,0},{16,8},{24,16},{1,25},{9,1},{17,9},{25,17},{2,26},{10... | collective-permute-start | bytes 393224 | tf_op jit(solution)/shard_map/ppermute | solution.py:21
  78.3 3.0 %collective-permute-done.17 = bf16[32,2048]{1,0:T(8,128)(2,1)S(1)} collective-permute-done((bf16[32,2048]{1,0:T(8,128)(2,1)S(1)}, bf16[32,2048]{1,0:T(8,128)(2,1)S(1)}, u32[]{:S(2)}, u32[]{:S(2)}) %collective-permute-start.17) | collective-permute-done | bytes 131104 | tf_op jit(solution)/shard_map/ppermute | solution.py:21
  81.3 0.7 copy.19
  81.9 0.7 copy.20
Async XLA Ops:
  1.8 14.1 %collective-permute-start.5 = (bf16[32,6272]{1,0:T(8,128)(2,1)S(1)}, bf16[32,6272]{1,0:T(8,128)(2,1)S(1)}, u32[]{:S(2)}, u32[]{:S(2)}) collective-permute-start(bf16[32,6272]{1,0:T(8,128)(2,1)S(1)} %pack.1.refs_0_.refs_10_), channel_id=1, source_target_pairs={{0,6},{1,7},{2,4},{3,5},{4,2},{5,3},{6,0},{7,1},{8,14},{9,15},{10,... | collective-permute-start | bytes 1204232 | tf_op jit(solution)/shard_map/ppermute | solution.py:138
  5.8 17.9 %collective-permute-start.3 = (bf16[32,6272]{1,0:T(8,128)(2,1)S(1)}, bf16[32,6272]{1,0:T(8,128)(2,1)S(1)}, u32[]{:S(2)}, u32[]{:S(2)}) collective-permute-start(bf16[32,6272]{1,0:T(8,128)(2,1)S(1)} %pack.1.refs_0_.refs_10_), channel_id=1, source_target_pairs={{0,4},{1,5},{2,6},{3,7},{4,0},{5,1},{6,2},{7,3},{8,12},{9,13},{10,... | collective-permute-start | bytes 1204232 | tf_op jit(solution)/shard_map/ppermute | solution.py:138
  6.3 17.7 %collective-permute-start.1 = (bf16[32,6272]{1,0:T(8,128)(2,1)S(1)}, bf16[32,6272]{1,0:T(8,128)(2,1)S(1)}, u32[]{:S(2)}, u32[]{:S(2)}) collective-permute-start(bf16[32,6272]{1,0:T(8,128)(2,1)S(1)} %pack.1.refs_0_.refs_10_), channel_id=1, source_target_pairs={{0,2},{1,3},{2,0},{3,1},{4,6},{5,7},{6,4},{7,5},{8,10},{9,11},{10,... | collective-permute-start | bytes 1204232 | tf_op jit(solution)/shard_map/ppermute | solution.py:138
  6.4 17.9 %collective-permute-start = (bf16[32,6272]{1,0:T(8,128)(2,1)S(1)}, bf16[32,6272]{1,0:T(8,128)(2,1)S(1)}, u32[]{:S(2)}, u32[]{:S(2)}) collective-permute-start(bf16[32,6272]{1,0:T(8,128)(2,1)S(1)} %pack.1.refs_0_.refs_10_), channel_id=1, source_target_pairs={{0,1},{1,0},{2,3},{3,2},{4,5},{5,4},{6,7},{7,6},{8,9},{9,8},{10,11... | collective-permute-start | bytes 1204232 | tf_op jit(solution)/shard_map/ppermute | solution.py:138
  15.9 8.3 %collective-permute-start.6 = (bf16[32,6272]{1,0:T(8,128)(2,1)S(1)}, bf16[32,6272]{1,0:T(8,128)(2,1)S(1)}, u32[]{:S(2)}, u32[]{:S(2)}) collective-permute-start(bf16[32,6272]{1,0:T(8,128)(2,1)S(1)} %collective-permute-done.5.refs_6_.refs_16_), channel_id=1, source_target_pairs={{0,1},{1,0},{2,3},{3,2},{4,5},{5,4},{6,7},{7,6},{8,9},{9,8},{10,11... | collective-permute-start | bytes 1204232 | tf_op jit(solution)/shard_map/ppermute | solution.py:138
  23.7 1.7 %collective-permute-start.4 = (bf16[32,6272]{1,0:T(8,128)(2,1)S(1)}, bf16[32,6272]{1,0:T(8,128)(2,1)S(1)}, u32[]{:S(2)}, u32[]{:S(2)}) collective-permute-start(bf16[32,6272]{1,0:T(8,128)(2,1)S(1)} %collective-permute-done.3.refs_4_.refs_14_), channel_id=1, source_target_pairs={{0,1},{1,0},{2,3},{3,2},{4,5},{5,4},{6,7},{7,6},{8,9},{9,8},{10,11... | collective-permute-start | bytes 1204232 | tf_op jit(solution)/shard_map/ppermute | solution.py:138
  24.0 2.0 %collective-permute-start.2 = (bf16[32,6272]{1,0:T(8,128)(2,1)S(1)}, bf16[32,6272]{1,0:T(8,128)(2,1)S(1)}, u32[]{:S(2)}, u32[]{:S(2)}) collective-permute-start(bf16[32,6272]{1,0:T(8,128)(2,1)S(1)} %collective-permute-done.1.refs_2_.refs_12_), channel_id=1, source_target_pairs={{0,1},{1,0},{2,3},{3,2},{4,5},{5,4},{6,7},{7,6},{8,9},{9,8},{10,11... | collective-permute-start | bytes 1204232 | tf_op jit(solution)/shard_map/ppermute | solution.py:138
  47.6 8.9 %collective-permute-start.11 = (bf16[8,96,768]{2,1,0:T(8,128)(2,1)S(1)}, bf16[8,96,768]{2,1,0:T(8,128)(2,1)S(1)}, u32[]{:S(2)}, u32[]{:S(2)}) collective-permute-start(bf16[8,96,768]{2,1,0:T(8,128)(2,1)S(1)} %get-tuple-element.42.refs_1_), channel_id=1, source_target_pairs={{0,1},{1,0},{2,3},{3,2},{4,5},{5,4},{6,7},{7,6},{8,9},{9,8},{10,11... | collective-permute-start | bytes 3538952 | tf_op jit(solution)/shard_map/ppermute | solution.py:138
  47.8 5.0 %collective-permute-start.7 = (bf16[4,32,2048]{2,1,0:T(8,128)(2,1)S(1)}, bf16[4,32,2048]{2,1,0:T(8,128)(2,1)S(1)}, u32[]{:S(2)}, u32[]{:S(2)}) collective-permute-start(bf16[4,32,2048]{2,1,0:T(8,128)(2,1)S(1)} %get-tuple-element.40), channel_id=1, source_target_pairs={{0,1},{1,0},{2,3},{3,2},{4,5},{5,4},{6,7},{7,6},{8,9},{9,8},{10,11... | collective-permute-start | bytes 1572872 | tf_op jit(solution)/shard_map/ppermute | solution.py:138
  48.2 8.3 %collective-permute-start.12 = (bf16[4,32,2048]{2,1,0:T(8,128)(2,1)S(1)}, bf16[4,32,2048]{2,1,0:T(8,128)(2,1)S(1)}, u32[]{:S(2)}, u32[]{:S(2)}) collective-permute-start(bf16[4,32,2048]{2,1,0:T(8,128)(2,1)S(1)} %get-tuple-element.49), channel_id=1, source_target_pairs={{0,1},{1,0},{2,3},{3,2},{4,5},{5,4},{6,7},{7,6},{8,9},{9,8},{10,11... | collective-permute-start | bytes 1572872 | tf_op jit(solution)/shard_map/ppermute | solution.py:138
  52.9 16.3 %collective-permute-start.10 = (bf16[32,2048]{1,0:T(8,128)(2,1)S(1)}, bf16[32,2048]{1,0:T(8,128)(2,1)S(1)}, u32[]{:S(2)}, u32[]{:S(2)}) collective-permute-start(bf16[32,2048]{1,0:T(8,128)(2,1)S(1)} %get-tuple-element.68), channel_id=1, source_target_pairs={{0,6},{1,7},{2,4},{3,5},{4,2},{5,3},{6,0},{7,1},{8,14},{9,15},{10,... | collective-permute-start | bytes 393224 | tf_op jit(solution)/shard_map/ppermute | solution.py:138
  54.8 14.4 %collective-permute-start.9 = (bf16[32,2048]{1,0:T(8,128)(2,1)S(1)}, bf16[32,2048]{1,0:T(8,128)(2,1)S(1)}, u32[]{:S(2)}, u32[]{:S(2)}) collective-permute-start(bf16[32,2048]{1,0:T(8,128)(2,1)S(1)} %get-tuple-element.69), channel_id=1, source_target_pairs={{0,4},{1,5},{2,6},{3,7},{4,0},{5,1},{6,2},{7,3},{8,12},{9,13},{10,... | collective-permute-start | bytes 393224 | tf_op jit(solution)/shard_map/ppermute | solution.py:138
  56.1 8.2 %collective-permute-start.8 = (bf16[32,2048]{1,0:T(8,128)(2,1)S(1)}, bf16[32,2048]{1,0:T(8,128)(2,1)S(1)}, u32[]{:S(2)}, u32[]{:S(2)}) collective-permute-start(bf16[32,2048]{1,0:T(8,128)(2,1)S(1)} %get-tuple-element.70), channel_id=1, source_target_pairs={{0,2},{1,3},{2,0},{3,1},{4,6},{5,7},{6,4},{7,5},{8,10},{9,11},{10,... | collective-permute-start | bytes 393224 | tf_op jit(solution)/shard_map/ppermute | solution.py:138
  56.6 19.0 %collective-permute-start.16 = (bf16[32,2048]{1,0:T(8,128)(2,1)S(1)}, bf16[32,2048]{1,0:T(8,128)(2,1)S(1)}, u32[]{:S(2)}, u32[]{:S(2)}) collective-permute-start(bf16[32,2048]{1,0:T(8,128)(2,1)S(1)} %get-tuple-element.63), channel_id=1, source_target_pairs={{0,6},{1,7},{2,4},{3,5},{4,2},{5,3},{6,0},{7,1},{8,14},{9,15},{10,... | collective-permute-start | bytes 393224 | tf_op jit(solution)/shard_map/ppermute | solution.py:138
  58.5 17.1 %collective-permute-start.15 = (bf16[32,2048]{1,0:T(8,128)(2,1)S(1)}, bf16[32,2048]{1,0:T(8,128)(2,1)S(1)}, u32[]{:S(2)}, u32[]{:S(2)}) collective-permute-start(bf16[32,2048]{1,0:T(8,128)(2,1)S(1)} %get-tuple-element.64), channel_id=1, source_target_pairs={{0,4},{1,5},{2,6},{3,7},{4,0},{5,1},{6,2},{7,3},{8,12},{9,13},{10,... | collective-permute-start | bytes 393224 | tf_op jit(solution)/shard_map/ppermute | solution.py:138
  64.3 4.9 %copy-start = (bf16[1,32,2048]{2,1,0:T(8,128)(2,1)S(1)}, bf16[1,32,2048]{2,1,0:T(8,128)(2,1)}, u32[]{:S(2)}) copy-start(bf16[1,32,2048]{2,1,0:T(8,128)(2,1)} %param.8) | copy-start | bytes 393220
  64.3 11.3 %collective-permute-start.14 = (bf16[32,2048]{1,0:T(8,128)(2,1)S(1)}, bf16[32,2048]{1,0:T(8,128)(2,1)S(1)}, u32[]{:S(2)}, u32[]{:S(2)}) collective-permute-start(bf16[32,2048]{1,0:T(8,128)(2,1)S(1)} %get-tuple-element.65), channel_id=1, source_target_pairs={{0,2},{1,3},{2,0},{3,1},{4,6},{5,7},{6,4},{7,5},{8,10},{9,11},{10,... | collective-permute-start | bytes 393224 | tf_op jit(solution)/shard_map/ppermute | solution.py:138
  69.3 6.8 %copy-start.1 = (bf16[1,32,2048]{2,1,0:T(8,128)(2,1)S(1)}, bf16[1,32,2048]{2,1,0:T(8,128)(2,1)}, u32[]{:S(2)}) copy-start(bf16[1,32,2048]{2,1,0:T(8,128)(2,1)} %param.10) | copy-start | bytes 393220
  69.3 6.8 %collective-permute-start.13 = (bf16[32,2048]{1,0:T(8,128)(2,1)S(1)}, bf16[32,2048]{1,0:T(8,128)(2,1)S(1)}, u32[]{:S(2)}, u32[]{:S(2)}) collective-permute-start(bf16[32,2048]{1,0:T(8,128)(2,1)S(1)} %add_convert_fusion.1), channel_id=1, source_target_pairs={{0,8},{8,16},{16,24},{24,0},{1,9},{9,17},{17,25},{25,1},{2,10},{10... | collective-permute-start | bytes 393224 | tf_op jit(solution)/shard_map/ppermute | solution.py:21
  76.2 5.0 %collective-permute-start.17 = (bf16[32,2048]{1,0:T(8,128)(2,1)S(1)}, bf16[32,2048]{1,0:T(8,128)(2,1)S(1)}, u32[]{:S(2)}, u32[]{:S(2)}) collective-permute-start(bf16[32,2048]{1,0:T(8,128)(2,1)S(1)} %add_convert_fusion), channel_id=1, source_target_pairs={{0,24},{8,0},{16,8},{24,16},{1,25},{9,1},{17,9},{25,17},{2,26},{10... | collective-permute-start | bytes 393224 | tf_op jit(solution)/shard_map/ppermute | solution.py:21

commit v9 on v8

--- a/solution.py
+++ b/solution.py
@@ -139,10 +139,13 @@
 
 
 def pack_kernel(*refs):
-    sources, out_ref, (*held, notes, done) = refs[:7], refs[7], refs[8:]
+    sources, (one, two), (*held, notes, done) = list(refs[:7]), refs[7:9], refs[9:]
     size, width = sources[0].shape
+    half = width // 2
     top = sources[3].shape[0]
-    targets = [out_ref.at[:, pl.ds(place * width, width)] for place in range(3)] + held
+    targets = [one.at[:, pl.ds(0, width)], one.at[:, pl.ds(width, half)]]
+    targets += [two.at[:, pl.ds(0, half)], two.at[:, pl.ds(half, width)]] + held
+    sources[1:2] = [sources[1].at[:, pl.ds(0, half)], sources[1].at[:, pl.ds(half, half)]]
     copies = [
         pltpu.make_async_copy(source, target, done.at[place])
         for place, (source, target) in enumerate(zip(sources, targets))
@@ -161,7 +164,7 @@
             part = rest.astype(jnp.bfloat16).astype(jnp.float32)
             notes[pl.ds(first + term * top, top), 0:size] = part
             rest = rest - part
-    out_ref[:, pl.ds(3 * width, LANES)] = notes[...].T[:size, :].astype(jnp.bfloat16)
+    one[:, pl.ds(width + half, LANES)] = notes[...].T[:size, :].astype(jnp.bfloat16)
 
 
 def picks_kernel(count, top, slots, devices, place_ref, *refs):
@@ -214,11 +217,16 @@
     return jnp.broadcast_to(gate, (gate.shape[0], width))
 
 
-def assemble(place_ref, blocks, columns, tokens):
-    for code, block in enumerate(blocks):
-        size = block.shape[0]
+def assemble(place_ref, first, second, tokens):
+    width = tokens[0].shape[1]
+    half = width // 2
+    for code, (one, two) in enumerate(zip(first, second)):
+        size = one.shape[0]
         rows = pl.ds(pl.multiple_of(place_ref[3 + code], size), size)
-        tokens[rows, :] = block[:, columns]
+        tokens[0][rows, :] = one[:, pl.ds(0, width)]
+        tokens[1][rows, pl.ds(0, half)] = one[:, pl.ds(width, half)]
+        tokens[1][rows, pl.ds(half, half)] = two[:, pl.ds(0, half)]
+        tokens[2][rows, :] = two[:, pl.ds(half, width)]
 
 
 def combine(flipped, results, sums):
@@ -245,10 +253,10 @@
 
 def expert_kernel(count, slots, devices, pair, place_ref, *refs):
     fore_picks, fore_gates, fore_flip, back_picks, back_gates, back_flip = refs[:6]
-    weights, blocks = refs[6 : 6 + WEIGHT_CUTS], refs[6 + WEIGHT_CUTS :][:devices]
+    weights, blocks = refs[6 : 6 + WEIGHT_CUTS], refs[6 + WEIGHT_CUTS :][: 2 * devices]
     groups = devices // pair
-    outs = refs[6 + WEIGHT_CUTS + devices :][: 2 * groups + 2]
-    inner, turned, *scratch = refs[8 + WEIGHT_CUTS + devices + 2 * groups :]
+    outs = refs[6 + WEIGHT_CUTS + 2 * devices :][: 2 * groups + 2]
+    inner, turned, gradient, *scratch = refs[8 + WEIGHT_CUTS + 2 * devices + 2 * groups :]
     tokens, (rows, fore_results, back_results, second) = scratch[:3], scratch[3:]
     total, width = tokens[0].shape
     step = pl.program_id(0)
@@ -256,8 +264,8 @@
     @pl.when(step == 0)
     def _():
         taken = ((fore_picks, None), (back_picks, None), (back_picks, back_gates))
+        assemble(place_ref, blocks[:devices], blocks[devices:], tokens)
         for place, (picks, gates) in enumerate(taken):
-            assemble(place_ref, blocks, pl.ds(place * width, width), tokens[place])
             gather(count, slots, picks, gates, tokens[place], rows, place * slots, 3 * slots)
 
     mine = pl.ds(pl.multiple_of(step * slots, slots), slots)
@@ -299,8 +307,17 @@
         fore_results[mine, columns] = result[:slots]
         back_results[mine, columns] = result[slots:]
 
+    half = gradient.shape[1]
+    two = pl.ds(pl.multiple_of(step * 3 * slots + slots, slots), 2 * slots)
+    flat = rows[two, pl.ds(pl.multiple_of(place_ref[0] * half, LANES), half)].T
+    for start in range(0, gradient.shape[2], CHUNK):
+        columns = pl.ds(start, CHUNK)
+        gradient[0, :, columns] = jnp.dot(
+            flat, inner[0, :, columns], preferred_element_type=jnp.float32
+        ).astype(gradient.dtype)
+
     span = turned.shape[0]
-    first = place_ref[0] * (width // pair) + step * span
+    first = place_ref[0] * half + step * span
     for place in range(2):
         some = tokens[1 + place][:, pl.ds(pl.multiple_of(first, LANES), span)]
         turned[:, pl.ds(place * total, total)] = some.T
@@ -323,17 +340,16 @@
                 far_out[group] = sums[far, :]
 
 
-def weight_kernel(whose, first, number, count, slots, place_ref, *refs):
+def weight_kernel(first, number, count, slots, place_ref, *refs):
     columns, inner, turned = refs[:3]
     out_ref, picks, rows, staged, out_done = refs[-5:]
     total, half = columns.shape[0], turned.shape[0]
-    side = place_ref[0]
-    owner = side if whose == 0 else 1 - side
+    owner = 1 - place_ref[0]
     lane = lax.broadcasted_iota(jnp.int32, (total, LANES), 1).astype(jnp.float32)
     is_saved = lax.broadcasted_iota(jnp.int32, (1, LANES), 1) < slots
     scales = []
     for step in range(number):
-        column = whose * count + first + step
+        column = count + first + step
         slot = jnp.broadcast_to(columns[:, column : column + 1], (total, LANES))
         column += 2 * count
         gate = jnp.broadcast_to(columns[:, column : column + 1], (total, LANES))
@@ -442,11 +458,14 @@
     def summed(*blocks):
         return functools.reduce(jnp.add, [block.astype(jnp.float32) for block in blocks])
 
-    packed = jax.ShapeDtypeStruct((token_count, 3 * width + LANES), jnp.bfloat16)
+    packed = [
+        jax.ShapeDtypeStruct((token_count, 3 * width // 2 + extra), jnp.bfloat16)
+        for extra in (LANES, 0)
+    ]
     own = pl.pallas_call(
         pack_kernel,
         in_specs=[pl.BlockSpec(memory_space=pl.ANY)] * 7,
-        out_specs=pl.BlockSpec(memory_space=pltpu.VMEM),
+        out_specs=[pl.BlockSpec(memory_space=pltpu.VMEM)] * 2,
         out_shape=packed,
         scratch_shapes=[
             pltpu.VMEM((top, token_count), jnp.int32),
@@ -454,7 +473,7 @@
             pltpu.VMEM((top, token_count), jnp.int32),
             pltpu.VMEM((top, token_count), jnp.float32),
             pltpu.VMEM((LANES, LANES), jnp.float32),
-            pltpu.SemaphoreType.DMA((7,)),
+            pltpu.SemaphoreType.DMA((8,)),
         ],
         compiler_params=pltpu.CompilerParams(vmem_limit_bytes=VMEM_LIMIT),
         name="pack",
@@ -472,8 +491,17 @@
             )
         ]
     )
-    near = [own] + across([own] * (groups - 1))
-    blocks = [block for one in near for block in (one, onward(one))]
+    near = [[half_block] for half_block in own]
+    code = pair
+    while code < devices:
+        near[0] += [swapped(block, code) for block in near[0]]
+        near[1] += [swapped(block, devices // code) for block in near[1]]
+        code *= 2
+    bits = groups.bit_length() - 1
+    near[1] = [
+        near[1][int(f"{group:0{bits}b}"[::-1], 2) if bits else 0] for group in range(groups)
+    ]
+    blocks = [block for half_blocks in near for one in half_blocks for block in (one, onward(one))]
 
     pick = jax.ShapeDtypeStruct((rows, total), jnp.bfloat16)
     flip = jax.ShapeDtypeStruct((total, rows), jnp.bfloat16)
@@ -484,11 +512,11 @@
         functools.partial(picks_kernel, count, top, slots, devices),
         "slot_picks",
         1,
-        [pl.BlockSpec((token_count, LANES), lambda *_: (0, 3 * width // LANES))] * devices,
+        [pl.BlockSpec((token_count, LANES), lambda *_: (0, 3 * width // 2 // LANES))] * devices,
         [whole(out.shape) for out in pick_outs],
         pick_outs,
         [pltpu.VMEM((total, LANES), jnp.float32), pltpu.VMEM((LANES, total), jnp.float32)],
-    )(place, *blocks)
+    )(place, *blocks[:devices])
 
     pass_flops = 2 * 2 * count * CHUNK * width * inner_width
     near_part = jax.ShapeDtypeStruct((token_count, width), jnp.bfloat16)
@@ -500,7 +528,8 @@
     )
     tokens = pltpu.VMEM((total, width), jnp.bfloat16)
     cut = width // WEIGHT_CUTS
-    *parts, inner_own, tokens_turned = pl.pallas_call(
+    whole_gradient = jax.ShapeDtypeStruct((local_count, half, inner_width), jnp.bfloat16)
+    *parts, inner_own, tokens_turned, done = pl.pallas_call(
         functools.partial(expert_kernel, count, slots, devices, pair),
         grid_spec=pltpu.PrefetchScalarGridSpec(
             num_scalar_prefetch=1,
@@ -513,11 +542,14 @@
                 )
                 for part in range(WEIGHT_CUTS)
             ]
-            + [whole(packed.shape)] * devices,
+            + [whole(one.shape) for one in packed for _ in range(devices)],
             out_specs=([whole(near_part.shape)] * groups + [whole(far_part.shape)]) * 2
             + [
                 pl.BlockSpec((1, 2 * slots, inner_width), lambda step, place: (step, 0, 0)),
                 pl.BlockSpec((half // count, 2 * total), lambda step, place: (step, 0)),
+                pl.BlockSpec(
+                    (1, half, inner_width), lambda step, place: (place[0] * count + step, 0, 0)
+                ),
             ],
             scratch_shapes=[tokens] * 3
             + [
@@ -527,7 +559,7 @@
                 pltpu.VMEM((2 * slots, inner_width), jnp.bfloat16),
             ],
         ),
-        out_shape=([near_part] * groups + [far_part]) * 2 + [inner, turned],
+        out_shape=([near_part] * groups + [far_part]) * 2 + [inner, turned, whole_gradient],
         compiler_params=pltpu.CompilerParams(
             vmem_limit_bytes=EXPERTS_LIMIT, dimension_semantics=("arbitrary",)
         ),
@@ -540,14 +572,13 @@
     *grad_parts, grad_far = parts[groups + 1 :]
     layer_far, grad_far, inner_other = onward(layer_far), onward(grad_far), onward(inner_own)
 
-    def gradient(whose, first, number, inner_rows, earlier):
-        earlier = [] if earlier is None else [earlier]
-        operands = [picks[6], inner_rows, tokens_turned] + earlier
+    def gradient(first, number, earlier):
+        operands = [picks[6], inner_other, tokens_turned, earlier]
         return pl.pallas_call(
-            functools.partial(weight_kernel, whose, first, number, count, slots),
-            in_specs=[in_smem, in_vmem, in_vmem, in_vmem] + [anywhere] * len(earlier),
+            functools.partial(weight_kernel, first, number, count, slots),
+            in_specs=[in_smem, in_vmem, in_vmem, in_vmem, anywhere],
             out_specs=anywhere,
-            out_shape=jax.ShapeDtypeStruct((local_count, half, inner_width), jnp.bfloat16),
+            out_shape=whole_gradient,
             scratch_shapes=[
                 pltpu.VMEM((2 * total, number * LANES), jnp.bfloat16),
                 pltpu.VMEM((half, number * LANES), jnp.bfloat16),
@@ -560,29 +591,23 @@
                 bytes_accessed=number * half * inner_width * 4,
                 transcendentals=0,
             ),
-            input_output_aliases={len(operands): 0} if earlier else {},
-            name=f"weight_gradient_{whose}_{first}",
+            input_output_aliases={len(operands): 0},
+            name=f"weight_gradient_{first}",
         )(place, *operands)
 
     def pair_sums(near_parts, far):
         return [summed(part, far[group]).astype(jnp.bfloat16) for group, part in enumerate(near_parts)]
 
-    piece = -(-count // 2)
-    done = gradient(0, 0, piece, inner_own, None)
-    layer_sums = pair_sums(layer_parts, after(done, layer_far))
+    piece = count // 2
+    layer_sums = pair_sums(layer_parts, layer_far)
     layer_near = across(layer_sums[1:])
     grad_sums = pair_sums(grad_parts, after((layer_sums, inner_other), grad_far))
     grad_near = across(grad_sums[1:])
-    done = after(grad_sums, done)
-    if piece < count:
-        done = gradient(0, piece, count - piece, inner_own, done)
-    done = gradient(1, 0, piece, inner_other, after(layer_near[0], done))
-    layer_near = after(done, layer_near)
+    done = gradient(0, piece, after(grad_sums, done))
+    layer_near = after((done, grad_near[:-1]), layer_near)
     layer_out = summed(section_inputs[0], layer_sums[0], *layer_near).astype(jnp.bfloat16)
     next_inputs = shifted(layer_out, "pipe", 1)[None]
-    done = after(layer_out, done)
-    if piece < count:
-        done = gradient(1, piece, count - piece, inner_other, done)
+    done = gradient(piece, count - piece, after(layer_out, done))
     grad_near = after((done, next_inputs), grad_near)
     input_grads = summed(output_grads[0], grad_sums[0], *grad_near).astype(jnp.bfloat16)
     prior_grads = shifted(input_grads, "pipe", -1)[None]

time: 82.8 us -> 81.6 us (0.986)
  Pallas kernels: 40.6 us -> 36 us
  starting transfers between devices: 16.6 us -> 20.5 us
    pallas_call x4 -> x2, Pallas kernels: 17.8 us -> 8.9 us  [gradient(): pl.pallas_call(functools.partial(weight_kernel, first, number, count, slo...]
    pallas_call x1, Pallas kernels: 20.5 us -> 24.7 us  [gathered_plan(): pl.pallas_call(functools.partial(expert_kernel, count, slots, devices, pa...]
    ppermute x16 -> x23, starting transfers between devices: 12.8 us -> 16.9 us  [swapped(): lax.ppermute(value, axes, [(source, source ^ code) for source in range(co...]
    ppermute x16 -> x23, waiting for transfers between devices: 19.2 us -> 18.4 us  [swapped(): lax.ppermute(value, axes, [(source, source ^ code) for source in range(co...]
  transfers between devices with their start and end apart: 18 -> 25, of which waited for: 7 -> 10; matrix products, arithmetic and copies ran while one was open for 1% -> 1% of each run, Pallas kernels for 22% -> 12%
where the time goes in v9:
time: 81.6 us; the launch traced here: 81.4 us
  Pallas kernels  36 us (44%)
  waiting for transfers between devices  22.3 us (27%)
  starting transfers between devices  20.5 us (25%)
  local copies, waits for them, and re-layouts  1.41 us (2%)
    pallas_call x1, Pallas kernels, gathered_plan(): pl.pallas_call(functools.partial(expert_kernel, count, slots, devices, pa...  24.7 us
    ppermute x23, waiting for transfers between devices, swapped(): lax.ppermute(value, axes, [(source, source ^ code) for source in range(co...  18.4 us
    ppermute x23, starting transfers between devices, swapped(): lax.ppermute(value, axes, [(source, source ^ code) for source in range(co...  16.9 us
    pallas_call x2, Pallas kernels, gradient(): pl.pallas_call(functools.partial(weight_kernel, first, number, count, slo...  8.9 us
    ppermute x2, waiting for transfers between devices, shifted(): return lax.ppermute(value, axis, pairs)  3.87 us
    ppermute x2, starting transfers between devices, shifted(): return lax.ppermute(value, axis, pairs)  3.68 us
  transfers between devices with their start and end apart: 25, of which 10 were waited for; matrix products, arithmetic and copies ran while one was open for 1% of the time, Pallas kernels for 12%

profile of v9, /device:TPU:0, one launch (start us, length us, event | category | flops | bytes accessed | tf_op | source)
XLA Modules:
  0.0 81.4 jit_solution(14355552244494518749)
XLA Ops:
  0.6 1.2 %pack.1 = (bf16[32,3200]{1,0:T(8,128)(2,1)S(1)}, bf16[32,3072]{1,0:T(8,128)(2,1)S(1)}) custom-call(bf16[32,2048]{1,0:T(8,128)(2,1)} %bitcast.69, bf16[32,2048]{1,0:T(8,128)(2,1)} %bitcast.71, bf16[32,2048]{1,0:T(8,128)(2,1)} %bitcast.70, s32[8,32]{1,0:T(8,128)} %bitcast.74, f32[8,32]{1,0:T(8,128)} %bitcast.75, s32[8,32]{1,0:T(8,128)} %bitcast.76, ...), custom_call_target="tpu_custom_call" | custom-call | tf_op jit(solution)/shard_map/pack/pallas_call | solution.py:465
  1.8 3.0 %collective-permute-start.1 = (bf16[32,3200]{1,0:T(8,128)(2,1)S(1)}, bf16[32,3200]{1,0:T(8,128)(2,1)S(1)}, u32[]{:S(2)}, u32[]{:S(2)}) collective-permute-start(bf16[32,3200]{1,0:T(8,128)(2,1)S(1)} %get-tuple-element.34.refs_0_.refs_10_), channel_id=1, source_target_pairs={{0,2},{1,3},{2,0},{3,1},{4,6},{5,7},{6,4},{7,5},{8,10},{9,11},{10,... | collective-permute-start | bytes 614408 | tf_op jit(solution)/shard_map/ppermute | solution.py:138
  4.8 1.5 %collective-permute-start.3 = (bf16[32,3200]{1,0:T(8,128)(2,1)S(1)}, bf16[32,3200]{1,0:T(8,128)(2,1)S(1)}, u32[]{:S(2)}, u32[]{:S(2)}) collective-permute-start(bf16[32,3200]{1,0:T(8,128)(2,1)S(1)} %get-tuple-element.34.refs_0_.refs_10_), channel_id=1, source_target_pairs={{0,4},{1,5},{2,6},{3,7},{4,0},{5,1},{6,2},{7,3},{8,12},{9,13},{10,... | collective-permute-start | bytes 614408 | tf_op jit(solution)/shard_map/ppermute | solution.py:138
  6.4 0.5 collective-permute-start.10
  6.9 0.1 collective-permute-start.8
  6.9 3.8 %collective-permute-done.1.refs_2_.refs_12_ = bf16[32,3200]{1,0:T(8,128)(2,1)S(1)} collective-permute-done((bf16[32,3200]{1,0:T(8,128)(2,1)S(1)}, bf16[32,3200]{1,0:T(8,128)(2,1)S(1)}, u32[]{:S(2)}, u32[]{:S(2)}) %collective-permute-start.1) | collective-permute-done | bytes 204832 | tf_op jit(solution)/shard_map/ppermute | solution.py:138
  10.7 2.1 %collective-permute-start.5 = (bf16[32,3200]{1,0:T(8,128)(2,1)S(1)}, bf16[32,3200]{1,0:T(8,128)(2,1)S(1)}, u32[]{:S(2)}, u32[]{:S(2)}) collective-permute-start(bf16[32,3200]{1,0:T(8,128)(2,1)S(1)} %collective-permute-done.1.refs_2_.refs_12_), channel_id=1, source_target_pairs={{0,4},{1,5},{2,6},{3,7},{4,0},{5,1},{6,2},{7,3},{8,12},{9,13},{10,... | collective-permute-start | bytes 614408 | tf_op jit(solution)/shard_map/ppermute | solution.py:138
  12.8 0.0 collective-permute-start
  12.8 0.0 collective-permute-done.3.refs_4_.refs_14_
  12.8 0.5 collective-permute-start.4
  13.3 3.7 %collective-permute-done.10.refs_22_ = bf16[32,3072]{1,0:T(8,128)(2,1)S(1)} collective-permute-done((bf16[32,3072]{1,0:T(8,128)(2,1)S(1)}, bf16[32,3072]{1,0:T(8,128)(2,1)S(1)}, u32[]{:S(2)}, u32[]{:S(2)}) %collective-permute-start.10) | collective-permute-done | bytes 196640 | tf_op jit(solution)/shard_map/ppermute | solution.py:138
  17.1 0.0 collective-permute-start.2
  17.1 0.0 collective-permute-done.8.refs_20_
  17.1 0.0 collective-permute-start.12
  17.1 2.9 %collective-permute-done.5.refs_6_.refs_16_ = bf16[32,3200]{1,0:T(8,128)(2,1)S(1)} collective-permute-done((bf16[32,3200]{1,0:T(8,128)(2,1)S(1)}, bf16[32,3200]{1,0:T(8,128)(2,1)S(1)}, u32[]{:S(2)}, u32[]{:S(2)}) %collective-permute-start.5) | collective-permute-done | bytes 204832 | tf_op jit(solution)/shard_map/ppermute | solution.py:138
  20.0 0.0 collective-permute-start.6
  20.0 0.0 collective-permute-done.refs_1_.refs_11_
  20.0 0.5 collective-permute-start.7
  20.5 3.9 %collective-permute-done.12.refs_24_ = bf16[32,3072]{1,0:T(8,128)(2,1)S(1)} collective-permute-done((bf16[32,3072]{1,0:T(8,128)(2,1)S(1)}, bf16[32,3072]{1,0:T(8,128)(2,1)S(1)}, u32[]{:S(2)}, u32[]{:S(2)}) %collective-permute-start.12) | collective-permute-done | bytes 196640 | tf_op jit(solution)/shard_map/ppermute | solution.py:138
  24.4 0.0 collective-permute-start.11
  24.4 0.0 collective-permute-done.4.refs_5_.refs_15_
  24.4 0.5 collective-permute-start.9
  24.9 0.0 collective-permute-done.2.refs_3_.refs_13_
  24.9 0.1 collective-permute-start.13
  25.0 0.1 stack.47.place_ref
  25.1 0.0 collective-permute-done.6.refs_7_.refs_17_
  25.1 1.1 %slot_picks.1 = (bf16[384,256]{1,0:T(8,128)(2,1)S(1)}, f32[384,128]{1,0:T(8,128)S(1)}, bf16[256,384]{1,0:T(8,128)(2,1)S(1)}, bf16[384,256]{1,0:T(8,128)(2,1)S(1)...) custom-call(s32[11]{0:T(128)S(1)} %stack.47.place_ref, ...), custom_call_target="tpu_custom_call" | custom-call | bytes 1024 | tf_op jit(solution)/shard_map/slot_picks/pallas_call | solution.py:511
  26.2 0.0 collective-permute-done.7.refs_19_
  26.2 0.0 collective-permute-done.11.refs_23_
  26.2 0.0 collective-permute-done.9.refs_21_
  26.2 0.2 collective-permute-done.13.refs_25_
  26.4 24.7 %experts.1 = (bf16[32,2048]{1,0:T(8,128)(2,1)S(1)}, bf16[32,2048]{1,0:T(8,128)(2,1)S(1)}, bf16[32,2048]{1,0:T(8,128)(2,1)S(1)}, bf16[32,2048]{1,0:T(8,128)(2,1)S...) custom-call(s32[11]{0:T(128)S(1)} %stack.47.place_ref, ...), custom_call_target="tpu_custom_call" | custom-call | flops 12884901888 | bytes 25165824 | tf_op jit(solution)/shard_map/experts/pallas_call | solution.py:532
  51.1 0.3 collective-permute-start.18
  51.5 0.2 collective-permute-start.14
  51.6 0.3 collective-permute-start.19
  52.0 2.8 %collective-permute-done.14 = bf16[4,32,2048]{2,1,0:T(8,128)(2,1)S(1)} collective-permute-done((bf16[4,32,2048]{2,1,0:T(8,128)(2,1)S(1)}, bf16[4,32,2048]{2,1,0:T(8,128)(2,1)S(1)}, u32[]{:S(2)}, u32[]{:S(2)}) %collective-permute-start.14) | collective-permute-done | bytes 524320 | tf_op jit(solution)/shard_map/ppermute | solution.py:138
  54.7 0.1 fusion.7
  54.9 1.5 %collective-permute-start.17 = (bf16[32,2048]{1,0:T(8,128)(2,1)S(1)}, bf16[32,2048]{1,0:T(8,128)(2,1)S(1)}, u32[]{:S(2)}, u32[]{:S(2)}) collective-permute-start(bf16[32,2048]{1,0:T(8,128)(2,1)S(1)} %get-tuple-element.70), channel_id=1, source_target_pairs={{0,6},{1,7},{2,4},{3,5},{4,2},{5,3},{6,0},{7,1},{8,14},{9,15},{10,... | collective-permute-start | bytes 393224 | tf_op jit(solution)/shard_map/ppermute | solution.py:138
  56.4 0.3 collective-permute-start.16
  56.7 1.8 %collective-permute-start.15 = (bf16[32,2048]{1,0:T(8,128)(2,1)S(1)}, bf16[32,2048]{1,0:T(8,128)(2,1)S(1)}, u32[]{:S(2)}, u32[]{:S(2)}) collective-permute-start(bf16[32,2048]{1,0:T(8,128)(2,1)S(1)} %get-tuple-element.72), channel_id=1, source_target_pairs={{0,2},{1,3},{2,0},{3,1},{4,6},{5,7},{6,4},{7,5},{8,10},{9,11},{10,... | collective-permute-start | bytes 393224 | tf_op jit(solution)/shard_map/ppermute | solution.py:138
  58.4 0.0 collective-permute-done.19
  58.4 0.0 collective-permute-done.18.refs_1_
  58.4 0.1 fusion
  58.6 1.6 %collective-permute-start.21 = (bf16[32,2048]{1,0:T(8,128)(2,1)S(1)}, bf16[32,2048]{1,0:T(8,128)(2,1)S(1)}, u32[]{:S(2)}, u32[]{:S(2)}) collective-permute-start(bf16[32,2048]{1,0:T(8,128)(2,1)S(1)} %get-tuple-element.66), channel_id=1, source_target_pairs={{0,4},{1,5},{2,6},{3,7},{4,0},{5,1},{6,2},{7,3},{8,12},{9,13},{10,... | collective-permute-start | bytes 393224 | tf_op jit(solution)/shard_map/ppermute | solution.py:138
  60.1 0.5 collective-permute-start.20
  60.7 4.5 %weight_gradient_0.1.refs_3_ = bf16[16,1024,768]{2,1,0:T(8,128)(2,1)} custom-call(s32[11]{0:T(128)S(1)} %stack.47.place_ref, f32[256,128]{1,0:T(8,128)S(1)} %get-tuple-element.47.refs_0_, bf16[8,96,768]{2,1,0:T(8,128)(2,1)S(1)} %collective-permute-done.18.refs_1_, bf16[1024,512]{1,0:T(8,128)(2,1)S(1)} %get-tuple-element.49.refs_2_, ...), custom_call_target="tpu_custom_call", output_to_operand_aliasing={{}: (4, {})} | custom-call | flops 3221225472 | bytes 12582912 | tf_op jit(solution)/shard_map/weight_gradient_0/pallas_call | solution.py:577
  65.1 0.0 collective-permute-done.17
  65.1 1.5 %collective-permute-start.23 = (bf16[32,2048]{1,0:T(8,128)(2,1)S(1)}, bf16[32,2048]{1,0:T(8,128)(2,1)S(1)}, u32[]{:S(2)}, u32[]{:S(2)}) collective-permute-start(bf16[32,2048]{1,0:T(8,128)(2,1)S(1)} %get-tuple-element.65), channel_id=1, source_target_pairs={{0,6},{1,7},{2,4},{3,5},{4,2},{5,3},{6,0},{7,1},{8,14},{9,15},{10,... | collective-permute-start | bytes 393224 | tf_op jit(solution)/shard_map/ppermute | solution.py:138
  66.7 0.0 collective-permute-done.16
  66.7 0.0 collective-permute-done.15
  66.7 0.5 collective-permute-done.21
  67.2 0.7 collective-permute-done.20
  67.9 0.0 copy-done
  67.9 0.1 add_convert_fusion.1
  68.0 0.0 copy-start.1
  68.0 1.8 %collective-permute-start.22 = (bf16[32,2048]{1,0:T(8,128)(2,1)S(1)}, bf16[32,2048]{1,0:T(8,128)(2,1)S(1)}, u32[]{:S(2)}, u32[]{:S(2)}) collective-permute-start(bf16[32,2048]{1,0:T(8,128)(2,1)S(1)} %add_convert_fusion.1), channel_id=1, source_target_pairs={{0,8},{8,16},{16,24},{24,0},{1,9},{9,17},{17,25},{25,1},{2,10},{10... | collective-permute-start | bytes 393224 | tf_op jit(solution)/shard_map/ppermute | solution.py:21
  69.8 4.4 %weight_gradient_4.1 = bf16[16,1024,768]{2,1,0:T(8,128)(2,1)} custom-call(s32[11]{0:T(128)S(1)} %stack.47.place_ref, f32[256,128]{1,0:T(8,128)S(1)} %get-tuple-element.47.refs_0_, bf16[8,96,768]{2,1,0:T(8,128)(2,1)S(1)} %collective-permute-done.18.refs_1_, bf16[1024,512]{1,0:T(8,128)(2,1)S(1)} %get-tuple-element.49.refs_2_, ...), custom_call_target="tpu_custom_call", output_to_operand_aliasing={{}: (4, {})} | custom-call | flops 3221225472 | bytes 12582912 | tf_op jit(solution)/shard_map/weight_gradient_4/pallas_call | solution.py:577
  74.2 0.0 collective-permute-done.23
  74.3 0.7 collective-permute-done.22
  75.0 0.1 add_convert_fusion
  75.1 1.9 %collective-permute-start.24 = (bf16[32,2048]{1,0:T(8,128)(2,1)S(1)}, bf16[32,2048]{1,0:T(8,128)(2,1)S(1)}, u32[]{:S(2)}, u32[]{:S(2)}) collective-permute-start(bf16[32,2048]{1,0:T(8,128)(2,1)S(1)} %add_convert_fusion), channel_id=1, source_target_pairs={{0,24},{8,0},{16,8},{24,16},{1,25},{9,1},{17,9},{25,17},{2,26},{10... | collective-permute-start | bytes 393224 | tf_op jit(solution)/shard_map/ppermute | solution.py:21
  76.9 3.2 %collective-permute-done.24 = bf16[32,2048]{1,0:T(8,128)(2,1)S(1)} collective-permute-done((bf16[32,2048]{1,0:T(8,128)(2,1)S(1)}, bf16[32,2048]{1,0:T(8,128)(2,1)S(1)}, u32[]{:S(2)}, u32[]{:S(2)}) %collective-permute-start.24) | collective-permute-done | bytes 131104 | tf_op jit(solution)/shard_map/ppermute | solution.py:21
  80.1 0.7 copy.17
  80.7 0.7 copy.18
  (2 shorter events, 0.0 us)
Async XLA Ops:
  1.8 8.9 %collective-permute-start.1 = (bf16[32,3200]{1,0:T(8,128)(2,1)S(1)}, bf16[32,3200]{1,0:T(8,128)(2,1)S(1)}, u32[]{:S(2)}, u32[]{:S(2)}) collective-permute-start(bf16[32,3200]{1,0:T(8,128)(2,1)S(1)} %get-tuple-element.34.refs_0_.refs_10_), channel_id=1, source_target_pairs={{0,2},{1,3},{2,0},{3,1},{4,6},{5,7},{6,4},{7,5},{8,10},{9,11},{10,... | collective-permute-start | bytes 614408 | tf_op jit(solution)/shard_map/ppermute | solution.py:138
  4.8 8.0 %collective-permute-start.3 = (bf16[32,3200]{1,0:T(8,128)(2,1)S(1)}, bf16[32,3200]{1,0:T(8,128)(2,1)S(1)}, u32[]{:S(2)}, u32[]{:S(2)}) collective-permute-start(bf16[32,3200]{1,0:T(8,128)(2,1)S(1)} %get-tuple-element.34.refs_0_.refs_10_), channel_id=1, source_target_pairs={{0,4},{1,5},{2,6},{3,7},{4,0},{5,1},{6,2},{7,3},{8,12},{9,13},{10,... | collective-permute-start | bytes 614408 | tf_op jit(solution)/shard_map/ppermute | solution.py:138
  6.4 10.7 %collective-permute-start.10 = (bf16[32,3072]{1,0:T(8,128)(2,1)S(1)}, bf16[32,3072]{1,0:T(8,128)(2,1)S(1)}, u32[]{:S(2)}, u32[]{:S(2)}) collective-permute-start(bf16[32,3072]{1,0:T(8,128)(2,1)S(1)} %get-tuple-element.41.refs_18_), channel_id=1, source_target_pairs={{0,4},{1,5},{2,6},{3,7},{4,0},{5,1},{6,2},{7,3},{8,12},{9,13},{10,... | collective-permute-start | bytes 589832 | tf_op jit(solution)/shard_map/ppermute | solution.py:138
  6.9 10.2 %collective-permute-start.8 = (bf16[32,3072]{1,0:T(8,128)(2,1)S(1)}, bf16[32,3072]{1,0:T(8,128)(2,1)S(1)}, u32[]{:S(2)}, u32[]{:S(2)}) collective-permute-start(bf16[32,3072]{1,0:T(8,128)(2,1)S(1)} %get-tuple-element.41.refs_18_), channel_id=1, source_target_pairs={{0,2},{1,3},{2,0},{3,1},{4,6},{5,7},{6,4},{7,5},{8,10},{9,11},{10,... | collective-permute-start | bytes 589832 | tf_op jit(solution)/shard_map/ppermute | solution.py:138
  10.7 9.2 %collective-permute-start.5 = (bf16[32,3200]{1,0:T(8,128)(2,1)S(1)}, bf16[32,3200]{1,0:T(8,128)(2,1)S(1)}, u32[]{:S(2)}, u32[]{:S(2)}) collective-permute-start(bf16[32,3200]{1,0:T(8,128)(2,1)S(1)} %collective-permute-done.1.refs_2_.refs_12_), channel_id=1, source_target_pairs={{0,4},{1,5},{2,6},{3,7},{4,0},{5,1},{6,2},{7,3},{8,12},{9,13},{10,... | collective-permute-start | bytes 614408 | tf_op jit(solution)/shard_map/ppermute | solution.py:138
  12.8 7.2 %collective-permute-start = (bf16[32,3200]{1,0:T(8,128)(2,1)S(1)}, bf16[32,3200]{1,0:T(8,128)(2,1)S(1)}, u32[]{:S(2)}, u32[]{:S(2)}) collective-permute-start(bf16[32,3200]{1,0:T(8,128)(2,1)S(1)} %get-tuple-element.34.refs_0_.refs_10_), channel_id=1, source_target_pairs={{0,1},{1,0},{2,3},{3,2},{4,5},{5,4},{6,7},{7,6},{8,9},{9,8},{10,11... | collective-permute-start | bytes 614408 | tf_op jit(solution)/shard_map/ppermute | solution.py:138
  12.8 11.5 %collective-permute-start.4 = (bf16[32,3200]{1,0:T(8,128)(2,1)S(1)}, bf16[32,3200]{1,0:T(8,128)(2,1)S(1)}, u32[]{:S(2)}, u32[]{:S(2)}) collective-permute-start(bf16[32,3200]{1,0:T(8,128)(2,1)S(1)} %collective-permute-done.3.refs_4_.refs_14_), channel_id=1, source_target_pairs={{0,1},{1,0},{2,3},{3,2},{4,5},{5,4},{6,7},{7,6},{8,9},{9,8},{10,11... | collective-permute-start | bytes 614408 | tf_op jit(solution)/shard_map/ppermute | solution.py:138
  17.1 7.8 %collective-permute-start.2 = (bf16[32,3200]{1,0:T(8,128)(2,1)S(1)}, bf16[32,3200]{1,0:T(8,128)(2,1)S(1)}, u32[]{:S(2)}, u32[]{:S(2)}) collective-permute-start(bf16[32,3200]{1,0:T(8,128)(2,1)S(1)} %collective-permute-done.1.refs_2_.refs_12_), channel_id=1, source_target_pairs={{0,1},{1,0},{2,3},{3,2},{4,5},{5,4},{6,7},{7,6},{8,9},{9,8},{10,11... | collective-permute-start | bytes 614408 | tf_op jit(solution)/shard_map/ppermute | solution.py:138
  17.1 7.3 %collective-permute-start.12 = (bf16[32,3072]{1,0:T(8,128)(2,1)S(1)}, bf16[32,3072]{1,0:T(8,128)(2,1)S(1)}, u32[]{:S(2)}, u32[]{:S(2)}) collective-permute-start(bf16[32,3072]{1,0:T(8,128)(2,1)S(1)} %collective-permute-done.10.refs_22_), channel_id=1, source_target_pairs={{0,2},{1,3},{2,0},{3,1},{4,6},{5,7},{6,4},{7,5},{8,10},{9,11},{10,... | collective-permute-start | bytes 589832 | tf_op jit(solution)/shard_map/ppermute | solution.py:138
  20.0 5.1 %collective-permute-start.6 = (bf16[32,3200]{1,0:T(8,128)(2,1)S(1)}, bf16[32,3200]{1,0:T(8,128)(2,1)S(1)}, u32[]{:S(2)}, u32[]{:S(2)}) collective-permute-start(bf16[32,3200]{1,0:T(8,128)(2,1)S(1)} %collective-permute-done.5.refs_6_.refs_16_), channel_id=1, source_target_pairs={{0,1},{1,0},{2,3},{3,2},{4,5},{5,4},{6,7},{7,6},{8,9},{9,8},{10,11... | collective-permute-start | bytes 614408 | tf_op jit(solution)/shard_map/ppermute | solution.py:138
  20.0 6.2 %collective-permute-start.7 = (bf16[32,3072]{1,0:T(8,128)(2,1)S(1)}, bf16[32,3072]{1,0:T(8,128)(2,1)S(1)}, u32[]{:S(2)}, u32[]{:S(2)}) collective-permute-start(bf16[32,3072]{1,0:T(8,128)(2,1)S(1)} %get-tuple-element.41.refs_18_), channel_id=1, source_target_pairs={{0,1},{1,0},{2,3},{3,2},{4,5},{5,4},{6,7},{7,6},{8,9},{9,8},{10,11... | collective-permute-start | bytes 589832 | tf_op jit(solution)/shard_map/ppermute | solution.py:138
  24.4 1.8 %collective-permute-start.11 = (bf16[32,3072]{1,0:T(8,128)(2,1)S(1)}, bf16[32,3072]{1,0:T(8,128)(2,1)S(1)}, u32[]{:S(2)}, u32[]{:S(2)}) collective-permute-start(bf16[32,3072]{1,0:T(8,128)(2,1)S(1)} %collective-permute-done.10.refs_22_), channel_id=1, source_target_pairs={{0,1},{1,0},{2,3},{3,2},{4,5},{5,4},{6,7},{7,6},{8,9},{9,8},{10,11... | collective-permute-start | bytes 589832 | tf_op jit(solution)/shard_map/ppermute | solution.py:138
  24.4 1.8 %collective-permute-start.9 = (bf16[32,3072]{1,0:T(8,128)(2,1)S(1)}, bf16[32,3072]{1,0:T(8,128)(2,1)S(1)}, u32[]{:S(2)}, u32[]{:S(2)}) collective-permute-start(bf16[32,3072]{1,0:T(8,128)(2,1)S(1)} %collective-permute-done.8.refs_20_), channel_id=1, source_target_pairs={{0,1},{1,0},{2,3},{3,2},{4,5},{5,4},{6,7},{7,6},{8,9},{9,8},{10,11... | collective-permute-start | bytes 589832 | tf_op jit(solution)/shard_map/ppermute | solution.py:138
  24.9 1.5 %collective-permute-start.13 = (bf16[32,3072]{1,0:T(8,128)(2,1)S(1)}, bf16[32,3072]{1,0:T(8,128)(2,1)S(1)}, u32[]{:S(2)}, u32[]{:S(2)}) collective-permute-start(bf16[32,3072]{1,0:T(8,128)(2,1)S(1)} %collective-permute-done.12.refs_24_), channel_id=1, source_target_pairs={{0,1},{1,0},{2,3},{3,2},{4,5},{5,4},{6,7},{7,6},{8,9},{9,8},{10,11... | collective-permute-start | bytes 589832 | tf_op jit(solution)/shard_map/ppermute | solution.py:138
  51.1 7.3 %collective-permute-start.18 = (bf16[8,96,768]{2,1,0:T(8,128)(2,1)S(1)}, bf16[8,96,768]{2,1,0:T(8,128)(2,1)S(1)}, u32[]{:S(2)}, u32[]{:S(2)}) collective-permute-start(bf16[8,96,768]{2,1,0:T(8,128)(2,1)S(1)} %get-tuple-element.48), channel_id=1, source_target_pairs={{0,1},{1,0},{2,3},{3,2},{4,5},{5,4},{6,7},{7,6},{8,9},{9,8},{10,11... | collective-permute-start | bytes 3538952 | tf_op jit(solution)/shard_map/ppermute | solution.py:138
  51.5 3.3 %collective-permute-start.14 = (bf16[4,32,2048]{2,1,0:T(8,128)(2,1)S(1)}, bf16[4,32,2048]{2,1,0:T(8,128)(2,1)S(1)}, u32[]{:S(2)}, u32[]{:S(2)}) collective-permute-start(bf16[4,32,2048]{2,1,0:T(8,128)(2,1)S(1)} %get-tuple-element.43), channel_id=1, source_target_pairs={{0,1},{1,0},{2,3},{3,2},{4,5},{5,4},{6,7},{7,6},{8,9},{9,8},{10,11... | collective-permute-start | bytes 1572872 | tf_op jit(solution)/shard_map/ppermute | solution.py:138
  51.6 6.8 %collective-permute-start.19 = (bf16[4,32,2048]{2,1,0:T(8,128)(2,1)S(1)}, bf16[4,32,2048]{2,1,0:T(8,128)(2,1)S(1)}, u32[]{:S(2)}, u32[]{:S(2)}) collective-permute-start(bf16[4,32,2048]{2,1,0:T(8,128)(2,1)S(1)} %get-tuple-element.52), channel_id=1, source_target_pairs={{0,1},{1,0},{2,3},{3,2},{4,5},{5,4},{6,7},{7,6},{8,9},{9,8},{10,11... | collective-permute-start | bytes 1572872 | tf_op jit(solution)/shard_map/ppermute | solution.py:138
  54.9 10.3 %collective-permute-start.17 = (bf16[32,2048]{1,0:T(8,128)(2,1)S(1)}, bf16[32,2048]{1,0:T(8,128)(2,1)S(1)}, u32[]{:S(2)}, u32[]{:S(2)}) collective-permute-start(bf16[32,2048]{1,0:T(8,128)(2,1)S(1)} %get-tuple-element.70), channel_id=1, source_target_pairs={{0,6},{1,7},{2,4},{3,5},{4,2},{5,3},{6,0},{7,1},{8,14},{9,15},{10,... | collective-permute-start | bytes 393224 | tf_op jit(solution)/shard_map/ppermute | solution.py:138
  56.4 10.2 %collective-permute-start.16 = (bf16[32,2048]{1,0:T(8,128)(2,1)S(1)}, bf16[32,2048]{1,0:T(8,128)(2,1)S(1)}, u32[]{:S(2)}, u32[]{:S(2)}) collective-permute-start(bf16[32,2048]{1,0:T(8,128)(2,1)S(1)} %get-tuple-element.71), channel_id=1, source_target_pairs={{0,4},{1,5},{2,6},{3,7},{4,0},{5,1},{6,2},{7,3},{8,12},{9,13},{10,... | collective-permute-start | bytes 393224 | tf_op jit(solution)/shard_map/ppermute | solution.py:138
  56.7 10.0 %collective-permute-start.15 = (bf16[32,2048]{1,0:T(8,128)(2,1)S(1)}, bf16[32,2048]{1,0:T(8,128)(2,1)S(1)}, u32[]{:S(2)}, u32[]{:S(2)}) collective-permute-start(bf16[32,2048]{1,0:T(8,128)(2,1)S(1)} %get-tuple-element.72), channel_id=1, source_target_pairs={{0,2},{1,3},{2,0},{3,1},{4,6},{5,7},{6,4},{7,5},{8,10},{9,11},{10,... | collective-permute-start | bytes 393224 | tf_op jit(solution)/shard_map/ppermute | solution.py:138
  58.6 8.6 %collective-permute-start.21 = (bf16[32,2048]{1,0:T(8,128)(2,1)S(1)}, bf16[32,2048]{1,0:T(8,128)(2,1)S(1)}, u32[]{:S(2)}, u32[]{:S(2)}) collective-permute-start(bf16[32,2048]{1,0:T(8,128)(2,1)S(1)} %get-tuple-element.66), channel_id=1, source_target_pairs={{0,4},{1,5},{2,6},{3,7},{4,0},{5,1},{6,2},{7,3},{8,12},{9,13},{10,... | collective-permute-start | bytes 393224 | tf_op jit(solution)/shard_map/ppermute | solution.py:138
  60.1 7.7 %collective-permute-start.20 = (bf16[32,2048]{1,0:T(8,128)(2,1)S(1)}, bf16[32,2048]{1,0:T(8,128)(2,1)S(1)}, u32[]{:S(2)}, u32[]{:S(2)}) collective-permute-start(bf16[32,2048]{1,0:T(8,128)(2,1)S(1)} %get-tuple-element.67), channel_id=1, source_target_pairs={{0,2},{1,3},{2,0},{3,1},{4,6},{5,7},{6,4},{7,5},{8,10},{9,11},{10,... | collective-permute-start | bytes 393224 | tf_op jit(solution)/shard_map/ppermute | solution.py:138
  60.7 7.2 %copy-start = (bf16[1,32,2048]{2,1,0:T(8,128)(2,1)S(1)}, bf16[1,32,2048]{2,1,0:T(8,128)(2,1)}, u32[]{:S(2)}) copy-start(bf16[1,32,2048]{2,1,0:T(8,128)(2,1)} %param.8) | copy-start | bytes 393220
  65.1 9.1 %collective-permute-start.23 = (bf16[32,2048]{1,0:T(8,128)(2,1)S(1)}, bf16[32,2048]{1,0:T(8,128)(2,1)S(1)}, u32[]{:S(2)}, u32[]{:S(2)}) collective-permute-start(bf16[32,2048]{1,0:T(8,128)(2,1)S(1)} %get-tuple-element.65), channel_id=1, source_target_pairs={{0,6},{1,7},{2,4},{3,5},{4,2},{5,3},{6,0},{7,1},{8,14},{9,15},{10,... | collective-permute-start | bytes 393224 | tf_op jit(solution)/shard_map/ppermute | solution.py:138
  68.0 7.0 %copy-start.1 = (bf16[1,32,2048]{2,1,0:T(8,128)(2,1)S(1)}, bf16[1,32,2048]{2,1,0:T(8,128)(2,1)}, u32[]{:S(2)}) copy-start(bf16[1,32,2048]{2,1,0:T(8,128)(2,1)} %param.10) | copy-start | bytes 393220
  68.0 7.0 %collective-permute-start.22 = (bf16[32,2048]{1,0:T(8,128)(2,1)S(1)}, bf16[32,2048]{1,0:T(8,128)(2,1)S(1)}, u32[]{:S(2)}, u32[]{:S(2)}) collective-permute-start(bf16[32,2048]{1,0:T(8,128)(2,1)S(1)} %add_convert_fusion.1), channel_id=1, source_target_pairs={{0,8},{8,16},{16,24},{24,0},{1,9},{9,17},{17,25},{25,1},{2,10},{10... | collective-permute-start | bytes 393224 | tf_op jit(solution)/shard_map/ppermute | solution.py:21
  75.1 5.0 %collective-permute-start.24 = (bf16[32,2048]{1,0:T(8,128)(2,1)S(1)}, bf16[32,2048]{1,0:T(8,128)(2,1)S(1)}, u32[]{:S(2)}, u32[]{:S(2)}) collective-permute-start(bf16[32,2048]{1,0:T(8,128)(2,1)S(1)} %add_convert_fusion), channel_id=1, source_target_pairs={{0,24},{8,0},{16,8},{24,16},{1,25},{9,1},{17,9},{25,17},{2,26},{10... | collective-permute-start | bytes 393224 | tf_op jit(solution)/shard_map/ppermute | solution.py:21

commit v10 on v9

--- a/solution.py
+++ b/solution.py
@@ -491,17 +491,25 @@
             )
         ]
     )
-    near = [[half_block] for half_block in own]
-    code = pair
-    while code < devices:
-        near[0] += [swapped(block, code) for block in near[0]]
-        near[1] += [swapped(block, devices // code) for block in near[1]]
-        code *= 2
     bits = groups.bit_length() - 1
-    near[1] = [
-        near[1][int(f"{group:0{bits}b}"[::-1], 2) if bits else 0] for group in range(groups)
-    ]
-    blocks = [block for half_blocks in near for one in half_blocks for block in (one, onward(one))]
+    far_own = [onward(block) for block in own]
+    near = []
+    for way, (block, far) in enumerate(zip(own, far_own)):
+        held = {0: block}
+        for bit in range(bits):
+            step = 1 << (bit if way == 0 else bits - 1 - bit)
+            sources = dict(held) if bit == 0 else {0: block} | after(far, {k: v for k, v in held.items() if k})
+            held |= {group ^ step: swapped(source, step * pair) for group, source in sources.items()}
+        near.append([held[group] for group in range(groups)])
+    direct = [1 << bit for bit in range(bits)]
+    settled = lax.optimization_barrier([[half_blocks[group] for group in direct] for half_blocks in near])
+    blocks = []
+    for half_blocks, far, firm in zip(near, far_own, settled):
+        ready = list(half_blocks)
+        for group, block in zip(direct, firm):
+            ready[group] = block
+        distant = [far] + [onward(block) for block in ready[1:]]
+        blocks += [block for both in zip(half_blocks, distant) for block in both]
 
     pick = jax.ShapeDtypeStruct((rows, total), jnp.bfloat16)
     flip = jax.ShapeDtypeStruct((total, rows), jnp.bfloat16)
@@ -570,7 +578,8 @@
     )(place, *picks[:6], *[weights] * WEIGHT_CUTS, *blocks)
     *layer_parts, layer_far = parts[: groups + 1]
     *grad_parts, grad_far = parts[groups + 1 :]
-    layer_far, grad_far, inner_other = onward(layer_far), onward(grad_far), onward(inner_own)
+    layer_far, grad_far = onward(layer_far), onward(grad_far)
+    inner_other = onward(after(layer_far, inner_own))
 
     def gradient(first, number, earlier):
         operands = [picks[6], inner_other, tokens_turned, earlier]

time: 81.6 us -> 79.7 us (0.977)
  waiting for transfers between devices: 22.3 us -> 20.9 us
    ppermute x23, waiting for transfers between devices: 18.4 us -> 16.8 us  [swapped(): lax.ppermute(value, axes, [(source, source ^ code) for source in range(co...]
  transfers between devices with their start and end apart: 25 -> 25, of which waited for: 10 -> 9; matrix products, arithmetic and copies ran while one was open for 1% -> 1% of each run, Pallas kernels for 12% -> 13%
where the time goes in v10:
time: 79.7 us; the launch traced here: 79.6 us
  Pallas kernels  36 us (45%)
  waiting for transfers between devices  20.9 us (26%)
  starting transfers between devices  20 us (25%)
  local copies, waits for them, and re-layouts  1.41 us (2%)
    pallas_call x1, Pallas kernels, gathered_plan(): pl.pallas_call(functools.partial(expert_kernel, count, slots, devices, pa...  24.8 us
    ppermute x23, waiting for transfers between devices, swapped(): lax.ppermute(value, axes, [(source, source ^ code) for source in range(co...  16.8 us
    ppermute x23, starting transfers between devices, swapped(): lax.ppermute(value, axes, [(source, source ^ code) for source in range(co...  16.6 us
    pallas_call x2, Pallas kernels, gradient(): pl.pallas_call(functools.partial(weight_kernel, first, number, count, slo...  8.9 us
    ppermute x2, waiting for transfers between devices, shifted(): return lax.ppermute(value, axis, pairs)  4.08 us
    ppermute x2, starting transfers between devices, shifted(): return lax.ppermute(value, axis, pairs)  3.47 us
  transfers between devices with their start and end apart: 25, of which 9 were waited for; matrix products, arithmetic and copies ran while one was open for 1% of the time, Pallas kernels for 13%

profile of v10, /device:TPU:0, one launch (start us, length us, event | category | flops | bytes accessed | tf_op | source)
XLA Modules:
  0.0 79.6 jit_solution(843635569008662956)
XLA Ops:
  0.6 1.2 %pack.1 = (bf16[32,3200]{1,0:T(8,128)(2,1)S(1)}, bf16[32,3072]{1,0:T(8,128)(2,1)S(1)}) custom-call(bf16[32,2048]{1,0:T(8,128)(2,1)} %bitcast.69, bf16[32,2048]{1,0:T(8,128)(2,1)} %bitcast.71, bf16[32,2048]{1,0:T(8,128)(2,1)} %bitcast.70, s32[8,32]{1,0:T(8,128)} %bitcast.74, f32[8,32]{1,0:T(8,128)} %bitcast.75, s32[8,32]{1,0:T(8,128)} %bitcast.76, ...), custom_call_target="tpu_custom_call" | custom-call | tf_op jit(solution)/shard_map/pack/pallas_call | solution.py:465
  1.8 3.0 %collective-permute-start.1 = (bf16[32,3200]{1,0:T(8,128)(2,1)S(1)}, bf16[32,3200]{1,0:T(8,128)(2,1)S(1)}, u32[]{:S(2)}, u32[]{:S(2)}) collective-permute-start(bf16[32,3200]{1,0:T(8,128)(2,1)S(1)} %get-tuple-element.41.refs_0_.refs_10_), channel_id=1, source_target_pairs={{0,2},{1,3},{2,0},{3,1},{4,6},{5,7},{6,4},{7,5},{8,10},{9,11},{10,... | collective-permute-start | bytes 614408 | tf_op jit(solution)/shard_map/ppermute | solution.py:138
  4.8 0.0 collective-permute-start
  4.8 1.5 %collective-permute-start.2 = (bf16[32,3200]{1,0:T(8,128)(2,1)S(1)}, bf16[32,3200]{1,0:T(8,128)(2,1)S(1)}, u32[]{:S(2)}, u32[]{:S(2)}) collective-permute-start(bf16[32,3200]{1,0:T(8,128)(2,1)S(1)} %get-tuple-element.41.refs_0_.refs_10_), channel_id=1, source_target_pairs={{0,4},{1,5},{2,6},{3,7},{4,0},{5,1},{6,2},{7,3},{8,12},{9,13},{10,... | collective-permute-start | bytes 614408 | tf_op jit(solution)/shard_map/ppermute | solution.py:138
  6.4 0.5 collective-permute-start.4
  6.9 0.2 collective-permute-start.3
  7.1 3.3 %collective-permute-done.1.refs_2_.refs_12_ = bf16[32,3200]{1,0:T(8,128)(2,1)S(1)} collective-permute-done((bf16[32,3200]{1,0:T(8,128)(2,1)S(1)}, bf16[32,3200]{1,0:T(8,128)(2,1)S(1)}, u32[]{:S(2)}, u32[]{:S(2)}) %collective-permute-start.1) | collective-permute-done | bytes 204832 | tf_op jit(solution)/shard_map/ppermute | solution.py:138
  10.4 0.0 collective-permute-start.9
  10.4 0.0 collective-permute-done.refs_1_.refs_11_
  10.4 2.0 %collective-permute-start.7 = (bf16[32,3200]{1,0:T(8,128)(2,1)S(1)}, bf16[32,3200]{1,0:T(8,128)(2,1)S(1)}, u32[]{:S(2)}, u32[]{:S(2)}) collective-permute-start(bf16[32,3200]{1,0:T(8,128)(2,1)S(1)} %collective-permute-done.1.refs_2_.refs_12_), channel_id=1, source_target_pairs={{0,4},{1,5},{2,6},{3,7},{4,0},{5,1},{6,2},{7,3},{8,12},{9,13},{10,... | collective-permute-start | bytes 614408 | tf_op jit(solution)/shard_map/ppermute | solution.py:138
  12.4 4.6 %collective-permute-done.4.refs_22_ = bf16[32,3072]{1,0:T(8,128)(2,1)S(1)} collective-permute-done((bf16[32,3072]{1,0:T(8,128)(2,1)S(1)}, bf16[32,3072]{1,0:T(8,128)(2,1)S(1)}, u32[]{:S(2)}, u32[]{:S(2)}) %collective-permute-start.4) | collective-permute-done | bytes 196640 | tf_op jit(solution)/shard_map/ppermute | solution.py:138
  16.9 0.0 collective-permute-done.3.refs_20_
  16.9 0.0 collective-permute-done.2.refs_4_.refs_14_
  16.9 0.0 collective-permute-start.5
  16.9 0.0 collective-permute-done.9.refs_19_
  17.0 0.3 collective-permute-start.12
  17.3 0.2 collective-permute-start.6
  17.5 3.5 %collective-permute-done.7.refs_6_.refs_16_ = bf16[32,3200]{1,0:T(8,128)(2,1)S(1)} collective-permute-done((bf16[32,3200]{1,0:T(8,128)(2,1)S(1)}, bf16[32,3200]{1,0:T(8,128)(2,1)S(1)}, u32[]{:S(2)}, u32[]{:S(2)}) %collective-permute-start.7) | collective-permute-done | bytes 204832 | tf_op jit(solution)/shard_map/ppermute | solution.py:138
  20.9 0.0 collective-permute-start.8
  20.9 0.5 collective-permute-start.10
  21.4 2.8 %collective-permute-done.12.refs_24_ = bf16[32,3072]{1,0:T(8,128)(2,1)S(1)} collective-permute-done((bf16[32,3072]{1,0:T(8,128)(2,1)S(1)}, bf16[32,3072]{1,0:T(8,128)(2,1)S(1)}, u32[]{:S(2)}, u32[]{:S(2)}) %collective-permute-start.12) | collective-permute-done | bytes 196640 | tf_op jit(solution)/shard_map/ppermute | solution.py:138
  24.3 0.0 collective-permute-start.11
  24.3 0.0 collective-permute-done.5.refs_3_.refs_13_
  24.3 0.5 collective-permute-start.13
  24.8 0.1 stack.47.place_ref
  24.9 0.0 collective-permute-done.6.refs_5_.refs_15_
  24.9 0.0 collective-permute-done.8.refs_7_.refs_17_
  24.9 1.1 %slot_picks.1 = (bf16[384,256]{1,0:T(8,128)(2,1)S(1)}, f32[384,128]{1,0:T(8,128)S(1)}, bf16[256,384]{1,0:T(8,128)(2,1)S(1)}, bf16[384,256]{1,0:T(8,128)(2,1)S(1)...) custom-call(s32[11]{0:T(128)S(1)} %stack.47.place_ref, ...), custom_call_target="tpu_custom_call" | custom-call | bytes 1024 | tf_op jit(solution)/shard_map/slot_picks/pallas_call | solution.py:519
  26.0 0.0 collective-permute-done.10.refs_21_
  26.0 0.0 collective-permute-done.11.refs_23_
  26.0 0.0 collective-permute-done.13.refs_25_
  26.0 24.8 %experts.1 = (bf16[32,2048]{1,0:T(8,128)(2,1)S(1)}, bf16[32,2048]{1,0:T(8,128)(2,1)S(1)}, bf16[32,2048]{1,0:T(8,128)(2,1)S(1)}, bf16[32,2048]{1,0:T(8,128)(2,1)S...) custom-call(s32[11]{0:T(128)S(1)} %stack.47.place_ref, ...), custom_call_target="tpu_custom_call" | custom-call | flops 12884901888 | bytes 25165824 | tf_op jit(solution)/shard_map/experts/pallas_call | solution.py:540
  50.9 0.1 collective-permute-start.14
  51.0 1.8 %collective-permute-done.14 = bf16[4,32,2048]{2,1,0:T(8,128)(2,1)S(1)} collective-permute-done((bf16[4,32,2048]{2,1,0:T(8,128)(2,1)S(1)}, bf16[4,32,2048]{2,1,0:T(8,128)(2,1)S(1)}, u32[]{:S(2)}, u32[]{:S(2)}) %collective-permute-start.14) | collective-permute-done | bytes 524320 | tf_op jit(solution)/shard_map/ppermute | solution.py:138
  52.8 0.1 collective-permute-start.18
  52.9 0.4 collective-permute-start.19
  53.3 0.1 fusion.7
  53.4 1.6 %collective-permute-start.17 = (bf16[32,2048]{1,0:T(8,128)(2,1)S(1)}, bf16[32,2048]{1,0:T(8,128)(2,1)S(1)}, u32[]{:S(2)}, u32[]{:S(2)}) collective-permute-start(bf16[32,2048]{1,0:T(8,128)(2,1)S(1)} %get-tuple-element.84), channel_id=1, source_target_pairs={{0,6},{1,7},{2,4},{3,5},{4,2},{5,3},{6,0},{7,1},{8,14},{9,15},{10,... | collective-permute-start | bytes 393224 | tf_op jit(solution)/shard_map/ppermute | solution.py:138
  55.0 0.2 collective-permute-start.16
  55.2 1.8 %collective-permute-start.15 = (bf16[32,2048]{1,0:T(8,128)(2,1)S(1)}, bf16[32,2048]{1,0:T(8,128)(2,1)S(1)}, u32[]{:S(2)}, u32[]{:S(2)}) collective-permute-start(bf16[32,2048]{1,0:T(8,128)(2,1)S(1)} %get-tuple-element.86), channel_id=1, source_target_pairs={{0,2},{1,3},{2,0},{3,1},{4,6},{5,7},{6,4},{7,5},{8,10},{9,11},{10,... | collective-permute-start | bytes 393224 | tf_op jit(solution)/shard_map/ppermute | solution.py:138
  57.0 0.0 collective-permute-done.19
  57.0 0.0 collective-permute-done.18.refs_1_
  57.0 0.1 fusion
  57.1 1.6 %collective-permute-start.21 = (bf16[32,2048]{1,0:T(8,128)(2,1)S(1)}, bf16[32,2048]{1,0:T(8,128)(2,1)S(1)}, u32[]{:S(2)}, u32[]{:S(2)}) collective-permute-start(bf16[32,2048]{1,0:T(8,128)(2,1)S(1)} %get-tuple-element.80), channel_id=1, source_target_pairs={{0,4},{1,5},{2,6},{3,7},{4,0},{5,1},{6,2},{7,3},{8,12},{9,13},{10,... | collective-permute-start | bytes 393224 | tf_op jit(solution)/shard_map/ppermute | solution.py:138
  58.7 0.5 collective-permute-start.20
  59.2 4.4 %weight_gradient_0.1.refs_3_ = bf16[16,1024,768]{2,1,0:T(8,128)(2,1)} custom-call(s32[11]{0:T(128)S(1)} %stack.47.place_ref, f32[256,128]{1,0:T(8,128)S(1)} %get-tuple-element.60.refs_0_, bf16[8,96,768]{2,1,0:T(8,128)(2,1)S(1)} %collective-permute-done.18.refs_1_, bf16[1024,512]{1,0:T(8,128)(2,1)S(1)} %get-tuple-element.63.refs_2_, ...), custom_call_target="tpu_custom_call", output_to_operand_aliasing={{}: (4, {})} | custom-call | flops 3221225472 | bytes 12582912 | tf_op jit(solution)/shard_map/weight_gradient_0/pallas_call | solution.py:586
  63.7 0.0 collective-permute-done.17
  63.7 1.5 %collective-permute-start.23 = (bf16[32,2048]{1,0:T(8,128)(2,1)S(1)}, bf16[32,2048]{1,0:T(8,128)(2,1)S(1)}, u32[]{:S(2)}, u32[]{:S(2)}) collective-permute-start(bf16[32,2048]{1,0:T(8,128)(2,1)S(1)} %get-tuple-element.79), channel_id=1, source_target_pairs={{0,6},{1,7},{2,4},{3,5},{4,2},{5,3},{6,0},{7,1},{8,14},{9,15},{10,... | collective-permute-start | bytes 393224 | tf_op jit(solution)/shard_map/ppermute | solution.py:138
  65.2 0.0 collective-permute-done.16
  65.2 0.0 collective-permute-done.15
  65.2 0.3 collective-permute-done.21
  65.5 0.5 collective-permute-done.20
  66.0 0.0 copy-done
  66.0 0.1 add_convert_fusion.1
  66.1 0.0 copy-start.1
  66.1 1.7 %collective-permute-start.22 = (bf16[32,2048]{1,0:T(8,128)(2,1)S(1)}, bf16[32,2048]{1,0:T(8,128)(2,1)S(1)}, u32[]{:S(2)}, u32[]{:S(2)}) collective-permute-start(bf16[32,2048]{1,0:T(8,128)(2,1)S(1)} %add_convert_fusion.1), channel_id=1, source_target_pairs={{0,8},{8,16},{16,24},{24,0},{1,9},{9,17},{17,25},{25,1},{2,10},{10... | collective-permute-start | bytes 393224 | tf_op jit(solution)/shard_map/ppermute | solution.py:21
  67.8 4.4 %weight_gradient_4.1 = bf16[16,1024,768]{2,1,0:T(8,128)(2,1)} custom-call(s32[11]{0:T(128)S(1)} %stack.47.place_ref, f32[256,128]{1,0:T(8,128)S(1)} %get-tuple-element.60.refs_0_, bf16[8,96,768]{2,1,0:T(8,128)(2,1)S(1)} %collective-permute-done.18.refs_1_, bf16[1024,512]{1,0:T(8,128)(2,1)S(1)} %get-tuple-element.63.refs_2_, ...), custom_call_target="tpu_custom_call", output_to_operand_aliasing={{}: (4, {})} | custom-call | flops 3221225472 | bytes 12582912 | tf_op jit(solution)/shard_map/weight_gradient_4/pallas_call | solution.py:586
  72.3 0.0 collective-permute-done.23
  72.3 0.8 %collective-permute-done.22 = bf16[32,2048]{1,0:T(8,128)(2,1)S(1)} collective-permute-done((bf16[32,2048]{1,0:T(8,128)(2,1)S(1)}, bf16[32,2048]{1,0:T(8,128)(2,1)S(1)}, u32[]{:S(2)}, u32[]{:S(2)}) %collective-permute-start.22) | collective-permute-done | bytes 131104 | tf_op jit(solution)/shard_map/ppermute | solution.py:21
  73.2 0.1 add_convert_fusion
  73.2 1.8 %collective-permute-start.24 = (bf16[32,2048]{1,0:T(8,128)(2,1)S(1)}, bf16[32,2048]{1,0:T(8,128)(2,1)S(1)}, u32[]{:S(2)}, u32[]{:S(2)}) collective-permute-start(bf16[32,2048]{1,0:T(8,128)(2,1)S(1)} %add_convert_fusion), channel_id=1, source_target_pairs={{0,24},{8,0},{16,8},{24,16},{1,25},{9,1},{17,9},{25,17},{2,26},{10... | collective-permute-start | bytes 393224 | tf_op jit(solution)/shard_map/ppermute | solution.py:21
  75.0 3.2 %collective-permute-done.24 = bf16[32,2048]{1,0:T(8,128)(2,1)S(1)} collective-permute-done((bf16[32,2048]{1,0:T(8,128)(2,1)S(1)}, bf16[32,2048]{1,0:T(8,128)(2,1)S(1)}, u32[]{:S(2)}, u32[]{:S(2)}) %collective-permute-start.24) | collective-permute-done | bytes 131104 | tf_op jit(solution)/shard_map/ppermute | solution.py:21
  78.3 0.7 copy.17
  78.9 0.7 copy.18
  (2 shorter events, 0.0 us)
Async XLA Ops:
  1.8 8.5 %collective-permute-start.1 = (bf16[32,3200]{1,0:T(8,128)(2,1)S(1)}, bf16[32,3200]{1,0:T(8,128)(2,1)S(1)}, u32[]{:S(2)}, u32[]{:S(2)}) collective-permute-start(bf16[32,3200]{1,0:T(8,128)(2,1)S(1)} %get-tuple-element.41.refs_0_.refs_10_), channel_id=1, source_target_pairs={{0,2},{1,3},{2,0},{3,1},{4,6},{5,7},{6,4},{7,5},{8,10},{9,11},{10,... | collective-permute-start | bytes 614408 | tf_op jit(solution)/shard_map/ppermute | solution.py:138
  4.8 5.5 %collective-permute-start = (bf16[32,3200]{1,0:T(8,128)(2,1)S(1)}, bf16[32,3200]{1,0:T(8,128)(2,1)S(1)}, u32[]{:S(2)}, u32[]{:S(2)}) collective-permute-start(bf16[32,3200]{1,0:T(8,128)(2,1)S(1)} %get-tuple-element.41.refs_0_.refs_10_), channel_id=1, source_target_pairs={{0,1},{1,0},{2,3},{3,2},{4,5},{5,4},{6,7},{7,6},{8,9},{9,8},{10,11... | collective-permute-start | bytes 614408 | tf_op jit(solution)/shard_map/ppermute | solution.py:138
  4.8 12.1 %collective-permute-start.2 = (bf16[32,3200]{1,0:T(8,128)(2,1)S(1)}, bf16[32,3200]{1,0:T(8,128)(2,1)S(1)}, u32[]{:S(2)}, u32[]{:S(2)}) collective-permute-start(bf16[32,3200]{1,0:T(8,128)(2,1)S(1)} %get-tuple-element.41.refs_0_.refs_10_), channel_id=1, source_target_pairs={{0,4},{1,5},{2,6},{3,7},{4,0},{5,1},{6,2},{7,3},{8,12},{9,13},{10,... | collective-permute-start | bytes 614408 | tf_op jit(solution)/shard_map/ppermute | solution.py:138
  6.4 10.6 %collective-permute-start.4 = (bf16[32,3072]{1,0:T(8,128)(2,1)S(1)}, bf16[32,3072]{1,0:T(8,128)(2,1)S(1)}, u32[]{:S(2)}, u32[]{:S(2)}) collective-permute-start(bf16[32,3072]{1,0:T(8,128)(2,1)S(1)} %get-tuple-element.42.refs_18_), channel_id=1, source_target_pairs={{0,4},{1,5},{2,6},{3,7},{4,0},{5,1},{6,2},{7,3},{8,12},{9,13},{10,... | collective-permute-start | bytes 589832 | tf_op jit(solution)/shard_map/ppermute | solution.py:138
  6.9 10.1 %collective-permute-start.3 = (bf16[32,3072]{1,0:T(8,128)(2,1)S(1)}, bf16[32,3072]{1,0:T(8,128)(2,1)S(1)}, u32[]{:S(2)}, u32[]{:S(2)}) collective-permute-start(bf16[32,3072]{1,0:T(8,128)(2,1)S(1)} %get-tuple-element.42.refs_18_), channel_id=1, source_target_pairs={{0,2},{1,3},{2,0},{3,1},{4,6},{5,7},{6,4},{7,5},{8,10},{9,11},{10,... | collective-permute-start | bytes 589832 | tf_op jit(solution)/shard_map/ppermute | solution.py:138
  10.4 6.6 %collective-permute-start.9 = (bf16[32,3072]{1,0:T(8,128)(2,1)S(1)}, bf16[32,3072]{1,0:T(8,128)(2,1)S(1)}, u32[]{:S(2)}, u32[]{:S(2)}) collective-permute-start(bf16[32,3072]{1,0:T(8,128)(2,1)S(1)} %get-tuple-element.42.refs_18_), channel_id=1, source_target_pairs={{0,1},{1,0},{2,3},{3,2},{4,5},{5,4},{6,7},{7,6},{8,9},{9,8},{10,11... | collective-permute-start | bytes 589832 | tf_op jit(solution)/shard_map/ppermute | solution.py:138
  10.4 10.6 %collective-permute-start.7 = (bf16[32,3200]{1,0:T(8,128)(2,1)S(1)}, bf16[32,3200]{1,0:T(8,128)(2,1)S(1)}, u32[]{:S(2)}, u32[]{:S(2)}) collective-permute-start(bf16[32,3200]{1,0:T(8,128)(2,1)S(1)} %collective-permute-done.1.refs_2_.refs_12_), channel_id=1, source_target_pairs={{0,4},{1,5},{2,6},{3,7},{4,0},{5,1},{6,2},{7,3},{8,12},{9,13},{10,... | collective-permute-start | bytes 614408 | tf_op jit(solution)/shard_map/ppermute | solution.py:138
  16.9 7.3 %collective-permute-start.5 = (bf16[32,3200]{1,0:T(8,128)(2,1)S(1)}, bf16[32,3200]{1,0:T(8,128)(2,1)S(1)}, u32[]{:S(2)}, u32[]{:S(2)}) collective-permute-start(bf16[32,3200]{1,0:T(8,128)(2,1)S(1)} %collective-permute-done.1.refs_2_.refs_12_), channel_id=1, source_target_pairs={{0,1},{1,0},{2,3},{3,2},{4,5},{5,4},{6,7},{7,6},{8,9},{9,8},{10,11... | collective-permute-start | bytes 614408 | tf_op jit(solution)/shard_map/ppermute | solution.py:138
  17.0 7.3 %collective-permute-start.12 = (bf16[32,3072]{1,0:T(8,128)(2,1)S(1)}, bf16[32,3072]{1,0:T(8,128)(2,1)S(1)}, u32[]{:S(2)}, u32[]{:S(2)}) collective-permute-start(bf16[32,3072]{1,0:T(8,128)(2,1)S(1)} %collective-permute-done.4.refs_22_), channel_id=1, source_target_pairs={{0,2},{1,3},{2,0},{3,1},{4,6},{5,7},{6,4},{7,5},{8,10},{9,11},{10,... | collective-permute-start | bytes 589832 | tf_op jit(solution)/shard_map/ppermute | solution.py:138
  17.3 7.6 %collective-permute-start.6 = (bf16[32,3200]{1,0:T(8,128)(2,1)S(1)}, bf16[32,3200]{1,0:T(8,128)(2,1)S(1)}, u32[]{:S(2)}, u32[]{:S(2)}) collective-permute-start(bf16[32,3200]{1,0:T(8,128)(2,1)S(1)} %collective-permute-done.2.refs_4_.refs_14_), channel_id=1, source_target_pairs={{0,1},{1,0},{2,3},{3,2},{4,5},{5,4},{6,7},{7,6},{8,9},{9,8},{10,11... | collective-permute-start | bytes 614408 | tf_op jit(solution)/shard_map/ppermute | solution.py:138
  20.9 3.9 %collective-permute-start.8 = (bf16[32,3200]{1,0:T(8,128)(2,1)S(1)}, bf16[32,3200]{1,0:T(8,128)(2,1)S(1)}, u32[]{:S(2)}, u32[]{:S(2)}) collective-permute-start(bf16[32,3200]{1,0:T(8,128)(2,1)S(1)} %collective-permute-done.7.refs_6_.refs_16_), channel_id=1, source_target_pairs={{0,1},{1,0},{2,3},{3,2},{4,5},{5,4},{6,7},{7,6},{8,9},{9,8},{10,11... | collective-permute-start | bytes 614408 | tf_op jit(solution)/shard_map/ppermute | solution.py:138
  20.9 5.1 %collective-permute-start.10 = (bf16[32,3072]{1,0:T(8,128)(2,1)S(1)}, bf16[32,3072]{1,0:T(8,128)(2,1)S(1)}, u32[]{:S(2)}, u32[]{:S(2)}) collective-permute-start(bf16[32,3072]{1,0:T(8,128)(2,1)S(1)} %collective-permute-done.3.refs_20_), channel_id=1, source_target_pairs={{0,1},{1,0},{2,3},{3,2},{4,5},{5,4},{6,7},{7,6},{8,9},{9,8},{10,11... | collective-permute-start | bytes 589832 | tf_op jit(solution)/shard_map/ppermute | solution.py:138
  24.3 1.8 %collective-permute-start.11 = (bf16[32,3072]{1,0:T(8,128)(2,1)S(1)}, bf16[32,3072]{1,0:T(8,128)(2,1)S(1)}, u32[]{:S(2)}, u32[]{:S(2)}) collective-permute-start(bf16[32,3072]{1,0:T(8,128)(2,1)S(1)} %collective-permute-done.4.refs_22_), channel_id=1, source_target_pairs={{0,1},{1,0},{2,3},{3,2},{4,5},{5,4},{6,7},{7,6},{8,9},{9,8},{10,11... | collective-permute-start | bytes 589832 | tf_op jit(solution)/shard_map/ppermute | solution.py:138
  24.3 1.8 %collective-permute-start.13 = (bf16[32,3072]{1,0:T(8,128)(2,1)S(1)}, bf16[32,3072]{1,0:T(8,128)(2,1)S(1)}, u32[]{:S(2)}, u32[]{:S(2)}) collective-permute-start(bf16[32,3072]{1,0:T(8,128)(2,1)S(1)} %collective-permute-done.12.refs_24_), channel_id=1, source_target_pairs={{0,1},{1,0},{2,3},{3,2},{4,5},{5,4},{6,7},{7,6},{8,9},{9,8},{10,11... | collective-permute-start | bytes 589832 | tf_op jit(solution)/shard_map/ppermute | solution.py:138
  50.9 1.9 %collective-permute-start.14 = (bf16[4,32,2048]{2,1,0:T(8,128)(2,1)S(1)}, bf16[4,32,2048]{2,1,0:T(8,128)(2,1)S(1)}, u32[]{:S(2)}, u32[]{:S(2)}) collective-permute-start(bf16[4,32,2048]{2,1,0:T(8,128)(2,1)S(1)} %get-tuple-element.56), channel_id=1, source_target_pairs={{0,1},{1,0},{2,3},{3,2},{4,5},{5,4},{6,7},{7,6},{8,9},{9,8},{10,11... | collective-permute-start | bytes 1572872 | tf_op jit(solution)/shard_map/ppermute | solution.py:138
  52.8 4.2 %collective-permute-start.18 = (bf16[8,96,768]{2,1,0:T(8,128)(2,1)S(1)}, bf16[8,96,768]{2,1,0:T(8,128)(2,1)S(1)}, u32[]{:S(2)}, u32[]{:S(2)}) collective-permute-start(bf16[8,96,768]{2,1,0:T(8,128)(2,1)S(1)} %get-tuple-element.62), channel_id=1, source_target_pairs={{0,1},{1,0},{2,3},{3,2},{4,5},{5,4},{6,7},{7,6},{8,9},{9,8},{10,11... | collective-permute-start | bytes 3538952 | tf_op jit(solution)/shard_map/ppermute | solution.py:138
  52.9 4.1 %collective-permute-start.19 = (bf16[4,32,2048]{2,1,0:T(8,128)(2,1)S(1)}, bf16[4,32,2048]{2,1,0:T(8,128)(2,1)S(1)}, u32[]{:S(2)}, u32[]{:S(2)}) collective-permute-start(bf16[4,32,2048]{2,1,0:T(8,128)(2,1)S(1)} %get-tuple-element.66), channel_id=1, source_target_pairs={{0,1},{1,0},{2,3},{3,2},{4,5},{5,4},{6,7},{7,6},{8,9},{9,8},{10,11... | collective-permute-start | bytes 1572872 | tf_op jit(solution)/shard_map/ppermute | solution.py:138
  53.4 10.3 %collective-permute-start.17 = (bf16[32,2048]{1,0:T(8,128)(2,1)S(1)}, bf16[32,2048]{1,0:T(8,128)(2,1)S(1)}, u32[]{:S(2)}, u32[]{:S(2)}) collective-permute-start(bf16[32,2048]{1,0:T(8,128)(2,1)S(1)} %get-tuple-element.84), channel_id=1, source_target_pairs={{0,6},{1,7},{2,4},{3,5},{4,2},{5,3},{6,0},{7,1},{8,14},{9,15},{10,... | collective-permute-start | bytes 393224 | tf_op jit(solution)/shard_map/ppermute | solution.py:138
  55.0 10.2 %collective-permute-start.16 = (bf16[32,2048]{1,0:T(8,128)(2,1)S(1)}, bf16[32,2048]{1,0:T(8,128)(2,1)S(1)}, u32[]{:S(2)}, u32[]{:S(2)}) collective-permute-start(bf16[32,2048]{1,0:T(8,128)(2,1)S(1)} %get-tuple-element.85), channel_id=1, source_target_pairs={{0,4},{1,5},{2,6},{3,7},{4,0},{5,1},{6,2},{7,3},{8,12},{9,13},{10,... | collective-permute-start | bytes 393224 | tf_op jit(solution)/shard_map/ppermute | solution.py:138
  55.2 10.0 %collective-permute-start.15 = (bf16[32,2048]{1,0:T(8,128)(2,1)S(1)}, bf16[32,2048]{1,0:T(8,128)(2,1)S(1)}, u32[]{:S(2)}, u32[]{:S(2)}) collective-permute-start(bf16[32,2048]{1,0:T(8,128)(2,1)S(1)} %get-tuple-element.86), channel_id=1, source_target_pairs={{0,2},{1,3},{2,0},{3,1},{4,6},{5,7},{6,4},{7,5},{8,10},{9,11},{10,... | collective-permute-start | bytes 393224 | tf_op jit(solution)/shard_map/ppermute | solution.py:138
  57.1 8.4 %collective-permute-start.21 = (bf16[32,2048]{1,0:T(8,128)(2,1)S(1)}, bf16[32,2048]{1,0:T(8,128)(2,1)S(1)}, u32[]{:S(2)}, u32[]{:S(2)}) collective-permute-start(bf16[32,2048]{1,0:T(8,128)(2,1)S(1)} %get-tuple-element.80), channel_id=1, source_target_pairs={{0,4},{1,5},{2,6},{3,7},{4,0},{5,1},{6,2},{7,3},{8,12},{9,13},{10,... | collective-permute-start | bytes 393224 | tf_op jit(solution)/shard_map/ppermute | solution.py:138
  58.7 7.3 %collective-permute-start.20 = (bf16[32,2048]{1,0:T(8,128)(2,1)S(1)}, bf16[32,2048]{1,0:T(8,128)(2,1)S(1)}, u32[]{:S(2)}, u32[]{:S(2)}) collective-permute-start(bf16[32,2048]{1,0:T(8,128)(2,1)S(1)} %get-tuple-element.81), channel_id=1, source_target_pairs={{0,2},{1,3},{2,0},{3,1},{4,6},{5,7},{6,4},{7,5},{8,10},{9,11},{10,... | collective-permute-start | bytes 393224 | tf_op jit(solution)/shard_map/ppermute | solution.py:138
  59.2 6.8 %copy-start = (bf16[1,32,2048]{2,1,0:T(8,128)(2,1)S(1)}, bf16[1,32,2048]{2,1,0:T(8,128)(2,1)}, u32[]{:S(2)}) copy-start(bf16[1,32,2048]{2,1,0:T(8,128)(2,1)} %param.8) | copy-start | bytes 393220
  63.7 8.6 %collective-permute-start.23 = (bf16[32,2048]{1,0:T(8,128)(2,1)S(1)}, bf16[32,2048]{1,0:T(8,128)(2,1)S(1)}, u32[]{:S(2)}, u32[]{:S(2)}) collective-permute-start(bf16[32,2048]{1,0:T(8,128)(2,1)S(1)} %get-tuple-element.79), channel_id=1, source_target_pairs={{0,6},{1,7},{2,4},{3,5},{4,2},{5,3},{6,0},{7,1},{8,14},{9,15},{10,... | collective-permute-start | bytes 393224 | tf_op jit(solution)/shard_map/ppermute | solution.py:138
  66.1 7.0 %copy-start.1 = (bf16[1,32,2048]{2,1,0:T(8,128)(2,1)S(1)}, bf16[1,32,2048]{2,1,0:T(8,128)(2,1)}, u32[]{:S(2)}) copy-start(bf16[1,32,2048]{2,1,0:T(8,128)(2,1)} %param.10) | copy-start | bytes 393220
  66.1 7.0 %collective-permute-start.22 = (bf16[32,2048]{1,0:T(8,128)(2,1)S(1)}, bf16[32,2048]{1,0:T(8,128)(2,1)S(1)}, u32[]{:S(2)}, u32[]{:S(2)}) collective-permute-start(bf16[32,2048]{1,0:T(8,128)(2,1)S(1)} %add_convert_fusion.1), channel_id=1, source_target_pairs={{0,8},{8,16},{16,24},{24,0},{1,9},{9,17},{17,25},{25,1},{2,10},{10... | collective-permute-start | bytes 393224 | tf_op jit(solution)/shard_map/ppermute | solution.py:21
  73.2 5.0 %collective-permute-start.24 = (bf16[32,2048]{1,0:T(8,128)(2,1)S(1)}, bf16[32,2048]{1,0:T(8,128)(2,1)S(1)}, u32[]{:S(2)}, u32[]{:S(2)}) collective-permute-start(bf16[32,2048]{1,0:T(8,128)(2,1)S(1)} %add_convert_fusion), channel_id=1, source_target_pairs={{0,24},{8,0},{16,8},{24,16},{1,25},{9,1},{17,9},{25,17},{2,26},{10... | collective-permute-start | bytes 393224 | tf_op jit(solution)/shard_map/ppermute | solution.py:21

commit v11 on v10

--- a/solution.py
+++ b/solution.py
@@ -155,25 +155,27 @@
     for copy in copies:
         copy.wait()
     back_routes, back_gates, fore_routes, fore_gates = held
-    notes[...] = jnp.zeros_like(notes)
-    for place, (routes, gates) in enumerate(((back_routes, back_gates), (fore_routes, fore_gates))):
+    for place, (target, lane, routes, gates) in enumerate(
+        ((two, half + width, back_routes, back_gates), (one, width + half, fore_routes, fore_gates))
+    ):
         first = place * 4 * top
+        notes[...] = jnp.zeros_like(notes)
         notes[pl.ds(first, top), 0:size] = routes[...].astype(jnp.float32)
         rest = gates[...]
         for term in range(1, 4):
             part = rest.astype(jnp.bfloat16).astype(jnp.float32)
             notes[pl.ds(first + term * top, top), 0:size] = part
             rest = rest - part
-    one[:, pl.ds(width + half, LANES)] = notes[...].T[:size, :].astype(jnp.bfloat16)
+        target[:, pl.ds(lane, LANES)] = notes[...].T[:size, :].astype(jnp.bfloat16)
 
 
 def picks_kernel(count, top, slots, devices, place_ref, *refs):
-    blocks, outs, (notes, turned) = refs[:devices], refs[devices:-2], refs[-2:]
+    blocks, outs, (notes, turned) = refs[: 2 * devices], refs[2 * devices : -2], refs[-2:]
     tokens = notes.shape[0]
-    for code, block in enumerate(blocks):
-        size = block.shape[0]
+    for code, (one, two) in enumerate(zip(blocks[:devices], blocks[devices:])):
+        size = one.shape[0]
         rows = pl.ds(pl.multiple_of(place_ref[3 + code], size), size)
-        notes[rows, :] = block[...].astype(jnp.float32)
+        notes[rows, :] = one[...].astype(jnp.float32) + two[...].astype(jnp.float32)
     turned[...] = notes[...].T
     row = lax.broadcasted_iota(jnp.int32, (tokens, tokens), 0)
     column = lax.broadcasted_iota(jnp.int32, (tokens, tokens), 1)
@@ -361,15 +363,14 @@
         ).astype(picks.dtype)
         scale = jnp.sum(jnp.where(grads, gate, 0.0), axis=0, keepdims=True)
         scales.append(jnp.where(is_saved, 1.0, scale))
-    for step in range(0, number, 2):
-        lanes = pl.ds(step * LANES, 2 * LANES)
-        scale = jnp.concatenate(scales[step : step + 2], axis=1)
-        rows[:, lanes] = (
-            jnp.dot(turned[...], picks[:, lanes], preferred_element_type=jnp.float32) * scale
-        ).astype(rows.dtype)
-
     leaving = []
     for step in range(number):
+        if step % 2 == 0:
+            lanes = pl.ds(step * LANES, 2 * LANES)
+            scale = jnp.concatenate(scales[step : step + 2], axis=1)
+            rows[:, lanes] = (
+                jnp.dot(turned[...], picks[:, lanes], preferred_element_type=jnp.float32) * scale
+            ).astype(rows.dtype)
         for start in range(0, half, CHUNK):
             chunk = pl.ds(start, CHUNK)
             for corner in range(start, start + CHUNK, LANES):
@@ -459,9 +460,8 @@
         return functools.reduce(jnp.add, [block.astype(jnp.float32) for block in blocks])
 
     packed = [
-        jax.ShapeDtypeStruct((token_count, 3 * width // 2 + extra), jnp.bfloat16)
-        for extra in (LANES, 0)
-    ]
+        jax.ShapeDtypeStruct((token_count, 3 * width // 2 + LANES), jnp.bfloat16)
+    ] * 2
     own = pl.pallas_call(
         pack_kernel,
         in_specs=[pl.BlockSpec(memory_space=pl.ANY)] * 7,
@@ -520,11 +520,12 @@
         functools.partial(picks_kernel, count, top, slots, devices),
         "slot_picks",
         1,
-        [pl.BlockSpec((token_count, LANES), lambda *_: (0, 3 * width // 2 // LANES))] * devices,
+        [pl.BlockSpec((token_count, LANES), lambda *_: (0, 3 * width // 2 // LANES))]
+        * (2 * devices),
         [whole(out.shape) for out in pick_outs],
         pick_outs,
         [pltpu.VMEM((total, LANES), jnp.float32), pltpu.VMEM((LANES, total), jnp.float32)],
-    )(place, *blocks[:devices])
+    )(place, *blocks)
 
     pass_flops = 2 * 2 * count * CHUNK * width * inner_width
     near_part = jax.ShapeDtypeStruct((token_count, width), jnp.bfloat16)

time: 79.7 us -> 78.1 us (0.980)
  waiting for transfers between devices: 20.9 us -> 16.5 us
  starting transfers between devices: 20 us -> 21.8 us
  Pallas kernels: 36 us -> 37 us
    ppermute x23, waiting for transfers between devices: 16.8 us -> 12.6 us  [swapped(): lax.ppermute(value, axes, [(source, source ^ code) for source in range(co...]
    ppermute x23, starting transfers between devices: 16.6 us -> 18.2 us  [swapped(): lax.ppermute(value, axes, [(source, source ^ code) for source in range(co...]
    pallas_call x2, Pallas kernels: 8.9 us -> 9.87 us  [gradient(): pl.pallas_call(functools.partial(weight_kernel, first, number, count, slo...]
  transfers between devices with their start and end apart: 25 -> 25, of which waited for: 9 -> 11; matrix products, arithmetic and copies ran while one was open for 1% -> 1% of each run, Pallas kernels for 13% -> 13%
where the time goes in v11:
time: 78.1 us; the launch traced here: 77.9 us
  Pallas kernels  37 us (47%)
  starting transfers between devices  21.8 us (28%)
  waiting for transfers between devices  16.5 us (21%)
  local copies, waits for them, and re-layouts  1.41 us (2%)
    pallas_call x1, Pallas kernels, gathered_plan(): pl.pallas_call(functools.partial(expert_kernel, count, slots, devices, pa...  24.8 us
    ppermute x23, starting transfers between devices, swapped(): lax.ppermute(value, axes, [(source, source ^ code) for source in range(co...  18.2 us
    ppermute x23, waiting for transfers between devices, swapped(): lax.ppermute(value, axes, [(source, source ^ code) for source in range(co...  12.6 us
    pallas_call x2, Pallas kernels, gradient(): pl.pallas_call(functools.partial(weight_kernel, first, number, count, slo...  9.87 us
    ppermute x2, waiting for transfers between devices, shifted(): return lax.ppermute(value, axis, pairs)  3.88 us
    ppermute x2, starting transfers between devices, shifted(): return lax.ppermute(value, axis, pairs)  3.6 us
  transfers between devices with their start and end apart: 25, of which 11 were waited for; matrix products, arithmetic and copies ran while one was open for 1% of the time, Pallas kernels for 13%

profile of v11, /device:TPU:0, one launch (start us, length us, event | category | flops | bytes accessed | tf_op | source)
XLA Modules:
  0.0 77.9 jit_solution(5996257797486908270)
XLA Ops:
  0.6 1.2 %pack.1 = (bf16[32,3200]{1,0:T(8,128)(2,1)S(1)}, bf16[32,3200]{1,0:T(8,128)(2,1)S(1)}) custom-call(bf16[32,2048]{1,0:T(8,128)(2,1)} %bitcast.69, bf16[32,2048]{1,0:T(8,128)(2,1)} %bitcast.71, bf16[32,2048]{1,0:T(8,128)(2,1)} %bitcast.70, s32[8,32]{1,0:T(8,128)} %bitcast.74, f32[8,32]{1,0:T(8,128)} %bitcast.75, s32[8,32]{1,0:T(8,128)} %bitcast.76, ...), custom_call_target="tpu_custom_call" | custom-call | tf_op jit(solution)/shard_map/pack/pallas_call | solution.py:465
  1.8 3.0 %collective-permute-start.1 = (bf16[32,3200]{1,0:T(8,128)(2,1)S(1)}, bf16[32,3200]{1,0:T(8,128)(2,1)S(1)}, u32[]{:S(2)}, u32[]{:S(2)}) collective-permute-start(bf16[32,3200]{1,0:T(8,128)(2,1)S(1)} %get-tuple-element.41.refs_0_.refs_10_), channel_id=1, source_target_pairs={{0,2},{1,3},{2,0},{3,1},{4,6},{5,7},{6,4},{7,5},{8,10},{9,11},{10,... | collective-permute-start | bytes 614408 | tf_op jit(solution)/shard_map/ppermute | solution.py:138
  4.8 0.0 collective-permute-start
  4.8 0.5 collective-permute-start.9
  5.4 1.5 %collective-permute-start.4 = (bf16[32,3200]{1,0:T(8,128)(2,1)S(1)}, bf16[32,3200]{1,0:T(8,128)(2,1)S(1)}, u32[]{:S(2)}, u32[]{:S(2)}) collective-permute-start(bf16[32,3200]{1,0:T(8,128)(2,1)S(1)} %get-tuple-element.42.refs_8_.refs_18_), channel_id=1, source_target_pairs={{0,4},{1,5},{2,6},{3,7},{4,0},{5,1},{6,2},{7,3},{8,12},{9,13},{10,... | collective-permute-start | bytes 614408 | tf_op jit(solution)/shard_map/ppermute | solution.py:138
  6.9 0.5 collective-permute-start.2
  7.4 2.5 %collective-permute-done.1.refs_2_.refs_12_ = bf16[32,3200]{1,0:T(8,128)(2,1)S(1)} collective-permute-done((bf16[32,3200]{1,0:T(8,128)(2,1)S(1)}, bf16[32,3200]{1,0:T(8,128)(2,1)S(1)}, u32[]{:S(2)}, u32[]{:S(2)}) %collective-permute-start.1) | collective-permute-done | bytes 204832 | tf_op jit(solution)/shard_map/ppermute | solution.py:138
  9.9 1.7 %collective-permute-start.3 = (bf16[32,3200]{1,0:T(8,128)(2,1)S(1)}, bf16[32,3200]{1,0:T(8,128)(2,1)S(1)}, u32[]{:S(2)}, u32[]{:S(2)}) collective-permute-start(bf16[32,3200]{1,0:T(8,128)(2,1)S(1)} %get-tuple-element.42.refs_8_.refs_18_), channel_id=1, source_target_pairs={{0,2},{1,3},{2,0},{3,1},{4,6},{5,7},{6,4},{7,5},{8,10},{9,11},{10,... | collective-permute-start | bytes 614408 | tf_op jit(solution)/shard_map/ppermute | solution.py:138
  11.7 0.0 collective-permute-done.refs_1_.refs_11_
  11.7 1.5 %collective-permute-start.7 = (bf16[32,3200]{1,0:T(8,128)(2,1)S(1)}, bf16[32,3200]{1,0:T(8,128)(2,1)S(1)}, u32[]{:S(2)}, u32[]{:S(2)}) collective-permute-start(bf16[32,3200]{1,0:T(8,128)(2,1)S(1)} %collective-permute-done.1.refs_2_.refs_12_), channel_id=1, source_target_pairs={{0,4},{1,5},{2,6},{3,7},{4,0},{5,1},{6,2},{7,3},{8,12},{9,13},{10,... | collective-permute-start | bytes 614408 | tf_op jit(solution)/shard_map/ppermute | solution.py:138
  13.2 0.0 collective-permute-done.9.refs_9_.refs_19_
  13.2 0.1 collective-permute-done.4.refs_12_.refs_22_
  13.3 0.4 collective-permute-start.12
  13.7 4.0 %collective-permute-done.2.refs_4_.refs_14_ = bf16[32,3200]{1,0:T(8,128)(2,1)S(1)} collective-permute-done((bf16[32,3200]{1,0:T(8,128)(2,1)S(1)}, bf16[32,3200]{1,0:T(8,128)(2,1)S(1)}, u32[]{:S(2)}, u32[]{:S(2)}) %collective-permute-start.2) | collective-permute-done | bytes 204832 | tf_op jit(solution)/shard_map/ppermute | solution.py:138
  17.7 0.2 collective-permute-done.3.refs_10_.refs_20_
  17.9 0.0 collective-permute-start.5
  17.9 0.5 collective-permute-start.6
  18.4 0.0 collective-permute-start.10
  18.4 2.7 %collective-permute-done.7.refs_6_.refs_16_ = bf16[32,3200]{1,0:T(8,128)(2,1)S(1)} collective-permute-done((bf16[32,3200]{1,0:T(8,128)(2,1)S(1)}, bf16[32,3200]{1,0:T(8,128)(2,1)S(1)}, u32[]{:S(2)}, u32[]{:S(2)}) %collective-permute-start.7) | collective-permute-done | bytes 204832 | tf_op jit(solution)/shard_map/ppermute | solution.py:138
  21.1 0.0 collective-permute-start.11
  21.1 0.0 collective-permute-done.12.refs_14_.refs_24_
  21.1 0.5 collective-permute-start.8
  21.6 0.0 collective-permute-done.5.refs_3_.refs_13_
  21.6 0.1 collective-permute-start.13
  21.7 0.1 stack.47.place_ref
  21.8 0.0 collective-permute-done.6.refs_5_.refs_15_
  21.8 0.0 collective-permute-done.10.refs_11_.refs_21_
  21.8 0.8 collective-permute-done.11.refs_13_.refs_23_
  22.6 0.3 collective-permute-done.8.refs_7_.refs_17_
  22.9 0.3 collective-permute-done.13.refs_15_.refs_25_
  23.2 1.1 %slot_picks.1 = (bf16[384,256]{1,0:T(8,128)(2,1)S(1)}, f32[384,128]{1,0:T(8,128)S(1)}, bf16[256,384]{1,0:T(8,128)(2,1)S(1)}, bf16[384,256]{1,0:T(8,128)(2,1)S(1)...) custom-call(s32[11]{0:T(128)S(1)} %stack.47.place_ref, ...), custom_call_target="tpu_custom_call" | custom-call | bytes 1024 | tf_op jit(solution)/shard_map/slot_picks/pallas_call | solution.py:519
  24.3 24.8 %experts.1 = (bf16[32,2048]{1,0:T(8,128)(2,1)S(1)}, bf16[32,2048]{1,0:T(8,128)(2,1)S(1)}, bf16[32,2048]{1,0:T(8,128)(2,1)S(1)}, bf16[32,2048]{1,0:T(8,128)(2,1)S...) custom-call(s32[11]{0:T(128)S(1)} %stack.47.place_ref, ...), custom_call_target="tpu_custom_call" | custom-call | flops 12884901888 | bytes 25165824 | tf_op jit(solution)/shard_map/experts/pallas_call | solution.py:541
  49.1 0.2 collective-permute-start.14
  49.3 1.7 %collective-permute-done.14 = bf16[4,32,2048]{2,1,0:T(8,128)(2,1)S(1)} collective-permute-done((bf16[4,32,2048]{2,1,0:T(8,128)(2,1)S(1)}, bf16[4,32,2048]{2,1,0:T(8,128)(2,1)S(1)}, u32[]{:S(2)}, u32[]{:S(2)}) %collective-permute-start.14) | collective-permute-done | bytes 524320 | tf_op jit(solution)/shard_map/ppermute | solution.py:138
  51.0 0.2 collective-permute-start.18
  51.2 0.3 collective-permute-start.19
  51.5 0.1 fusion.7
  51.6 1.6 %collective-permute-start.17 = (bf16[32,2048]{1,0:T(8,128)(2,1)S(1)}, bf16[32,2048]{1,0:T(8,128)(2,1)S(1)}, u32[]{:S(2)}, u32[]{:S(2)}) collective-permute-start(bf16[32,2048]{1,0:T(8,128)(2,1)S(1)} %get-tuple-element.84), channel_id=1, source_target_pairs={{0,6},{1,7},{2,4},{3,5},{4,2},{5,3},{6,0},{7,1},{8,14},{9,15},{10,... | collective-permute-start | bytes 393224 | tf_op jit(solution)/shard_map/ppermute | solution.py:138
  53.3 0.5 collective-permute-start.16
  53.8 1.4 %collective-permute-start.15 = (bf16[32,2048]{1,0:T(8,128)(2,1)S(1)}, bf16[32,2048]{1,0:T(8,128)(2,1)S(1)}, u32[]{:S(2)}, u32[]{:S(2)}) collective-permute-start(bf16[32,2048]{1,0:T(8,128)(2,1)S(1)} %get-tuple-element.86), channel_id=1, source_target_pairs={{0,2},{1,3},{2,0},{3,1},{4,6},{5,7},{6,4},{7,5},{8,10},{9,11},{10,... | collective-permute-start | bytes 393224 | tf_op jit(solution)/shard_map/ppermute | solution.py:138
  55.2 0.0 collective-permute-done.19
  55.2 0.0 collective-permute-done.18.refs_1_
  55.2 0.1 fusion
  55.3 1.6 %collective-permute-start.21 = (bf16[32,2048]{1,0:T(8,128)(2,1)S(1)}, bf16[32,2048]{1,0:T(8,128)(2,1)S(1)}, u32[]{:S(2)}, u32[]{:S(2)}) collective-permute-start(bf16[32,2048]{1,0:T(8,128)(2,1)S(1)} %get-tuple-element.80), channel_id=1, source_target_pairs={{0,4},{1,5},{2,6},{3,7},{4,0},{5,1},{6,2},{7,3},{8,12},{9,13},{10,... | collective-permute-start | bytes 393224 | tf_op jit(solution)/shard_map/ppermute | solution.py:138
  56.9 0.6 collective-permute-start.20
  57.5 4.9 %weight_gradient_0.1.refs_3_ = bf16[16,1024,768]{2,1,0:T(8,128)(2,1)} custom-call(s32[11]{0:T(128)S(1)} %stack.47.place_ref, f32[256,128]{1,0:T(8,128)S(1)} %get-tuple-element.60.refs_0_, bf16[8,96,768]{2,1,0:T(8,128)(2,1)S(1)} %collective-permute-done.18.refs_1_, bf16[1024,512]{1,0:T(8,128)(2,1)S(1)} %get-tuple-element.63.refs_2_, ...), custom_call_target="tpu_custom_call", output_to_operand_aliasing={{}: (4, {})} | custom-call | flops 3221225472 | bytes 12582912 | tf_op jit(solution)/shard_map/weight_gradient_0/pallas_call | solution.py:587
  62.5 0.0 collective-permute-done.17
  62.5 1.4 %collective-permute-start.23 = (bf16[32,2048]{1,0:T(8,128)(2,1)S(1)}, bf16[32,2048]{1,0:T(8,128)(2,1)S(1)}, u32[]{:S(2)}, u32[]{:S(2)}) collective-permute-start(bf16[32,2048]{1,0:T(8,128)(2,1)S(1)} %get-tuple-element.79), channel_id=1, source_target_pairs={{0,6},{1,7},{2,4},{3,5},{4,2},{5,3},{6,0},{7,1},{8,14},{9,15},{10,... | collective-permute-start | bytes 393224 | tf_op jit(solution)/shard_map/ppermute | solution.py:138
  63.9 0.0 collective-permute-done.16
  63.9 0.0 collective-permute-done.15
  63.9 0.0 collective-permute-done.21
  63.9 0.0 collective-permute-done.20
  64.0 0.0 copy-done
  64.0 0.1 add_convert_fusion.1
  64.1 0.0 copy-start.1
  64.1 1.8 %collective-permute-start.22 = (bf16[32,2048]{1,0:T(8,128)(2,1)S(1)}, bf16[32,2048]{1,0:T(8,128)(2,1)S(1)}, u32[]{:S(2)}, u32[]{:S(2)}) collective-permute-start(bf16[32,2048]{1,0:T(8,128)(2,1)S(1)} %add_convert_fusion.1), channel_id=1, source_target_pairs={{0,8},{8,16},{16,24},{24,0},{1,9},{9,17},{17,25},{25,1},{2,10},{10... | collective-permute-start | bytes 393224 | tf_op jit(solution)/shard_map/ppermute | solution.py:21
  65.9 4.9 %weight_gradient_4.1 = bf16[16,1024,768]{2,1,0:T(8,128)(2,1)} custom-call(s32[11]{0:T(128)S(1)} %stack.47.place_ref, f32[256,128]{1,0:T(8,128)S(1)} %get-tuple-element.60.refs_0_, bf16[8,96,768]{2,1,0:T(8,128)(2,1)S(1)} %collective-permute-done.18.refs_1_, bf16[1024,512]{1,0:T(8,128)(2,1)S(1)} %get-tuple-element.63.refs_2_, ...), custom_call_target="tpu_custom_call", output_to_operand_aliasing={{}: (4, {})} | custom-call | flops 3221225472 | bytes 12582912 | tf_op jit(solution)/shard_map/weight_gradient_4/pallas_call | solution.py:587
  70.8 0.0 collective-permute-done.23
  70.8 0.7 collective-permute-done.22
  71.5 0.1 add_convert_fusion
  71.6 1.8 %collective-permute-start.24 = (bf16[32,2048]{1,0:T(8,128)(2,1)S(1)}, bf16[32,2048]{1,0:T(8,128)(2,1)S(1)}, u32[]{:S(2)}, u32[]{:S(2)}) collective-permute-start(bf16[32,2048]{1,0:T(8,128)(2,1)S(1)} %add_convert_fusion), channel_id=1, source_target_pairs={{0,24},{8,0},{16,8},{24,16},{1,25},{9,1},{17,9},{25,17},{2,26},{10... | collective-permute-start | bytes 393224 | tf_op jit(solution)/shard_map/ppermute | solution.py:21
  73.4 3.2 %collective-permute-done.24 = bf16[32,2048]{1,0:T(8,128)(2,1)S(1)} collective-permute-done((bf16[32,2048]{1,0:T(8,128)(2,1)S(1)}, bf16[32,2048]{1,0:T(8,128)(2,1)S(1)}, u32[]{:S(2)}, u32[]{:S(2)}) %collective-permute-start.24) | collective-permute-done | bytes 131104 | tf_op jit(solution)/shard_map/ppermute | solution.py:21
  76.6 0.7 copy.17
  77.3 0.7 copy.18
  (2 shorter events, 0.0 us)
Async XLA Ops:
  1.8 8.1 %collective-permute-start.1 = (bf16[32,3200]{1,0:T(8,128)(2,1)S(1)}, bf16[32,3200]{1,0:T(8,128)(2,1)S(1)}, u32[]{:S(2)}, u32[]{:S(2)}) collective-permute-start(bf16[32,3200]{1,0:T(8,128)(2,1)S(1)} %get-tuple-element.41.refs_0_.refs_10_), channel_id=1, source_target_pairs={{0,2},{1,3},{2,0},{3,1},{4,6},{5,7},{6,4},{7,5},{8,10},{9,11},{10,... | collective-permute-start | bytes 614408 | tf_op jit(solution)/shard_map/ppermute | solution.py:138
  4.8 6.8 %collective-permute-start = (bf16[32,3200]{1,0:T(8,128)(2,1)S(1)}, bf16[32,3200]{1,0:T(8,128)(2,1)S(1)}, u32[]{:S(2)}, u32[]{:S(2)}) collective-permute-start(bf16[32,3200]{1,0:T(8,128)(2,1)S(1)} %get-tuple-element.41.refs_0_.refs_10_), channel_id=1, source_target_pairs={{0,1},{1,0},{2,3},{3,2},{4,5},{5,4},{6,7},{7,6},{8,9},{9,8},{10,11... | collective-permute-start | bytes 614408 | tf_op jit(solution)/shard_map/ppermute | solution.py:138
  4.8 8.4 %collective-permute-start.9 = (bf16[32,3200]{1,0:T(8,128)(2,1)S(1)}, bf16[32,3200]{1,0:T(8,128)(2,1)S(1)}, u32[]{:S(2)}, u32[]{:S(2)}) collective-permute-start(bf16[32,3200]{1,0:T(8,128)(2,1)S(1)} %get-tuple-element.42.refs_8_.refs_18_), channel_id=1, source_target_pairs={{0,1},{1,0},{2,3},{3,2},{4,5},{5,4},{6,7},{7,6},{8,9},{9,8},{10,11... | collective-permute-start | bytes 614408 | tf_op jit(solution)/shard_map/ppermute | solution.py:138
  5.4 7.9 %collective-permute-start.4 = (bf16[32,3200]{1,0:T(8,128)(2,1)S(1)}, bf16[32,3200]{1,0:T(8,128)(2,1)S(1)}, u32[]{:S(2)}, u32[]{:S(2)}) collective-permute-start(bf16[32,3200]{1,0:T(8,128)(2,1)S(1)} %get-tuple-element.42.refs_8_.refs_18_), channel_id=1, source_target_pairs={{0,4},{1,5},{2,6},{3,7},{4,0},{5,1},{6,2},{7,3},{8,12},{9,13},{10,... | collective-permute-start | bytes 614408 | tf_op jit(solution)/shard_map/ppermute | solution.py:138
  6.9 10.8 %collective-permute-start.2 = (bf16[32,3200]{1,0:T(8,128)(2,1)S(1)}, bf16[32,3200]{1,0:T(8,128)(2,1)S(1)}, u32[]{:S(2)}, u32[]{:S(2)}) collective-permute-start(bf16[32,3200]{1,0:T(8,128)(2,1)S(1)} %get-tuple-element.41.refs_0_.refs_10_), channel_id=1, source_target_pairs={{0,4},{1,5},{2,6},{3,7},{4,0},{5,1},{6,2},{7,3},{8,12},{9,13},{10,... | collective-permute-start | bytes 614408 | tf_op jit(solution)/shard_map/ppermute | solution.py:138
  9.9 8.0 %collective-permute-start.3 = (bf16[32,3200]{1,0:T(8,128)(2,1)S(1)}, bf16[32,3200]{1,0:T(8,128)(2,1)S(1)}, u32[]{:S(2)}, u32[]{:S(2)}) collective-permute-start(bf16[32,3200]{1,0:T(8,128)(2,1)S(1)} %get-tuple-element.42.refs_8_.refs_18_), channel_id=1, source_target_pairs={{0,2},{1,3},{2,0},{3,1},{4,6},{5,7},{6,4},{7,5},{8,10},{9,11},{10,... | collective-permute-start | bytes 614408 | tf_op jit(solution)/shard_map/ppermute | solution.py:138
  11.7 9.5 %collective-permute-start.7 = (bf16[32,3200]{1,0:T(8,128)(2,1)S(1)}, bf16[32,3200]{1,0:T(8,128)(2,1)S(1)}, u32[]{:S(2)}, u32[]{:S(2)}) collective-permute-start(bf16[32,3200]{1,0:T(8,128)(2,1)S(1)} %collective-permute-done.1.refs_2_.refs_12_), channel_id=1, source_target_pairs={{0,4},{1,5},{2,6},{3,7},{4,0},{5,1},{6,2},{7,3},{8,12},{9,13},{10,... | collective-permute-start | bytes 614408 | tf_op jit(solution)/shard_map/ppermute | solution.py:138
  13.3 7.8 %collective-permute-start.12 = (bf16[32,3200]{1,0:T(8,128)(2,1)S(1)}, bf16[32,3200]{1,0:T(8,128)(2,1)S(1)}, u32[]{:S(2)}, u32[]{:S(2)}) collective-permute-start(bf16[32,3200]{1,0:T(8,128)(2,1)S(1)} %collective-permute-done.4.refs_12_.refs_22_), channel_id=1, source_target_pairs={{0,2},{1,3},{2,0},{3,1},{4,6},{5,7},{6,4},{7,5},{8,10},{9,11},{10,... | collective-permute-start | bytes 614408 | tf_op jit(solution)/shard_map/ppermute | solution.py:138
  17.9 3.7 %collective-permute-start.5 = (bf16[32,3200]{1,0:T(8,128)(2,1)S(1)}, bf16[32,3200]{1,0:T(8,128)(2,1)S(1)}, u32[]{:S(2)}, u32[]{:S(2)}) collective-permute-start(bf16[32,3200]{1,0:T(8,128)(2,1)S(1)} %collective-permute-done.1.refs_2_.refs_12_), channel_id=1, source_target_pairs={{0,1},{1,0},{2,3},{3,2},{4,5},{5,4},{6,7},{7,6},{8,9},{9,8},{10,11... | collective-permute-start | bytes 614408 | tf_op jit(solution)/shard_map/ppermute | solution.py:138
  17.9 3.9 %collective-permute-start.6 = (bf16[32,3200]{1,0:T(8,128)(2,1)S(1)}, bf16[32,3200]{1,0:T(8,128)(2,1)S(1)}, u32[]{:S(2)}, u32[]{:S(2)}) collective-permute-start(bf16[32,3200]{1,0:T(8,128)(2,1)S(1)} %collective-permute-done.2.refs_4_.refs_14_), channel_id=1, source_target_pairs={{0,1},{1,0},{2,3},{3,2},{4,5},{5,4},{6,7},{7,6},{8,9},{9,8},{10,11... | collective-permute-start | bytes 614408 | tf_op jit(solution)/shard_map/ppermute | solution.py:138
  18.4 3.4 %collective-permute-start.10 = (bf16[32,3200]{1,0:T(8,128)(2,1)S(1)}, bf16[32,3200]{1,0:T(8,128)(2,1)S(1)}, u32[]{:S(2)}, u32[]{:S(2)}) collective-permute-start(bf16[32,3200]{1,0:T(8,128)(2,1)S(1)} %collective-permute-done.3.refs_10_.refs_20_), channel_id=1, source_target_pairs={{0,1},{1,0},{2,3},{3,2},{4,5},{5,4},{6,7},{7,6},{8,9},{9,8},{10,11... | collective-permute-start | bytes 614408 | tf_op jit(solution)/shard_map/ppermute | solution.py:138
  21.1 1.5 %collective-permute-start.11 = (bf16[32,3200]{1,0:T(8,128)(2,1)S(1)}, bf16[32,3200]{1,0:T(8,128)(2,1)S(1)}, u32[]{:S(2)}, u32[]{:S(2)}) collective-permute-start(bf16[32,3200]{1,0:T(8,128)(2,1)S(1)} %collective-permute-done.4.refs_12_.refs_22_), channel_id=1, source_target_pairs={{0,1},{1,0},{2,3},{3,2},{4,5},{5,4},{6,7},{7,6},{8,9},{9,8},{10,11... | collective-permute-start | bytes 614408 | tf_op jit(solution)/shard_map/ppermute | solution.py:138
  21.1 1.7 %collective-permute-start.8 = (bf16[32,3200]{1,0:T(8,128)(2,1)S(1)}, bf16[32,3200]{1,0:T(8,128)(2,1)S(1)}, u32[]{:S(2)}, u32[]{:S(2)}) collective-permute-start(bf16[32,3200]{1,0:T(8,128)(2,1)S(1)} %collective-permute-done.7.refs_6_.refs_16_), channel_id=1, source_target_pairs={{0,1},{1,0},{2,3},{3,2},{4,5},{5,4},{6,7},{7,6},{8,9},{9,8},{10,11... | collective-permute-start | bytes 614408 | tf_op jit(solution)/shard_map/ppermute | solution.py:138
  21.6 1.5 %collective-permute-start.13 = (bf16[32,3200]{1,0:T(8,128)(2,1)S(1)}, bf16[32,3200]{1,0:T(8,128)(2,1)S(1)}, u32[]{:S(2)}, u32[]{:S(2)}) collective-permute-start(bf16[32,3200]{1,0:T(8,128)(2,1)S(1)} %collective-permute-done.12.refs_14_.refs_24_), channel_id=1, source_target_pairs={{0,1},{1,0},{2,3},{3,2},{4,5},{5,4},{6,7},{7,6},{8,9},{9,8},{10,11... | collective-permute-start | bytes 614408 | tf_op jit(solution)/shard_map/ppermute | solution.py:138
  49.1 1.9 %collective-permute-start.14 = (bf16[4,32,2048]{2,1,0:T(8,128)(2,1)S(1)}, bf16[4,32,2048]{2,1,0:T(8,128)(2,1)S(1)}, u32[]{:S(2)}, u32[]{:S(2)}) collective-permute-start(bf16[4,32,2048]{2,1,0:T(8,128)(2,1)S(1)} %get-tuple-element.56), channel_id=1, source_target_pairs={{0,1},{1,0},{2,3},{3,2},{4,5},{5,4},{6,7},{7,6},{8,9},{9,8},{10,11... | collective-permute-start | bytes 1572872 | tf_op jit(solution)/shard_map/ppermute | solution.py:138
  51.0 4.2 %collective-permute-start.18 = (bf16[8,96,768]{2,1,0:T(8,128)(2,1)S(1)}, bf16[8,96,768]{2,1,0:T(8,128)(2,1)S(1)}, u32[]{:S(2)}, u32[]{:S(2)}) collective-permute-start(bf16[8,96,768]{2,1,0:T(8,128)(2,1)S(1)} %get-tuple-element.62), channel_id=1, source_target_pairs={{0,1},{1,0},{2,3},{3,2},{4,5},{5,4},{6,7},{7,6},{8,9},{9,8},{10,11... | collective-permute-start | bytes 3538952 | tf_op jit(solution)/shard_map/ppermute | solution.py:138
  51.2 4.0 %collective-permute-start.19 = (bf16[4,32,2048]{2,1,0:T(8,128)(2,1)S(1)}, bf16[4,32,2048]{2,1,0:T(8,128)(2,1)S(1)}, u32[]{:S(2)}, u32[]{:S(2)}) collective-permute-start(bf16[4,32,2048]{2,1,0:T(8,128)(2,1)S(1)} %get-tuple-element.66), channel_id=1, source_target_pairs={{0,1},{1,0},{2,3},{3,2},{4,5},{5,4},{6,7},{7,6},{8,9},{9,8},{10,11... | collective-permute-start | bytes 1572872 | tf_op jit(solution)/shard_map/ppermute | solution.py:138
  51.6 10.8 %collective-permute-start.17 = (bf16[32,2048]{1,0:T(8,128)(2,1)S(1)}, bf16[32,2048]{1,0:T(8,128)(2,1)S(1)}, u32[]{:S(2)}, u32[]{:S(2)}) collective-permute-start(bf16[32,2048]{1,0:T(8,128)(2,1)S(1)} %get-tuple-element.84), channel_id=1, source_target_pairs={{0,6},{1,7},{2,4},{3,5},{4,2},{5,3},{6,0},{7,1},{8,14},{9,15},{10,... | collective-permute-start | bytes 393224 | tf_op jit(solution)/shard_map/ppermute | solution.py:138
  53.3 10.7 %collective-permute-start.16 = (bf16[32,2048]{1,0:T(8,128)(2,1)S(1)}, bf16[32,2048]{1,0:T(8,128)(2,1)S(1)}, u32[]{:S(2)}, u32[]{:S(2)}) collective-permute-start(bf16[32,2048]{1,0:T(8,128)(2,1)S(1)} %get-tuple-element.85), channel_id=1, source_target_pairs={{0,4},{1,5},{2,6},{3,7},{4,0},{5,1},{6,2},{7,3},{8,12},{9,13},{10,... | collective-permute-start | bytes 393224 | tf_op jit(solution)/shard_map/ppermute | solution.py:138
  53.8 10.2 %collective-permute-start.15 = (bf16[32,2048]{1,0:T(8,128)(2,1)S(1)}, bf16[32,2048]{1,0:T(8,128)(2,1)S(1)}, u32[]{:S(2)}, u32[]{:S(2)}) collective-permute-start(bf16[32,2048]{1,0:T(8,128)(2,1)S(1)} %get-tuple-element.86), channel_id=1, source_target_pairs={{0,2},{1,3},{2,0},{3,1},{4,6},{5,7},{6,4},{7,5},{8,10},{9,11},{10,... | collective-permute-start | bytes 393224 | tf_op jit(solution)/shard_map/ppermute | solution.py:138
  55.3 8.6 %collective-permute-start.21 = (bf16[32,2048]{1,0:T(8,128)(2,1)S(1)}, bf16[32,2048]{1,0:T(8,128)(2,1)S(1)}, u32[]{:S(2)}, u32[]{:S(2)}) collective-permute-start(bf16[32,2048]{1,0:T(8,128)(2,1)S(1)} %get-tuple-element.80), channel_id=1, source_target_pairs={{0,4},{1,5},{2,6},{3,7},{4,0},{5,1},{6,2},{7,3},{8,12},{9,13},{10,... | collective-permute-start | bytes 393224 | tf_op jit(solution)/shard_map/ppermute | solution.py:138
  56.9 7.0 %collective-permute-start.20 = (bf16[32,2048]{1,0:T(8,128)(2,1)S(1)}, bf16[32,2048]{1,0:T(8,128)(2,1)S(1)}, u32[]{:S(2)}, u32[]{:S(2)}) collective-permute-start(bf16[32,2048]{1,0:T(8,128)(2,1)S(1)} %get-tuple-element.81), channel_id=1, source_target_pairs={{0,2},{1,3},{2,0},{3,1},{4,6},{5,7},{6,4},{7,5},{8,10},{9,11},{10,... | collective-permute-start | bytes 393224 | tf_op jit(solution)/shard_map/ppermute | solution.py:138
  57.5 6.4 %copy-start = (bf16[1,32,2048]{2,1,0:T(8,128)(2,1)S(1)}, bf16[1,32,2048]{2,1,0:T(8,128)(2,1)}, u32[]{:S(2)}) copy-start(bf16[1,32,2048]{2,1,0:T(8,128)(2,1)} %param.8) | copy-start | bytes 393220
  62.5 8.3 %collective-permute-start.23 = (bf16[32,2048]{1,0:T(8,128)(2,1)S(1)}, bf16[32,2048]{1,0:T(8,128)(2,1)S(1)}, u32[]{:S(2)}, u32[]{:S(2)}) collective-permute-start(bf16[32,2048]{1,0:T(8,128)(2,1)S(1)} %get-tuple-element.79), channel_id=1, source_target_pairs={{0,6},{1,7},{2,4},{3,5},{4,2},{5,3},{6,0},{7,1},{8,14},{9,15},{10,... | collective-permute-start | bytes 393224 | tf_op jit(solution)/shard_map/ppermute | solution.py:138
  64.1 7.4 %copy-start.1 = (bf16[1,32,2048]{2,1,0:T(8,128)(2,1)S(1)}, bf16[1,32,2048]{2,1,0:T(8,128)(2,1)}, u32[]{:S(2)}) copy-start(bf16[1,32,2048]{2,1,0:T(8,128)(2,1)} %param.10) | copy-start | bytes 393220
  64.1 7.4 %collective-permute-start.22 = (bf16[32,2048]{1,0:T(8,128)(2,1)S(1)}, bf16[32,2048]{1,0:T(8,128)(2,1)S(1)}, u32[]{:S(2)}, u32[]{:S(2)}) collective-permute-start(bf16[32,2048]{1,0:T(8,128)(2,1)S(1)} %add_convert_fusion.1), channel_id=1, source_target_pairs={{0,8},{8,16},{16,24},{24,0},{1,9},{9,17},{17,25},{25,1},{2,10},{10... | collective-permute-start | bytes 393224 | tf_op jit(solution)/shard_map/ppermute | solution.py:21
  71.6 5.0 %collective-permute-start.24 = (bf16[32,2048]{1,0:T(8,128)(2,1)S(1)}, bf16[32,2048]{1,0:T(8,128)(2,1)S(1)}, u32[]{:S(2)}, u32[]{:S(2)}) collective-permute-start(bf16[32,2048]{1,0:T(8,128)(2,1)S(1)} %add_convert_fusion), channel_id=1, source_target_pairs={{0,24},{8,0},{16,8},{24,16},{1,25},{9,1},{17,9},{25,17},{2,26},{10... | collective-permute-start | bytes 393224 | tf_op jit(solution)/shard_map/ppermute | solution.py:21

commit v12 on v11

--- a/solution.py
+++ b/solution.py
@@ -363,14 +363,15 @@
         ).astype(picks.dtype)
         scale = jnp.sum(jnp.where(grads, gate, 0.0), axis=0, keepdims=True)
         scales.append(jnp.where(is_saved, 1.0, scale))
+    for step in range(0, number, 2):
+        lanes = pl.ds(step * LANES, 2 * LANES)
+        scale = jnp.concatenate(scales[step : step + 2], axis=1)
+        rows[:, lanes] = (
+            jnp.dot(turned[...], picks[:, lanes], preferred_element_type=jnp.float32) * scale
+        ).astype(rows.dtype)
+
     leaving = []
     for step in range(number):
-        if step % 2 == 0:
-            lanes = pl.ds(step * LANES, 2 * LANES)
-            scale = jnp.concatenate(scales[step : step + 2], axis=1)
-            rows[:, lanes] = (
-                jnp.dot(turned[...], picks[:, lanes], preferred_element_type=jnp.float32) * scale
-            ).astype(rows.dtype)
         for start in range(0, half, CHUNK):
             chunk = pl.ds(start, CHUNK)
             for corner in range(start, start + CHUNK, LANES):
@@ -390,6 +391,18 @@
             )
             leaving[-1].start()
     for copy in leaving:
+        copy.wait()
+
+
+def deliver_kernel(*refs):
+    sources, targets, done = refs[:2], refs[2:4], refs[4]
+    copies = [
+        pltpu.make_async_copy(source, target, done.at[place])
+        for place, (source, target) in enumerate(zip(sources, targets))
+    ]
+    for copy in copies:
+        copy.start()
+    for copy in copies:
         copy.wait()
 
 
@@ -621,7 +634,15 @@
     grad_near = after((done, next_inputs), grad_near)
     input_grads = summed(output_grads[0], grad_sums[0], *grad_near).astype(jnp.bfloat16)
     prior_grads = shifted(input_grads, "pipe", -1)[None]
-    return (next_inputs, prior_grads, done[None])
+    delivered = pl.pallas_call(
+        deliver_kernel,
+        in_specs=[anywhere] * 2,
+        out_specs=[anywhere] * 2,
+        out_shape=[pltpu.HBM(array.shape, array.dtype) for array in (next_inputs, prior_grads)],
+        scratch_shapes=[pltpu.SemaphoreType.DMA((2,))],
+        name="deliver",
+    )(next_inputs, prior_grads)
+    return (*delivered, done[None])
 
 
 def on_device(*arrays):

time: 78.1 us -> 86.6 us (1.11)
  Pallas kernels: 37 us -> 45.1 us
  waiting for transfers between devices: 16.5 us -> 17.5 us
    pallas_call x0 -> x1, Pallas kernels: none -> 9.06 us  [gathered_plan(): pl.pallas_call(deliver_kernel, in_specs=[anywhere] * 2, out_specs=[anywhe...]
    pallas_call x2, Pallas kernels: 9.87 us -> 8.9 us  [gradient(): pl.pallas_call(functools.partial(weight_kernel, first, number, count, slo...]
  transfers between devices with their start and end apart: 25 -> 25, of which waited for: 11 -> 13; matrix products, arithmetic and copies ran while one was open for 1% -> 0% of each run, Pallas kernels for 13% -> 10%
where the time goes in v12:
time: 86.6 us; the launch traced here: 86.5 us
  Pallas kernels  45.1 us (52%)
  starting transfers between devices  21.8 us (25%)
  waiting for transfers between devices  17.5 us (20%)
  between operations  0.9 us (1%)
    pallas_call x1, Pallas kernels, gathered_plan(): pl.pallas_call(functools.partial(expert_kernel, count, slots, devices, pa...  24.8 us
    ppermute x23, starting transfers between devices, swapped(): lax.ppermute(value, axes, [(source, source ^ code) for source in range(co...  18.2 us
    ppermute x23, waiting for transfers between devices, swapped(): lax.ppermute(value, axes, [(source, source ^ code) for source in range(co...  13.3 us
    pallas_call x1, Pallas kernels, gathered_plan(): pl.pallas_call(deliver_kernel, in_specs=[anywhere] * 2, out_specs=[anywhe...  9.06 us
    pallas_call x2, Pallas kernels, gradient(): pl.pallas_call(functools.partial(weight_kernel, first, number, count, slo...  8.9 us
    ppermute x2, waiting for transfers between devices, shifted(): return lax.ppermute(value, axis, pairs)  4.13 us
    ppermute x2, starting transfers between devices, shifted(): return lax.ppermute(value, axis, pairs)  3.6 us
  transfers between devices with their start and end apart: 25, of which 13 were waited for; matrix products, arithmetic and copies ran while one was open for 0% of the time, Pallas kernels for 10%

profile of v12, /device:TPU:0, one launch (start us, length us, event | category | flops | bytes accessed | tf_op | source)
XLA Modules:
  0.0 86.5 jit_solution(15595602544037181574)
XLA Ops:
  0.6 1.2 %pack.1 = (bf16[32,3200]{1,0:T(8,128)(2,1)S(1)}, bf16[32,3200]{1,0:T(8,128)(2,1)S(1)}) custom-call(bf16[32,2048]{1,0:T(8,128)(2,1)} %bitcast.69, bf16[32,2048]{1,0:T(8,128)(2,1)} %bitcast.71, bf16[32,2048]{1,0:T(8,128)(2,1)} %bitcast.70, s32[8,32]{1,0:T(8,128)} %bitcast.74, f32[8,32]{1,0:T(8,128)} %bitcast.75, s32[8,32]{1,0:T(8,128)} %bitcast.76, ...), custom_call_target="tpu_custom_call" | custom-call | tf_op jit(solution)/shard_map/pack/pallas_call | solution.py:478
  1.8 3.0 %collective-permute-start.1 = (bf16[32,3200]{1,0:T(8,128)(2,1)S(1)}, bf16[32,3200]{1,0:T(8,128)(2,1)S(1)}, u32[]{:S(2)}, u32[]{:S(2)}) collective-permute-start(bf16[32,3200]{1,0:T(8,128)(2,1)S(1)} %get-tuple-element.43.refs_0_.refs_10_), channel_id=1, source_target_pairs={{0,2},{1,3},{2,0},{3,1},{4,6},{5,7},{6,4},{7,5},{8,10},{9,11},{10,... | collective-permute-start | bytes 614408 | tf_op jit(solution)/shard_map/ppermute | solution.py:138
  4.8 0.0 collective-permute-start
  4.8 0.5 collective-permute-start.9
  5.4 1.5 %collective-permute-start.4 = (bf16[32,3200]{1,0:T(8,128)(2,1)S(1)}, bf16[32,3200]{1,0:T(8,128)(2,1)S(1)}, u32[]{:S(2)}, u32[]{:S(2)}) collective-permute-start(bf16[32,3200]{1,0:T(8,128)(2,1)S(1)} %get-tuple-element.44.refs_8_.refs_18_), channel_id=1, source_target_pairs={{0,4},{1,5},{2,6},{3,7},{4,0},{5,1},{6,2},{7,3},{8,12},{9,13},{10,... | collective-permute-start | bytes 614408 | tf_op jit(solution)/shard_map/ppermute | solution.py:138
  6.9 0.5 collective-permute-start.2
  7.4 2.5 %collective-permute-done.1.refs_2_.refs_12_ = bf16[32,3200]{1,0:T(8,128)(2,1)S(1)} collective-permute-done((bf16[32,3200]{1,0:T(8,128)(2,1)S(1)}, bf16[32,3200]{1,0:T(8,128)(2,1)S(1)}, u32[]{:S(2)}, u32[]{:S(2)}) %collective-permute-start.1) | collective-permute-done | bytes 204832 | tf_op jit(solution)/shard_map/ppermute | solution.py:138
  9.9 1.7 %collective-permute-start.3 = (bf16[32,3200]{1,0:T(8,128)(2,1)S(1)}, bf16[32,3200]{1,0:T(8,128)(2,1)S(1)}, u32[]{:S(2)}, u32[]{:S(2)}) collective-permute-start(bf16[32,3200]{1,0:T(8,128)(2,1)S(1)} %get-tuple-element.44.refs_8_.refs_18_), channel_id=1, source_target_pairs={{0,2},{1,3},{2,0},{3,1},{4,6},{5,7},{6,4},{7,5},{8,10},{9,11},{10,... | collective-permute-start | bytes 614408 | tf_op jit(solution)/shard_map/ppermute | solution.py:138
  11.7 0.0 collective-permute-done.refs_1_.refs_11_
  11.7 1.5 %collective-permute-start.7 = (bf16[32,3200]{1,0:T(8,128)(2,1)S(1)}, bf16[32,3200]{1,0:T(8,128)(2,1)S(1)}, u32[]{:S(2)}, u32[]{:S(2)}) collective-permute-start(bf16[32,3200]{1,0:T(8,128)(2,1)S(1)} %collective-permute-done.1.refs_2_.refs_12_), channel_id=1, source_target_pairs={{0,4},{1,5},{2,6},{3,7},{4,0},{5,1},{6,2},{7,3},{8,12},{9,13},{10,... | collective-permute-start | bytes 614408 | tf_op jit(solution)/shard_map/ppermute | solution.py:138
  13.2 0.0 collective-permute-done.9.refs_9_.refs_19_
  13.2 0.1 collective-permute-done.4.refs_12_.refs_22_
  13.3 0.4 collective-permute-start.12
  13.7 4.0 %collective-permute-done.2.refs_4_.refs_14_ = bf16[32,3200]{1,0:T(8,128)(2,1)S(1)} collective-permute-done((bf16[32,3200]{1,0:T(8,128)(2,1)S(1)}, bf16[32,3200]{1,0:T(8,128)(2,1)S(1)}, u32[]{:S(2)}, u32[]{:S(2)}) %collective-permute-start.2) | collective-permute-done | bytes 204832 | tf_op jit(solution)/shard_map/ppermute | solution.py:138
  17.7 0.2 collective-permute-done.3.refs_10_.refs_20_
  17.9 0.0 collective-permute-start.5
  17.9 0.5 collective-permute-start.6
  18.4 0.0 collective-permute-start.10
  18.4 2.7 %collective-permute-done.7.refs_6_.refs_16_ = bf16[32,3200]{1,0:T(8,128)(2,1)S(1)} collective-permute-done((bf16[32,3200]{1,0:T(8,128)(2,1)S(1)}, bf16[32,3200]{1,0:T(8,128)(2,1)S(1)}, u32[]{:S(2)}, u32[]{:S(2)}) %collective-permute-start.7) | collective-permute-done | bytes 204832 | tf_op jit(solution)/shard_map/ppermute | solution.py:138
  21.1 0.0 collective-permute-start.11
  21.1 0.0 collective-permute-done.12.refs_14_.refs_24_
  21.1 0.5 collective-permute-start.8
  21.6 0.0 collective-permute-done.5.refs_3_.refs_13_
  21.6 0.1 collective-permute-start.13
  21.7 0.1 stack.47.place_ref
  21.8 0.0 collective-permute-done.6.refs_5_.refs_15_
  21.8 0.0 collective-permute-done.10.refs_11_.refs_21_
  21.8 0.8 collective-permute-done.11.refs_13_.refs_23_
  22.6 0.3 collective-permute-done.8.refs_7_.refs_17_
  22.9 0.3 collective-permute-done.13.refs_15_.refs_25_
  23.2 1.1 %slot_picks.1 = (bf16[384,256]{1,0:T(8,128)(2,1)S(1)}, f32[384,128]{1,0:T(8,128)S(1)}, bf16[256,384]{1,0:T(8,128)(2,1)S(1)}, bf16[384,256]{1,0:T(8,128)(2,1)S(1)...) custom-call(s32[11]{0:T(128)S(1)} %stack.47.place_ref, ...), custom_call_target="tpu_custom_call" | custom-call | bytes 1024 | tf_op jit(solution)/shard_map/slot_picks/pallas_call | solution.py:532
  24.3 24.8 %experts.1 = (bf16[32,2048]{1,0:T(8,128)(2,1)S(1)}, bf16[32,2048]{1,0:T(8,128)(2,1)S(1)}, bf16[32,2048]{1,0:T(8,128)(2,1)S(1)}, bf16[32,2048]{1,0:T(8,128)(2,1)S...) custom-call(s32[11]{0:T(128)S(1)} %stack.47.place_ref, ...), custom_call_target="tpu_custom_call" | custom-call | flops 12884901888 | bytes 25165824 | tf_op jit(solution)/shard_map/experts/pallas_call | solution.py:554
  49.1 0.2 collective-permute-start.14
  49.3 1.7 %collective-permute-done.14 = bf16[4,32,2048]{2,1,0:T(8,128)(2,1)S(1)} collective-permute-done((bf16[4,32,2048]{2,1,0:T(8,128)(2,1)S(1)}, bf16[4,32,2048]{2,1,0:T(8,128)(2,1)S(1)}, u32[]{:S(2)}, u32[]{:S(2)}) %collective-permute-start.14) | collective-permute-done | bytes 524320 | tf_op jit(solution)/shard_map/ppermute | solution.py:138
  51.0 0.2 collective-permute-start.18
  51.2 0.3 collective-permute-start.19
  51.5 0.1 fusion.7
  51.6 1.6 %collective-permute-start.17 = (bf16[32,2048]{1,0:T(8,128)(2,1)S(1)}, bf16[32,2048]{1,0:T(8,128)(2,1)S(1)}, u32[]{:S(2)}, u32[]{:S(2)}) collective-permute-start(bf16[32,2048]{1,0:T(8,128)(2,1)S(1)} %get-tuple-element.88), channel_id=1, source_target_pairs={{0,6},{1,7},{2,4},{3,5},{4,2},{5,3},{6,0},{7,1},{8,14},{9,15},{10,... | collective-permute-start | bytes 393224 | tf_op jit(solution)/shard_map/ppermute | solution.py:138
  53.3 0.5 collective-permute-start.16
  53.8 1.4 %collective-permute-start.15 = (bf16[32,2048]{1,0:T(8,128)(2,1)S(1)}, bf16[32,2048]{1,0:T(8,128)(2,1)S(1)}, u32[]{:S(2)}, u32[]{:S(2)}) collective-permute-start(bf16[32,2048]{1,0:T(8,128)(2,1)S(1)} %get-tuple-element.90), channel_id=1, source_target_pairs={{0,2},{1,3},{2,0},{3,1},{4,6},{5,7},{6,4},{7,5},{8,10},{9,11},{10,... | collective-permute-start | bytes 393224 | tf_op jit(solution)/shard_map/ppermute | solution.py:138
  55.2 0.0 collective-permute-done.19
  55.2 0.0 collective-permute-done.18.refs_1_
  55.2 0.1 fusion
  55.3 1.6 %collective-permute-start.21 = (bf16[32,2048]{1,0:T(8,128)(2,1)S(1)}, bf16[32,2048]{1,0:T(8,128)(2,1)S(1)}, u32[]{:S(2)}, u32[]{:S(2)}) collective-permute-start(bf16[32,2048]{1,0:T(8,128)(2,1)S(1)} %get-tuple-element.84), channel_id=1, source_target_pairs={{0,4},{1,5},{2,6},{3,7},{4,0},{5,1},{6,2},{7,3},{8,12},{9,13},{10,... | collective-permute-start | bytes 393224 | tf_op jit(solution)/shard_map/ppermute | solution.py:138
  56.9 0.6 collective-permute-start.20
  57.5 4.5 %weight_gradient_0.1.refs_3_ = bf16[16,1024,768]{2,1,0:T(8,128)(2,1)} custom-call(s32[11]{0:T(128)S(1)} %stack.47.place_ref, f32[256,128]{1,0:T(8,128)S(1)} %get-tuple-element.62.refs_0_, bf16[8,96,768]{2,1,0:T(8,128)(2,1)S(1)} %collective-permute-done.18.refs_1_, bf16[1024,512]{1,0:T(8,128)(2,1)S(1)} %get-tuple-element.65.refs_2_, ...), custom_call_target="tpu_custom_call", output_to_operand_aliasing={{}: (4, {})} | custom-call | flops 3221225472 | bytes 12582912 | tf_op jit(solution)/shard_map/weight_gradient_0/pallas_call | solution.py:600
  62.0 0.0 collective-permute-done.17
  62.0 1.4 %collective-permute-start.23 = (bf16[32,2048]{1,0:T(8,128)(2,1)S(1)}, bf16[32,2048]{1,0:T(8,128)(2,1)S(1)}, u32[]{:S(2)}, u32[]{:S(2)}) collective-permute-start(bf16[32,2048]{1,0:T(8,128)(2,1)S(1)} %get-tuple-element.83), channel_id=1, source_target_pairs={{0,6},{1,7},{2,4},{3,5},{4,2},{5,3},{6,0},{7,1},{8,14},{9,15},{10,... | collective-permute-start | bytes 393224 | tf_op jit(solution)/shard_map/ppermute | solution.py:138
  63.4 0.0 collective-permute-done.16
  63.4 0.0 collective-permute-done.15
  63.4 0.4 collective-permute-done.21
  63.9 0.3 collective-permute-done.20
  64.2 0.1 add_convert_fusion.1
  64.3 0.0 copy-start.1
  64.3 1.8 %collective-permute-start.22 = (bf16[32,2048]{1,0:T(8,128)(2,1)S(1)}, bf16[32,2048]{1,0:T(8,128)(2,1)S(1)}, u32[]{:S(2)}, u32[]{:S(2)}) collective-permute-start(bf16[32,2048]{1,0:T(8,128)(2,1)S(1)} %add_convert_fusion.1), channel_id=1, source_target_pairs={{0,8},{8,16},{16,24},{24,0},{1,9},{9,17},{17,25},{25,1},{2,10},{10... | collective-permute-start | bytes 393224 | tf_op jit(solution)/shard_map/ppermute | solution.py:21
  66.1 4.4 %weight_gradient_4.1 = bf16[16,1024,768]{2,1,0:T(8,128)(2,1)} custom-call(s32[11]{0:T(128)S(1)} %stack.47.place_ref, f32[256,128]{1,0:T(8,128)S(1)} %get-tuple-element.62.refs_0_, bf16[8,96,768]{2,1,0:T(8,128)(2,1)S(1)} %collective-permute-done.18.refs_1_, bf16[1024,512]{1,0:T(8,128)(2,1)S(1)} %get-tuple-element.65.refs_2_, ...), custom_call_target="tpu_custom_call", output_to_operand_aliasing={{}: (4, {})} | custom-call | flops 3221225472 | bytes 12582912 | tf_op jit(solution)/shard_map/weight_gradient_4/pallas_call | solution.py:600
  70.6 0.0 collective-permute-done.23
  70.6 0.9 %collective-permute-done.22 = bf16[32,2048]{1,0:T(8,128)(2,1)S(1)} collective-permute-done((bf16[32,2048]{1,0:T(8,128)(2,1)S(1)}, bf16[32,2048]{1,0:T(8,128)(2,1)S(1)}, u32[]{:S(2)}, u32[]{:S(2)}) %collective-permute-start.22) | collective-permute-done | bytes 131104 | tf_op jit(solution)/shard_map/ppermute | solution.py:21
  71.5 0.0 copy-done.1
  71.5 0.1 add_convert_fusion
  71.6 1.8 %collective-permute-start.24 = (bf16[32,2048]{1,0:T(8,128)(2,1)S(1)}, bf16[32,2048]{1,0:T(8,128)(2,1)S(1)}, u32[]{:S(2)}, u32[]{:S(2)}) collective-permute-start(bf16[32,2048]{1,0:T(8,128)(2,1)S(1)} %add_convert_fusion), channel_id=1, source_target_pairs={{0,24},{8,0},{16,8},{24,16},{1,25},{9,1},{17,9},{25,17},{2,26},{10... | collective-permute-start | bytes 393224 | tf_op jit(solution)/shard_map/ppermute | solution.py:21
  73.4 3.2 %collective-permute-done.24 = bf16[32,2048]{1,0:T(8,128)(2,1)S(1)} collective-permute-done((bf16[32,2048]{1,0:T(8,128)(2,1)S(1)}, bf16[32,2048]{1,0:T(8,128)(2,1)S(1)}, u32[]{:S(2)}, u32[]{:S(2)}) %collective-permute-start.24) | collective-permute-done | bytes 131104 | tf_op jit(solution)/shard_map/ppermute | solution.py:21
  76.6 0.6 copy-done.3
  77.2 9.1 %deliver.1 = (bf16[1,32,2048]{2,1,0:T(8,128)(2,1)}, bf16[1,32,2048]{2,1,0:T(8,128)(2,1)}) custom-call(bf16[1,32,2048]{2,1,0:T(8,128)(2,1)} %bitcast.72, bf16[1,32,2048]{2,1,0:T(8,128)(2,1)} %bitcast.73), custom_call_target="tpu_custom_call" | custom-call | tf_op jit(solution)/shard_map/deliver/pallas_call | solution.py:637
  (5 shorter events, 0.0 us)
Async XLA Ops:
  1.8 8.1 %collective-permute-start.1 = (bf16[32,3200]{1,0:T(8,128)(2,1)S(1)}, bf16[32,3200]{1,0:T(8,128)(2,1)S(1)}, u32[]{:S(2)}, u32[]{:S(2)}) collective-permute-start(bf16[32,3200]{1,0:T(8,128)(2,1)S(1)} %get-tuple-element.43.refs_0_.refs_10_), channel_id=1, source_target_pairs={{0,2},{1,3},{2,0},{3,1},{4,6},{5,7},{6,4},{7,5},{8,10},{9,11},{10,... | collective-permute-start | bytes 614408 | tf_op jit(solution)/shard_map/ppermute | solution.py:138
  4.8 6.8 %collective-permute-start = (bf16[32,3200]{1,0:T(8,128)(2,1)S(1)}, bf16[32,3200]{1,0:T(8,128)(2,1)S(1)}, u32[]{:S(2)}, u32[]{:S(2)}) collective-permute-start(bf16[32,3200]{1,0:T(8,128)(2,1)S(1)} %get-tuple-element.43.refs_0_.refs_10_), channel_id=1, source_target_pairs={{0,1},{1,0},{2,3},{3,2},{4,5},{5,4},{6,7},{7,6},{8,9},{9,8},{10,11... | collective-permute-start | bytes 614408 | tf_op jit(solution)/shard_map/ppermute | solution.py:138
  4.8 8.4 %collective-permute-start.9 = (bf16[32,3200]{1,0:T(8,128)(2,1)S(1)}, bf16[32,3200]{1,0:T(8,128)(2,1)S(1)}, u32[]{:S(2)}, u32[]{:S(2)}) collective-permute-start(bf16[32,3200]{1,0:T(8,128)(2,1)S(1)} %get-tuple-element.44.refs_8_.refs_18_), channel_id=1, source_target_pairs={{0,1},{1,0},{2,3},{3,2},{4,5},{5,4},{6,7},{7,6},{8,9},{9,8},{10,11... | collective-permute-start | bytes 614408 | tf_op jit(solution)/shard_map/ppermute | solution.py:138
  5.4 7.9 %collective-permute-start.4 = (bf16[32,3200]{1,0:T(8,128)(2,1)S(1)}, bf16[32,3200]{1,0:T(8,128)(2,1)S(1)}, u32[]{:S(2)}, u32[]{:S(2)}) collective-permute-start(bf16[32,3200]{1,0:T(8,128)(2,1)S(1)} %get-tuple-element.44.refs_8_.refs_18_), channel_id=1, source_target_pairs={{0,4},{1,5},{2,6},{3,7},{4,0},{5,1},{6,2},{7,3},{8,12},{9,13},{10,... | collective-permute-start | bytes 614408 | tf_op jit(solution)/shard_map/ppermute | solution.py:138
  6.9 10.8 %collective-permute-start.2 = (bf16[32,3200]{1,0:T(8,128)(2,1)S(1)}, bf16[32,3200]{1,0:T(8,128)(2,1)S(1)}, u32[]{:S(2)}, u32[]{:S(2)}) collective-permute-start(bf16[32,3200]{1,0:T(8,128)(2,1)S(1)} %get-tuple-element.43.refs_0_.refs_10_), channel_id=1, source_target_pairs={{0,4},{1,5},{2,6},{3,7},{4,0},{5,1},{6,2},{7,3},{8,12},{9,13},{10,... | collective-permute-start | bytes 614408 | tf_op jit(solution)/shard_map/ppermute | solution.py:138
  9.9 8.0 %collective-permute-start.3 = (bf16[32,3200]{1,0:T(8,128)(2,1)S(1)}, bf16[32,3200]{1,0:T(8,128)(2,1)S(1)}, u32[]{:S(2)}, u32[]{:S(2)}) collective-permute-start(bf16[32,3200]{1,0:T(8,128)(2,1)S(1)} %get-tuple-element.44.refs_8_.refs_18_), channel_id=1, source_target_pairs={{0,2},{1,3},{2,0},{3,1},{4,6},{5,7},{6,4},{7,5},{8,10},{9,11},{10,... | collective-permute-start | bytes 614408 | tf_op jit(solution)/shard_map/ppermute | solution.py:138
  11.7 9.5 %collective-permute-start.7 = (bf16[32,3200]{1,0:T(8,128)(2,1)S(1)}, bf16[32,3200]{1,0:T(8,128)(2,1)S(1)}, u32[]{:S(2)}, u32[]{:S(2)}) collective-permute-start(bf16[32,3200]{1,0:T(8,128)(2,1)S(1)} %collective-permute-done.1.refs_2_.refs_12_), channel_id=1, source_target_pairs={{0,4},{1,5},{2,6},{3,7},{4,0},{5,1},{6,2},{7,3},{8,12},{9,13},{10,... | collective-permute-start | bytes 614408 | tf_op jit(solution)/shard_map/ppermute | solution.py:138
  13.3 7.8 %collective-permute-start.12 = (bf16[32,3200]{1,0:T(8,128)(2,1)S(1)}, bf16[32,3200]{1,0:T(8,128)(2,1)S(1)}, u32[]{:S(2)}, u32[]{:S(2)}) collective-permute-start(bf16[32,3200]{1,0:T(8,128)(2,1)S(1)} %collective-permute-done.4.refs_12_.refs_22_), channel_id=1, source_target_pairs={{0,2},{1,3},{2,0},{3,1},{4,6},{5,7},{6,4},{7,5},{8,10},{9,11},{10,... | collective-permute-start | bytes 614408 | tf_op jit(solution)/shard_map/ppermute | solution.py:138
  17.9 3.7 %collective-permute-start.5 = (bf16[32,3200]{1,0:T(8,128)(2,1)S(1)}, bf16[32,3200]{1,0:T(8,128)(2,1)S(1)}, u32[]{:S(2)}, u32[]{:S(2)}) collective-permute-start(bf16[32,3200]{1,0:T(8,128)(2,1)S(1)} %collective-permute-done.1.refs_2_.refs_12_), channel_id=1, source_target_pairs={{0,1},{1,0},{2,3},{3,2},{4,5},{5,4},{6,7},{7,6},{8,9},{9,8},{10,11... | collective-permute-start | bytes 614408 | tf_op jit(solution)/shard_map/ppermute | solution.py:138
  17.9 3.9 %collective-permute-start.6 = (bf16[32,3200]{1,0:T(8,128)(2,1)S(1)}, bf16[32,3200]{1,0:T(8,128)(2,1)S(1)}, u32[]{:S(2)}, u32[]{:S(2)}) collective-permute-start(bf16[32,3200]{1,0:T(8,128)(2,1)S(1)} %collective-permute-done.2.refs_4_.refs_14_), channel_id=1, source_target_pairs={{0,1},{1,0},{2,3},{3,2},{4,5},{5,4},{6,7},{7,6},{8,9},{9,8},{10,11... | collective-permute-start | bytes 614408 | tf_op jit(solution)/shard_map/ppermute | solution.py:138
  18.4 3.4 %collective-permute-start.10 = (bf16[32,3200]{1,0:T(8,128)(2,1)S(1)}, bf16[32,3200]{1,0:T(8,128)(2,1)S(1)}, u32[]{:S(2)}, u32[]{:S(2)}) collective-permute-start(bf16[32,3200]{1,0:T(8,128)(2,1)S(1)} %collective-permute-done.3.refs_10_.refs_20_), channel_id=1, source_target_pairs={{0,1},{1,0},{2,3},{3,2},{4,5},{5,4},{6,7},{7,6},{8,9},{9,8},{10,11... | collective-permute-start | bytes 614408 | tf_op jit(solution)/shard_map/ppermute | solution.py:138
  21.1 1.5 %collective-permute-start.11 = (bf16[32,3200]{1,0:T(8,128)(2,1)S(1)}, bf16[32,3200]{1,0:T(8,128)(2,1)S(1)}, u32[]{:S(2)}, u32[]{:S(2)}) collective-permute-start(bf16[32,3200]{1,0:T(8,128)(2,1)S(1)} %collective-permute-done.4.refs_12_.refs_22_), channel_id=1, source_target_pairs={{0,1},{1,0},{2,3},{3,2},{4,5},{5,4},{6,7},{7,6},{8,9},{9,8},{10,11... | collective-permute-start | bytes 614408 | tf_op jit(solution)/shard_map/ppermute | solution.py:138
  21.1 1.7 %collective-permute-start.8 = (bf16[32,3200]{1,0:T(8,128)(2,1)S(1)}, bf16[32,3200]{1,0:T(8,128)(2,1)S(1)}, u32[]{:S(2)}, u32[]{:S(2)}) collective-permute-start(bf16[32,3200]{1,0:T(8,128)(2,1)S(1)} %collective-permute-done.7.refs_6_.refs_16_), channel_id=1, source_target_pairs={{0,1},{1,0},{2,3},{3,2},{4,5},{5,4},{6,7},{7,6},{8,9},{9,8},{10,11... | collective-permute-start | bytes 614408 | tf_op jit(solution)/shard_map/ppermute | solution.py:138
  21.6 1.5 %collective-permute-start.13 = (bf16[32,3200]{1,0:T(8,128)(2,1)S(1)}, bf16[32,3200]{1,0:T(8,128)(2,1)S(1)}, u32[]{:S(2)}, u32[]{:S(2)}) collective-permute-start(bf16[32,3200]{1,0:T(8,128)(2,1)S(1)} %collective-permute-done.12.refs_14_.refs_24_), channel_id=1, source_target_pairs={{0,1},{1,0},{2,3},{3,2},{4,5},{5,4},{6,7},{7,6},{8,9},{9,8},{10,11... | collective-permute-start | bytes 614408 | tf_op jit(solution)/shard_map/ppermute | solution.py:138
  49.1 1.9 %collective-permute-start.14 = (bf16[4,32,2048]{2,1,0:T(8,128)(2,1)S(1)}, bf16[4,32,2048]{2,1,0:T(8,128)(2,1)S(1)}, u32[]{:S(2)}, u32[]{:S(2)}) collective-permute-start(bf16[4,32,2048]{2,1,0:T(8,128)(2,1)S(1)} %get-tuple-element.58), channel_id=1, source_target_pairs={{0,1},{1,0},{2,3},{3,2},{4,5},{5,4},{6,7},{7,6},{8,9},{9,8},{10,11... | collective-permute-start | bytes 1572872 | tf_op jit(solution)/shard_map/ppermute | solution.py:138
  51.0 4.2 %collective-permute-start.18 = (bf16[8,96,768]{2,1,0:T(8,128)(2,1)S(1)}, bf16[8,96,768]{2,1,0:T(8,128)(2,1)S(1)}, u32[]{:S(2)}, u32[]{:S(2)}) collective-permute-start(bf16[8,96,768]{2,1,0:T(8,128)(2,1)S(1)} %get-tuple-element.64), channel_id=1, source_target_pairs={{0,1},{1,0},{2,3},{3,2},{4,5},{5,4},{6,7},{7,6},{8,9},{9,8},{10,11... | collective-permute-start | bytes 3538952 | tf_op jit(solution)/shard_map/ppermute | solution.py:138
  51.2 4.0 %collective-permute-start.19 = (bf16[4,32,2048]{2,1,0:T(8,128)(2,1)S(1)}, bf16[4,32,2048]{2,1,0:T(8,128)(2,1)S(1)}, u32[]{:S(2)}, u32[]{:S(2)}) collective-permute-start(bf16[4,32,2048]{2,1,0:T(8,128)(2,1)S(1)} %get-tuple-element.68), channel_id=1, source_target_pairs={{0,1},{1,0},{2,3},{3,2},{4,5},{5,4},{6,7},{7,6},{8,9},{9,8},{10,11... | collective-permute-start | bytes 1572872 | tf_op jit(solution)/shard_map/ppermute | solution.py:138
  51.6 10.3 %collective-permute-start.17 = (bf16[32,2048]{1,0:T(8,128)(2,1)S(1)}, bf16[32,2048]{1,0:T(8,128)(2,1)S(1)}, u32[]{:S(2)}, u32[]{:S(2)}) collective-permute-start(bf16[32,2048]{1,0:T(8,128)(2,1)S(1)} %get-tuple-element.88), channel_id=1, source_target_pairs={{0,6},{1,7},{2,4},{3,5},{4,2},{5,3},{6,0},{7,1},{8,14},{9,15},{10,... | collective-permute-start | bytes 393224 | tf_op jit(solution)/shard_map/ppermute | solution.py:138
  53.3 10.2 %collective-permute-start.16 = (bf16[32,2048]{1,0:T(8,128)(2,1)S(1)}, bf16[32,2048]{1,0:T(8,128)(2,1)S(1)}, u32[]{:S(2)}, u32[]{:S(2)}) collective-permute-start(bf16[32,2048]{1,0:T(8,128)(2,1)S(1)} %get-tuple-element.89), channel_id=1, source_target_pairs={{0,4},{1,5},{2,6},{3,7},{4,0},{5,1},{6,2},{7,3},{8,12},{9,13},{10,... | collective-permute-start | bytes 393224 | tf_op jit(solution)/shard_map/ppermute | solution.py:138
  53.8 9.7 %collective-permute-start.15 = (bf16[32,2048]{1,0:T(8,128)(2,1)S(1)}, bf16[32,2048]{1,0:T(8,128)(2,1)S(1)}, u32[]{:S(2)}, u32[]{:S(2)}) collective-permute-start(bf16[32,2048]{1,0:T(8,128)(2,1)S(1)} %get-tuple-element.90), channel_id=1, source_target_pairs={{0,2},{1,3},{2,0},{3,1},{4,6},{5,7},{6,4},{7,5},{8,10},{9,11},{10,... | collective-permute-start | bytes 393224 | tf_op jit(solution)/shard_map/ppermute | solution.py:138
  55.3 8.5 %collective-permute-start.21 = (bf16[32,2048]{1,0:T(8,128)(2,1)S(1)}, bf16[32,2048]{1,0:T(8,128)(2,1)S(1)}, u32[]{:S(2)}, u32[]{:S(2)}) collective-permute-start(bf16[32,2048]{1,0:T(8,128)(2,1)S(1)} %get-tuple-element.84), channel_id=1, source_target_pairs={{0,4},{1,5},{2,6},{3,7},{4,0},{5,1},{6,2},{7,3},{8,12},{9,13},{10,... | collective-permute-start | bytes 393224 | tf_op jit(solution)/shard_map/ppermute | solution.py:138
  56.9 7.3 %collective-permute-start.20 = (bf16[32,2048]{1,0:T(8,128)(2,1)S(1)}, bf16[32,2048]{1,0:T(8,128)(2,1)S(1)}, u32[]{:S(2)}, u32[]{:S(2)}) collective-permute-start(bf16[32,2048]{1,0:T(8,128)(2,1)S(1)} %get-tuple-element.85), channel_id=1, source_target_pairs={{0,2},{1,3},{2,0},{3,1},{4,6},{5,7},{6,4},{7,5},{8,10},{9,11},{10,... | collective-permute-start | bytes 393224 | tf_op jit(solution)/shard_map/ppermute | solution.py:138
  57.5 6.7 %copy-start = (bf16[1,32,2048]{2,1,0:T(8,128)(2,1)S(1)}, bf16[1,32,2048]{2,1,0:T(8,128)(2,1)}, u32[]{:S(2)}) copy-start(bf16[1,32,2048]{2,1,0:T(8,128)(2,1)} %param.8) | copy-start | bytes 393220
  62.0 8.6 %collective-permute-start.23 = (bf16[32,2048]{1,0:T(8,128)(2,1)S(1)}, bf16[32,2048]{1,0:T(8,128)(2,1)S(1)}, u32[]{:S(2)}, u32[]{:S(2)}) collective-permute-start(bf16[32,2048]{1,0:T(8,128)(2,1)S(1)} %get-tuple-element.83), channel_id=1, source_target_pairs={{0,6},{1,7},{2,4},{3,5},{4,2},{5,3},{6,0},{7,1},{8,14},{9,15},{10,... | collective-permute-start | bytes 393224 | tf_op jit(solution)/shard_map/ppermute | solution.py:138
  64.3 7.2 %copy-start.1 = (bf16[1,32,2048]{2,1,0:T(8,128)(2,1)S(1)}, bf16[1,32,2048]{2,1,0:T(8,128)(2,1)}, u32[]{:S(2)}) copy-start(bf16[1,32,2048]{2,1,0:T(8,128)(2,1)} %param.10) | copy-start | bytes 393220
  64.3 7.2 %collective-permute-start.22 = (bf16[32,2048]{1,0:T(8,128)(2,1)S(1)}, bf16[32,2048]{1,0:T(8,128)(2,1)S(1)}, u32[]{:S(2)}, u32[]{:S(2)}) collective-permute-start(bf16[32,2048]{1,0:T(8,128)(2,1)S(1)} %add_convert_fusion.1), channel_id=1, source_target_pairs={{0,8},{8,16},{16,24},{24,0},{1,9},{9,17},{17,25},{25,1},{2,10},{10... | collective-permute-start | bytes 393224 | tf_op jit(solution)/shard_map/ppermute | solution.py:21
  71.5 5.1 %copy-start.2 = (bf16[32,2048]{1,0:T(8,128)(2,1)}, bf16[32,2048]{1,0:T(8,128)(2,1)S(1)}, u32[]{:S(2)}) copy-start(bf16[32,2048]{1,0:T(8,128)(2,1)S(1)} %collective-permute-done.22) | copy-start | bytes 393220
  71.6 5.0 %collective-permute-start.24 = (bf16[32,2048]{1,0:T(8,128)(2,1)S(1)}, bf16[32,2048]{1,0:T(8,128)(2,1)S(1)}, u32[]{:S(2)}, u32[]{:S(2)}) collective-permute-start(bf16[32,2048]{1,0:T(8,128)(2,1)S(1)} %add_convert_fusion), channel_id=1, source_target_pairs={{0,24},{8,0},{16,8},{24,16},{1,25},{9,1},{17,9},{25,17},{2,26},{10... | collective-permute-start | bytes 393224 | tf_op jit(solution)/shard_map/ppermute | solution.py:21
  76.6 0.6 copy-start.3

commit v13 on v11

--- a/solution.py
+++ b/solution.py
@@ -363,14 +363,15 @@
         ).astype(picks.dtype)
         scale = jnp.sum(jnp.where(grads, gate, 0.0), axis=0, keepdims=True)
         scales.append(jnp.where(is_saved, 1.0, scale))
+    for step in range(0, number, 2):
+        lanes = pl.ds(step * LANES, 2 * LANES)
+        scale = jnp.concatenate(scales[step : step + 2], axis=1)
+        rows[:, lanes] = (
+            jnp.dot(turned[...], picks[:, lanes], preferred_element_type=jnp.float32) * scale
+        ).astype(rows.dtype)
+
     leaving = []
     for step in range(number):
-        if step % 2 == 0:
-            lanes = pl.ds(step * LANES, 2 * LANES)
-            scale = jnp.concatenate(scales[step : step + 2], axis=1)
-            rows[:, lanes] = (
-                jnp.dot(turned[...], picks[:, lanes], preferred_element_type=jnp.float32) * scale
-            ).astype(rows.dtype)
         for start in range(0, half, CHUNK):
             chunk = pl.ds(start, CHUNK)
             for corner in range(start, start + CHUNK, LANES):

time: 78.1 us -> 78.1 us (level)
  Pallas kernels: 37 us -> 36 us
  waiting for transfers between devices: 16.5 us -> 17.5 us
    pallas_call x2, Pallas kernels: 9.87 us -> 8.9 us  [gradient(): pl.pallas_call(functools.partial(weight_kernel, first, number, count, slo...]
  transfers between devices with their start and end apart: 25 -> 25, of which waited for: 11 -> 13; matrix products, arithmetic and copies ran while one was open for 1% -> 1% of each run, Pallas kernels for 13% -> 11%
where the time goes in v13:
time: 78.1 us; the launch traced here: 77.9 us
  Pallas kernels  36 us (46%)
  starting transfers between devices  21.8 us (28%)
  waiting for transfers between devices  17.5 us (22%)
  local copies, waits for them, and re-layouts  1.41 us (2%)
    pallas_call x1, Pallas kernels, gathered_plan(): pl.pallas_call(functools.partial(expert_kernel, count, slots, devices, pa...  24.8 us
    ppermute x23, starting transfers between devices, swapped(): lax.ppermute(value, axes, [(source, source ^ code) for source in range(co...  18.2 us
    ppermute x23, waiting for transfers between devices, swapped(): lax.ppermute(value, axes, [(source, source ^ code) for source in range(co...  13.3 us
    pallas_call x2, Pallas kernels, gradient(): pl.pallas_call(functools.partial(weight_kernel, first, number, count, slo...  8.9 us
    ppermute x2, waiting for transfers between devices, shifted(): return lax.ppermute(value, axis, pairs)  4.13 us
    ppermute x2, starting transfers between devices, shifted(): return lax.ppermute(value, axis, pairs)  3.6 us
  transfers between devices with their start and end apart: 25, of which 13 were waited for; matrix products, arithmetic and copies ran while one was open for 1% of the time, Pallas kernels for 11%

profile of v13, /device:TPU:0, one launch (start us, length us, event | category | flops | bytes accessed | tf_op | source)
XLA Modules:
  0.0 77.9 jit_solution(547286656492590897)
XLA Ops:
  0.6 1.2 %pack.1 = (bf16[32,3200]{1,0:T(8,128)(2,1)S(1)}, bf16[32,3200]{1,0:T(8,128)(2,1)S(1)}) custom-call(bf16[32,2048]{1,0:T(8,128)(2,1)} %bitcast.69, bf16[32,2048]{1,0:T(8,128)(2,1)} %bitcast.71, bf16[32,2048]{1,0:T(8,128)(2,1)} %bitcast.70, s32[8,32]{1,0:T(8,128)} %bitcast.74, f32[8,32]{1,0:T(8,128)} %bitcast.75, s32[8,32]{1,0:T(8,128)} %bitcast.76, ...), custom_call_target="tpu_custom_call" | custom-call | tf_op jit(solution)/shard_map/pack/pallas_call | solution.py:466
  1.8 3.0 %collective-permute-start.1 = (bf16[32,3200]{1,0:T(8,128)(2,1)S(1)}, bf16[32,3200]{1,0:T(8,128)(2,1)S(1)}, u32[]{:S(2)}, u32[]{:S(2)}) collective-permute-start(bf16[32,3200]{1,0:T(8,128)(2,1)S(1)} %get-tuple-element.41.refs_0_.refs_10_), channel_id=1, source_target_pairs={{0,2},{1,3},{2,0},{3,1},{4,6},{5,7},{6,4},{7,5},{8,10},{9,11},{10,... | collective-permute-start | bytes 614408 | tf_op jit(solution)/shard_map/ppermute | solution.py:138
  4.8 0.0 collective-permute-start
  4.8 0.5 collective-permute-start.9
  5.4 1.5 %collective-permute-start.4 = (bf16[32,3200]{1,0:T(8,128)(2,1)S(1)}, bf16[32,3200]{1,0:T(8,128)(2,1)S(1)}, u32[]{:S(2)}, u32[]{:S(2)}) collective-permute-start(bf16[32,3200]{1,0:T(8,128)(2,1)S(1)} %get-tuple-element.42.refs_8_.refs_18_), channel_id=1, source_target_pairs={{0,4},{1,5},{2,6},{3,7},{4,0},{5,1},{6,2},{7,3},{8,12},{9,13},{10,... | collective-permute-start | bytes 614408 | tf_op jit(solution)/shard_map/ppermute | solution.py:138
  6.9 0.5 collective-permute-start.2
  7.4 2.5 %collective-permute-done.1.refs_2_.refs_12_ = bf16[32,3200]{1,0:T(8,128)(2,1)S(1)} collective-permute-done((bf16[32,3200]{1,0:T(8,128)(2,1)S(1)}, bf16[32,3200]{1,0:T(8,128)(2,1)S(1)}, u32[]{:S(2)}, u32[]{:S(2)}) %collective-permute-start.1) | collective-permute-done | bytes 204832 | tf_op jit(solution)/shard_map/ppermute | solution.py:138
  9.9 1.7 %collective-permute-start.3 = (bf16[32,3200]{1,0:T(8,128)(2,1)S(1)}, bf16[32,3200]{1,0:T(8,128)(2,1)S(1)}, u32[]{:S(2)}, u32[]{:S(2)}) collective-permute-start(bf16[32,3200]{1,0:T(8,128)(2,1)S(1)} %get-tuple-element.42.refs_8_.refs_18_), channel_id=1, source_target_pairs={{0,2},{1,3},{2,0},{3,1},{4,6},{5,7},{6,4},{7,5},{8,10},{9,11},{10,... | collective-permute-start | bytes 614408 | tf_op jit(solution)/shard_map/ppermute | solution.py:138
  11.7 0.0 collective-permute-done.refs_1_.refs_11_
  11.7 1.5 %collective-permute-start.7 = (bf16[32,3200]{1,0:T(8,128)(2,1)S(1)}, bf16[32,3200]{1,0:T(8,128)(2,1)S(1)}, u32[]{:S(2)}, u32[]{:S(2)}) collective-permute-start(bf16[32,3200]{1,0:T(8,128)(2,1)S(1)} %collective-permute-done.1.refs_2_.refs_12_), channel_id=1, source_target_pairs={{0,4},{1,5},{2,6},{3,7},{4,0},{5,1},{6,2},{7,3},{8,12},{9,13},{10,... | collective-permute-start | bytes 614408 | tf_op jit(solution)/shard_map/ppermute | solution.py:138
  13.2 0.0 collective-permute-done.9.refs_9_.refs_19_
  13.2 0.1 collective-permute-done.4.refs_12_.refs_22_
  13.3 0.4 collective-permute-start.12
  13.7 4.0 %collective-permute-done.2.refs_4_.refs_14_ = bf16[32,3200]{1,0:T(8,128)(2,1)S(1)} collective-permute-done((bf16[32,3200]{1,0:T(8,128)(2,1)S(1)}, bf16[32,3200]{1,0:T(8,128)(2,1)S(1)}, u32[]{:S(2)}, u32[]{:S(2)}) %collective-permute-start.2) | collective-permute-done | bytes 204832 | tf_op jit(solution)/shard_map/ppermute | solution.py:138
  17.7 0.2 collective-permute-done.3.refs_10_.refs_20_
  17.9 0.0 collective-permute-start.5
  17.9 0.5 collective-permute-start.6
  18.4 0.0 collective-permute-start.10
  18.4 2.7 %collective-permute-done.7.refs_6_.refs_16_ = bf16[32,3200]{1,0:T(8,128)(2,1)S(1)} collective-permute-done((bf16[32,3200]{1,0:T(8,128)(2,1)S(1)}, bf16[32,3200]{1,0:T(8,128)(2,1)S(1)}, u32[]{:S(2)}, u32[]{:S(2)}) %collective-permute-start.7) | collective-permute-done | bytes 204832 | tf_op jit(solution)/shard_map/ppermute | solution.py:138
  21.1 0.0 collective-permute-start.11
  21.1 0.0 collective-permute-done.12.refs_14_.refs_24_
  21.1 0.5 collective-permute-start.8
  21.6 0.0 collective-permute-done.5.refs_3_.refs_13_
  21.6 0.1 collective-permute-start.13
  21.7 0.1 stack.47.place_ref
  21.8 0.0 collective-permute-done.6.refs_5_.refs_15_
  21.8 0.0 collective-permute-done.10.refs_11_.refs_21_
  21.8 0.8 collective-permute-done.11.refs_13_.refs_23_
  22.6 0.3 collective-permute-done.8.refs_7_.refs_17_
  22.9 0.3 collective-permute-done.13.refs_15_.refs_25_
  23.2 1.1 %slot_picks.1 = (bf16[384,256]{1,0:T(8,128)(2,1)S(1)}, f32[384,128]{1,0:T(8,128)S(1)}, bf16[256,384]{1,0:T(8,128)(2,1)S(1)}, bf16[384,256]{1,0:T(8,128)(2,1)S(1)...) custom-call(s32[11]{0:T(128)S(1)} %stack.47.place_ref, ...), custom_call_target="tpu_custom_call" | custom-call | bytes 1024 | tf_op jit(solution)/shard_map/slot_picks/pallas_call | solution.py:520
  24.3 24.8 %experts.1 = (bf16[32,2048]{1,0:T(8,128)(2,1)S(1)}, bf16[32,2048]{1,0:T(8,128)(2,1)S(1)}, bf16[32,2048]{1,0:T(8,128)(2,1)S(1)}, bf16[32,2048]{1,0:T(8,128)(2,1)S...) custom-call(s32[11]{0:T(128)S(1)} %stack.47.place_ref, ...), custom_call_target="tpu_custom_call" | custom-call | flops 12884901888 | bytes 25165824 | tf_op jit(solution)/shard_map/experts/pallas_call | solution.py:542
  49.1 0.2 collective-permute-start.14
  49.3 1.7 %collective-permute-done.14 = bf16[4,32,2048]{2,1,0:T(8,128)(2,1)S(1)} collective-permute-done((bf16[4,32,2048]{2,1,0:T(8,128)(2,1)S(1)}, bf16[4,32,2048]{2,1,0:T(8,128)(2,1)S(1)}, u32[]{:S(2)}, u32[]{:S(2)}) %collective-permute-start.14) | collective-permute-done | bytes 524320 | tf_op jit(solution)/shard_map/ppermute | solution.py:138
  51.0 0.2 collective-permute-start.18
  51.2 0.3 collective-permute-start.19
  51.5 0.1 fusion.7
  51.6 1.6 %collective-permute-start.17 = (bf16[32,2048]{1,0:T(8,128)(2,1)S(1)}, bf16[32,2048]{1,0:T(8,128)(2,1)S(1)}, u32[]{:S(2)}, u32[]{:S(2)}) collective-permute-start(bf16[32,2048]{1,0:T(8,128)(2,1)S(1)} %get-tuple-element.84), channel_id=1, source_target_pairs={{0,6},{1,7},{2,4},{3,5},{4,2},{5,3},{6,0},{7,1},{8,14},{9,15},{10,... | collective-permute-start | bytes 393224 | tf_op jit(solution)/shard_map/ppermute | solution.py:138
  53.3 0.5 collective-permute-start.16
  53.8 1.4 %collective-permute-start.15 = (bf16[32,2048]{1,0:T(8,128)(2,1)S(1)}, bf16[32,2048]{1,0:T(8,128)(2,1)S(1)}, u32[]{:S(2)}, u32[]{:S(2)}) collective-permute-start(bf16[32,2048]{1,0:T(8,128)(2,1)S(1)} %get-tuple-element.86), channel_id=1, source_target_pairs={{0,2},{1,3},{2,0},{3,1},{4,6},{5,7},{6,4},{7,5},{8,10},{9,11},{10,... | collective-permute-start | bytes 393224 | tf_op jit(solution)/shard_map/ppermute | solution.py:138
  55.2 0.0 collective-permute-done.19
  55.2 0.0 collective-permute-done.18.refs_1_
  55.2 0.1 fusion
  55.3 1.6 %collective-permute-start.21 = (bf16[32,2048]{1,0:T(8,128)(2,1)S(1)}, bf16[32,2048]{1,0:T(8,128)(2,1)S(1)}, u32[]{:S(2)}, u32[]{:S(2)}) collective-permute-start(bf16[32,2048]{1,0:T(8,128)(2,1)S(1)} %get-tuple-element.80), channel_id=1, source_target_pairs={{0,4},{1,5},{2,6},{3,7},{4,0},{5,1},{6,2},{7,3},{8,12},{9,13},{10,... | collective-permute-start | bytes 393224 | tf_op jit(solution)/shard_map/ppermute | solution.py:138
  56.9 0.6 collective-permute-start.20
  57.5 4.5 %weight_gradient_0.1.refs_3_ = bf16[16,1024,768]{2,1,0:T(8,128)(2,1)} custom-call(s32[11]{0:T(128)S(1)} %stack.47.place_ref, f32[256,128]{1,0:T(8,128)S(1)} %get-tuple-element.60.refs_0_, bf16[8,96,768]{2,1,0:T(8,128)(2,1)S(1)} %collective-permute-done.18.refs_1_, bf16[1024,512]{1,0:T(8,128)(2,1)S(1)} %get-tuple-element.63.refs_2_, ...), custom_call_target="tpu_custom_call", output_to_operand_aliasing={{}: (4, {})} | custom-call | flops 3221225472 | bytes 12582912 | tf_op jit(solution)/shard_map/weight_gradient_0/pallas_call | solution.py:588
  62.0 0.0 collective-permute-done.17
  62.0 1.4 %collective-permute-start.23 = (bf16[32,2048]{1,0:T(8,128)(2,1)S(1)}, bf16[32,2048]{1,0:T(8,128)(2,1)S(1)}, u32[]{:S(2)}, u32[]{:S(2)}) collective-permute-start(bf16[32,2048]{1,0:T(8,128)(2,1)S(1)} %get-tuple-element.79), channel_id=1, source_target_pairs={{0,6},{1,7},{2,4},{3,5},{4,2},{5,3},{6,0},{7,1},{8,14},{9,15},{10,... | collective-permute-start | bytes 393224 | tf_op jit(solution)/shard_map/ppermute | solution.py:138
  63.4 0.0 collective-permute-done.16
  63.4 0.0 collective-permute-done.15
  63.4 0.4 collective-permute-done.21
  63.9 0.3 collective-permute-done.20
  64.2 0.0 copy-done
  64.2 0.1 add_convert_fusion.1
  64.3 0.0 copy-start.1
  64.3 1.8 %collective-permute-start.22 = (bf16[32,2048]{1,0:T(8,128)(2,1)S(1)}, bf16[32,2048]{1,0:T(8,128)(2,1)S(1)}, u32[]{:S(2)}, u32[]{:S(2)}) collective-permute-start(bf16[32,2048]{1,0:T(8,128)(2,1)S(1)} %add_convert_fusion.1), channel_id=1, source_target_pairs={{0,8},{8,16},{16,24},{24,0},{1,9},{9,17},{17,25},{25,1},{2,10},{10... | collective-permute-start | bytes 393224 | tf_op jit(solution)/shard_map/ppermute | solution.py:21
  66.1 4.4 %weight_gradient_4.1 = bf16[16,1024,768]{2,1,0:T(8,128)(2,1)} custom-call(s32[11]{0:T(128)S(1)} %stack.47.place_ref, f32[256,128]{1,0:T(8,128)S(1)} %get-tuple-element.60.refs_0_, bf16[8,96,768]{2,1,0:T(8,128)(2,1)S(1)} %collective-permute-done.18.refs_1_, bf16[1024,512]{1,0:T(8,128)(2,1)S(1)} %get-tuple-element.63.refs_2_, ...), custom_call_target="tpu_custom_call", output_to_operand_aliasing={{}: (4, {})} | custom-call | flops 3221225472 | bytes 12582912 | tf_op jit(solution)/shard_map/weight_gradient_4/pallas_call | solution.py:588
  70.6 0.0 collective-permute-done.23
  70.6 0.9 %collective-permute-done.22 = bf16[32,2048]{1,0:T(8,128)(2,1)S(1)} collective-permute-done((bf16[32,2048]{1,0:T(8,128)(2,1)S(1)}, bf16[32,2048]{1,0:T(8,128)(2,1)S(1)}, u32[]{:S(2)}, u32[]{:S(2)}) %collective-permute-start.22) | collective-permute-done | bytes 131104 | tf_op jit(solution)/shard_map/ppermute | solution.py:21
  71.5 0.1 add_convert_fusion
  71.6 1.8 %collective-permute-start.24 = (bf16[32,2048]{1,0:T(8,128)(2,1)S(1)}, bf16[32,2048]{1,0:T(8,128)(2,1)S(1)}, u32[]{:S(2)}, u32[]{:S(2)}) collective-permute-start(bf16[32,2048]{1,0:T(8,128)(2,1)S(1)} %add_convert_fusion), channel_id=1, source_target_pairs={{0,24},{8,0},{16,8},{24,16},{1,25},{9,1},{17,9},{25,17},{2,26},{10... | collective-permute-start | bytes 393224 | tf_op jit(solution)/shard_map/ppermute | solution.py:21
  73.4 3.2 %collective-permute-done.24 = bf16[32,2048]{1,0:T(8,128)(2,1)S(1)} collective-permute-done((bf16[32,2048]{1,0:T(8,128)(2,1)S(1)}, bf16[32,2048]{1,0:T(8,128)(2,1)S(1)}, u32[]{:S(2)}, u32[]{:S(2)}) %collective-permute-start.24) | collective-permute-done | bytes 131104 | tf_op jit(solution)/shard_map/ppermute | solution.py:21
  76.6 0.7 copy.17
  77.3 0.7 copy.18
  (2 shorter events, 0.0 us)
Async XLA Ops:
  1.8 8.1 %collective-permute-start.1 = (bf16[32,3200]{1,0:T(8,128)(2,1)S(1)}, bf16[32,3200]{1,0:T(8,128)(2,1)S(1)}, u32[]{:S(2)}, u32[]{:S(2)}) collective-permute-start(bf16[32,3200]{1,0:T(8,128)(2,1)S(1)} %get-tuple-element.41.refs_0_.refs_10_), channel_id=1, source_target_pairs={{0,2},{1,3},{2,0},{3,1},{4,6},{5,7},{6,4},{7,5},{8,10},{9,11},{10,... | collective-permute-start | bytes 614408 | tf_op jit(solution)/shard_map/ppermute | solution.py:138
  4.8 6.8 %collective-permute-start = (bf16[32,3200]{1,0:T(8,128)(2,1)S(1)}, bf16[32,3200]{1,0:T(8,128)(2,1)S(1)}, u32[]{:S(2)}, u32[]{:S(2)}) collective-permute-start(bf16[32,3200]{1,0:T(8,128)(2,1)S(1)} %get-tuple-element.41.refs_0_.refs_10_), channel_id=1, source_target_pairs={{0,1},{1,0},{2,3},{3,2},{4,5},{5,4},{6,7},{7,6},{8,9},{9,8},{10,11... | collective-permute-start | bytes 614408 | tf_op jit(solution)/shard_map/ppermute | solution.py:138
  4.8 8.4 %collective-permute-start.9 = (bf16[32,3200]{1,0:T(8,128)(2,1)S(1)}, bf16[32,3200]{1,0:T(8,128)(2,1)S(1)}, u32[]{:S(2)}, u32[]{:S(2)}) collective-permute-start(bf16[32,3200]{1,0:T(8,128)(2,1)S(1)} %get-tuple-element.42.refs_8_.refs_18_), channel_id=1, source_target_pairs={{0,1},{1,0},{2,3},{3,2},{4,5},{5,4},{6,7},{7,6},{8,9},{9,8},{10,11... | collective-permute-start | bytes 614408 | tf_op jit(solution)/shard_map/ppermute | solution.py:138
  5.4 7.9 %collective-permute-start.4 = (bf16[32,3200]{1,0:T(8,128)(2,1)S(1)}, bf16[32,3200]{1,0:T(8,128)(2,1)S(1)}, u32[]{:S(2)}, u32[]{:S(2)}) collective-permute-start(bf16[32,3200]{1,0:T(8,128)(2,1)S(1)} %get-tuple-element.42.refs_8_.refs_18_), channel_id=1, source_target_pairs={{0,4},{1,5},{2,6},{3,7},{4,0},{5,1},{6,2},{7,3},{8,12},{9,13},{10,... | collective-permute-start | bytes 614408 | tf_op jit(solution)/shard_map/ppermute | solution.py:138
  6.9 10.8 %collective-permute-start.2 = (bf16[32,3200]{1,0:T(8,128)(2,1)S(1)}, bf16[32,3200]{1,0:T(8,128)(2,1)S(1)}, u32[]{:S(2)}, u32[]{:S(2)}) collective-permute-start(bf16[32,3200]{1,0:T(8,128)(2,1)S(1)} %get-tuple-element.41.refs_0_.refs_10_), channel_id=1, source_target_pairs={{0,4},{1,5},{2,6},{3,7},{4,0},{5,1},{6,2},{7,3},{8,12},{9,13},{10,... | collective-permute-start | bytes 614408 | tf_op jit(solution)/shard_map/ppermute | solution.py:138
  9.9 8.0 %collective-permute-start.3 = (bf16[32,3200]{1,0:T(8,128)(2,1)S(1)}, bf16[32,3200]{1,0:T(8,128)(2,1)S(1)}, u32[]{:S(2)}, u32[]{:S(2)}) collective-permute-start(bf16[32,3200]{1,0:T(8,128)(2,1)S(1)} %get-tuple-element.42.refs_8_.refs_18_), channel_id=1, source_target_pairs={{0,2},{1,3},{2,0},{3,1},{4,6},{5,7},{6,4},{7,5},{8,10},{9,11},{10,... | collective-permute-start | bytes 614408 | tf_op jit(solution)/shard_map/ppermute | solution.py:138
  11.7 9.5 %collective-permute-start.7 = (bf16[32,3200]{1,0:T(8,128)(2,1)S(1)}, bf16[32,3200]{1,0:T(8,128)(2,1)S(1)}, u32[]{:S(2)}, u32[]{:S(2)}) collective-permute-start(bf16[32,3200]{1,0:T(8,128)(2,1)S(1)} %collective-permute-done.1.refs_2_.refs_12_), channel_id=1, source_target_pairs={{0,4},{1,5},{2,6},{3,7},{4,0},{5,1},{6,2},{7,3},{8,12},{9,13},{10,... | collective-permute-start | bytes 614408 | tf_op jit(solution)/shard_map/ppermute | solution.py:138
  13.3 7.8 %collective-permute-start.12 = (bf16[32,3200]{1,0:T(8,128)(2,1)S(1)}, bf16[32,3200]{1,0:T(8,128)(2,1)S(1)}, u32[]{:S(2)}, u32[]{:S(2)}) collective-permute-start(bf16[32,3200]{1,0:T(8,128)(2,1)S(1)} %collective-permute-done.4.refs_12_.refs_22_), channel_id=1, source_target_pairs={{0,2},{1,3},{2,0},{3,1},{4,6},{5,7},{6,4},{7,5},{8,10},{9,11},{10,... | collective-permute-start | bytes 614408 | tf_op jit(solution)/shard_map/ppermute | solution.py:138
  17.9 3.7 %collective-permute-start.5 = (bf16[32,3200]{1,0:T(8,128)(2,1)S(1)}, bf16[32,3200]{1,0:T(8,128)(2,1)S(1)}, u32[]{:S(2)}, u32[]{:S(2)}) collective-permute-start(bf16[32,3200]{1,0:T(8,128)(2,1)S(1)} %collective-permute-done.1.refs_2_.refs_12_), channel_id=1, source_target_pairs={{0,1},{1,0},{2,3},{3,2},{4,5},{5,4},{6,7},{7,6},{8,9},{9,8},{10,11... | collective-permute-start | bytes 614408 | tf_op jit(solution)/shard_map/ppermute | solution.py:138
  17.9 3.9 %collective-permute-start.6 = (bf16[32,3200]{1,0:T(8,128)(2,1)S(1)}, bf16[32,3200]{1,0:T(8,128)(2,1)S(1)}, u32[]{:S(2)}, u32[]{:S(2)}) collective-permute-start(bf16[32,3200]{1,0:T(8,128)(2,1)S(1)} %collective-permute-done.2.refs_4_.refs_14_), channel_id=1, source_target_pairs={{0,1},{1,0},{2,3},{3,2},{4,5},{5,4},{6,7},{7,6},{8,9},{9,8},{10,11... | collective-permute-start | bytes 614408 | tf_op jit(solution)/shard_map/ppermute | solution.py:138
  18.4 3.4 %collective-permute-start.10 = (bf16[32,3200]{1,0:T(8,128)(2,1)S(1)}, bf16[32,3200]{1,0:T(8,128)(2,1)S(1)}, u32[]{:S(2)}, u32[]{:S(2)}) collective-permute-start(bf16[32,3200]{1,0:T(8,128)(2,1)S(1)} %collective-permute-done.3.refs_10_.refs_20_), channel_id=1, source_target_pairs={{0,1},{1,0},{2,3},{3,2},{4,5},{5,4},{6,7},{7,6},{8,9},{9,8},{10,11... | collective-permute-start | bytes 614408 | tf_op jit(solution)/shard_map/ppermute | solution.py:138
  21.1 1.5 %collective-permute-start.11 = (bf16[32,3200]{1,0:T(8,128)(2,1)S(1)}, bf16[32,3200]{1,0:T(8,128)(2,1)S(1)}, u32[]{:S(2)}, u32[]{:S(2)}) collective-permute-start(bf16[32,3200]{1,0:T(8,128)(2,1)S(1)} %collective-permute-done.4.refs_12_.refs_22_), channel_id=1, source_target_pairs={{0,1},{1,0},{2,3},{3,2},{4,5},{5,4},{6,7},{7,6},{8,9},{9,8},{10,11... | collective-permute-start | bytes 614408 | tf_op jit(solution)/shard_map/ppermute | solution.py:138
  21.1 1.7 %collective-permute-start.8 = (bf16[32,3200]{1,0:T(8,128)(2,1)S(1)}, bf16[32,3200]{1,0:T(8,128)(2,1)S(1)}, u32[]{:S(2)}, u32[]{:S(2)}) collective-permute-start(bf16[32,3200]{1,0:T(8,128)(2,1)S(1)} %collective-permute-done.7.refs_6_.refs_16_), channel_id=1, source_target_pairs={{0,1},{1,0},{2,3},{3,2},{4,5},{5,4},{6,7},{7,6},{8,9},{9,8},{10,11... | collective-permute-start | bytes 614408 | tf_op jit(solution)/shard_map/ppermute | solution.py:138
  21.6 1.5 %collective-permute-start.13 = (bf16[32,3200]{1,0:T(8,128)(2,1)S(1)}, bf16[32,3200]{1,0:T(8,128)(2,1)S(1)}, u32[]{:S(2)}, u32[]{:S(2)}) collective-permute-start(bf16[32,3200]{1,0:T(8,128)(2,1)S(1)} %collective-permute-done.12.refs_14_.refs_24_), channel_id=1, source_target_pairs={{0,1},{1,0},{2,3},{3,2},{4,5},{5,4},{6,7},{7,6},{8,9},{9,8},{10,11... | collective-permute-start | bytes 614408 | tf_op jit(solution)/shard_map/ppermute | solution.py:138
  49.1 1.9 %collective-permute-start.14 = (bf16[4,32,2048]{2,1,0:T(8,128)(2,1)S(1)}, bf16[4,32,2048]{2,1,0:T(8,128)(2,1)S(1)}, u32[]{:S(2)}, u32[]{:S(2)}) collective-permute-start(bf16[4,32,2048]{2,1,0:T(8,128)(2,1)S(1)} %get-tuple-element.56), channel_id=1, source_target_pairs={{0,1},{1,0},{2,3},{3,2},{4,5},{5,4},{6,7},{7,6},{8,9},{9,8},{10,11... | collective-permute-start | bytes 1572872 | tf_op jit(solution)/shard_map/ppermute | solution.py:138
  51.0 4.2 %collective-permute-start.18 = (bf16[8,96,768]{2,1,0:T(8,128)(2,1)S(1)}, bf16[8,96,768]{2,1,0:T(8,128)(2,1)S(1)}, u32[]{:S(2)}, u32[]{:S(2)}) collective-permute-start(bf16[8,96,768]{2,1,0:T(8,128)(2,1)S(1)} %get-tuple-element.62), channel_id=1, source_target_pairs={{0,1},{1,0},{2,3},{3,2},{4,5},{5,4},{6,7},{7,6},{8,9},{9,8},{10,11... | collective-permute-start | bytes 3538952 | tf_op jit(solution)/shard_map/ppermute | solution.py:138
  51.2 4.0 %collective-permute-start.19 = (bf16[4,32,2048]{2,1,0:T(8,128)(2,1)S(1)}, bf16[4,32,2048]{2,1,0:T(8,128)(2,1)S(1)}, u32[]{:S(2)}, u32[]{:S(2)}) collective-permute-start(bf16[4,32,2048]{2,1,0:T(8,128)(2,1)S(1)} %get-tuple-element.66), channel_id=1, source_target_pairs={{0,1},{1,0},{2,3},{3,2},{4,5},{5,4},{6,7},{7,6},{8,9},{9,8},{10,11... | collective-permute-start | bytes 1572872 | tf_op jit(solution)/shard_map/ppermute | solution.py:138
  51.6 10.3 %collective-permute-start.17 = (bf16[32,2048]{1,0:T(8,128)(2,1)S(1)}, bf16[32,2048]{1,0:T(8,128)(2,1)S(1)}, u32[]{:S(2)}, u32[]{:S(2)}) collective-permute-start(bf16[32,2048]{1,0:T(8,128)(2,1)S(1)} %get-tuple-element.84), channel_id=1, source_target_pairs={{0,6},{1,7},{2,4},{3,5},{4,2},{5,3},{6,0},{7,1},{8,14},{9,15},{10,... | collective-permute-start | bytes 393224 | tf_op jit(solution)/shard_map/ppermute | solution.py:138
  53.3 10.2 %collective-permute-start.16 = (bf16[32,2048]{1,0:T(8,128)(2,1)S(1)}, bf16[32,2048]{1,0:T(8,128)(2,1)S(1)}, u32[]{:S(2)}, u32[]{:S(2)}) collective-permute-start(bf16[32,2048]{1,0:T(8,128)(2,1)S(1)} %get-tuple-element.85), channel_id=1, source_target_pairs={{0,4},{1,5},{2,6},{3,7},{4,0},{5,1},{6,2},{7,3},{8,12},{9,13},{10,... | collective-permute-start | bytes 393224 | tf_op jit(solution)/shard_map/ppermute | solution.py:138
  53.8 9.7 %collective-permute-start.15 = (bf16[32,2048]{1,0:T(8,128)(2,1)S(1)}, bf16[32,2048]{1,0:T(8,128)(2,1)S(1)}, u32[]{:S(2)}, u32[]{:S(2)}) collective-permute-start(bf16[32,2048]{1,0:T(8,128)(2,1)S(1)} %get-tuple-element.86), channel_id=1, source_target_pairs={{0,2},{1,3},{2,0},{3,1},{4,6},{5,7},{6,4},{7,5},{8,10},{9,11},{10,... | collective-permute-start | bytes 393224 | tf_op jit(solution)/shard_map/ppermute | solution.py:138
  55.3 8.5 %collective-permute-start.21 = (bf16[32,2048]{1,0:T(8,128)(2,1)S(1)}, bf16[32,2048]{1,0:T(8,128)(2,1)S(1)}, u32[]{:S(2)}, u32[]{:S(2)}) collective-permute-start(bf16[32,2048]{1,0:T(8,128)(2,1)S(1)} %get-tuple-element.80), channel_id=1, source_target_pairs={{0,4},{1,5},{2,6},{3,7},{4,0},{5,1},{6,2},{7,3},{8,12},{9,13},{10,... | collective-permute-start | bytes 393224 | tf_op jit(solution)/shard_map/ppermute | solution.py:138
  56.9 7.3 %collective-permute-start.20 = (bf16[32,2048]{1,0:T(8,128)(2,1)S(1)}, bf16[32,2048]{1,0:T(8,128)(2,1)S(1)}, u32[]{:S(2)}, u32[]{:S(2)}) collective-permute-start(bf16[32,2048]{1,0:T(8,128)(2,1)S(1)} %get-tuple-element.81), channel_id=1, source_target_pairs={{0,2},{1,3},{2,0},{3,1},{4,6},{5,7},{6,4},{7,5},{8,10},{9,11},{10,... | collective-permute-start | bytes 393224 | tf_op jit(solution)/shard_map/ppermute | solution.py:138
  57.5 6.7 %copy-start = (bf16[1,32,2048]{2,1,0:T(8,128)(2,1)S(1)}, bf16[1,32,2048]{2,1,0:T(8,128)(2,1)}, u32[]{:S(2)}) copy-start(bf16[1,32,2048]{2,1,0:T(8,128)(2,1)} %param.8) | copy-start | bytes 393220
  62.0 8.6 %collective-permute-start.23 = (bf16[32,2048]{1,0:T(8,128)(2,1)S(1)}, bf16[32,2048]{1,0:T(8,128)(2,1)S(1)}, u32[]{:S(2)}, u32[]{:S(2)}) collective-permute-start(bf16[32,2048]{1,0:T(8,128)(2,1)S(1)} %get-tuple-element.79), channel_id=1, source_target_pairs={{0,6},{1,7},{2,4},{3,5},{4,2},{5,3},{6,0},{7,1},{8,14},{9,15},{10,... | collective-permute-start | bytes 393224 | tf_op jit(solution)/shard_map/ppermute | solution.py:138
  64.3 7.2 %copy-start.1 = (bf16[1,32,2048]{2,1,0:T(8,128)(2,1)S(1)}, bf16[1,32,2048]{2,1,0:T(8,128)(2,1)}, u32[]{:S(2)}) copy-start(bf16[1,32,2048]{2,1,0:T(8,128)(2,1)} %param.10) | copy-start | bytes 393220
  64.3 7.2 %collective-permute-start.22 = (bf16[32,2048]{1,0:T(8,128)(2,1)S(1)}, bf16[32,2048]{1,0:T(8,128)(2,1)S(1)}, u32[]{:S(2)}, u32[]{:S(2)}) collective-permute-start(bf16[32,2048]{1,0:T(8,128)(2,1)S(1)} %add_convert_fusion.1), channel_id=1, source_target_pairs={{0,8},{8,16},{16,24},{24,0},{1,9},{9,17},{17,25},{25,1},{2,10},{10... | collective-permute-start | bytes 393224 | tf_op jit(solution)/shard_map/ppermute | solution.py:21
  71.6 5.0 %collective-permute-start.24 = (bf16[32,2048]{1,0:T(8,128)(2,1)S(1)}, bf16[32,2048]{1,0:T(8,128)(2,1)S(1)}, u32[]{:S(2)}, u32[]{:S(2)}) collective-permute-start(bf16[32,2048]{1,0:T(8,128)(2,1)S(1)} %add_convert_fusion), channel_id=1, source_target_pairs={{0,24},{8,0},{16,8},{24,16},{1,25},{9,1},{17,9},{25,17},{2,26},{10... | collective-permute-start | bytes 393224 | tf_op jit(solution)/shard_map/ppermute | solution.py:21
